TPU v7x, 32 devices: a whole 2x2x4 slice. The times are simulated.
32 devices in a mesh: seq: 16 (over z, y, x), head: 2 (over core).
Axes of the slice: x: 2, y: 2, z: 4, core: 2. Of those that a mesh axis runs over, the one named last changes fastest.
Arguments:
- resid_in: bfloat16 [1, 4096, 1536], P(None, 'seq'), may hold values from -6 to 6
- cotangent: bfloat16 [1, 4096, 1536], P(None, 'seq'), may hold values from -6 to 6
- norm_gain: bfloat16 [2, 1536], replicated, may hold values from 0.5 to 1.5
- w_zx: bfloat16 [2, 2, 1536, 3072], P(None, None, 'seq', 'head'), may hold values from -0.15625 to 0.15625
- w_dt: bfloat16 [2, 1536, 48], P(None, 'seq', 'head'), may hold values from -0.15625 to 0.15625
- w_bc: bfloat16 [2, 1536, 256], P(None, 'seq'), may hold values from -0.15625 to 0.15625
- conv_x: bfloat16 [2, 5, 3072], P(None, None, 'head'), may hold values from -0.5 to 0.5
- conv_bc: bfloat16 [2, 5, 256], replicated, may hold values from -0.5 to 0.5
- head_params: float32 [2, 3, 48], P(None, None, 'head'), may hold values from -15 to 3, as said below
- gated_gain: bfloat16 [2, 3072], P(None, 'head'), may hold values from 0.5 to 1.5
- w_out: bfloat16 [2, 3072, 1536], P(None, 'head', 'seq'), may hold values from -0.109375 to 0.109375
Outputs:
- block_out: bfloat16 [1, 4096, 1536], P(None, 'seq')
- grad_input: bfloat16 [1, 4096, 1536], P(None, 'seq')
- grad_norm_gain: bfloat16 [2, 1536], replicated
- grad_w_zx: bfloat16 [2, 2, 1536, 3072], P(None, None, 'seq', 'head')
- grad_w_dt: bfloat16 [2, 1536, 48], P(None, 'seq', 'head')
- grad_w_bc: bfloat16 [2, 1536, 256], P(None, 'seq')
- grad_conv_x: bfloat16 [2, 5, 3072], P(None, None, 'head')
- grad_conv_bc: bfloat16 [2, 5, 256], replicated
- grad_head_params: bfloat16 [2, 3, 48], P(None, None, 'head')
- grad_gated_gain: bfloat16 [2, 3072], P(None, 'head')
- grad_w_out: bfloat16 [2, 3072, 1536], P(None, 'head', 'seq')
Inputs may be any that keep to these rules, and one draw needn't show every extreme that they name: `head_params`: row 0 of each layer holds the logarithm of each head's decay rate, which lies between 0 and log(16); row 1 holds the time-step biases; row 2 the skip gains, between 0.2 and 1.
All inputs are finite; a program needn't handle non-finite values.
Results may differ from a plain program's by a relative error of at most 0.03.
Values may be sent and summed in bfloat16 or wider, within the bound.
A program may use at most 256 MiB of HBM per device.

v0:
```python
import jax
import jax.numpy as jnp
from jax import lax
from jax.sharding import PartitionSpec as P

HEADDIM = 64
STATE = 128
CONV = 4
INNER = 3072


epsilon = 1e-05
highest = lax.Precision.HIGHEST


def passed_along(block, axis, distance):
    devices = range(lax.axis_size(axis))
    route = [(i - distance, i) for i in devices if i - distance in devices]
    return lax.ppermute(block, axis, route)


def entering(shard, axis, join, neutral, backward):
    count = lax.axis_size(axis)
    place = lax.axis_index(axis)
    ahead = count - 1 - place if backward else place
    gathered = jax.tree.map(
        lambda a, kind: lax.all_gather(a.astype(kind), axis), shard, (jnp.bfloat16, jnp.bfloat16)
    )
    state = jax.tree.map(lambda a, e: jnp.zeros_like(a) + jnp.asarray(e, a.dtype), shard, neutral)

    def one(turn, state):
        source = count - 1 - turn if backward else turn
        return join(
            state,
            jax.tree.map(
                lambda a, own: lax.dynamic_index_in_dim(a, source, 0, False).astype(own.dtype),
                gathered,
                shard,
            ),
        )

    return lax.fori_loop(0, ahead, one, state)


def silu_slope(values):
    sigmoid_val = jax.nn.sigmoid(values)
    return sigmoid_val * (1.0 + values * (1.0 - sigmoid_val))


def combine_states(earlier_item, later_item):
    return (
        earlier_item[0] * later_item[0],
        later_item[1] + later_item[0][..., None, None] * earlier_item[1],
    )


def causal_conv(local_vals, edge_vals, weights):
    length = local_vals.shape[1]
    extended = jnp.concatenate([edge_vals, local_vals], axis=1).astype(jnp.float32)
    weights = weights.astype(jnp.float32)
    running = jnp.broadcast_to(weights[CONV], local_vals.shape)
    for offset in range(CONV):
        running = running + weights[offset] * extended[:, offset : offset + length]
    return (running, extended)


def conv_backward(d_pre, extended, weights):
    length = d_pre.shape[1]
    weights = weights.astype(jnp.float32)
    d_ext = jnp.zeros(extended.shape, jnp.float32)
    grad_rows = []
    for offset in range(CONV):
        d_ext = d_ext.at[:, offset : offset + length].add(weights[offset] * d_pre)
        grad_rows.append(jnp.sum(d_pre * extended[:, offset : offset + length], axis=(0, 1)))
    grad_rows.append(jnp.sum(d_pre, axis=(0, 1)))
    return (d_ext, jnp.stack(grad_rows))


def decay_tables(cum_log, step_size):
    length = cum_log.shape[1]
    row_ids = lax.broadcasted_iota(jnp.int32, (length, length), 0)
    col_ids = lax.broadcasted_iota(jnp.int32, (length, length), 1)
    causal = (col_ids <= row_ids)[None, :, :, None]
    log_gap = cum_log[:, :, None, :] - cum_log[:, None, :, :]
    decay_in = jnp.where(causal, jnp.exp(jnp.where(causal, log_gap, 0.0)), 0.0)
    weights_tk = decay_in * step_size[:, None, :, :]
    to_end = jnp.exp(cum_log[:, -1:, :] - cum_log)
    return (decay_in, weights_tk, to_end)


def forward_layer(residual, local_params, full_weights):
    gain_in, conv_xw, conv_bcw, head_vals, gate_gain = local_params
    w_zx, w_dt, w_bc, w_out = full_weights
    seq_count, length, model_width = residual.shape
    flat_in = residual.reshape(seq_count * length, model_width)
    inv_rms = lax.rsqrt(jnp.mean(flat_in * flat_in, axis=-1, keepdims=True) + epsilon)
    normed = (flat_in * inv_rms * gain_in.astype(jnp.float32)).astype(jnp.bfloat16)
    z_proj = jnp.dot(normed, w_zx[0], preferred_element_type=jnp.float32).astype(jnp.bfloat16)
    x_proj = jnp.dot(normed, w_zx[1], preferred_element_type=jnp.float32).astype(jnp.bfloat16)
    dt_raw = jnp.dot(normed, w_dt, preferred_element_type=jnp.float32).astype(jnp.bfloat16)
    bc_proj = jnp.dot(normed, w_bc, preferred_element_type=jnp.float32).astype(jnp.bfloat16)
    inner_local = x_proj.shape[1]
    x_seq = x_proj.reshape(seq_count, length, inner_local)
    bc_seq = bc_proj.reshape(seq_count, length, 2 * STATE)
    tail_rows = jnp.concatenate(
        [x_seq[:, length - CONV + 1 :], bc_seq[:, length - CONV + 1 :]], axis=2
    )
    edge_rows = passed_along(tail_rows, "seq", 1)
    pre_x, ext_x = causal_conv(x_seq, edge_rows[..., :inner_local], conv_xw)
    pre_bc, ext_bc = causal_conv(bc_seq, edge_rows[..., inner_local:], conv_bcw)
    x_low = jax.nn.silu(pre_x).astype(jnp.bfloat16)
    bc_low = jax.nn.silu(pre_bc).astype(jnp.bfloat16)
    b_low = bc_low[..., :STATE]
    c_low = bc_low[..., STATE:]
    heads_local = head_vals.shape[1]
    x_heads = x_low.reshape(seq_count, length, heads_local, HEADDIM)
    step_size = jax.nn.softplus(dt_raw.astype(jnp.float32) + head_vals[1]).reshape(
        seq_count, length, heads_local
    )
    decay_rate = -jnp.exp(head_vals[0])
    cum_log = jnp.cumsum(step_size * decay_rate, axis=1)
    decay_in, weights_tk, to_end = decay_tables(cum_log, step_size)
    inner_cb = jnp.einsum("stn,skn->stk", c_low, b_low, preferred_element_type=jnp.float32)
    scores = (inner_cb[..., None] * weights_tk).astype(jnp.bfloat16)
    y_local = jnp.einsum("stkh,skhp->sthp", scores, x_heads, preferred_element_type=jnp.float32)
    weighted = (x_heads * (to_end * step_size)[..., None]).astype(jnp.bfloat16)
    local_state = jnp.einsum("skhp,skn->shpn", weighted, b_low, preferred_element_type=jnp.float32)
    total_decay = jnp.exp(cum_log[:, -1])
    identity = (jnp.ones_like(total_decay), jnp.zeros_like(local_state))
    prior_state = entering((total_decay, local_state), "seq", combine_states, identity, False)
    state_in = prior_state[1]
    c_decay = (jnp.exp(cum_log)[..., None] * c_low[:, :, None, :]).astype(jnp.bfloat16)
    y_carry = jnp.einsum(
        "sthn,shpn->sthp",
        c_decay,
        state_in.astype(jnp.bfloat16),
        preferred_element_type=jnp.float32,
    )
    y_full = y_local + y_carry + head_vals[2][:, None] * x_heads
    y_flat = y_full.reshape(seq_count * length, inner_local)
    gate_act = jax.nn.silu(z_proj.astype(jnp.float32))
    gated_vals = y_flat * gate_act
    total_sq = lax.psum(jnp.sum(gated_vals * gated_vals, axis=-1), "head")
    inv_gate = lax.rsqrt(total_sq / INNER + epsilon)[:, None]
    normed_out = (gated_vals * inv_gate * gate_gain.astype(jnp.float32)).astype(jnp.bfloat16)
    mixed = lax.psum(jnp.dot(normed_out, w_out, preferred_element_type=jnp.float32), "head")
    saved_vals = (
        flat_in,
        inv_rms,
        normed,
        z_proj,
        dt_raw,
        ext_x,
        ext_bc,
        pre_x,
        pre_bc,
        x_heads,
        b_low,
        c_low,
        step_size,
        cum_log,
        state_in,
        y_flat,
        gate_act,
        gated_vals,
        inv_gate,
        normed_out,
    )
    return ((flat_in + mixed).reshape(residual.shape), saved_vals)


def backward_layer(d_resid, saved_vals, local_params, full_weights):
    (
        flat_in,
        inv_rms,
        normed,
        z_proj,
        dt_raw,
        ext_x,
        ext_bc,
        pre_x,
        pre_bc,
        x_heads,
        b_low,
        c_low,
        step_size,
        cum_log,
        state_in,
        y_flat,
        gate_act,
        gated_vals,
        inv_gate,
        normed_out,
    ) = saved_vals
    gain_in, conv_xw, conv_bcw, head_vals, gate_gain = local_params
    w_zx, w_dt, w_bc, w_out = full_weights
    seq_count, length, heads_local, head_size = x_heads.shape
    row_count = seq_count * length
    d_mix = d_resid.astype(jnp.bfloat16)
    grad_out = jnp.einsum("tc,td->cd", normed_out, d_mix, preferred_element_type=jnp.float32)
    d_normed_out = jnp.einsum("td,cd->tc", d_mix, w_out, preferred_element_type=jnp.float32)
    grad_gate_gain = jnp.sum(d_normed_out * gated_vals * inv_gate, axis=0)
    d_scaled = d_normed_out * gate_gain.astype(jnp.float32)
    total_dot = lax.psum(jnp.sum(d_scaled * gated_vals, axis=-1), "head")
    d_gated = inv_gate * d_scaled - gated_vals * (inv_gate**3 * total_dot[:, None] / INNER)
    d_y = d_gated * gate_act
    d_z = (d_gated * y_flat * silu_slope(z_proj.astype(jnp.float32))).astype(jnp.bfloat16)
    d_heads = d_y.reshape(x_heads.shape)
    grad_skip = jnp.sum(d_heads * x_heads, axis=(0, 1, 3))
    d_x = d_heads * head_vals[2][:, None]
    d_ssd = d_heads.astype(jnp.bfloat16)
    decay_in, weights_tk, to_end = decay_tables(cum_log, step_size)
    state_weight = to_end * step_size
    inner_cb = jnp.einsum("stn,skn->stk", c_low, b_low, preferred_element_type=jnp.float32)
    scores = (inner_cb[..., None] * weights_tk).astype(jnp.bfloat16)
    weighted = (x_heads * state_weight[..., None]).astype(jnp.bfloat16)
    exp_cum = jnp.exp(cum_log)
    c_single = c_low.astype(jnp.float32)
    b_single = b_low.astype(jnp.float32)
    c_exact = exp_cum[..., None] * c_single[:, :, None, :]
    c_decay = c_exact.astype(jnp.bfloat16)
    d_cdecay = jnp.einsum(
        "sthp,shpn->sthn", d_ssd, state_in.astype(jnp.bfloat16), preferred_element_type=jnp.float32
    )
    d_prior = jnp.einsum("sthp,sthn->shpn", d_ssd, c_decay, preferred_element_type=jnp.float32)
    d_c = jnp.einsum("sth,sthn->stn", exp_cum, d_cdecay, precision=highest)
    d_cum = jnp.sum(d_cdecay * c_exact, axis=-1)
    d_scores = jnp.einsum("sthp,skhp->stkh", d_ssd, x_heads, preferred_element_type=jnp.float32)
    d_x = d_x + jnp.einsum("stkh,sthp->skhp", scores, d_ssd, preferred_element_type=jnp.float32)
    d_cb = jnp.sum(d_scores * weights_tk, axis=-1)
    d_weights = d_scores * inner_cb[..., None]
    flow_pairs = d_weights * weights_tk
    d_cum = d_cum + jnp.sum(flow_pairs, axis=2) - jnp.sum(flow_pairs, axis=1)
    d_step = jnp.sum(d_weights * decay_in, axis=1)
    d_c = d_c + jnp.einsum("stk,skn->stn", d_cb, b_single, precision=highest)
    d_b = jnp.einsum("stk,stn->skn", d_cb, c_single, precision=highest)
    total_decay = exp_cum[:, -1]
    identity = (jnp.ones_like(total_decay), jnp.zeros_like(d_prior))
    later_grads = entering((total_decay, d_prior), "seq", combine_states, identity, True)
    d_end = later_grads[1]
    d_end_low = d_end.astype(jnp.bfloat16)
    d_weighted = jnp.einsum("skn,shpn->skhp", b_low, d_end_low, preferred_element_type=jnp.float32)
    d_b = d_b + jnp.einsum(
        "skhp,shpn->skn", weighted, d_end_low, preferred_element_type=jnp.float32
    )
    d_x = d_x + d_weighted * state_weight[..., None]
    d_sweight = jnp.sum(d_weighted * x_heads, axis=-1)
    flow_end = d_sweight * state_weight
    d_step = d_step + d_sweight * to_end
    d_total = jnp.sum(d_end * state_in, axis=(2, 3)) * total_decay
    d_cum = d_cum - flow_end
    d_cum = d_cum.at[:, -1].add(jnp.sum(flow_end, axis=1) + d_total)
    d_log = jnp.flip(jnp.cumsum(jnp.flip(d_cum, 1), axis=1), 1)
    decay_rate = -jnp.exp(head_vals[0])
    d_step = d_step + d_log * decay_rate
    grad_alog = jnp.sum(d_log * step_size * decay_rate, axis=(0, 1))
    pre_step = dt_raw.astype(jnp.float32).reshape(seq_count, length, heads_local) + head_vals[1]
    d_raw = d_step * jax.nn.sigmoid(pre_step)
    grad_bias = jnp.sum(d_raw, axis=(0, 1))
    d_raw_low = d_raw.reshape(row_count, heads_local).astype(jnp.bfloat16)
    d_bc = lax.psum(jnp.concatenate([d_b, d_c], axis=-1).astype(jnp.bfloat16), "head").astype(
        jnp.float32
    )
    inner_local = heads_local * head_size
    d_prex = d_x.reshape(seq_count, length, inner_local) * silu_slope(pre_x)
    d_prebc = d_bc * silu_slope(pre_bc)
    d_extx, grad_convx = conv_backward(d_prex, ext_x, conv_xw)
    d_extbc, grad_convbc = conv_backward(d_prebc, ext_bc, conv_bcw)
    head_rows = jnp.concatenate([d_extx[:, : CONV - 1], d_extbc[:, : CONV - 1]], axis=2)
    back_rows = passed_along(head_rows, "seq", -1)
    d_xproj = d_extx[:, CONV - 1 :].at[:, length - CONV + 1 :].add(back_rows[..., :inner_local])
    d_bcproj = d_extbc[:, CONV - 1 :].at[:, length - CONV + 1 :].add(back_rows[..., inner_local:])
    d_xlow = d_xproj.reshape(row_count, inner_local).astype(jnp.bfloat16)
    d_bclow = d_bcproj.reshape(row_count, 2 * STATE).astype(jnp.bfloat16)
    grad_zx = jnp.stack(
        [
            jnp.einsum("td,tc->dc", normed, d_z, preferred_element_type=jnp.float32),
            jnp.einsum("td,tc->dc", normed, d_xlow, preferred_element_type=jnp.float32),
        ]
    )
    grad_dt = jnp.einsum("td,tc->dc", normed, d_raw_low, preferred_element_type=jnp.float32)
    grad_bc = jnp.einsum("td,tc->dc", normed, d_bclow, preferred_element_type=jnp.float32)
    first_head = (lax.axis_index("head") == 0).astype(jnp.float32)
    d_normed = (
        jnp.einsum("tc,dc->td", d_z, w_zx[0], preferred_element_type=jnp.float32)
        + jnp.einsum("tc,dc->td", d_xlow, w_zx[1], preferred_element_type=jnp.float32)
        + jnp.einsum("tc,dc->td", d_raw_low, w_dt, preferred_element_type=jnp.float32)
        + first_head * jnp.einsum("tc,dc->td", d_bclow, w_bc, preferred_element_type=jnp.float32)
    )
    d_normed = lax.psum(d_normed.astype(jnp.bfloat16), "head").astype(jnp.float32)
    grad_gain = jnp.sum(d_normed * flat_in * inv_rms, axis=0)
    d_hidden = d_normed * gain_in.astype(jnp.float32)
    d_flat = (
        d_resid
        + inv_rms * d_hidden
        - flat_in * inv_rms**3 * jnp.mean(d_hidden * flat_in, axis=-1, keepdims=True)
    )
    big_grads = (grad_zx, grad_dt, grad_bc, grad_out)
    small_grads = (
        grad_gain,
        grad_convx,
        grad_convbc,
        jnp.stack([grad_alog, grad_bias, grad_skip]),
        grad_gate_gain,
    )
    return (d_flat, big_grads, small_grads)


def on_device(
    resid_in,
    cotangent,
    norm_gain,
    w_zx,
    w_dt,
    w_bc,
    conv_x,
    conv_bc,
    head_params,
    gated_gain,
    w_out,
):
    layer_count = norm_gain.shape[0]

    def layer_params(layer_index):
        return (
            norm_gain[layer_index],
            conv_x[layer_index],
            conv_bc[layer_index],
            head_params[layer_index],
            gated_gain[layer_index],
        )

    residual = resid_in.astype(jnp.float32)
    saved_all = []
    weights_all = []
    for layer_index in range(layer_count):
        full_weights = (
            lax.all_gather(w_zx[layer_index], "seq", axis=1, tiled=True),
            lax.all_gather(w_dt[layer_index], "seq", axis=0, tiled=True),
            lax.all_gather(w_bc[layer_index], "seq", axis=0, tiled=True),
            lax.all_gather(w_out[layer_index], "seq", axis=1, tiled=True),
        )
        residual, saved_vals = forward_layer(residual, layer_params(layer_index), full_weights)
        saved_all.append(saved_vals)
        weights_all.append(None)
    block_out = residual.astype(jnp.bfloat16)
    d_flat = cotangent.astype(jnp.float32).reshape(-1, cotangent.shape[2])
    big_all = [None] * layer_count
    small_all = [None] * layer_count
    for layer_index in reversed(range(layer_count)):
        full_weights = (
            lax.all_gather(w_zx[layer_index], "seq", axis=1, tiled=True),
            lax.all_gather(w_dt[layer_index], "seq", axis=0, tiled=True),
            lax.all_gather(w_bc[layer_index], "seq", axis=0, tiled=True),
            lax.all_gather(w_out[layer_index], "seq", axis=1, tiled=True),
        )
        d_flat, big_grads, small_grads = backward_layer(
            d_flat, saved_all[layer_index], layer_params(layer_index), full_weights
        )
        big_all[layer_index] = (
            lax.psum_scatter(big_grads[0], "seq", scatter_dimension=1, tiled=True),
            lax.psum_scatter(big_grads[1], "seq", scatter_dimension=0, tiled=True),
            lax.psum_scatter(big_grads[2], "seq", scatter_dimension=0, tiled=True),
            lax.psum_scatter(big_grads[3], "seq", scatter_dimension=1, tiled=True),
        )
        small_all[layer_index] = lax.psum(
            (small_grads[0], small_grads[1], small_grads[2], small_grads[3], small_grads[4]), "seq"
        )
    stacked = tuple(
        (
            jnp.stack([small_all[layer_index][member] for layer_index in range(layer_count)])
            for member in range(5)
        )
    )
    big_stacked = tuple(
        (
            jnp.stack([big_all[layer_index][member] for layer_index in range(layer_count)])
            for member in range(4)
        )
    )
    grad_input = d_flat.reshape(cotangent.shape).astype(jnp.bfloat16)
    return (
        block_out,
        grad_input,
        stacked[0].astype(jnp.bfloat16),
        big_stacked[0].astype(jnp.bfloat16),
        big_stacked[1].astype(jnp.bfloat16),
        big_stacked[2].astype(jnp.bfloat16),
        stacked[1].astype(jnp.bfloat16),
        stacked[2].astype(jnp.bfloat16),
        stacked[3].astype(jnp.bfloat16),
        stacked[4].astype(jnp.bfloat16),
        big_stacked[3].astype(jnp.bfloat16),
    )


def solution(mesh):
    return jax.shard_map(
        on_device,
        mesh=mesh,
        in_specs=(
            P(None, "seq", None),
            P(None, "seq", None),
            P(),
            P(None, None, "seq", "head"),
            P(None, "seq", "head"),
            P(None, "seq", None),
            P(None, None, "head"),
            P(),
            P(None, None, "head"),
            P(None, "head"),
            P(None, "head", "seq"),
        ),
        out_specs=(
            P(None, "seq", None),
            P(None, "seq", None),
            P(),
            P(None, None, "seq", "head"),
            P(None, "seq", "head"),
            P(None, "seq", None),
            P(None, None, "head"),
            P(),
            P(None, None, "head"),
            P(None, "head"),
            P(None, "head", "seq"),
        ),
        check_vma=False,
    )
```

profile of v0, /device:TPU:0, one launch (start us, length us, event | category | flops | bytes accessed | tf_op | source)
XLA Modules:
  0.0 2640.7 jit_solution(13983895391041911244)
XLA Ops:
  10.4 50.9 %all-gather.2 = bf16[1,1536,24]{2,0,1:T(2,128)(2,1)S(1)} all-gather(bf16[1,96,24]{2,0,1:T(2,128)(2,1)S(1)} %copy.465), channel_id=4, replica_groups=mesh['seq'=16,'head'=2] {'seq'}, dimensions={1}, use_global_device_ids=true | all-gather | bytes 78336 | tf_op jit(solution)/shard_map/all_gather | solution.py:339
  65.1 45.7 %all-gather.1 = bf16[1,1536,256]{2,1,0:T(8,128)(2,1)S(1)} all-gather(bf16[1,96,256]{2,1,0:T(8,128)(2,1)S(1)} %get-tuple-element.911), channel_id=3, replica_groups=mesh['seq'=16,'head'=2] {'seq'}, dimensions={1}, use_global_device_ids=true | all-gather | bytes 835584 | tf_op jit(solution)/shard_map/all_gather | solution.py:340
  114.7 34.6 %all-gather.21.cloned.1.call-done = bf16[1,2,1536,1536]{3,2,1,0:T(8,128)(2,1)} async-done(((bf16[1,2,96,1536]{3,2,1,0:T(8,128)(2,1)}), bf16[1,2,1536,1536]{3,2,1,0:T(8,128)(2,1)}) %all-gather.21.cloned.1.call-update) | async-done | bytes 9437200 | tf_op jit(solution)/shard_map/all_gather | solution.py:338
  172.5 38.0 %all_gather.77 = bf16[16,1,24]{2,1,0:T(2,128)(2,1)} all-gather(bf16[1,1,24]{2,1,0:T(2,128)(2,1)} %get-tuple-element.904), channel_id=1, replica_groups=mesh['seq'=16,'head'=2] {'seq'}, dimensions={0}, use_global_device_ids=true | all-gather | bytes 816 | tf_op jit(solution)/shard_map/all_gather | solution.py:27
  219.1 42.8 %all-gather.23.cloned.1.call-done = bf16[384,64,128]{2,1,0:T(8,128)(2,1)} async-done(((bf16[24,64,128]{2,1,0:T(8,128)(2,1)}), bf16[384,64,128]{2,1,0:T(8,128)(2,1)}) %all-gather.23.cloned.1.call-update) | async-done | bytes 6291472 | tf_op jit(solution)/shard_map/all_gather | solution.py:27
  278.1 65.4 %all-gather.25.cloned.1.call-done = bf16[1,1536,1536]{1,2,0:T(8,128)(2,1)} async-done(((bf16[1,1536,96]{1,2,0:T(8,128)(2,1)}), bf16[1,1536,1536]{1,2,0:T(8,128)(2,1)}) %all-gather.25.cloned.1.call-update) | async-done | bytes 4718608 | tf_op jit(solution)/shard_map/all_gather | solution.py:341
  349.9 44.8 %all-gather.7 = bf16[1,1536,24]{2,0,1:T(2,128)(2,1)S(1)} all-gather(bf16[1,96,24]{2,0,1:T(2,128)(2,1)S(1)} %copy.466), channel_id=9, replica_groups=mesh['seq'=16,'head'=2] {'seq'}, dimensions={1}, use_global_device_ids=true | all-gather | bytes 78336 | tf_op jit(solution)/shard_map/all_gather | solution.py:339
  395.8 46.1 %all-gather.6 = bf16[1,1536,256]{2,1,0:T(8,128)(2,1)S(1)} all-gather(bf16[1,96,256]{2,1,0:T(8,128)(2,1)S(1)} %get-tuple-element.910), channel_id=8, replica_groups=mesh['seq'=16,'head'=2] {'seq'}, dimensions={1}, use_global_device_ids=true | all-gather | bytes 835584 | tf_op jit(solution)/shard_map/all_gather | solution.py:340
  447.1 57.8 %all-gather.27.cloned.1.call-done = bf16[1,2,1536,1536]{3,2,1,0:T(8,128)(2,1)} async-done(((bf16[1,2,96,1536]{3,2,1,0:T(8,128)(2,1)}), bf16[1,2,1536,1536]{3,2,1,0:T(8,128)(2,1)}) %all-gather.27.cloned.1.call-update) | async-done | bytes 9437200 | tf_op jit(solution)/shard_map/all_gather | solution.py:338
  533.2 38.4 %all_gather.84 = bf16[16,1,24]{2,1,0:T(2,128)(2,1)} all-gather(bf16[1,1,24]{2,1,0:T(2,128)(2,1)S(1)} %copy-done.202), channel_id=1, replica_groups=mesh['seq'=16,'head'=2] {'seq'}, dimensions={0}, use_global_device_ids=true | all-gather | bytes 816 | tf_op jit(solution)/shard_map/all_gather | solution.py:27
  584.4 35.8 %all-gather.29.cloned.1.call-done = bf16[384,64,128]{2,1,0:T(8,128)(2,1)} async-done(((bf16[24,64,128]{2,1,0:T(8,128)(2,1)}), bf16[384,64,128]{2,1,0:T(8,128)(2,1)}) %all-gather.29.cloned.1.call-update) | async-done | bytes 6291472 | tf_op jit(solution)/shard_map/all_gather | solution.py:27
  640.3 61.9 %all-gather.31.cloned.1.call-done = bf16[1,1536,1536]{1,2,0:T(8,128)(2,1)} async-done(((bf16[1,1536,96]{1,2,0:T(8,128)(2,1)}), bf16[1,1536,1536]{1,2,0:T(8,128)(2,1)}) %all-gather.31.cloned.1.call-update) | async-done | bytes 4718608 | tf_op jit(solution)/shard_map/all_gather | solution.py:341
  726.4 39.6 %all_gather.88 = bf16[16,1,24]{2,1,0:T(2,128)(2,1)} all-gather(bf16[1,1,24]{2,1,0:T(2,128)(2,1)S(1)} %slice.1271), channel_id=1, replica_groups=mesh['seq'=16,'head'=2] {'seq'}, dimensions={0}, use_global_device_ids=true | all-gather | bytes 816 | tf_op jit(solution)/shard_map/all_gather | solution.py:27
  819.6 43.5 %while.76 = (s32[]{:T(128)}, f32[1,24,64,128]{3,2,1,0:T(8,128)}, s32[]{:T(128)}, bf16[16,1,24,64,128]{4,3,2,1,0:T(8,128)(2,1)}, bf16[16,1,24]{2,1,0:T(2,128)(2,1...) while((s32[]{:T(128)}, f32[1,24,64,128]{3,2,1,0:T(8,128)}, s32[]{:T(128)}, ...), condition=%wide.region_19.20_spmd, body=%wide.region_18.19_spmd.sunk | while | flops 589854 | bytes 1966467 | solution.py:42
  1020.3 41.4 %all_gather.91 = bf16[16,1,24]{2,1,0:T(2,128)(2,1)} all-gather(bf16[1,1,24]{2,1,0:T(2,128)(2,1)S(1)} %slice.1270), channel_id=1, replica_groups=mesh['seq'=16,'head'=2] {'seq'}, dimensions={0}, use_global_device_ids=true | all-gather | bytes 816 | tf_op jit(solution)/shard_map/all_gather | solution.py:27
  1081.6 34.2 %all-gather.35.cloned.1.call-done = bf16[384,64,128]{2,1,0:T(8,128)(2,1)} async-done(((bf16[24,64,128]{2,1,0:T(8,128)(2,1)}), bf16[384,64,128]{2,1,0:T(8,128)(2,1)}) %all-gather.35.cloned.1.call-update) | async-done | bytes 6291472 | tf_op jit(solution)/shard_map/all_gather | solution.py:27
  1291.0 128.0 %reduce-scatter.19.cloned.1.call-done = f32[96,256]{1,0:T(8,128)} async-done(((f32[1536,256]{1,0:T(8,128)}), f32[96,256]{1,0:T(8,128)}) %reduce-scatter.19.cloned.1.call-update) | async-done | bytes 98320 | tf_op jit(solution)/shard_map/reduce_scatter | solution.py:363
  1420.6 174.9 %reduce-scatter.23.cloned.1.call-done = f32[1536,96]{0,1:T(8,128)} async-done(((f32[1536,1536]{0,1:T(8,128)}), f32[1536,96]{0,1:T(8,128)}) %reduce-scatter.23.cloned.1.call-update) | async-done | bytes 589840 | tf_op jit(solution)/shard_map/reduce_scatter | solution.py:364
  1597.5 124.0 %reduce-scatter.25.cloned.1.call-done = f32[96,24]{1,0:T(8,128)} async-done(((f32[1536,24]{1,0:T(8,128)}), f32[96,24]{1,0:T(8,128)}) %reduce-scatter.25.cloned.1.call-update) | async-done | bytes 9232
  1744.3 79.8 %all-reduce.4 = (bf16[1536]{0:T(1024)(128)(2,1)S(1)}, bf16[1536]{0:T(1024)(128)(2,1)S(1)}, bf16[5,1536]{1,0:T(8,128)(2,1)}, bf16[5,1536]{1,0:T(8,128)(2,1)}, bf1...) all-reduce(f32[1536]{0:T(1024)S(1)} %copy-done.126, ...), channel_id=1, replica_groups=mesh['seq'=16,'head'=2] {'seq'}, use_global_device_ids=true, to_apply=%region_53.54 | all-reduce | flops 24208 | bytes 145248 | tf_op jit(solution)/shard_map/psum | solution.py:366
  1832.7 41.4 %reduce-scatter.17.cloned.1.call-done = f32[96,256]{1,0:T(8,128)} async-done(((f32[1536,256]{1,0:T(8,128)}), f32[96,256]{1,0:T(8,128)}) %reduce-scatter.17.cloned.1.call-update) | async-done | bytes 98320 | tf_op jit(solution)/shard_map/reduce_scatter | solution.py:363
  1875.7 174.7 %reduce-scatter.21.cloned.1.call-done = f32[1536,96]{0,1:T(8,128)} async-done(((f32[1536,1536]{0,1:T(8,128)}), f32[1536,96]{0,1:T(8,128)}) %reduce-scatter.21.cloned.1.call-update) | async-done | bytes 589840 | tf_op jit(solution)/shard_map/reduce_scatter | solution.py:364
  2052.3 288.2 %reduce-scatter.15.cloned.1.call-done = f32[2,96,1536]{2,1,0:T(8,128)} async-done(((f32[2,1536,1536]{2,1,0:T(8,128)}), f32[2,96,1536]{2,1,0:T(8,128)}) %reduce-scatter.15.cloned.1.call-update) | async-done | bytes 1179664 | tf_op jit(solution)/shard_map/reduce_scatter | solution.py:361
  2341.8 289.2 %reduce-scatter.13.cloned.1.call-done = f32[2,96,1536]{2,1,0:T(8,128)} async-done(((f32[2,1536,1536]{2,1,0:T(8,128)}), f32[2,96,1536]{2,1,0:T(8,128)}) %reduce-scatter.13.cloned.1.call-update) | async-done | bytes 1179664 | tf_op jit(solution)/shard_map/reduce_scatter | solution.py:361
  (831 shorter events, 673.1 us)
Async XLA Ops:
  7.2 142.2 %all-gather.21.cloned.1.call-start = ((), (), s32[]{:S(2)}) async-start(), calls=%async_computation.20 | async-start | bytes 10027008 | tf_op jit(solution)/shard_map/all_gather | solution.py:338
  9.6 252.3 %all-gather.23.cloned.1.call-start = ((), (), s32[]{:S(2)}) async-start(), calls=%async_computation.21 | async-start | bytes 6684672 | tf_op jit(solution)/shard_map/all_gather | solution.py:27
  168.2 175.4 %all-gather.25.cloned.1.call-start = ((), (), s32[]{:S(2)}) async-start(), calls=%async_computation.22 | async-start | bytes 5013504 | tf_op jit(solution)/shard_map/all_gather | solution.py:341
  170.1 271.8 %all-reduce.12.cloned.1.call-start = ((), (), s32[]{:S(2)}) async-start(), calls=%async_computation.8 | async-start | bytes 3145728 | tf_op jit(solution)/shard_map/psum | solution.py:146
  349.0 155.9 %all-gather.27.cloned.1.call-start = ((), (), s32[]{:S(2)}) async-start(), calls=%async_computation.23 | async-start | bytes 10027008 | tf_op jit(solution)/shard_map/all_gather | solution.py:338
  349.6 270.6 %all-gather.29.cloned.1.call-start = ((), (), s32[]{:S(2)}) async-start(), calls=%async_computation.24 | async-start | bytes 6684672 | tf_op jit(solution)/shard_map/all_gather | solution.py:27
  509.5 8.0 collective-permute-start.1
  527.6 174.5 %all-gather.31.cloned.1.call-start = ((), (), s32[]{:S(2)}) async-start(), calls=%async_computation.25 | async-start | bytes 5013504 | tf_op jit(solution)/shard_map/all_gather | solution.py:341
  528.4 290.3 %all-gather.33.cloned.1.call-start = ((), (), s32[]{:S(2)}) async-start(), calls=%async_computation.26 | async-start | bytes 6684672 | tf_op jit(solution)/shard_map/all_gather | solution.py:27
  725.7 204.4 %all-reduce.16.cloned.1.call-start = ((), (), s32[]{:S(2)}) async-start(), calls=%async_computation.10 | async-start | bytes 262144 | tf_op jit(solution)/shard_map/psum | solution.py:261
  916.2 58.4 %all-reduce.18.cloned.1.call-start = ((), (), s32[]{:S(2)}) async-start(), calls=%async_computation.11 | async-start | bytes 1572864 | tf_op jit(solution)/shard_map/psum | solution.py:290
  953.1 45.4 %all-reduce.14.cloned.1.call-start = ((), (), s32[]{:S(2)}) async-start(), calls=%async_computation.9 | async-start | bytes 3145728 | tf_op jit(solution)/shard_map/psum | solution.py:146
  958.3 157.5 %all-gather.35.cloned.1.call-start = ((), (), s32[]{:S(2)}) async-start(), calls=%async_computation.27 | async-start | bytes 6684672 | tf_op jit(solution)/shard_map/all_gather | solution.py:27
  1020.2 183.1 %all-reduce.20.cloned.1.call-start = ((), (), s32[]{:S(2)}) async-start(), calls=%async_computation.12 | async-start | bytes 262144 | tf_op jit(solution)/shard_map/psum | solution.py:261
  1146.8 143.2 %reduce-scatter.27.cloned.1.call-start = ((), (), s32[]{:S(2)}) async-start(), calls=%async_computation.29 | async-start | bytes 835584
  1149.3 269.7 %reduce-scatter.19.cloned.1.call-start = ((), (), s32[]{:S(2)}) async-start(), calls=%async_computation.17 | async-start | bytes 1671168 | tf_op jit(solution)/shard_map/reduce_scatter | solution.py:363
  1152.2 443.3 %reduce-scatter.23.cloned.1.call-start = ((), (), s32[]{:S(2)}) async-start(), calls=%async_computation.19 | async-start | bytes 10027008 | tf_op jit(solution)/shard_map/reduce_scatter | solution.py:364
  1159.3 562.2 %reduce-scatter.25.cloned.1.call-start = ((), (), s32[]{:S(2)}) async-start(), calls=%async_computation.28 | async-start | bytes 835584
  1203.3 539.3 %all-reduce.22.cloned.1.call-start = ((), (), s32[]{:S(2)}) async-start(), calls=%async_computation.13 | async-start | bytes 1572864 | tf_op jit(solution)/shard_map/psum | solution.py:290
  1207.6 5.8 collective-permute-start.3
  1224.4 649.7 %reduce-scatter.17.cloned.1.call-start = ((), (), s32[]{:S(2)}) async-start(), calls=%async_computation.16 | async-start | bytes 1671168 | tf_op jit(solution)/shard_map/reduce_scatter | solution.py:363
  1226.2 824.2 %reduce-scatter.21.cloned.1.call-start = ((), (), s32[]{:S(2)}) async-start(), calls=%async_computation.18 | async-start | bytes 10027008 | tf_op jit(solution)/shard_map/reduce_scatter | solution.py:364
  1233.0 1107.5 %reduce-scatter.15.cloned.1.call-start = ((), (), s32[]{:S(2)}) async-start(), calls=%async_computation.15 | async-start | bytes 20054016 | tf_op jit(solution)/shard_map/reduce_scatter | solution.py:361
  1245.0 1386.0 %reduce-scatter.13.cloned.1.call-start = ((), (), s32[]{:S(2)}) async-start(), calls=%async_computation.14 | async-start | bytes 20054016 | tf_op jit(solution)/shard_map/reduce_scatter | solution.py:361
  (205 other events, 6424.4 us)
Sparse Core Ops, SparseCore 0:
  11.3 138.0 all-gather.20
  168.3 93.6 all-gather.22
  264.7 78.7 all-gather.24
  349.1 19.0 all-reduce.11
  371.7 133.1 all-gather.26
  527.8 92.3 all-gather.28
  623.4 78.7 all-gather.30
  725.8 92.8 all-gather.32
  916.3 13.7 all-reduce.15
  953.2 21.2 all-reduce.17
  976.9 21.5 all-reduce.13
  1020.4 95.3 all-gather.34
  1146.9 13.7 all-reduce.19
  1166.6 123.3 reduce-scatter.26
  1295.4 123.6 reduce-scatter.18
  1425.5 169.9 reduce-scatter.22
  1600.1 121.4 reduce-scatter.24
  1724.3 18.3 all-reduce.21
  1748.2 125.9 reduce-scatter.16
  1880.6 169.7 reduce-scatter.20
  2056.1 284.3 reduce-scatter.14
  2346.2 284.6 reduce-scatter.12
where the time goes:
time: 2650 us; the launch traced here: 2640 us
  waiting for transfers between devices  1690 us (64%)
  blocking collectives  436 us (16%)
  other arithmetic  182 us (7%)
  matrix products  171 us (6%)
  local copies, waits for them, and re-layouts  137 us (5%)
    reduce_scatter x2, waiting for transfers between devices, on_device(): lax.psum_scatter(big_grads[0], 'seq', scatter_dimension=1, tiled=True)  577 us
    reduce_scatter x2, waiting for transfers between devices, on_device(): lax.psum_scatter(big_grads[3], 'seq', scatter_dimension=1, tiled=True)  350 us
    reduce_scatter x2, waiting for transfers between devices, on_device(): lax.psum_scatter(big_grads[2], 'seq', scatter_dimension=0, tiled=True)  169 us
    unnamed x24, waiting for transfers between devices  158 us
    all_gather x4, blocking collectives, entering(): lax.all_gather(a.astype(kind), axis)  157 us
    all_gather x4, waiting for transfers between devices, entering(): lax.all_gather(a.astype(kind), axis)  134 us
    all_gather x2, waiting for transfers between devices, on_device(): lax.all_gather(w_out[layer_index], 'seq', axis=1, tiled=True)  127 us
    all_gather x2, blocking collectives, on_device(): lax.all_gather(w_dt[layer_index], 'seq', axis=0, tiled=True)  95.8 us
  transfers between devices with their start and end apart: 26, of which 22 were waited for; matrix products, arithmetic and copies ran while one was open for 10% of the time, Pallas kernels for 0%

commit v1 on v0

v1 whole, which is shorter than its diff:
```python
import functools

import jax
import jax.numpy as jnp
from jax import lax
from jax.experimental import pallas as pl
from jax.experimental.pallas import tpu as pltpu
from jax.sharding import Mesh, PartitionSpec as P

HEADDIM = 64
STATE = 128
CONV = 4
SPAN = 256
GROUP = 4
EDGE = 16
EPS = 1e-05
HIGH = lax.Precision.HIGHEST
F32, BF16 = jnp.float32, jnp.bfloat16
NN = (((1,), (0,)), ((), ()))
NT = (((1,), (1,)), ((), ()))
TN = (((0,), (0,)), ((), ()))
VMEM_BYTES = 58 << 20


def dot(a, b, dims=NN):
    return lax.dot_general(a, b, dims, preferred_element_type=F32)


def dot_exact(a, b, dims=NN):
    return lax.dot_general(a, b, dims, precision=HIGH, preferred_element_type=F32)


def dot_split(a, b, dims=NN):
    high = a.astype(BF16)
    rest = (a - high.astype(F32)).astype(BF16)
    return dot(high, b, dims) + dot(rest, b, dims)


def sigmoid(v):
    return 1.0 / (1.0 + jnp.exp(-v))


def softplus(v):
    return jnp.maximum(v, 0.0) + jnp.log1p(jnp.exp(-jnp.abs(v)))


def silu_slope(v):
    sig = sigmoid(v)
    return sig * (1.0 + v * (1.0 - sig))


def iota(shape, dim):
    return lax.broadcasted_iota(jnp.int32, shape, dim)


def head_spread(inner):
    return (iota((128, inner), 0) == lax.shift_right_logical(iota((128, inner), 1), 6)).astype(BF16)


def triangle(lower):
    rows, cols = iota((SPAN, SPAN), 0), iota((SPAN, SPAN), 1)
    return ((cols <= rows) if lower else (cols >= rows)).astype(F32)


def half_masks():
    lane = iota((SPAN, 128), 1)
    return (lane < HEADDIM).astype(BF16), (lane >= HEADDIM).astype(BF16)


def conv_taps(window, taps):
    total = jnp.broadcast_to(taps[CONV : CONV + 1], (SPAN, window.shape[1]))
    for j in range(CONV):
        total = total + taps[j : j + 1] * window[EDGE - 3 + j : EDGE - 3 + j + SPAN]
    return total


def forward_local(
    normed, wx, wz, wbc, wdt, rowp, bcp, headp,
    z_out, xin_out, bcin_out, x_out, bc_out, dtraw_out, dt_out, s_out, y_out, local_out, decay_out, sum_out,
    ext,
):
    inner = x_out.shape[1]
    spans = x_out.shape[0] // SPAN

    edge = normed[0:EDGE]
    edge_x = dot(edge, wx[...]).astype(BF16)
    edge_bc = dot(edge, wbc[...]).astype(BF16)
    xin_out[0:EDGE] = edge_x
    bcin_out[0:EDGE] = edge_bc
    ext[0:EDGE, 0:inner] = edge_x.astype(F32)
    ext[0:EDGE, inner:] = edge_bc.astype(F32)
    spread = head_spread(inner)
    low_tri = triangle(True)
    rate = -jnp.exp(headp[0:1])
    bias = headp[1:2]

    def block(q, carry):
        state_sum, decay_all = carry
        at = pl.multiple_of(q * SPAN, SPAN)
        tok = pl.ds(at, SPAN)
        after = pl.ds(pl.multiple_of(at + EDGE, EDGE), SPAN)
        rows = normed[after, :]
        z_out[tok, :] = dot(rows, wz[...]).astype(BF16)
        xin = dot(rows, wx[...]).astype(BF16)
        bcin = dot(rows, wbc[...]).astype(BF16)
        dtraw = dot(rows, wdt[...]).astype(BF16)
        xin_out[after, :] = xin
        bcin_out[after, :] = bcin
        dtraw_out[tok, :] = dtraw
        ext[after, 0:inner] = xin.astype(F32)
        ext[after, inner:] = bcin.astype(F32)
        window = pl.ds(at, SPAN + EDGE)
        pre_x = conv_taps(ext[window, 0:inner], rowp)
        x = (pre_x * sigmoid(pre_x)).astype(BF16)
        x_out[tok, :] = x
        pre_bc = conv_taps(ext[window, inner:], bcp)
        bc = (pre_bc * sigmoid(pre_bc)).astype(BF16)
        bc_out[tok, :] = bc
        b, c = bc[:, :STATE], bc[:, STATE:]
        dt = softplus(dtraw.astype(F32) + bias)
        s = dot_exact(low_tri, dt * rate)
        dt_out[tok, :] = dt
        s_out[tok, :] = s
        s_row, dt_row = s.T, dt.T
        cb = dot(c, b, NT)
        causal = iota((SPAN, SPAN), 1) <= iota((SPAN, SPAN), 0)
        masks = half_masks()
        for pair in range(inner // 128):
            lanes = slice(pair * 128, pair * 128 + 128)
            x_pair = x[:, lanes]
            total = None
            for e in range(2):
                h = pair * 2 + e
                gap = jnp.where(causal, s[:, h : h + 1] - s_row[h : h + 1, :], -1e30)
                scores = (cb * (jnp.exp(gap) * dt_row[h : h + 1, :])).astype(BF16)
                term = dot(scores, x_pair * masks[e])
                total = term if total is None else total + term
            y_out[tok, lanes] = total
        to_end = jnp.exp(s[SPAN - 1 : SPAN] - s) * dt
        weighted = (x.astype(F32) * dot_split(to_end, spread)).astype(BF16)
        local = dot(b, weighted, TN)
        decay = dot_split(jnp.exp(s[SPAN - 8 : SPAN]), spread)[7:8]
        local_out[q] = local
        decay_out[q] = jnp.broadcast_to(decay, (8, inner))
        return state_sum * decay + local, decay_all * decay

    state_sum, decay_all = lax.fori_loop(
        0, spans, block, (jnp.zeros((STATE, inner), F32), jnp.ones((1, inner), F32))
    )
    sum_out[0:STATE] = state_sum
    sum_out[STATE : STATE + 8] = jnp.broadcast_to(decay_all, (8, inner))


def entering_state(place, count, sums, backward):
    inner = sums.shape[2]
    state = jnp.zeros((STATE, inner), F32)
    for turn in range(count):
        other = count - 1 - turn if backward else turn
        ahead = (place < other) if backward else (other < place)
        state = jnp.where(ahead, sums[other, STATE : STATE + 1] * state + sums[other, 0:STATE], state)
    return state


def forward_carried(count, sums, local, decay, y_local, x, bc, z, s, wo, rowp, y_out, states_out, part_out, sq_out):
    inner = x.shape[1]
    spans = x.shape[0] // SPAN
    spread = head_spread(inner)
    gain, skip = rowp[5:6], rowp[6:7]
    ones = jnp.ones((8, inner), F32)

    def block(q, state):
        tok = pl.ds(pl.multiple_of(q * SPAN, SPAN), SPAN)
        states_out[q] = state
        c = bc[tok, STATE:]
        carried = dot_split(jnp.exp(s[tok, :]), spread) * dot(c, state.astype(BF16))
        y = y_local[tok, :] + carried + skip * x[tok, :].astype(F32)
        y_out[tok, :] = y
        zf = z[tok, :].astype(F32)
        gated = y * (zf * sigmoid(zf))
        sq_out[:, tok] = dot_exact(ones, gated * gated, NT)
        part_out[tok, :] = dot((gated * gain).astype(BF16), wo[...], NT).astype(BF16)
        return decay[q, 0:1] * state + local[q]

    lax.fori_loop(0, spans, block, entering_state(lax.axis_index("z"), count, sums, False))


def backward_gate(
    inner_all, dmix, wo, y_in, z, x, bc, s, decay, token_scalars, rowp,
    dz_out, dy_out, gwo_out, prior_out, sum_out, small_out,
    normed_out,
):
    inner = x.shape[1]
    spans = x.shape[0] // SPAN
    spread = head_spread(inner)
    gain = rowp[5:6]

    def block(i, carry):
        grad_sum, gain_sum, skip_sum = carry
        q = spans - 1 - i
        tok = pl.ds(pl.multiple_of(q * SPAN, SPAN), SPAN)
        columns = token_scalars[:, tok].T
        inv, total_dot = columns[:, 0:1], columns[:, 1:2]
        zf = z[tok, :].astype(F32)
        sig = sigmoid(zf)
        act = zf * sig
        y = y_in[tok, :]
        gated = y * act
        d_no = dot(dmix[tok, :], wo[...])
        scaled = gated * inv
        normed_out[tok, :] = (scaled * gain).astype(BF16)
        gain_sum = gain_sum + jnp.sum(d_no * scaled, axis=0, keepdims=True)
        d_gated = inv * (d_no * gain) - gated * (inv * inv * inv * total_dot * (1.0 / inner_all))
        dz_out[tok, :] = (d_gated * y * (sig * (1.0 + zf * (1.0 - sig)))).astype(BF16)
        dy = d_gated * act
        xf = x[tok, :].astype(F32)
        skip_sum = skip_sum + jnp.sum(dy * xf, axis=0, keepdims=True)
        dy_low = dy.astype(BF16)
        dy_out[tok, :] = dy_low
        scaled_dy = (dy_low.astype(F32) * dot_split(jnp.exp(s[tok, :]), spread)).astype(BF16)
        prior = dot(bc[tok, STATE:], scaled_dy, TN)
        prior_out[q] = prior
        return prior + decay[q, 0:1] * grad_sum, gain_sum, skip_sum

    zero = jnp.zeros((1, inner), F32)
    grad_sum, gain_sum, skip_sum = lax.fori_loop(
        0, spans, block, (jnp.zeros((STATE, inner), F32), zero, zero)
    )
    decay_all = decay[0, 0:1]
    for q in range(1, spans):
        decay_all = decay_all * decay[q, 0:1]
    sum_out[0:STATE] = grad_sum
    sum_out[STATE : STATE + 8] = jnp.broadcast_to(decay_all, (8, inner))
    small_out[0:1] = gain_sum
    small_out[1:2] = skip_sum
    small_out[2:8] = jnp.zeros((6, inner), F32)

    def out_grad(i, _):
        rows = pl.ds(pl.multiple_of(i * SPAN, SPAN), SPAN)
        gwo_out[rows, :] = dot(dmix[:, rows], normed_out[...], TN).astype(BF16)
        return 0

    lax.fori_loop(0, dmix.shape[1] // SPAN, out_grad, 0)


def backward_ssd(
    count, sums, prior, decay, states, dy_in, x, bc, s_in, dt_in, dtraw, xin, bcin, rowp, bcp, headp,
    dcat_out, row_out, bcrow_out, head_out,
    dpre, dend,
):
    inner = x.shape[1]
    spans = x.shape[0] // SPAN
    spread = head_spread(inner)
    up_tri = triangle(False)
    skip = rowp[6:7]
    rate = -jnp.exp(headp[0:1])
    bias = headp[1:2]
    width = inner + 2 * STATE

    def chain(i, grad):
        q = spans - 1 - i
        dend[q] = grad
        return prior[q] + decay[q, 0:1] * grad

    lax.fori_loop(0, spans, chain, entering_state(lax.axis_index("z"), count, sums, True))
    dpre[0:EDGE] = jnp.zeros((EDGE, width), F32)
    dpre[EDGE + spans * SPAN :] = jnp.zeros((EDGE, width), F32)
    row_out[...] = jnp.zeros_like(row_out)
    bcrow_out[...] = jnp.zeros_like(bcrow_out)
    head_out[...] = jnp.zeros_like(head_out)
    dcat_out[0:EDGE, width:] = jnp.zeros((EDGE, 128), BF16)

    def block(q, _):
        at = pl.multiple_of(q * SPAN, SPAN)
        tok = pl.ds(at, SPAN)
        after = pl.ds(pl.multiple_of(at + EDGE, EDGE), SPAN)
        window = pl.ds(at, SPAN + EDGE)
        x_low, dy = x[tok, :], dy_in[tok, :]
        xf, dyf = x_low.astype(F32), dy.astype(F32)
        b, c = bc[tok, :STATE], bc[tok, STATE:]
        s, dt = s_in[tok, :], dt_in[tok, :]
        exp_s = jnp.exp(s)
        to_end = jnp.exp(s[SPAN - 1 : SPAN] - s)
        w = to_end * dt
        w_all, s_all = dot_split(w, spread), dot_split(exp_s, spread)
        state, grad = states[q], dend[q]
        state_low, grad_low = state.astype(BF16), grad.astype(BF16)
        carried = s_all * dot(c, state_low)
        ds = dot_split(dyf * carried, spread, NT)
        d_c = dot((dyf * s_all).astype(BF16), state_low, NT)
        d_w = dot(b, grad_low)
        d_b = dot((xf * w_all).astype(BF16), grad_low, NT)
        dx = dyf * skip + d_w * w_all
        dsw = dot_split(d_w * xf, spread, NT)
        s_row = s.T
        cb = dot(b, c, NT)
        seen = iota((SPAN, SPAN), 0) <= iota((SPAN, SPAN), 1)
        masks = half_masks()
        d_cb = jnp.zeros((SPAN, SPAN), F32)
        lane = iota((SPAN, 128), 1)
        row_id = iota((128, SPAN), 0)
        sum_k = jnp.zeros((128, SPAN), F32)
        sum_t = jnp.zeros((SPAN, 128), F32)
        dx_pairs = []
        for pair in range(inner // 128):
            lanes = slice(pair * 128, pair * 128 + 128)
            x_pair, dy_pair = x_low[:, lanes], dy[:, lanes]
            total = dx[:, lanes]
            for e in range(2):
                h = pair * 2 + e
                d_scores = dot(x_pair * masks[e], dy_pair, NT)
                fade = jnp.exp(jnp.where(seen, s_row[h : h + 1, :] - s[:, h : h + 1], -1e30))
                dt_h = dt[:, h : h + 1]
                fade_cb = cb * fade
                total = total + dot((fade_cb * dt_h).astype(BF16), dy_pair * masks[e])
                d_cb = d_cb + d_scores * (fade * dt_h)
                flow = d_scores * fade_cb
                sum_t = jnp.where(lane == h, jnp.sum(flow, axis=1, keepdims=True), sum_t)
                sum_k = jnp.where(row_id == h, jnp.sum(flow * dt_h, axis=0, keepdims=True), sum_k)
            dx_pairs.append(total)
        d_cb_low = d_cb.astype(BF16)
        d_b = d_b + dot(d_cb_low, c)
        d_c = d_c + dot(d_cb_low, b, TN)
        end = dsw * w
        ds = ds + sum_k.T - sum_t * dt - end
        held = dot_split(jnp.broadcast_to(jnp.sum(grad * state, axis=0, keepdims=True), (8, inner)), spread, NT)[0:1]
        last = jnp.sum(end, axis=0, keepdims=True) + held * exp_s[SPAN - 1 : SPAN]
        ds = ds + jnp.where(iota((SPAN, 128), 0) == SPAN - 1, last, 0.0)
        da = dot_exact(up_tri, ds)
        d_dt = sum_t + dsw * to_end + da * rate
        d_raw = d_dt * sigmoid(dtraw[tok, :].astype(F32) + bias)
        d_raw = jnp.where(lane < inner // HEADDIM, d_raw, 0.0)
        head_out[0:1] += jnp.sum(da * (dt * rate), axis=0, keepdims=True)
        head_out[1:2] += jnp.sum(d_raw, axis=0, keepdims=True)
        dcat_out[after, width:] = d_raw.astype(BF16)

        win_x = xin[window, :].astype(F32)
        d_x = jnp.concatenate(dx_pairs, axis=1) * silu_slope(conv_taps(win_x, rowp))
        dpre[after, 0:inner] = d_x
        for j in range(CONV):
            row_out[j : j + 1] += jnp.sum(d_x * win_x[EDGE - 3 + j : EDGE - 3 + j + SPAN], axis=0, keepdims=True)
        row_out[CONV : CONV + 1] += jnp.sum(d_x, axis=0, keepdims=True)
        win_bc = bcin[window, :].astype(F32)
        d_bc = jnp.concatenate([d_b, d_c], axis=1) * silu_slope(conv_taps(win_bc, bcp))
        dpre[after, inner:] = d_bc
        for j in range(CONV):
            bcrow_out[j : j + 1] += jnp.sum(d_bc * win_bc[EDGE - 3 + j : EDGE - 3 + j + SPAN], axis=0, keepdims=True)
        bcrow_out[CONV : CONV + 1] += jnp.sum(d_bc, axis=0, keepdims=True)
        return 0

    lax.fori_loop(0, spans, block, 0)

    def back(window, taps, rows):
        total = None
        for j in range(CONV):
            term = taps[j : j + 1] * window[CONV - 1 - j : CONV - 1 - j + rows]
            total = term if total is None else total + term
        return total.astype(BF16)

    dcat_out[0:EDGE, 0:inner] = back(dpre[0 : 2 * EDGE, 0:inner], rowp, EDGE)
    dcat_out[0:EDGE, inner:width] = back(dpre[0 : 2 * EDGE, inner:], bcp, EDGE)

    def conv_block(q, _):
        at = pl.multiple_of(q * SPAN, SPAN)
        after = pl.ds(pl.multiple_of(at + EDGE, EDGE), SPAN)
        window = pl.ds(pl.multiple_of(at + EDGE, EDGE), SPAN + EDGE)
        dcat_out[after, 0:inner] = back(dpre[window, 0:inner], rowp, SPAN)
        dcat_out[after, inner:width] = back(dpre[window, inner:], bcp, SPAN)
        return 0

    lax.fori_loop(0, spans, conv_block, 0)


def backward_project(dcat, dz, normed, wx, wz, wbc, wdt, dn_out, gxz_out, gbc_out, gdt_out):
    inner = dz.shape[1]
    width = inner + 2 * STATE
    spans = dz.shape[0] // SPAN
    d_edge = dcat[0:EDGE]
    dn_out[0:EDGE] = (
        dot(d_edge[:, 0:inner], wx[...], NT)
        + dot(d_edge[:, inner:width], wbc[...], NT)
    ).astype(BF16)

    def rows_of(q, _):
        at = pl.multiple_of(q * SPAN, SPAN)
        tok = pl.ds(at, SPAN)
        after = pl.ds(pl.multiple_of(at + EDGE, EDGE), SPAN)
        dn_out[after, :] = (
            dot(dz[tok, :], wz[...], NT)
            + dot(dcat[after, 0:inner], wx[...], NT)
            + dot(dcat[after, inner:width], wbc[...], NT)
            + dot(dcat[after, width:], wdt[...], NT)
        ).astype(BF16)
        return 0

    lax.fori_loop(0, spans, rows_of, 0)

    def grads_of(i, _):
        cols = pl.ds(pl.multiple_of(i * SPAN, SPAN), SPAN)
        part = normed[:, cols]
        both = dot(part, dcat[...], TN).astype(BF16)
        gxz_out[cols, 0:inner] = both[:, 0:inner]
        gbc_out[cols, :] = both[:, inner:width]
        gdt_out[cols, :] = both[:, width:]
        gxz_out[cols, inner:] = dot(part[EDGE:], dz[...], TN).astype(BF16)
        return 0

    lax.fori_loop(0, normed.shape[1] // SPAN, grads_of, 0)


def call(body, outs, *args, scratch=()):
    vmem = pl.BlockSpec(memory_space=pltpu.VMEM)
    return pl.pallas_call(
        body,
        out_shape=tuple(jax.ShapeDtypeStruct(shape, kind) for shape, kind in outs),
        in_specs=[vmem] * len(args),
        out_specs=tuple([vmem] * len(outs)),
        scratch_shapes=list(scratch),
        compiler_params=pltpu.CompilerParams(vmem_limit_bytes=VMEM_BYTES),
    )(*args)


def on_device(resid_in, cotangent, norm_gain, w_zx, w_dt, w_bc, conv_x, conv_bc, head_params, gated_gain, w_out):
    layers, model = norm_gain.shape
    groups = lax.axis_size("z")
    place = lax.axis_index("p")
    shard = w_dt.shape[1]
    inner_core = conv_x.shape[2]
    inner = inner_core // GROUP
    heads_core = head_params.shape[2]
    heads = heads_core // GROUP
    inner_all = inner_core * lax.axis_size("head")
    length = resid_in.shape[1]
    tokens = GROUP * length
    spans = tokens // SPAN

    def my_part(array, size):
        return lax.dynamic_slice_in_dim(array, place * size, size, array.ndim - 1)

    row_all, bc_all, head_all, weights = [], [], [], []
    conv_mine = my_part(conv_x, inner).astype(F32)
    gain_mine = my_part(gated_gain, inner).astype(F32)
    head_mine = my_part(head_params, heads)
    for layer in range(layers):
        skip = jnp.repeat(head_mine[layer, 2], HEADDIM)
        row_all.append(
            jnp.concatenate([conv_mine[layer], gain_mine[layer][None], skip[None], jnp.zeros((1, inner), F32)])
        )
        bc_all.append(jnp.pad(conv_bc[layer].astype(F32), ((0, 3), (0, 0))))
        head_all.append(jnp.pad(head_mine[layer], ((0, 5), (0, 128 - heads))))
        stacked = jnp.stack([w_zx[layer, 1], w_zx[layer, 0], w_out[layer].T])
        sliced = stacked.reshape(3, shard, GROUP, inner)
        swapped = lax.all_to_all(sliced, "p", 2, 1)
        gathered = lax.all_gather(swapped.reshape(3, GROUP * shard, inner), "z", axis=1, tiled=True)
        dt_full = lax.all_gather(w_dt[layer], ("z", "p"), axis=0, tiled=True)
        bc_full = lax.all_gather(w_bc[layer], ("z", "p"), axis=0, tiled=True)
        dt_mine = jnp.pad(my_part(dt_full, heads), ((0, 0), (0, 128 - heads)))
        weights.append((gathered[0], gathered[1], gathered[2], bc_full, dt_mine))

    def gather_rows(block):
        return lax.all_gather(block, "p", axis=0, tiled=True)

    def scatter_rows(partial):
        return lax.psum(lax.psum_scatter(partial, "p", scatter_dimension=0, tiled=True), "head")

    resid = resid_in[0].astype(F32)
    saved = []
    for layer in range(layers):
        wx, wz, wo, wbc, wdt = weights[layer]
        rowp, bcp, headp = row_all[layer], bc_all[layer], head_all[layer]
        inv_rms = lax.rsqrt(jnp.mean(resid * resid, axis=-1, keepdims=True) + EPS)
        own = (resid * inv_rms * norm_gain[layer].astype(F32)).astype(BF16)
        normed = gather_rows(own)
        edge = lax.ppermute(normed[tokens - EDGE :], "z", [(i, i + 1) for i in range(groups - 1)])
        normed = jnp.concatenate([edge, normed])
        z, xin, bcin, x, bc, dtraw, dt, s, y_local, local, decay, sums = call(
            forward_local,
            [
                ((tokens, inner), BF16),
                ((tokens + EDGE, inner), BF16),
                ((tokens + EDGE, 2 * STATE), BF16),
                ((tokens, inner), BF16),
                ((tokens, 2 * STATE), BF16),
                ((tokens, 128), BF16),
                ((tokens, 128), F32),
                ((tokens, 128), F32),
                ((tokens, inner), F32),
                ((spans, STATE, inner), F32),
                ((spans, 8, inner), F32),
                ((STATE + 8, inner), F32),
            ],
            normed, wx, wz, wbc, wdt, rowp, bcp, headp,
            scratch=[pltpu.VMEM((tokens + EDGE, inner + 2 * STATE), F32)],
        )
        all_sums = lax.all_gather(sums, "z")
        y, states, part, squares = call(
            functools.partial(forward_carried, groups),
            [
                ((tokens, inner), F32),
                ((spans, STATE, inner), F32),
                ((tokens, model), BF16),
                ((8, tokens), F32),
            ],
            all_sums, local, decay, y_local, x, bc, z, s, wo, rowp,
        )
        mixed = scatter_rows(part).astype(F32)
        total_sq = lax.psum(squares[0], ("p", "head"))
        inv_all = lax.rsqrt(total_sq / inner_all + EPS)
        inv_own = lax.dynamic_slice_in_dim(inv_all, place * length, length)[:, None]
        saved.append((resid, inv_rms, normed, z, xin, bcin, x, bc, dtraw, dt, s, y, states, decay, mixed, inv_all))
        resid = resid + inv_own * mixed
    block_out = resid.astype(BF16)[None]

    d_resid = cotangent[0].astype(F32)
    big, small = [None] * layers, [None] * layers
    for layer in reversed(range(layers)):
        wx, wz, wo, wbc, wdt = weights[layer]
        rowp, bcp, headp = row_all[layer], bc_all[layer], head_all[layer]
        resid, inv_rms, normed, z, xin, bcin, x, bc, dtraw, dt, s, y, states, decay, mixed, inv_all = saved[layer]
        d_mix_own = d_resid.astype(BF16)
        dots = jnp.sum(d_mix_own.astype(F32) * mixed, axis=-1)
        d_mix = gather_rows(d_mix_own)
        token_scalars = jnp.pad(jnp.stack([inv_all, gather_rows(dots)]), ((0, 6), (0, 0)))
        dz, dy, gwo, prior, sums, gate_small = call(
            functools.partial(backward_gate, inner_all),
            [
                ((tokens, inner), BF16),
                ((tokens, inner), BF16),
                ((model, inner), BF16),
                ((spans, STATE, inner), F32),
                ((STATE + 8, inner), F32),
                ((8, inner), F32),
            ],
            d_mix, wo, y, z, x, bc, s, decay, token_scalars, rowp,
            scratch=[pltpu.VMEM((tokens, inner), BF16)],
        )
        all_sums = lax.all_gather(sums, "z")
        dcat, row_small, bc_small, head_small = call(
            functools.partial(backward_ssd, groups),
            [
                ((tokens + EDGE, inner + 2 * STATE + 128), BF16),
                ((8, inner), F32),
                ((8, 2 * STATE), F32),
                ((8, 128), F32),
            ],
            all_sums, prior, decay, states, dy, x, bc, s, dt, dtraw, xin, bcin, rowp, bcp, headp,
            scratch=[
                pltpu.VMEM((tokens + 2 * EDGE, inner + 2 * STATE), F32),
                pltpu.VMEM((spans, STATE, inner), F32),
            ],
        )
        d_normed_part, gxz, gbc, gdt = call(
            backward_project,
            [
                ((tokens + EDGE, model), BF16),
                ((model, 2 * inner), BF16),
                ((model, 2 * STATE), BF16),
                ((model, 128), BF16),
            ],
            dcat, dz, normed, wx, wz, wbc, wdt,
        )
        d_normed = scatter_rows(d_normed_part[EDGE:]).astype(F32)
        edge = lax.psum(d_normed_part[:EDGE], ("p", "head"))
        edge = lax.ppermute(edge, "z", [(i + 1, i) for i in range(groups - 1)]).astype(F32)
        edge = jnp.where(place == GROUP - 1, edge, 0.0)
        d_normed = d_normed.at[length - EDGE :].add(edge)
        gain_grad = jnp.sum(d_normed * resid * inv_rms, axis=0)
        d_hidden = d_normed * norm_gain[layer].astype(F32)
        d_resid = (
            d_resid
            + inv_rms * d_hidden
            - resid * inv_rms**3 * jnp.mean(d_hidden * resid, axis=-1, keepdims=True)
        )

        grads = jnp.stack([gxz[:, :inner], gxz[:, inner:], gwo])
        grads = lax.psum_scatter(grads, "z", scatter_dimension=1, tiled=True)
        grads = lax.all_to_all(grads.reshape(3, GROUP, shard, inner), "p", 1, 2)
        grads = grads.reshape(3, shard, inner_core)
        g_zx = jnp.stack([grads[1], grads[0]])
        g_out = grads[2].T
        g_bc = lax.psum(lax.psum_scatter(gbc, ("z", "p"), scatter_dimension=0, tiled=True), "head")
        g_dt = lax.psum_scatter(gdt[:, :heads], "z", scatter_dimension=0, tiled=True)
        g_dt = lax.all_to_all(g_dt.reshape(GROUP, shard, heads), "p", 0, 1).reshape(shard, heads_core)
        big[layer] = (g_zx, g_dt, g_bc, g_out)
        skip_grad = jnp.sum(gate_small[1].reshape(heads, HEADDIM), axis=1)
        wide = jnp.concatenate([row_small[: CONV + 1], gate_small[0:1]])
        wide = jnp.zeros((CONV + 2, GROUP, inner), F32).at[:, place].set(wide).reshape(CONV + 2, inner_core)
        tall = jnp.concatenate([head_small[:2, :heads], skip_grad[None]])
        tall = jnp.zeros((3, GROUP, heads), F32).at[:, place].set(tall).reshape(3, heads_core)
        shared = lax.psum(bc_small[: CONV + 1], "head")
        small[layer] = lax.psum((gain_grad, wide, shared, tall), ("z", "p"))

    grad_input = d_resid.astype(BF16)[None]
    stack = lambda pick: jnp.stack([pick(layer) for layer in range(layers)]).astype(BF16)
    return (
        block_out,
        grad_input,
        stack(lambda l: small[l][0]),
        stack(lambda l: big[l][0]),
        stack(lambda l: big[l][1]),
        stack(lambda l: big[l][2]),
        stack(lambda l: small[l][1][: CONV + 1]),
        stack(lambda l: small[l][2]),
        stack(lambda l: small[l][3]),
        stack(lambda l: small[l][1][CONV + 1]),
        stack(lambda l: big[l][3]),
    )


def solution(mesh):
    seq, head = mesh.shape["seq"], mesh.shape["head"]
    split = Mesh(mesh.devices.reshape(seq // GROUP, GROUP, head), ("z", "p", "head"))
    seq_axes = ("z", "p")
    specs = (
        P(None, seq_axes, None),
        P(None, seq_axes, None),
        P(),
        P(None, None, seq_axes, "head"),
        P(None, seq_axes, "head"),
        P(None, seq_axes, None),
        P(None, None, "head"),
        P(),
        P(None, None, "head"),
        P(None, "head"),
        P(None, "head", seq_axes),
    )
    return jax.shard_map(on_device, mesh=split, in_specs=specs, out_specs=specs, check_vma=False)
```

time: 2650 us -> 1390 us (0.52)
  waiting for transfers between devices: 1690 us -> 589 us
  matrix products: 171 us -> 0 us
  Pallas kernels: 0 us -> 154 us
  other arithmetic: 182 us -> 42.8 us
  local copies, waits for them, and re-layouts: 137 us -> 61 us
  blocking collectives: 436 us -> 495 us
    reduce_scatter x6 -> x10, waiting for transfers between devices: 1100 us -> 427 us  [the longest x2 174 us: on_device(): lax.psum_scatter(gbc, ('z', 'p'), scatter_dimension=0, tiled=True)]
    all_gather x8 -> x6, waiting for transfers between devices: 354 us -> 124 us  [the longest x4 70.5 us: gather_rows(): return lax.all_gather(block, 'p', axis=0, tiled=True)]
    dot_general x54 -> x0, matrix products: 167 us -> none  [the longest x2 13.2 us: backward_layer(): jnp.einsum('tc,td->cd', normed_out, d_mix, preferred_element_type=jnp.flo...]
    unnamed x24 -> x21, waiting for transfers between devices: 158 us -> 2.2 us
    pallas_call x0 -> x10, Pallas kernels: none -> 154 us  [call(): pl.pallas_call(body, out_shape=tuple((jax.ShapeDtypeStruct(shape, kind) f...]
    psum x5 -> x6, blocking collectives: 91.1 us -> 160 us  [the longest x1 85 us: on_device(): small[layer] = lax.psum((gain_grad, wide, shared, tall), ('z', 'p'))]
    add x44 -> x0, other arithmetic: 67.1 us -> none  [the longest x30 51.6 us: combine_states(): later_item[1] + later_item[0][..., None, None] * earlier_item[1]]
    all_gather x8 -> x10, blocking collectives: 345 us -> 287 us  [the longest x2 96.7 us: on_device(): dt_full = lax.all_gather(w_dt[layer], ('z', 'p'), axis=0, tiled=True)]
  transfers between devices with their start and end apart: 26 -> 29, of which waited for: 22 -> 17; matrix products, arithmetic and copies ran while one was open for 10% -> 5% of each run, Pallas kernels for 0% -> 4%
where the time goes in v1:
time: 1390 us; the launch traced here: 1380 us
  waiting for transfers between devices  589 us (42%)
  blocking collectives  495 us (36%)
  Pallas kernels  154 us (11%)
  local copies, waits for them, and re-layouts  61 us (4%)
  other arithmetic  42.8 us (3%)
  starting transfers between devices  20.1 us (1%)
  between operations  15.4 us (1%)
    reduce_scatter x2, waiting for transfers between devices, on_device(): lax.psum_scatter(gbc, ('z', 'p'), scatter_dimension=0, tiled=True)  174 us
    reduce_scatter x4, waiting for transfers between devices, scatter_rows(): lax.psum_scatter(partial, 'p', scatter_dimension=0, tiled=True)  174 us
    pallas_call x10, Pallas kernels, call(): pl.pallas_call(body, out_shape=tuple((jax.ShapeDtypeStruct(shape, kind) f...  154 us
    all_gather x2, blocking collectives, on_device(): dt_full = lax.all_gather(w_dt[layer], ('z', 'p'), axis=0, tiled=True)  96.7 us
    all_gather x2, blocking collectives, on_device(): bc_full = lax.all_gather(w_bc[layer], ('z', 'p'), axis=0, tiled=True)  95 us
    psum x1, blocking collectives, on_device(): small[layer] = lax.psum((gain_grad, wide, shared, tall), ('z', 'p'))  85 us
    all_gather x4, blocking collectives, on_device(): all_sums = lax.all_gather(sums, 'z')  79.4 us
    all_gather x4, waiting for transfers between devices, gather_rows(): return lax.all_gather(block, 'p', axis=0, tiled=True)  70.5 us
  transfers between devices with their start and end apart: 29, of which 17 were waited for; matrix products, arithmetic and copies ran while one was open for 5% of the time, Pallas kernels for 4%

profile of v1, /device:TPU:0, one launch (start us, length us, event | category | flops | bytes accessed | tf_op | source)
XLA Modules:
  0.0 1377.7 jit_solution(4799165382327346914)
XLA Ops:
  15.2 24.7 %all_to_all.90 = bf16[3,1,96,4,384]{4,2,0,1,3:T(8,128)(2,1)S(1)} all-to-all(bf16[3,1,96,4,384]{4,2,0,1,3:T(8,128)(2,1)S(1)} %copy.98), channel_id=1, replica_groups=mesh['z'=4,'p'=4,'head'=2] {'p'}, dimensions={3} | all-to-all | bytes 1769472 | tf_op jit(solution)/shard_map/all_to_all | solution.py:452
  42.3 46.6 %all-gather.1 = bf16[1,1536,24]{2,0,1:T(2,128)(2,1)S(1)} all-gather(bf16[1,96,24]{2,0,1:T(2,128)(2,1)S(1)} %copy.132), channel_id=3, replica_groups=mesh['z'=4,'p'=4,'head'=2] {'z','p'}, dimensions={1}, use_global_device_ids=true | all-gather | bytes 78336 | tf_op jit(solution)/shard_map/all_gather | solution.py:454
  88.9 50.0 %all-gather.4 = bf16[1,1536,24]{2,0,1:T(2,128)(2,1)S(1)} all-gather(bf16[1,96,24]{2,0,1:T(2,128)(2,1)S(1)} %copy.136), channel_id=6, replica_groups=mesh['z'=4,'p'=4,'head'=2] {'z','p'}, dimensions={1}, use_global_device_ids=true | all-gather | bytes 78336 | tf_op jit(solution)/shard_map/all_gather | solution.py:454
  143.5 46.4 %all-gather = bf16[1,1536,256]{2,1,0:T(8,128)(2,1)} all-gather(bf16[1,96,256]{2,1,0:T(8,128)(2,1)S(1)} %get-tuple-element.292), channel_id=2, replica_groups=mesh['z'=4,'p'=4,'head'=2] {'z','p'}, dimensions={1}, use_global_device_ids=true | all-gather | bytes 835584 | tf_op jit(solution)/shard_map/all_gather | solution.py:455
  245.8 42.1 %reduce-scatter.11.cloned.1.call-done = bf16[256,1536]{1,0:T(8,128)(2,1)} async-done(((bf16[1024,1536]{1,0:T(8,128)(2,1)}), bf16[256,1536]{1,0:T(8,128)(2,1)}) %reduce-scatter.11.cloned.1.call-update) | async-done | bytes 786448 | tf_op jit(solution)/shard_map/reduce_scatter | solution.py:463
  314.2 23.6 %all_to_all.91 = bf16[3,1,96,4,384]{4,2,0,1,3:T(8,128)(2,1)S(1)} all-to-all(bf16[3,1,96,4,384]{4,2,0,1,3:T(8,128)(2,1)S(1)} %copy.105), channel_id=1, replica_groups=mesh['z'=4,'p'=4,'head'=2] {'p'}, dimensions={3} | all-to-all | bytes 1769472 | tf_op jit(solution)/shard_map/all_to_all | solution.py:452
  341.3 48.6 %all-gather.3 = bf16[1,1536,256]{2,1,0:T(8,128)(2,1)} all-gather(bf16[1,96,256]{2,1,0:T(8,128)(2,1)S(1)} %get-tuple-element.291), channel_id=5, replica_groups=mesh['z'=4,'p'=4,'head'=2] {'z','p'}, dimensions={1}, use_global_device_ids=true | all-gather | bytes 835584 | tf_op jit(solution)/shard_map/all_gather | solution.py:455
  392.0 53.7 %all-gather.24.cloned.1.call-done = bf16[3,1536,384]{2,1,0:T(8,128)(2,1)} async-done(((bf16[3,384,384]{2,1,0:T(8,128)(2,1)}), bf16[3,1536,384]{2,1,0:T(8,128)(2,1)}) %all-gather.24.cloned.1.call-update) | async-done | bytes 3538960 | tf_op jit(solution)/shard_map/all_gather | solution.py:453
  470.0 19.3 %all-gather.5 = f32[544,384]{1,0:T(8,128)} all-gather(f32[136,384]{1,0:T(8,128)} %get-tuple-element.153), channel_id=7, replica_groups=mesh['z'=4,'p'=4,'head'=2] {'z'}, dimensions={0}, use_global_device_ids=true | all-gather | bytes 1044480 | tf_op jit(solution)/shard_map/all_gather | solution.py:494
  499.1 43.5 %reduce-scatter.13.cloned.1.call-done = bf16[256,1536]{1,0:T(8,128)(2,1)} async-done(((bf16[1024,1536]{1,0:T(8,128)(2,1)}), bf16[256,1536]{1,0:T(8,128)(2,1)}) %reduce-scatter.13.cloned.1.call-update) | async-done | bytes 786448 | tf_op jit(solution)/shard_map/reduce_scatter | solution.py:463
  574.6 36.7 %all-gather.28.cloned.1.call-done = bf16[1,1024,1536]{2,1,0:T(8,128)(2,1)} async-done(((bf16[1,256,1536]{2,1,0:T(8,128)(2,1)}), bf16[1,1024,1536]{2,1,0:T(8,128)(2,1)}) %all-gather.28.cloned.1.call-update) | async-done | bytes 3145744 | tf_op jit(solution)/shard_map/all_gather | solution.py:460
  623.3 21.2 %all-gather.7 = f32[544,384]{1,0:T(8,128)} all-gather(f32[136,384]{1,0:T(8,128)} %get-tuple-element.164), channel_id=9, replica_groups=mesh['z'=4,'p'=4,'head'=2] {'z'}, dimensions={0}, use_global_device_ids=true | all-gather | bytes 1044480 | tf_op jit(solution)/shard_map/all_gather | solution.py:536
  644.5 19.9 %shard_map.199 = (bf16[1040,768]{1,0:T(8,128)(2,1)}, f32[8,384]{1,0:T(8,128)}, f32[8,256]{1,0:T(8,128)}, f32[8,128]{1,0:T(8,128)}) custom-call(f32[4,136,384]{2,1,0:T(8,128)} %bitcast.223, f32[4,128,384]{2,1,0:T(8,128)} %get-tuple-element.165.prior, f32[4,8,384]{2,1,0:T(8,128)} %get-tuple-element.155.decay, f32[4,128,384]{2,1,0:T(8,128)} %get-tuple-element.166.states, ...), custom_call_target="tpu_custom_call" | custom-call | tf_op jit(solution)/shard_map/pallas_call | solution.py:412
  685.7 42.6 %reduce-scatter.15.cloned.1.call-done = bf16[256,1536]{1,0:T(8,128)(2,1)} async-done(((bf16[1024,1536]{1,0:T(8,128)(2,1)}), bf16[256,1536]{1,0:T(8,128)(2,1)}) %reduce-scatter.15.cloned.1.call-update) | async-done | bytes 786448 | tf_op jit(solution)/shard_map/reduce_scatter | solution.py:463
  729.2 23.6 %psum.145 = bf16[16,1536]{1,0:T(8,128)(2,1)S(1)} all-reduce(bf16[16,1536]{1,0:T(8,128)(2,1)S(1)} %slice.354), channel_id=1, replica_groups=mesh['z'=4,'p'=4,'head'=2] {'p','head'}, use_global_device_ids=true, to_apply=%region_11.12 | all-reduce | flops 24576 | bytes 98304 | tf_op jit(solution)/shard_map/psum | solution.py:562
  771.8 33.8 %all-gather.26.cloned.1.call-done.dmix = bf16[1024,1536]{1,0:T(8,128)(2,1)} async-done(((bf16[256,1536]{1,0:T(8,128)(2,1)}), bf16[1024,1536]{1,0:T(8,128)(2,1)}) %all-gather.26.cloned.1.call-update) | async-done | bytes 3145744 | tf_op jit(solution)/shard_map/all_gather | solution.py:460
  817.6 22.0 %all-gather.8 = f32[544,384]{1,0:T(8,128)} all-gather(f32[136,384]{1,0:T(8,128)} %get-tuple-element.176), channel_id=10, replica_groups=mesh['z'=4,'p'=4,'head'=2] {'z'}, dimensions={0}, use_global_device_ids=true | all-gather | bytes 1044480 | tf_op jit(solution)/shard_map/all_gather | solution.py:536
  839.6 20.0 %shard_map.202 = (bf16[1040,768]{1,0:T(8,128)(2,1)}, f32[8,384]{1,0:T(8,128)}, f32[8,256]{1,0:T(8,128)}, f32[8,128]{1,0:T(8,128)}) custom-call(f32[4,136,384]{2,1,0:T(8,128)} %bitcast.224, f32[4,128,384]{2,1,0:T(8,128)} %get-tuple-element.177.prior, f32[4,8,384]{2,1,0:T(8,128)} %get-tuple-element.145.decay, f32[4,128,384]{2,1,0:T(8,128)} %get-tuple-element.178.states, ...), custom_call_target="tpu_custom_call" | custom-call | tf_op jit(solution)/shard_map/pallas_call | solution.py:412
  887.0 47.3 %reduce-scatter.29.cloned.1.call-done = bf16[96,256]{1,0:T(8,128)(2,1)} async-done(((bf16[1536,256]{1,0:T(8,128)(2,1)}), bf16[96,256]{1,0:T(8,128)(2,1)}) %reduce-scatter.29.cloned.1.call-update) | async-done | bytes 49168 | tf_op jit(solution)/shard_map/reduce_scatter | solution.py:580
  934.3 127.1 %reduce-scatter.27.cloned.1.call-done = bf16[96,256]{1,0:T(8,128)(2,1)} async-done(((bf16[1536,256]{1,0:T(8,128)(2,1)}), bf16[96,256]{1,0:T(8,128)(2,1)}) %reduce-scatter.27.cloned.1.call-update) | async-done | bytes 49168 | tf_op jit(solution)/shard_map/reduce_scatter | solution.py:580
  1061.5 46.1 %reduce-scatter.17.cloned.1.call-done = bf16[256,1536]{1,0:T(8,128)(2,1)} async-done(((bf16[1024,1536]{1,0:T(8,128)(2,1)}), bf16[256,1536]{1,0:T(8,128)(2,1)}) %reduce-scatter.17.cloned.1.call-update) | async-done | bytes 786448 | tf_op jit(solution)/shard_map/reduce_scatter | solution.py:463
  1136.7 60.6 %reduce-scatter.21.cloned.1.call-done = bf16[3,384,384]{2,1,0:T(8,128)(2,1)} async-done(((bf16[3,1536,384]{2,1,0:T(8,128)(2,1)}), bf16[3,384,384]{2,1,0:T(8,128)(2,1)}) %reduce-scatter.21.cloned.1.call-update) | async-done | bytes 884752 | tf_op jit(solution)/shard_map/reduce_scatter | solution.py:575
  1220.8 22.7 %psum.147 = bf16[16,1536]{1,0:T(8,128)(2,1)S(1)} all-reduce(bf16[16,1536]{1,0:T(8,128)(2,1)S(1)} %slice.357), channel_id=1, replica_groups=mesh['z'=4,'p'=4,'head'=2] {'p','head'}, use_global_device_ids=true, to_apply=%region_16.17 | all-reduce | flops 24576 | bytes 98304 | tf_op jit(solution)/shard_map/psum | solution.py:562
  1264.5 85.0 %all-reduce.8 = (bf16[1536]{0:T(1024)(128)(2,1)}, bf16[1536]{0:T(1024)(128)(2,1)}, bf16[6,1536]{1,0:T(8,128)(2,1)S(1)}, bf16[6,1536]{1,0:T(8,128)(2,1)S(1)}, bf1...) all-reduce(f32[1536]{0:T(1024)S(1)} %get-tuple-element.247, ...), channel_id=1, replica_groups=mesh['z'=4,'p'=4,'head'=2] {'z','p'}, use_global_device_ids=true, to_apply=%region_21.22 | all-reduce | flops 24208 | bytes 145248 | tf_op jit(solution)/shard_map/psum | solution.py:590
  (299 shorter events, 355.2 us)
Async XLA Ops:
  7.2 182.7 %all-gather.18.cloned.1.call-start = ((), (), s32[]{:S(2)}) async-start(), calls=%async_computation.16 | async-start | bytes 3932160 | tf_op jit(solution)/shard_map/all_gather | solution.py:460
  12.4 183.8 %all-gather.20.cloned.1.call-start = ((), (), s32[]{:S(2)}) async-start(), calls=%async_computation.17 | async-start | bytes 4423680 | tf_op jit(solution)/shard_map/all_gather | solution.py:453
  40.9 247.0 %reduce-scatter.11.cloned.1.call-start = ((), (), s32[]{:S(2)}) async-start(), calls=%async_computation.18 | async-start | bytes 3932160 | tf_op jit(solution)/shard_map/reduce_scatter | solution.py:463
  245.8 63.6 %all-reduce.17.cloned.1.call-start = ((), (), s32[]{:S(2)}) async-start(), calls=%async_computation.19 | async-start | bytes 1572864 | tf_op jit(solution)/shard_map/psum | solution.py:463
  287.9 102.0 %all-gather.22.cloned.1.call-start = ((), (), s32[]{:S(2)}) async-start(), calls=%async_computation.20 | async-start | bytes 3932160 | tf_op jit(solution)/shard_map/all_gather | solution.py:460
  312.3 133.4 %all-gather.24.cloned.1.call-start = ((), (), s32[]{:S(2)}) async-start(), calls=%async_computation.21 | async-start | bytes 4423680 | tf_op jit(solution)/shard_map/all_gather | solution.py:453
  338.9 203.7 %reduce-scatter.13.cloned.1.call-start = ((), (), s32[]{:S(2)}) async-start(), calls=%async_computation.22 | async-start | bytes 3932160 | tf_op jit(solution)/shard_map/reduce_scatter | solution.py:463
  390.7 59.0 %collective-permute-start.1 = (bf16[16,1536]{1,0:T(8,128)(2,1)S(1)}, bf16[16,1536]{1,0:T(8,128)(2,1)S(1)}, u32[]{:S(2)}, u32[]{:S(2)}) collective-permute-start(bf16[16,1536]{1,0:T(8,128)(2,1)S(1)} %slice.394), channel_id=1, source_target_pairs={{0,8},{8,16},{16,24},{1,9},{9,17},{17,25},{2,10},{10,18},{18,26},{... | collective-permute-start | bytes 147464 | tf_op jit(solution)/shard_map/ppermute | solution.py:473
  499.1 65.2 %all-reduce.19.cloned.1.call-start = ((), (), s32[]{:S(2)}) async-start(), calls=%async_computation.23 | async-start | bytes 1572864 | tf_op jit(solution)/shard_map/psum | solution.py:463
  542.6 68.7 %all-gather.28.cloned.1.call-start = ((), (), s32[]{:S(2)}) async-start(), calls=%async_computation.35 | async-start | bytes 3932160 | tf_op jit(solution)/shard_map/all_gather | solution.py:460
  543.4 184.9 %reduce-scatter.15.cloned.1.call-start = ((), (), s32[]{:S(2)}) async-start(), calls=%async_computation.24 | async-start | bytes 3932160 | tf_op jit(solution)/shard_map/reduce_scatter | solution.py:463
  685.7 68.5 %all-reduce.21.cloned.1.call-start = ((), (), s32[]{:S(2)}) async-start(), calls=%async_computation.25 | async-start | bytes 1572864 | tf_op jit(solution)/shard_map/psum | solution.py:463
  728.3 77.3 %all-gather.26.cloned.1.call-start = ((), (), s32[]{:S(2)}) async-start(), calls=%async_computation.26 | async-start | bytes 3932160 | tf_op jit(solution)/shard_map/all_gather | solution.py:460
  762.6 171.7 %reduce-scatter.29.cloned.1.call-start = ((), (), s32[]{:S(2)}) async-start(), calls=%async_computation.34 | async-start | bytes 835584 | tf_op jit(solution)/shard_map/reduce_scatter | solution.py:580
  763.3 298.1 %reduce-scatter.27.cloned.1.call-start = ((), (), s32[]{:S(2)}) async-start(), calls=%async_computation.33 | async-start | bytes 835584 | tf_op jit(solution)/shard_map/reduce_scatter | solution.py:580
  877.4 230.2 %reduce-scatter.17.cloned.1.call-start = ((), (), s32[]{:S(2)}) async-start(), calls=%async_computation.27 | async-start | bytes 3932160 | tf_op jit(solution)/shard_map/reduce_scatter | solution.py:463
  881.2 249.2 %reduce-scatter.25.cloned.1.call-start = ((), (), s32[]{:S(2)}) async-start(), calls=%async_computation.32 | async-start | bytes 491520 | tf_op jit(solution)/shard_map/reduce_scatter | solution.py:581
  883.2 314.1 %reduce-scatter.21.cloned.1.call-start = ((), (), s32[]{:S(2)}) async-start(), calls=%async_computation.30 | async-start | bytes 4423680 | tf_op jit(solution)/shard_map/reduce_scatter | solution.py:575
  886.3 358.5 %reduce-scatter.23.cloned.1.call-start = ((), (), s32[]{:S(2)}) async-start(), calls=%async_computation.31 | async-start | bytes 491520 | tf_op jit(solution)/shard_map/reduce_scatter | solution.py:581
  886.9 368.0 %all-reduce.25.cloned.1.call-start = ((), (), s32[]{:S(2)}) async-start(), calls=%async_computation.36 | async-start | bytes 196608 | tf_op jit(solution)/shard_map/psum | solution.py:580
  1061.4 200.8 %all-reduce.23.cloned.1.call-start = ((), (), s32[]{:S(2)}) async-start(), calls=%async_computation.28 | async-start | bytes 1572864 | tf_op jit(solution)/shard_map/psum | solution.py:463
  1107.6 243.8 %reduce-scatter.19.cloned.1.call-start = ((), (), s32[]{:S(2)}) async-start(), calls=%async_computation.29 | async-start | bytes 4423680 | tf_op jit(solution)/shard_map/reduce_scatter | solution.py:575
  1132.0 67.4 %all-to-all-start.5 = ((bf16[4,96,1,6]{1,3,2,0:T(8,128)(2,1)}), bf16[4,96,1,6]{1,3,2,0:T(8,128)(2,1)S(1)}, u32[]{:S(2)}, u32[]{:S(2)}) async-start(bf16[4,96,1,6]{1,3,2,0:T(8,128)(2,1)} %copy.118), calls=%async_computation.13 | async-start | bytes 16384 | tf_op jit(solution)/shard_map/all_to_all | solution.py:582
  1243.5 20.0 %collective-permute-start.3 = (bf16[16,1536]{1,0:T(8,128)(2,1)S(1)}, bf16[16,1536]{1,0:T(8,128)(2,1)S(1)}, u32[]{:S(2)}, u32[]{:S(2)}) collective-permute-start(bf16[16,1536]{1,0:T(8,128)(2,1)S(1)} %psum.147), channel_id=1, source_target_pairs={{8,0},{16,8},{24,16},{9,1},{17,9},{25,17},{10,2},{18,10},{26,18},{... | collective-permute-start | bytes 147464 | tf_op jit(solution)/shard_map/ppermute | solution.py:563
  (34 other events, 692.0 us)
Sparse Core Ops, SparseCore 0:
  12.5 62.7 all-gather.17
  77.5 80.4 all-gather.19
  245.9 41.9 reduce-scatter.10
  290.1 19.1 all-reduce.16
  312.5 60.8 all-gather.21
  374.9 70.7 all-gather.23
  499.2 43.3 reduce-scatter.12
  545.1 19.1 all-reduce.18
  566.1 45.1 all-gather.27
  685.8 42.4 reduce-scatter.14
  730.6 19.1 all-reduce.20
  762.7 42.8 all-gather.25
  811.0 123.2 reduce-scatter.28
  940.1 121.2 reduce-scatter.26
  1064.5 43.0 reduce-scatter.16
  1109.8 20.5 reduce-scatter.24
  1132.6 64.6 reduce-scatter.20
  1199.9 20.8 reduce-scatter.22
  1223.3 16.1 all-reduce.24
  1241.8 20.3 all-reduce.22
  1264.5 70.6 reduce-scatter.18

commit v2 on v1

--- a/solution.py
+++ b/solution.py
@@ -76,7 +76,7 @@
 
 def forward_local(
     normed, wx, wz, wbc, wdt, rowp, bcp, headp,
-    z_out, xin_out, bcin_out, x_out, bc_out, dtraw_out, dt_out, s_out, y_out, local_out, decay_out, sum_out,
+    z_out, xin_out, bcin_out, x_out, bc_out, dtraw_out, dt_out, s_out, y_out, local_out, decay_out, sum_out, all_decay_out,
     ext,
 ):
     inner = x_out.shape[1]
@@ -147,21 +147,21 @@
     state_sum, decay_all = lax.fori_loop(
         0, spans, block, (jnp.zeros((STATE, inner), F32), jnp.ones((1, inner), F32))
     )
-    sum_out[0:STATE] = state_sum
-    sum_out[STATE : STATE + 8] = jnp.broadcast_to(decay_all, (8, inner))
-
-
-def entering_state(place, count, sums, backward):
+    sum_out[...] = state_sum.astype(BF16)
+    all_decay_out[...] = jnp.broadcast_to(decay_all, (8, inner))
+
+
+def entering_state(place, count, sums, decays, backward):
     inner = sums.shape[2]
     state = jnp.zeros((STATE, inner), F32)
     for turn in range(count):
         other = count - 1 - turn if backward else turn
         ahead = (place < other) if backward else (other < place)
-        state = jnp.where(ahead, sums[other, STATE : STATE + 1] * state + sums[other, 0:STATE], state)
+        state = jnp.where(ahead, decays[other, 0:1] * state + sums[other].astype(F32), state)
     return state
 
 
-def forward_carried(count, sums, local, decay, y_local, x, bc, z, s, wo, rowp, y_out, states_out, part_out, sq_out):
+def forward_carried(count, sums, decays, local, decay, y_local, x, bc, z, s, wo, rowp, y_out, states_out, part_out, sq_out):
     inner = x.shape[1]
     spans = x.shape[0] // SPAN
     spread = head_spread(inner)
@@ -181,12 +181,12 @@
         part_out[tok, :] = dot((gated * gain).astype(BF16), wo[...], NT).astype(BF16)
         return decay[q, 0:1] * state + local[q]
 
-    lax.fori_loop(0, spans, block, entering_state(lax.axis_index("z"), count, sums, False))
+    lax.fori_loop(0, spans, block, entering_state(lax.axis_index("z"), count, sums, decays, False))
 
 
 def backward_gate(
     inner_all, dmix, wo, y_in, z, x, bc, s, decay, token_scalars, rowp,
-    dz_out, dy_out, gwo_out, prior_out, sum_out, small_out,
+    dz_out, dy_out, gwo_out, prior_out, sum_out, all_decay_out, small_out,
     normed_out,
 ):
     inner = x.shape[1]
@@ -228,8 +228,8 @@
     decay_all = decay[0, 0:1]
     for q in range(1, spans):
         decay_all = decay_all * decay[q, 0:1]
-    sum_out[0:STATE] = grad_sum
-    sum_out[STATE : STATE + 8] = jnp.broadcast_to(decay_all, (8, inner))
+    sum_out[...] = grad_sum.astype(BF16)
+    all_decay_out[...] = jnp.broadcast_to(decay_all, (8, inner))
     small_out[0:1] = gain_sum
     small_out[1:2] = skip_sum
     small_out[2:8] = jnp.zeros((6, inner), F32)
@@ -243,7 +243,7 @@
 
 
 def backward_ssd(
-    count, sums, prior, decay, states, dy_in, x, bc, s_in, dt_in, dtraw, xin, bcin, rowp, bcp, headp,
+    count, sums, decays, prior, decay, states, dy_in, x, bc, s_in, dt_in, dtraw, xin, bcin, rowp, bcp, headp,
     dcat_out, row_out, bcrow_out, head_out,
     dpre, dend,
 ):
@@ -261,7 +261,7 @@
         dend[q] = grad
         return prior[q] + decay[q, 0:1] * grad
 
-    lax.fori_loop(0, spans, chain, entering_state(lax.axis_index("z"), count, sums, True))
+    lax.fori_loop(0, spans, chain, entering_state(lax.axis_index("z"), count, sums, decays, True))
     dpre[0:EDGE] = jnp.zeros((EDGE, width), F32)
     dpre[EDGE + spans * SPAN :] = jnp.zeros((EDGE, width), F32)
     row_out[...] = jnp.zeros_like(row_out)
@@ -370,7 +370,7 @@
     lax.fori_loop(0, spans, conv_block, 0)
 
 
-def backward_project(dcat, dz, normed, wx, wz, wbc, wdt, dn_out, gxz_out, gbc_out, gdt_out):
+def backward_project(dcat, dz, normed, wx, wz, wbc, wdt, dn_out, gx_out, gz_out, gbc_out, gdt_out):
     inner = dz.shape[1]
     width = inner + 2 * STATE
     spans = dz.shape[0] // SPAN
@@ -397,32 +397,798 @@
     def grads_of(i, _):
         cols = pl.ds(pl.multiple_of(i * SPAN, SPAN), SPAN)
         part = normed[:, cols]
-        both = dot(part, dcat[...], TN).astype(BF16)
-        gxz_out[cols, 0:inner] = both[:, 0:inner]
-        gbc_out[cols, :] = both[:, inner:width]
-        gdt_out[cols, :] = both[:, width:]
-        gxz_out[cols, inner:] = dot(part[EDGE:], dz[...], TN).astype(BF16)
+        both = dot(part, dcat[:, 0:width], TN).astype(BF16)
+        gx_out[cols, :] = both[:, 0:inner]
+        gbc_out[cols, :] = both[:, inner:]
+        gdt_out[:, cols] = dot(dcat[:, width:], part, TN)[0:EDGE].astype(BF16)
+        gz_out[cols, :] = dot(part[EDGE:], dz[...], TN).astype(BF16)
         return 0
 
     lax.fori_loop(0, normed.shape[1] // SPAN, grads_of, 0)
 
 
-def call(body, outs, *args, scratch=()):
+HALF = 128
+MESH = pl.DeviceIdType.MESH
+
+
+class Links:
+    def __init__(self, sends, recvs):
+        self.z, self.p, self.c = lax.axis_index("z"), lax.axis_index("p"), lax.axis_index("head")
+        self.groups = lax.axis_size("z")
+        self.sends, self.recvs, self.used = sends, recvs, 0
+
+    def copy(self, src, dst, device):
+        i = self.used
+        self.used += 1
+        return pltpu.make_async_remote_copy(
+            src_ref=src, dst_ref=dst, send_sem=self.sends.at[i], recv_sem=self.recvs.at[i],
+            device_id=device, device_id_type=MESH,
+        )
+
+    def local(self, src, dst):
+        i = self.used
+        self.used += 1
+        return pltpu.make_async_copy(src, dst, self.sends.at[i])
+
+    def at(self, k, e):
+        return (self.z, lax.bitwise_xor(self.p, jnp.int32(k)), lax.bitwise_xor(self.c, jnp.int32(e)))
+
+    def last_of_plane(self):
+        return jnp.logical_and(self.p == GROUP - 1, self.c == 1)
+
+    def start_barrier(self, plane=False, lines=False, edge=0):
+        barrier = pltpu.get_barrier_semaphore()
+        z, groups = self.z, self.groups
+
+        def signal(device):
+            pl.semaphore_signal(barrier, 1, device_id=device, device_id_type=MESH)
+
+        if plane:
+            for k in range(GROUP):
+                for e in range(2):
+                    if k or e:
+                        signal(self.at(k, e))
+        has_below, has_above = z > 0, z < groups - 1
+        if lines:
+            pl.when(has_below)(lambda: signal((z - 1, self.p, self.c)))
+            pl.when(has_above)(lambda: signal((z + 1, self.p, self.c)))
+        if edge == 1:
+            pl.when(has_below)(lambda: signal((z - 1, jnp.int32(GROUP - 1), jnp.int32(1))))
+        if edge == -1:
+
+            @pl.when(jnp.logical_and(self.last_of_plane(), has_above))
+            def _():
+                for p in range(GROUP):
+                    for c in range(2):
+                        signal((z + 1, jnp.int32(p), jnp.int32(c)))
+
+        count = jnp.int32(2 * GROUP - 1 if plane else 0)
+        if lines:
+            count = count + has_below.astype(jnp.int32) + has_above.astype(jnp.int32)
+        if edge == 1:
+            sending = jnp.logical_and(self.last_of_plane(), has_above)
+            count = count + 2 * GROUP * sending.astype(jnp.int32)
+        if edge == -1:
+            count = count + has_below.astype(jnp.int32)
+        pl.semaphore_wait(barrier, count)
+
+
+class Gather:
+    def __init__(self, links, out, base):
+        self.links, self.out, self.base = links, out, base
+
+        def place(k, c):
+            row = base + lax.bitwise_xor(links.p, jnp.int32(k)) * (2 * HALF) + c * HALF
+            return out.at[pl.ds(pl.multiple_of(row, EDGE), HALF), :]
+
+        own = place(0, links.c)
+        self.out_copies = [links.copy(own, own, links.at(k, 0)) for k in (3, 1, 2)]
+        self.shared = [links.copy(own, own, links.at(0, 1))]
+        self.shared += [links.copy(place(k, links.c), place(k, links.c), links.at(0, 1)) for k in (1, 2, 3)]
+        self.arrivals = [self.out_copies[1], self.out_copies[2], self.out_copies[0]]
+
+    def own(self, start, size):
+        row = self.base + self.links.p * (2 * HALF) + self.links.c * HALF + start
+        return pl.ds(pl.multiple_of(row, EDGE), size)
+
+    def start(self):
+        for copy in self.out_copies:
+            copy.start()
+        self.shared[0].start()
+
+    def pass_on(self):
+        for k in range(3):
+            self.arrivals[k].wait_recv()
+            self.shared[k + 1].start()
+
+    def finish(self):
+        for copy in self.shared:
+            copy.wait_recv()
+        for copy in self.shared + self.out_copies:
+            copy.wait_send()
+
+
+class EdgeForward:
+    def __init__(self, links, gather):
+        self.links = links
+        tail = gather.out.at[gather.own(HALF - EDGE, EDGE), :]
+        first = links.used
+        links.used += 2 * GROUP + 1
+        recv = links.recvs.at[first + 2 * GROUP]
+        self.out = gather.out
+        self.copies = [
+            pltpu.make_async_remote_copy(
+                src_ref=tail, dst_ref=gather.out.at[0:EDGE, :], send_sem=links.sends.at[first + p * 2 + c], recv_sem=recv,
+                device_id=(links.z + 1, jnp.int32(p), jnp.int32(c)), device_id_type=MESH,
+            )
+            for p in range(GROUP)
+            for c in range(2)
+        ]
+        self.sending = jnp.logical_and(links.last_of_plane(), links.z < links.groups - 1)
+
+    def start(self):
+        @pl.when(self.sending)
+        def _():
+            for copy in self.copies:
+                copy.start()
+
+        @pl.when(self.links.z == 0)
+        def _():
+            self.out[0:EDGE, :] = jnp.zeros((EDGE, self.out.shape[1]), self.out.dtype)
+
+    def finish(self):
+        pl.when(self.links.z > 0)(self.copies[0].wait_recv)
+
+        @pl.when(self.sending)
+        def _():
+            for copy in self.copies:
+                copy.wait_send()
+
+
+class Scatter:
+    def __init__(self, links, part, base, sib, total, peer):
+        self.links, self.part, self.base = links, part, base
+        self.sib, self.total, self.peer = sib, total, peer
+        other = 1 - links.c
+        self.to_sibling = {
+            k: links.copy(part.at[self.rows(k, other, 0, HALF), :], sib.at[k], links.at(0, 1)) for k in (3, 1, 2, 0)
+        }
+        self.to_peer = {k: links.copy(total.at[k - 1], peer.at[k - 1], links.at(k, 0)) for k in (3, 1, 2)}
+
+    def rows(self, k, c, start, size):
+        row = self.base + lax.bitwise_xor(self.links.p, jnp.int32(k)) * (2 * HALF) + c * HALF + start
+        return pl.ds(pl.multiple_of(row, EDGE), size)
+
+    def start(self):
+        for copy in self.to_sibling.values():
+            copy.start()
+
+    def reduce(self):
+        for k in (3, 1, 2):
+            self.to_sibling[k].wait_recv()
+
+            def add(i, _, k=k):
+                at = pl.ds(pl.multiple_of(i * 32, 32), 32)
+                mine = self.part[self.rows(k, self.links.c, i * 32, 32), :].astype(F32)
+                self.total[k - 1, at, :] = (mine + self.sib[k, at, :].astype(F32)).astype(BF16)
+                return 0
+
+            lax.fori_loop(0, HALF // 32, add, 0)
+            self.to_peer[k].start()
+        self.to_sibling[0].wait_recv()
+        for copy in self.to_peer.values():
+            copy.wait_recv()
+
+    def own(self, start, size):
+        at = pl.ds(start, size)
+        total = self.part[self.rows(0, self.links.c, start, size), :].astype(F32) + self.sib[0, at, :].astype(F32)
+        for k in range(3):
+            total = total + self.peer[k, at, :].astype(F32)
+        return total
+
+    def finish(self):
+        for copy in list(self.to_sibling.values()) + list(self.to_peer.values()):
+            copy.wait_send()
+
+
+class SmallSum:
+    def __init__(self, links, squares, slots):
+        self.links, self.squares, self.slots = links, squares, slots
+        self.copies = [
+            links.copy(squares.at[:, self.lanes(k, e)], slots.at[2 * k + e - 1], links.at(k, e))
+            for k in range(GROUP)
+            for e in range(2)
+            if k or e
+        ]
+
+    def lanes(self, k, e):
+        links = self.links
+        column = lax.bitwise_xor(links.p, jnp.int32(k)) * (2 * HALF) + lax.bitwise_xor(links.c, jnp.int32(e)) * HALF
+        return pl.ds(pl.multiple_of(column, HALF), HALF)
+
+    def start(self):
+        for copy in self.copies:
+            copy.start()
+
+    def total(self):
+        for copy in self.copies:
+            copy.wait_recv()
+        total = self.squares[:, self.lanes(0, 0)]
+        for i in range(len(self.copies)):
+            total = total + self.slots[i]
+        return total
+
+    def finish(self):
+        for copy in self.copies:
+            copy.wait_send()
+
+
+class SmallGather:
+    def __init__(self, links, out):
+        self.out = out
+        self.lanes = pl.ds(pl.multiple_of(links.p * (2 * HALF) + links.c * HALF, HALF), HALF)
+        self.copies = [
+            links.copy(out.at[:, self.lanes], out.at[:, self.lanes], links.at(k, e))
+            for k in range(GROUP)
+            for e in range(2)
+            if k or e
+        ]
+
+    def start(self):
+        for copy in self.copies:
+            copy.start()
+
+    def finish(self):
+        for copy in self.copies:
+            copy.wait()
+
+
+def row_chunks(size=32):
+    return [(start, size) for start in range(0, HALF, size)]
+
+
+def rms_of(rows):
+    return lax.rsqrt(jnp.mean(rows * rows, axis=-1, keepdims=True) + EPS)
+
+
+def as_tile(columns):
+    lane = iota((HALF, HALF), 1)
+    wide = jnp.zeros((HALF, HALF), F32)
+    for i, column in enumerate(columns):
+        wide = jnp.where(lane == i, column, wide)
+    return wide.T[0:8]
+
+
+def begin_kernel(
+    resid, cot, gain, wx, wz, wo, wbd, normed_out, dmix_out, wx_out, wz_out, wo_out, wbd_out, resid_out, cot_out,
+    sends, recvs,
+):
+    links = Links(sends, recvs)
+    z, p, c = links.z, links.p, links.c
+    inner = wx_out.shape[2]
+    groups = links.groups
+
+    def columns(k):
+        return pl.ds(pl.multiple_of(lax.bitwise_xor(p, jnp.int32(k)) * inner, 128), inner)
+
+    mine = z * GROUP + p
+    pairs = ((wx, wx_out), (wz, wz_out), (wo, wo_out))
+    swaps = [[links.copy(w.at[:, columns(k)], out.at[mine], links.at(k, 0)) for k in (1, 2, 3)] for w, out in pairs]
+    swaps.append([links.copy(wbd, wbd_out.at[c, mine], links.at(k, 0)) for k in (1, 2, 3)])
+    keeps = [links.local(w.at[:, columns(0)], out.at[mine]) for w, out in pairs]
+    keeps.append(links.local(wbd, wbd_out.at[c, mine]))
+    for copy in keeps:
+        copy.start()
+
+    gather = Gather(links, normed_out, EDGE)
+    other = Gather(links, dmix_out, 0)
+    edge = EdgeForward(links, gather)
+    for start, size in row_chunks():
+        rows = pl.ds(pl.multiple_of(c * HALF + start, EDGE), size)
+        part = resid[rows, :].astype(F32)
+        resid_out[start : start + size] = part
+        normed_out[gather.own(start, size), :] = (part * rms_of(part) * gain[...]).astype(BF16)
+        part = cot[rows, :]
+        cot_out[start : start + size] = part.astype(F32)
+        dmix_out[other.own(start, size), :] = part
+
+    links.start_barrier(plane=True, lines=True, edge=1)
+    for group in swaps:
+        for copy in group:
+            copy.start()
+    gather.start()
+    edge.start()
+
+    def piece(i, index):
+        at = pl.ds(index * GROUP, GROUP)
+        return wbd_out.at[c, at] if i == 3 else pairs[i][1].at[at]
+
+    def lines(step):
+        found = []
+        up, down = z - step + 1, z + step - 1
+        for i in range(4):
+            block = piece(i, jnp.maximum(up, 0))
+            sending = jnp.logical_and(up >= 0, z < groups - 1)
+            found.append((sending, z - step >= 0, links.copy(block, block, (z + 1, p, c))))
+            block = piece(i, jnp.minimum(down, groups - 1))
+            sending = jnp.logical_and(down < groups, z > 0)
+            found.append((sending, z + step < groups, links.copy(block, block, (z - 1, p, c))))
+        return found
+
+    steps = [lines(step) for step in range(1, groups)]
+    share = links.copy(wbd_out.at[c], wbd_out.at[c], links.at(0, 1))
+    for i in range(4):
+        keeps[i].wait()
+        for copy in swaps[i]:
+            copy.wait_recv()
+        for can_send, _, copy in steps[0][2 * i : 2 * i + 2]:
+            pl.when(can_send)(copy.start)
+    gather.pass_on()
+    other.start()
+    for step in range(1, len(steps)):
+        for i in range(8):
+            pl.when(steps[step - 1][i][1])(steps[step - 1][i][2].wait_recv)
+            pl.when(steps[step][i][0])(steps[step][i][2].start)
+        if step == 1:
+            other.pass_on()
+    for i in range(8):
+        pl.when(steps[-1][i][1])(steps[-1][i][2].wait_recv)
+    share.start()
+    gather.finish()
+    other.finish()
+    edge.finish()
+    for group in swaps:
+        for copy in group:
+            copy.wait_send()
+    for found in steps:
+        for can_send, _, copy in found:
+            pl.when(can_send)(copy.wait_send)
+    share.wait()
+
+
+def exchange_kernel(backward, state, decay, states_out, decays_out, sends, recvs):
+    links = Links(sends, recvs)
+    z, groups = links.z, links.groups
+    states_out[z] = state[...]
+    decays_out[z] = decay[...]
+    barrier = pltpu.get_barrier_semaphore()
+    found = []
+    for k in range(1, groups):
+        to, source = (z - k, z + k) if backward else (z + k, z - k)
+        sending, receiving = (to >= 0, source < groups) if backward else (to < groups, source >= 0)
+        device = (jnp.clip(to, 0, groups - 1), links.p, links.c)
+        pair = [
+            links.copy(states_out.at[z], states_out.at[z], device),
+            links.copy(decays_out.at[z], decays_out.at[z], device),
+        ]
+        found.append((sending, receiving, pair))
+
+        @pl.when(receiving)
+        def _(source=source):
+            pl.semaphore_signal(barrier, 1, device_id=(source, links.p, links.c), device_id_type=MESH)
+
+    count = z if backward else groups - 1 - z
+    pl.when(count > 0)(lambda: pl.semaphore_wait(barrier, count))
+    for sending, _, pair in found:
+
+        @pl.when(sending)
+        def _(pair=pair):
+            for copy in pair:
+                copy.start()
+
+    for sending, receiving, pair in found:
+
+        @pl.when(receiving)
+        def _(pair=pair):
+            for copy in pair:
+                copy.wait_recv()
+
+        @pl.when(sending)
+        def _(pair=pair):
+            for copy in pair:
+                copy.wait_send()
+
+
+class SmallSums:
+    def __init__(self, links, bc, vec, dt, wide, bc_out, vec_out, dt_out, wide_out, bufs):
+        self.links = links
+        self.bc, self.vec, self.dt, self.wide = bc, vec, dt, wide
+        self.bc_out, self.vec_out, self.dt_out, self.wide_out = bc_out, vec_out, dt_out, wide_out
+        self.bc_in, self.bc_sum, self.bc_far, self.vec_in, self.vec_far, self.dt_far, self.wide_far = bufs
+        z, p, c, groups = links.z, links.p, links.c, links.groups
+        self.first, self.second, self.third = [], [], []
+        for k in range(GROUP):
+            for e in range(2):
+                if not (k or e):
+                    continue
+                slot = 2 * k + e
+                to_p, to_c = lax.bitwise_xor(p, jnp.int32(k)), lax.bitwise_xor(c, jnp.int32(e))
+                device = links.at(k, e)
+                for layer in range(bc.shape[0]):
+                    src = bc.at[layer, :, to_p, :, pl.ds(pl.multiple_of(to_c * STATE, STATE), STATE)]
+                    self.first.append(links.copy(src, self.bc_in.at[layer, slot - 1], device))
+                self.first.append(links.copy(vec.at[to_p * 2 + to_c], self.vec_in.at[slot - 1], device))
+                self.third.append(links.copy(vec_out.at[p * 2 + c], vec_out.at[p * 2 + c], device))
+        for k in range(1, groups):
+            to = lax.rem(z + k, groups)
+            device = (to, p, c)
+            for layer in range(bc.shape[0]):
+                self.second.append(links.copy(self.bc_sum.at[layer, to], self.bc_far.at[layer, k - 1], device))
+            self.second.append(links.copy(self.vec_in.at[7], self.vec_far.at[k - 1], device))
+            self.second.append(links.copy(dt.at[to], self.dt_far.at[k - 1], device))
+            self.second.append(links.copy(wide, self.wide_far.at[k - 1], device))
+        for k in range(1, GROUP):
+            device = links.at(k, 0)
+            self.third.append(links.copy(dt_out.at[p], dt_out.at[p], device))
+            self.third.append(links.copy(wide_out.at[p], wide_out.at[p], device))
+        lanes = pl.ds(pl.multiple_of(c * STATE, STATE), STATE)
+        self.third.append(links.copy(bc_out.at[:, :, lanes], bc_out.at[:, :, lanes], links.at(0, 1)))
+
+    def round_one(self):
+        for copy in self.first:
+            copy.start()
+
+    def round_two(self):
+        links = self.links
+        for copy in self.first:
+            copy.wait_recv()
+        own_lanes = pl.ds(pl.multiple_of(links.c * STATE, STATE), STATE)
+        for layer in range(self.bc.shape[0]):
+
+            def add(i, _, layer=layer):
+                total = self.bc[layer, i, links.p, :, own_lanes].astype(F32)
+                for slot in range(2 * GROUP - 1):
+                    total = total + self.bc_in[layer, slot, i].astype(F32)
+                self.bc_sum[layer, i] = total.astype(BF16)
+                return 0
+
+            lax.fori_loop(0, links.groups, add, 0)
+        total = self.vec[links.p * 2 + links.c]
+        for slot in range(2 * GROUP - 1):
+            total = total + self.vec_in[slot]
+        self.vec_in[7] = total
+        for copy in self.second:
+            copy.start()
+
+    def round_three(self):
+        links = self.links
+        z, p, c = links.z, links.p, links.c
+        for copy in self.second:
+            copy.wait_recv()
+        far = links.groups - 1
+        lanes = pl.ds(pl.multiple_of(c * STATE, STATE), STATE)
+        for layer in range(self.bc.shape[0]):
+            total = self.bc_sum[layer, z].astype(F32)
+            for k in range(far):
+                total = total + self.bc_far[layer, k].astype(F32)
+            self.bc_out[layer, :, lanes] = total.astype(BF16)
+        total = self.vec_in[7]
+        dt_total = self.dt[z].astype(F32)
+        wide_total = self.wide[...]
+        for k in range(far):
+            total = total + self.vec_far[k]
+            dt_total = dt_total + self.dt_far[k].astype(F32)
+            wide_total = wide_total + self.wide_far[k]
+        self.vec_out[p * 2 + c] = total
+        self.dt_out[p] = dt_total.astype(BF16)
+        self.wide_out[p] = wide_total
+        for copy in self.third:
+            copy.start()
+
+    def finish(self):
+        for copy in self.third:
+            copy.wait_recv()
+        for copy in self.first + self.second + self.third:
+            copy.wait_send()
+
+
+def grads_kernel(
+    gx, gz, go, bc, vec, dt, wide, gx_out, gz_out, go_out, bc_out, vec_out, dt_out, wide_out,
+    up_buf, down_buf, total, final, bc_in, bc_sum, bc_far, vec_in, vec_far, dt_far, wide_far, sends, recvs,
+):
+    links = Links(sends, recvs)
+    z, p, c, groups = links.z, links.p, links.c, links.groups
+    inner = gx.shape[2]
+    parts, outs = (gx, gz, go), (gx_out, gz_out, go_out)
+    small = SmallSums(
+        links, bc, vec, dt, wide, bc_out, vec_out, dt_out, wide_out,
+        (bc_in, bc_sum, bc_far, vec_in, vec_far, dt_far, wide_far),
+    )
+    barrier = pltpu.get_barrier_semaphore()
+    for k in range(GROUP):
+        for e in range(2):
+            if k or e:
+                pl.semaphore_signal(barrier, 1, device_id=links.at(k, e), device_id_type=MESH)
+    for k in range(1, groups):
+        pl.semaphore_signal(barrier, 1, device_id=(lax.rem(z + k, groups), p, c), device_id_type=MESH)
+    pl.semaphore_wait(barrier, 2 * GROUP - 1 + groups - 1)
+
+    def block(i, index):
+        return parts[i].at[pl.ds(index * GROUP, GROUP)]
+
+    def add_own(i, index, buf):
+        def add(j, _):
+            buf[j] = (buf[j].astype(F32) + parts[i][index * GROUP + j].astype(F32)).astype(BF16)
+            return 0
+
+        lax.fori_loop(0, GROUP, add, 0)
+
+    small.round_one()
+    waits = []
+    for s in range(groups - 1):
+        for i in range(3):
+            for up in (True, False):
+                target = groups - 1 - s if up else s
+                buf = (up_buf if up else down_buf).at[s, i]
+                if up:
+                    first, passing, ends, to = z == 0, jnp.logical_and(z > 0, z < target), z == target, z + 1
+                else:
+                    first, passing, ends, to = z == groups - 1, jnp.logical_and(z < groups - 1, z > target), z == target, z - 1
+                index = links.used
+                links.used += 1
+
+                def copy_from(src, index=index, buf=buf, to=to):
+                    return pltpu.make_async_remote_copy(
+                        src_ref=src, dst_ref=buf, send_sem=links.sends.at[index], recv_sem=links.recvs.at[index],
+                        device_id=(to, p, c), device_id_type=MESH,
+                    )
+
+                here = block(i, target)
+
+                @pl.when(first)
+                def _(copy_from=copy_from, here=here):
+                    copy_from(here).start()
+
+                @pl.when(passing)
+                def _(copy_from=copy_from, buf=buf, i=i, target=target):
+                    copy_from(buf).wait_recv()
+                    add_own(i, target, buf)
+                    copy_from(buf).start()
+
+                pl.when(ends)(copy_from(buf).wait_recv)
+                waits.append((jnp.logical_or(first, passing), copy_from(buf)))
+        if s == 0:
+            small.round_two()
+        if s == 1:
+            small.round_three()
+    swaps = []
+    for i in range(3):
+        mine = pl.ds(pl.multiple_of(p * inner, 128), inner)
+
+        def own(j, _, i=i):
+            total[j] = parts[i][z * GROUP + j].astype(F32)
+            return 0
+
+        lax.fori_loop(0, GROUP, own, 0)
+
+        @pl.when(z > 0)
+        def _(i=i):
+            def add(j, _):
+                total[j] = total[j] + up_buf[groups - 1 - z, i, j].astype(F32)
+                return 0
+
+            lax.fori_loop(0, GROUP, add, 0)
+
+        @pl.when(z < groups - 1)
+        def _(i=i):
+            def add(j, _):
+                total[j] = total[j] + down_buf[z, i, j].astype(F32)
+                return 0
+
+            lax.fori_loop(0, GROUP, add, 0)
+
+        def store(j, _, i=i):
+            final[i, j] = total[j].astype(BF16)
+            return 0
+
+        lax.fori_loop(0, GROUP, store, 0)
+        outs[i][:, mine] = final[i, p]
+        for k in (1, 2, 3):
+            swaps.append(links.copy(final.at[i, lax.bitwise_xor(p, jnp.int32(k))], outs[i].at[:, mine], links.at(k, 0)))
+            swaps[-1].start()
+    for copy in swaps:
+        copy.wait()
+    small.finish()
+    for sent, copy in waits:
+        pl.when(sent)(copy.wait_send)
+
+
+def next_layer_kernel(
+    inner_all, part, squares, resid, gain, normed_out, resid_out, mixed_out, inv_out,
+    sib, total, peer, slots, sends, recvs,
+):
+    links = Links(sends, recvs)
+    scatter = Scatter(links, part, 0, sib, total, peer)
+    small = SmallSum(links, squares, slots)
+    gather = Gather(links, normed_out, EDGE)
+    edge = EdgeForward(links, gather)
+    links.start_barrier(plane=True, edge=1)
+    scatter.start()
+    small.start()
+    scatter.reduce()
+    inv = lax.rsqrt(small.total() * (1.0 / inner_all) + EPS)
+    inv_out[...] = inv
+    column = inv.T[:, 0:1]
+    for start, size in row_chunks():
+        at = slice(start, start + size)
+        mixed = scatter.own(start, size)
+        mixed_out[at] = mixed
+        fresh = resid[at] + column[at] * mixed
+        resid_out[at] = fresh
+        normed_out[gather.own(start, size), :] = (fresh * rms_of(fresh) * gain[...]).astype(BF16)
+    gather.start()
+    edge.start()
+    gather.pass_on()
+    scatter.finish()
+    small.finish()
+    gather.finish()
+    edge.finish()
+
+
+def turn_kernel(
+    inner_all, part, squares, resid, cot, block_out, scalars_out,
+    sib, total, peer, slots, sends, recvs,
+):
+    links = Links(sends, recvs)
+    scatter = Scatter(links, part, 0, sib, total, peer)
+    small = SmallSum(links, squares, slots)
+    spread = SmallGather(links, scalars_out)
+    rows = pl.ds(pl.multiple_of(links.c * HALF, HALF), HALF)
+    share = links.copy(block_out.at[rows, :], block_out.at[rows, :], links.at(0, 1))
+    links.start_barrier(plane=True)
+    scatter.start()
+    small.start()
+    scatter.reduce()
+    inv = lax.rsqrt(small.total() * (1.0 / inner_all) + EPS)
+    column = inv.T[:, 0:1]
+    dots = []
+    for start, size in row_chunks():
+        at = slice(start, start + size)
+        mixed = scatter.own(start, size)
+        dots.append(jnp.sum(cot[at] * mixed, axis=-1, keepdims=True))
+        block_out[pl.ds(pl.multiple_of(links.c * HALF + start, EDGE), size), :] = (
+            resid[at] + column[at] * mixed
+        ).astype(BF16)
+    scalars_out[:, spread.lanes] = as_tile([column, jnp.concatenate(dots)])
+    spread.start()
+    share.start()
+    scatter.finish()
+    small.finish()
+    spread.finish()
+    share.wait()
+
+
+def grad_rows(links, scatter, edge_slots, grad, resid, gain, gain_out, start, size):
+    at = slice(start, start + size)
+    d_normed = scatter.own(start, size)
+    if start + size == HALF:
+        extra = edge_slots[0].astype(F32)
+        for i in range(1, 2 * GROUP):
+            extra = extra + edge_slots[i].astype(F32)
+        used = jnp.logical_and(links.last_of_plane(), links.z < links.groups - 1)
+        extra = jnp.where(used, extra, 0.0)
+        d_normed = d_normed + jnp.concatenate([jnp.zeros((size - EDGE, extra.shape[1]), F32), extra])
+    rows = resid[at]
+    inv_rms = rms_of(rows)
+    gain_sum = jnp.sum(d_normed * rows * inv_rms, axis=0, keepdims=True)
+    gain_out[0:1] = gain_sum if start == 0 else gain_out[0:1] + gain_sum
+    d_hidden = d_normed * gain[...]
+    return (
+        grad[at]
+        + inv_rms * d_hidden
+        - rows * (inv_rms * inv_rms * inv_rms * jnp.mean(d_hidden * rows, axis=-1, keepdims=True))
+    )
+
+
+class EdgeBackward:
+    def __init__(self, links, part, slots):
+        self.links = links
+        first = links.used
+        links.used += 2 * GROUP + 1
+        me = links.p * 2 + links.c
+        self.send = pltpu.make_async_remote_copy(
+            src_ref=part.at[0:EDGE, :], dst_ref=slots.at[me], send_sem=links.sends.at[first], recv_sem=links.recvs.at[first + me],
+            device_id=(links.z - 1, jnp.int32(GROUP - 1), jnp.int32(1)), device_id_type=MESH,
+        )
+        self.recvs = [
+            pltpu.make_async_remote_copy(
+                src_ref=part.at[0:EDGE, :], dst_ref=slots.at[i], send_sem=links.sends.at[first], recv_sem=links.recvs.at[first + i],
+                device_id=(links.z, links.p, 1 - links.c), device_id_type=MESH,
+            )
+            for i in range(2 * GROUP)
+        ]
+        self.receiving = jnp.logical_and(links.last_of_plane(), links.z < links.groups - 1)
+
+    def start(self):
+        pl.when(self.links.z > 0)(self.send.start)
+
+    def receive(self):
+        @pl.when(self.receiving)
+        def _():
+            for copy in self.recvs:
+                copy.wait_recv()
+
+    def finish(self):
+        pl.when(self.links.z > 0)(self.send.wait_send)
+
+
+def layer_below_kernel(
+    part, grad, resid, gain, mixed, inv, dmix_out, scalars_out, grad_out, gain_out,
+    sib, total, peer, edge_slots, sends, recvs,
+):
+    links = Links(sends, recvs)
+    scatter = Scatter(links, part, EDGE, sib, total, peer)
+    edge = EdgeBackward(links, part, edge_slots)
+    gather = Gather(links, dmix_out, 0)
+    spread = SmallGather(links, scalars_out)
+    edge_slots[...] = jnp.zeros_like(edge_slots)
+    links.start_barrier(plane=True, edge=-1)
+    edge.start()
+    scatter.start()
+    scatter.reduce()
+    edge.receive()
+    gain_out[...] = jnp.zeros_like(gain_out)
+    dots = []
+    for start, size in row_chunks():
+        at = slice(start, start + size)
+        fresh = grad_rows(links, scatter, edge_slots, grad, resid, gain, gain_out, start, size)
+        grad_out[at] = fresh
+        low = fresh.astype(BF16)
+        dmix_out[gather.own(start, size), :] = low
+        dots.append(jnp.sum(low.astype(F32) * mixed[at], axis=-1, keepdims=True))
+    scalars_out[:, spread.lanes] = as_tile([inv[...].T[:, 0:1], jnp.concatenate(dots)])
+    gather.start()
+    spread.start()
+    gather.pass_on()
+    scatter.finish()
+    edge.finish()
+    gather.finish()
+    spread.finish()
+
+
+def last_grad_kernel(part, grad, resid, gain, out, gain_out, sib, total, peer, edge_slots, sends, recvs):
+    links = Links(sends, recvs)
+    scatter = Scatter(links, part, EDGE, sib, total, peer)
+    edge = EdgeBackward(links, part, edge_slots)
+    rows = pl.ds(pl.multiple_of(links.c * HALF, HALF), HALF)
+    share = links.copy(out.at[rows, :], out.at[rows, :], links.at(0, 1))
+    edge_slots[...] = jnp.zeros_like(edge_slots)
+    links.start_barrier(plane=True, edge=-1)
+    edge.start()
+    scatter.start()
+    scatter.reduce()
+    edge.receive()
+    gain_out[...] = jnp.zeros_like(gain_out)
+    for start, size in row_chunks():
+        fresh = grad_rows(links, scatter, edge_slots, grad, resid, gain, gain_out, start, size)
+        out[pl.ds(pl.multiple_of(links.c * HALF + start, EDGE), size), :] = fresh.astype(BF16)
+    share.start()
+    scatter.finish()
+    edge.finish()
+    share.wait()
+
+
+def call(body, outs, *args, scratch=(), collective=None, copies=0):
     vmem = pl.BlockSpec(memory_space=pltpu.VMEM)
+    scratch = [pltpu.VMEM(shape, kind) for shape, kind in scratch]
+    if collective is not None:
+        scratch += [pltpu.SemaphoreType.DMA((copies,)), pltpu.SemaphoreType.DMA((copies,))]
     return pl.pallas_call(
         body,
         out_shape=tuple(jax.ShapeDtypeStruct(shape, kind) for shape, kind in outs),
         in_specs=[vmem] * len(args),
         out_specs=tuple([vmem] * len(outs)),
-        scratch_shapes=list(scratch),
-        compiler_params=pltpu.CompilerParams(vmem_limit_bytes=VMEM_BYTES),
+        scratch_shapes=scratch,
+        compiler_params=pltpu.CompilerParams(
+            vmem_limit_bytes=VMEM_BYTES, collective_id=collective, has_side_effects=collective is not None
+        ),
     )(*args)
 
 
 def on_device(resid_in, cotangent, norm_gain, w_zx, w_dt, w_bc, conv_x, conv_bc, head_params, gated_gain, w_out):
     layers, model = norm_gain.shape
     groups = lax.axis_size("z")
-    place = lax.axis_index("p")
+    level, place, core = lax.axis_index("z"), lax.axis_index("p"), lax.axis_index("head")
     shard = w_dt.shape[1]
     inner_core = conv_x.shape[2]
     inner = inner_core // GROUP
@@ -432,14 +1198,18 @@
     length = resid_in.shape[1]
     tokens = GROUP * length
     spans = tokens // SPAN
+    sources = groups * GROUP
+    dt_rows = -(-shard * heads_core // STATE)
+    bd_rows = -(-(shard + dt_rows) // EDGE) * EDGE
 
     def my_part(array, size):
         return lax.dynamic_slice_in_dim(array, place * size, size, array.ndim - 1)
 
-    row_all, bc_all, head_all, weights = [], [], [], []
+    row_all, bc_all, head_all = [], [], []
     conv_mine = my_part(conv_x, inner).astype(F32)
     gain_mine = my_part(gated_gain, inner).astype(F32)
     head_mine = my_part(head_params, heads)
+    gains = [norm_gain[layer].astype(F32)[None] for layer in range(layers)]
     for layer in range(layers):
         skip = jnp.repeat(head_mine[layer, 2], HEADDIM)
         row_all.append(
@@ -447,32 +1217,89 @@
         )
         bc_all.append(jnp.pad(conv_bc[layer].astype(F32), ((0, 3), (0, 0))))
         head_all.append(jnp.pad(head_mine[layer], ((0, 5), (0, 128 - heads))))
-        stacked = jnp.stack([w_zx[layer, 1], w_zx[layer, 0], w_out[layer].T])
-        sliced = stacked.reshape(3, shard, GROUP, inner)
-        swapped = lax.all_to_all(sliced, "p", 2, 1)
-        gathered = lax.all_gather(swapped.reshape(3, GROUP * shard, inner), "z", axis=1, tiled=True)
-        dt_full = lax.all_gather(w_dt[layer], ("z", "p"), axis=0, tiled=True)
-        bc_full = lax.all_gather(w_bc[layer], ("z", "p"), axis=0, tiled=True)
-        dt_mine = jnp.pad(my_part(dt_full, heads), ((0, 0), (0, 128 - heads)))
-        weights.append((gathered[0], gathered[1], gathered[2], bc_full, dt_mine))
-
-    def gather_rows(block):
-        return lax.all_gather(block, "p", axis=0, tiled=True)
-
-    def scatter_rows(partial):
-        return lax.psum(lax.psum_scatter(partial, "p", scatter_dimension=0, tiled=True), "head")
-
-    resid = resid_in[0].astype(F32)
+
+    def shards_of(layer):
+        flat = w_dt[layer].reshape(-1)
+        flat = jnp.pad(flat, (0, (bd_rows - shard) * STATE - flat.shape[0])).reshape(bd_rows - shard, STATE)
+        half = lax.dynamic_slice_in_dim(w_bc[layer], core * STATE, STATE, 1)
+        return w_zx[layer, 1], w_zx[layer, 0], w_out[layer].T, jnp.concatenate([half, flat])
+
+    def weights_of(wx, wz, wo, wbd):
+        wbc = jnp.concatenate([wbd[0, :, :shard], wbd[1, :, :shard]], axis=-1).reshape(model, 2 * STATE)
+        own = lax.dynamic_index_in_dim(wbd, core, 0, False)[:, shard:].reshape(sources, -1)
+        wdt = own[:, : shard * heads_core].reshape(model, heads_core)
+        wdt = jnp.pad(my_part(wdt, heads), ((0, 0), (0, 128 - heads)))
+        return wx.reshape(model, inner), wz.reshape(model, inner), wo.reshape(model, inner), wbc, wdt
+
+    def pass_plane(pieces):
+        own = jax.tree.map(lambda a: lax.dynamic_index_in_dim(a, place, 0), pieces)
+        out = jax.tree.map(lambda a, o: lax.dynamic_update_slice_in_dim(jnp.zeros_like(a), o, place, 0), pieces, own)
+        for k in range(1, GROUP):
+            there = lax.bitwise_xor(place, jnp.int32(k))
+            sent = jax.tree.map(lambda a: lax.dynamic_index_in_dim(a, there, 0), pieces)
+            got = jax.tree.map(lambda a: lax.ppermute(a, "p", [(i, i ^ k) for i in range(GROUP)]), sent)
+            out = jax.tree.map(lambda o, a: lax.dynamic_update_slice_in_dim(o, a, there, 0), out, got)
+        return out
+
+    def pass_groups(pieces):
+        out = jax.tree.map(
+            lambda a: lax.dynamic_update_slice_in_dim(jnp.zeros((groups, *a.shape), a.dtype), a[None], level, 0), pieces
+        )
+        for k in range(1, groups):
+            got = jax.tree.map(lambda a: lax.ppermute(a, "z", [(i, (i + k) % groups) for i in range(groups)]), pieces)
+            source = lax.rem(level + groups - k, groups)
+            out = jax.tree.map(lambda o, a: lax.dynamic_update_slice_in_dim(o, a[None], source, 0), out, got)
+        return out
+
+    def later_weights(layer):
+        wx, wz, wo, wbd = shards_of(layer)
+        wide = [jnp.swapaxes(w.reshape(shard, GROUP, inner), 0, 1) for w in (wx, wz, wo)]
+        pieces = pass_plane(wide + [jnp.broadcast_to(wbd, (GROUP, *wbd.shape))])
+        wx, wz, wo, wbd = [a.reshape(sources, *a.shape[2:]) for a in pass_groups(pieces)]
+        other = lax.ppermute(wbd, "head", [(0, 1), (1, 0)])
+        wbd = jnp.where(core == 0, jnp.stack([wbd, other]), jnp.stack([other, wbd]))
+        return weights_of(wx, wz, wo, wbd)
+
+    half_scratch = [
+        ((GROUP, HALF, model), BF16),
+        ((GROUP - 1, HALF, model), BF16),
+        ((GROUP - 1, HALF, model), BF16),
+    ]
+    slots = ((2 * GROUP - 1, 8, HALF), F32)
+    edges = ((2 * GROUP, EDGE, model), BF16)
+    own_rows = ((HALF, model), F32)
+
+    first_shards = shards_of(0)
+    normed, last_dmix, wx, wz, wo, wbd, resid, grad = call(
+        begin_kernel,
+        [
+            ((tokens + EDGE, model), BF16),
+            ((tokens, model), BF16),
+            ((sources, shard, inner), BF16),
+            ((sources, shard, inner), BF16),
+            ((sources, shard, inner), BF16),
+            ((2, sources, bd_rows, STATE), BF16),
+            own_rows,
+            own_rows,
+        ],
+        resid_in[0], cotangent[0], gains[0], *first_shards,
+        collective=0, copies=44 + 8 * (groups - 1),
+    )
+    weights = [weights_of(wx, wz, wo, wbd)] + [later_weights(layer) for layer in range(1, layers)]
+
+    def exchanged(state, decay, backward):
+        return call(
+            functools.partial(exchange_kernel, backward),
+            [((groups, STATE, inner), BF16), ((groups, 8, inner), F32)],
+            state, decay,
+            collective=2 if backward else 1, copies=2 * groups,
+        )
+
     saved = []
     for layer in range(layers):
         wx, wz, wo, wbc, wdt = weights[layer]
         rowp, bcp, headp = row_all[layer], bc_all[layer], head_all[layer]
-        inv_rms = lax.rsqrt(jnp.mean(resid * resid, axis=-1, keepdims=True) + EPS)
-        own = (resid * inv_rms * norm_gain[layer].astype(F32)).astype(BF16)
-        normed = gather_rows(own)
-        edge = lax.ppermute(normed[tokens - EDGE :], "z", [(i, i + 1) for i in range(groups - 1)])
-        normed = jnp.concatenate([edge, normed])
-        z, xin, bcin, x, bc, dtraw, dt, s, y_local, local, decay, sums = call(
+        z, xin, bcin, x, bc, dtraw, dt, s, y_local, local, decay, sums, decay_all = call(
             forward_local,
             [
                 ((tokens, inner), BF16),
@@ -486,12 +1313,13 @@
                 ((tokens, inner), F32),
                 ((spans, STATE, inner), F32),
                 ((spans, 8, inner), F32),
-                ((STATE + 8, inner), F32),
+                ((STATE, inner), BF16),
+                ((8, inner), F32),
             ],
             normed, wx, wz, wbc, wdt, rowp, bcp, headp,
-            scratch=[pltpu.VMEM((tokens + EDGE, inner + 2 * STATE), F32)],
+            scratch=[((tokens + EDGE, inner + 2 * STATE), F32)],
         )
-        all_sums = lax.all_gather(sums, "z")
+        all_sums, all_decays = exchanged(sums, decay_all, False)
         y, states, part, squares = call(
             functools.partial(forward_carried, groups),
             [
@@ -500,40 +1328,47 @@
                 ((tokens, model), BF16),
                 ((8, tokens), F32),
             ],
-            all_sums, local, decay, y_local, x, bc, z, s, wo, rowp,
+            all_sums, all_decays, local, decay, y_local, x, bc, z, s, wo, rowp,
         )
-        mixed = scatter_rows(part).astype(F32)
-        total_sq = lax.psum(squares[0], ("p", "head"))
-        inv_all = lax.rsqrt(total_sq / inner_all + EPS)
-        inv_own = lax.dynamic_slice_in_dim(inv_all, place * length, length)[:, None]
-        saved.append((resid, inv_rms, normed, z, xin, bcin, x, bc, dtraw, dt, s, y, states, decay, mixed, inv_all))
-        resid = resid + inv_own * mixed
-    block_out = resid.astype(BF16)[None]
-
-    d_resid = cotangent[0].astype(F32)
-    big, small = [None] * layers, [None] * layers
+        kept = (resid, normed, z, xin, bcin, x, bc, dtraw, dt, s, y, states, decay)
+        if layer < layers - 1:
+            normed, resid, mixed, inv = call(
+                functools.partial(next_layer_kernel, inner_all),
+                [((tokens + EDGE, model), BF16), own_rows, own_rows, ((8, HALF), F32)],
+                part, squares, resid, gains[layer + 1],
+                scratch=half_scratch + [slots], collective=3, copies=40,
+            )
+            saved.append((*kept, mixed, inv))
+        else:
+            block_out, token_scalars = call(
+                functools.partial(turn_kernel, inner_all),
+                [((length, model), BF16), ((8, tokens), F32)],
+                part, squares, resid, grad,
+                scratch=half_scratch + [slots], collective=4, copies=40,
+            )
+            saved.append((*kept, None, None))
+
+    d_mix = last_dmix
+    big, kinds, gain_rows = [None] * layers, [None] * layers, [None] * layers
     for layer in reversed(range(layers)):
         wx, wz, wo, wbc, wdt = weights[layer]
         rowp, bcp, headp = row_all[layer], bc_all[layer], head_all[layer]
-        resid, inv_rms, normed, z, xin, bcin, x, bc, dtraw, dt, s, y, states, decay, mixed, inv_all = saved[layer]
-        d_mix_own = d_resid.astype(BF16)
-        dots = jnp.sum(d_mix_own.astype(F32) * mixed, axis=-1)
-        d_mix = gather_rows(d_mix_own)
-        token_scalars = jnp.pad(jnp.stack([inv_all, gather_rows(dots)]), ((0, 6), (0, 0)))
-        dz, dy, gwo, prior, sums, gate_small = call(
+        resid, normed, z, xin, bcin, x, bc, dtraw, dt, s, y, states, decay, _, _ = saved[layer]
+        dz, dy, gwo, prior, sums, decay_all, gate_small = call(
             functools.partial(backward_gate, inner_all),
             [
                 ((tokens, inner), BF16),
                 ((tokens, inner), BF16),
                 ((model, inner), BF16),
                 ((spans, STATE, inner), F32),
-                ((STATE + 8, inner), F32),
+                ((STATE, inner), BF16),
+                ((8, inner), F32),
                 ((8, inner), F32),
             ],
             d_mix, wo, y, z, x, bc, s, decay, token_scalars, rowp,
-            scratch=[pltpu.VMEM((tokens, inner), BF16)],
+            scratch=[((tokens, inner), BF16)],
         )
-        all_sums = lax.all_gather(sums, "z")
+        all_sums, all_decays = exchanged(sums, decay_all, True)
         dcat, row_small, bc_small, head_small = call(
             functools.partial(backward_ssd, groups),
             [
@@ -542,67 +1377,115 @@
                 ((8, 2 * STATE), F32),
                 ((8, 128), F32),
             ],
-            all_sums, prior, decay, states, dy, x, bc, s, dt, dtraw, xin, bcin, rowp, bcp, headp,
+            all_sums, all_decays, prior, decay, states, dy, x, bc, s, dt, dtraw, xin, bcin, rowp, bcp, headp,
             scratch=[
-                pltpu.VMEM((tokens + 2 * EDGE, inner + 2 * STATE), F32),
-                pltpu.VMEM((spans, STATE, inner), F32),
+                ((tokens + 2 * EDGE, inner + 2 * STATE), F32),
+                ((spans, STATE, inner), F32),
             ],
         )
-        d_normed_part, gxz, gbc, gdt = call(
+        part, gx, gz, gbc, gdt = call(
             backward_project,
             [
                 ((tokens + EDGE, model), BF16),
-                ((model, 2 * inner), BF16),
+                ((model, inner), BF16),
+                ((model, inner), BF16),
                 ((model, 2 * STATE), BF16),
-                ((model, 128), BF16),
+                ((EDGE, model), BF16),
             ],
             dcat, dz, normed, wx, wz, wbc, wdt,
         )
-        d_normed = scatter_rows(d_normed_part[EDGE:]).astype(F32)
-        edge = lax.psum(d_normed_part[:EDGE], ("p", "head"))
-        edge = lax.ppermute(edge, "z", [(i + 1, i) for i in range(groups - 1)]).astype(F32)
-        edge = jnp.where(place == GROUP - 1, edge, 0.0)
-        d_normed = d_normed.at[length - EDGE :].add(edge)
-        gain_grad = jnp.sum(d_normed * resid * inv_rms, axis=0)
-        d_hidden = d_normed * norm_gain[layer].astype(F32)
-        d_resid = (
-            d_resid
-            + inv_rms * d_hidden
-            - resid * inv_rms**3 * jnp.mean(d_hidden * resid, axis=-1, keepdims=True)
-        )
-
-        grads = jnp.stack([gxz[:, :inner], gxz[:, inner:], gwo])
-        grads = lax.psum_scatter(grads, "z", scatter_dimension=1, tiled=True)
-        grads = lax.all_to_all(grads.reshape(3, GROUP, shard, inner), "p", 1, 2)
-        grads = grads.reshape(3, shard, inner_core)
-        g_zx = jnp.stack([grads[1], grads[0]])
-        g_out = grads[2].T
-        g_bc = lax.psum(lax.psum_scatter(gbc, ("z", "p"), scatter_dimension=0, tiled=True), "head")
-        g_dt = lax.psum_scatter(gdt[:, :heads], "z", scatter_dimension=0, tiled=True)
-        g_dt = lax.all_to_all(g_dt.reshape(GROUP, shard, heads), "p", 0, 1).reshape(shard, heads_core)
-        big[layer] = (g_zx, g_dt, g_bc, g_out)
-        skip_grad = jnp.sum(gate_small[1].reshape(heads, HEADDIM), axis=1)
-        wide = jnp.concatenate([row_small[: CONV + 1], gate_small[0:1]])
-        wide = jnp.zeros((CONV + 2, GROUP, inner), F32).at[:, place].set(wide).reshape(CONV + 2, inner_core)
-        tall = jnp.concatenate([head_small[:2, :heads], skip_grad[None]])
-        tall = jnp.zeros((3, GROUP, heads), F32).at[:, place].set(tall).reshape(3, heads_core)
-        shared = lax.psum(bc_small[: CONV + 1], "head")
-        small[layer] = lax.psum((gain_grad, wide, shared, tall), ("z", "p"))
-
-    grad_input = d_resid.astype(BF16)[None]
-    stack = lambda pick: jnp.stack([pick(layer) for layer in range(layers)]).astype(BF16)
+        if layer > 0:
+            d_mix, token_scalars, grad, gain_rows[layer] = call(
+                layer_below_kernel,
+                [((tokens, model), BF16), ((8, tokens), F32), own_rows, ((8, model), F32)],
+                part, grad, resid, gains[layer], *saved[layer - 1][-2:],
+                scratch=half_scratch + [edges], collective=5, copies=60,
+            )
+        else:
+            grad_input, gain_rows[layer] = call(
+                last_grad_kernel,
+                [((length, model), BF16), ((8, model), F32)],
+                part, grad, resid, gains[layer],
+                scratch=half_scratch + [edges], collective=6, copies=60,
+            )
+        big[layer] = [g.reshape(sources, shard, inner) for g in (gx, gz, gwo)]
+        tall = jnp.pad(head_small[:2], ((0, 0), (0, inner - 128)))
+        wide = jnp.concatenate([row_small[: CONV + 1], gate_small[:2], tall])
+        kinds[layer] = (gbc, gdt, jnp.pad(wide, ((0, 7), (0, 0))), bc_small[: CONV + 1])
+
+    def later_grads(layer):
+        sent = [g.reshape(groups, GROUP, shard, inner) for g in big[layer]]
+        total = [lax.dynamic_index_in_dim(g, level, 0, False).astype(F32) for g in sent]
+        for k in range(1, groups):
+            there = lax.rem(level + k, groups)
+            route = [(i, (i + k) % groups) for i in range(groups)]
+            for i in range(3):
+                got = lax.ppermute(lax.dynamic_index_in_dim(sent[i], there, 0, False), "z", route)
+                total[i] = total[i] + got.astype(F32)
+        total = pass_plane([t.astype(BF16) for t in total])
+        return [jnp.swapaxes(t, 0, 1).reshape(shard, inner_core) for t in total]
+
+    later = {layer: later_grads(layer) for layer in range(1, layers)}
+    vec = jnp.concatenate(
+        [gain_rows[layer][0] for layer in range(layers)] + [kinds[layer][3].reshape(-1) for layer in range(layers)]
+    )
+    vec = jnp.pad(vec, (0, 2 * GROUP * 1024 - vec.shape[0])).reshape(2 * GROUP, 8, 128)
+    bc_grads = jnp.stack([kinds[layer][0].reshape(groups, GROUP, shard, 2 * STATE) for layer in range(layers)])
+    dt_grads = jnp.concatenate([kinds[layer][1] for layer in range(layers)])
+    dt_grads = jnp.swapaxes(dt_grads.reshape(layers * EDGE, groups, GROUP * shard), 0, 1)
+    wide = jnp.concatenate([kinds[layer][2] for layer in range(layers)])
+    wide_shape, dt_shape, far = wide.shape, dt_grads.shape[1:], groups - 1
+    gx, gz, go, g_bc, vec, g_dt, wide = call(
+        grads_kernel,
+        [
+            ((shard, inner_core), BF16),
+            ((shard, inner_core), BF16),
+            ((shard, inner_core), BF16),
+            ((layers, shard, 2 * STATE), BF16),
+            (vec.shape, F32),
+            ((GROUP, *dt_shape), BF16),
+            ((GROUP, *wide_shape), F32),
+        ],
+        *big[0], bc_grads, vec, dt_grads, wide,
+        scratch=[
+            ((far, 3, GROUP, shard, inner), BF16),
+            ((far, 3, GROUP, shard, inner), BF16),
+            ((GROUP, shard, inner), F32),
+            ((3, GROUP, shard, inner), BF16),
+            ((layers, 2 * GROUP - 1, groups, shard, STATE), BF16),
+            ((layers, groups, shard, STATE), BF16),
+            ((layers, far, shard, STATE), BF16),
+            ((2 * GROUP, 8, 128), F32),
+            ((far, 8, 128), F32),
+            ((far, *dt_shape), BF16),
+            ((far, *wide_shape), F32),
+        ],
+        collective=7, copies=60 + 12 * groups,
+    )
+    later[0] = [gx, gz, go]
+    vec = vec.reshape(-1)
+    grad_gain = vec[: layers * model].reshape(layers, model)
+    grad_conv_bc = vec[layers * model :][: layers * (CONV + 1) * 2 * STATE].reshape(layers, CONV + 1, 2 * STATE)
+    wide = wide.reshape(GROUP, layers, 16, inner)
+    whole = jnp.moveaxis(wide, 0, 2).reshape(layers, 16, inner_core)
+    skip_grad = jnp.sum(whole[:, CONV + 2].reshape(layers, heads_core, HEADDIM), axis=-1)
+    tall = jnp.moveaxis(wide[:, :, CONV + 3 : CONV + 5, :heads], 0, 2).reshape(layers, 2, heads_core)
+    grad_heads = jnp.concatenate([tall, skip_grad[:, None]], axis=1)
+    g_dt = lax.dynamic_slice_in_dim(g_dt.reshape(GROUP, layers, EDGE, GROUP, shard), place, 1, 3)[:, :, :heads, 0]
+    grad_dt = jnp.transpose(g_dt, (1, 3, 0, 2)).reshape(layers, shard, heads_core)
+    low = lambda a: a.astype(BF16)
     return (
-        block_out,
-        grad_input,
-        stack(lambda l: small[l][0]),
-        stack(lambda l: big[l][0]),
-        stack(lambda l: big[l][1]),
-        stack(lambda l: big[l][2]),
-        stack(lambda l: small[l][1][: CONV + 1]),
-        stack(lambda l: small[l][2]),
-        stack(lambda l: small[l][3]),
-        stack(lambda l: small[l][1][CONV + 1]),
-        stack(lambda l: big[l][3]),
+        block_out[None],
+        grad_input[None],
+        low(grad_gain),
+        jnp.stack([jnp.stack([later[layer][1], later[layer][0]]) for layer in range(layers)]),
+        grad_dt,
+        g_bc,
+        low(whole[:, : CONV + 1]),
+        low(grad_conv_bc),
+        low(grad_heads),
+        low(whole[:, CONV + 1]),
+        jnp.stack([later[layer][2].T for layer in range(layers)]),
     )
 
 

time: 1390 us -> 956 us (0.69)
  waiting for transfers between devices: 589 us -> 61.5 us
  blocking collectives: 495 us -> 0 us
  Pallas kernels: 154 us -> 618 us
  starting transfers between devices: 20.1 us -> 117 us
  local copies, waits for them, and re-layouts: 61 us -> 122 us
  other arithmetic: 42.8 us -> 18.6 us
    pallas_call x10 -> x20, Pallas kernels: 154 us -> 618 us  [call(): pl.pallas_call(body, out_shape=tuple((jax.ShapeDtypeStruct(shape, kind) f...]
    reduce_scatter x10 -> x0, waiting for transfers between devices: 427 us -> none  [the longest x2 174 us: on_device(): lax.psum_scatter(gbc, ('z', 'p'), scatter_dimension=0, tiled=True)]
    all_gather x10 -> x0, blocking collectives: 287 us -> none  [the longest x2 96.7 us: on_device(): dt_full = lax.all_gather(w_dt[layer], ('z', 'p'), axis=0, tiled=True)]
    psum x6 -> x0, blocking collectives: 160 us -> none  [the longest x1 85 us: on_device(): small[layer] = lax.psum((gain_grad, wide, shared, tall), ('z', 'p'))]
    all_gather x6 -> x0, waiting for transfers between devices: 124 us -> none  [the longest x4 70.5 us: gather_rows(): return lax.all_gather(block, 'p', axis=0, tiled=True)]
    ppermute x4 -> x43, starting transfers between devices: 5.14 us -> 117 us  [the longest x9 62.9 us: later_grads(): lax.ppermute(lax.dynamic_index_in_dim(sent[i], there, 0, False), 'z', route)]
    dynamic_update_slice x0 -> x43, local copies, waits for them, and re-layouts: none -> 78.4 us  [the longest x21 54 us: pass_plane(): lax.dynamic_update_slice_in_dim(o, a, there, 0)]
    ppermute x4 -> x43, waiting for transfers between devices: 3.29 us -> 61.5 us  [the longest x12 38.4 us: pass_groups(): lax.ppermute(a, 'z', [(i, (i + k) % groups) for i in range(groups)])]
  transfers between devices with their start and end apart: 29 -> 43, of which waited for: 17 -> 6; matrix products, arithmetic and copies ran while one was open for 5% -> 11% of each run, Pallas kernels for 4% -> 9%
where the time goes in v2:
time: 956 us; the launch traced here: 939 us
  Pallas kernels  618 us (65%)
  local copies, waits for them, and re-layouts  122 us (13%)
  starting transfers between devices  117 us (12%)
  waiting for transfers between devices  61.5 us (6%)
  other arithmetic  18.6 us (2%)
    pallas_call x20, Pallas kernels, call(): pl.pallas_call(body, out_shape=tuple((jax.ShapeDtypeStruct(shape, kind) f...  618 us
    ppermute x9, starting transfers between devices, later_grads(): lax.ppermute(lax.dynamic_index_in_dim(sent[i], there, 0, False), 'z', route)  62.9 us
    dynamic_update_slice x21, local copies, waits for them, and re-layouts, pass_plane(): lax.dynamic_update_slice_in_dim(o, a, there, 0)  54 us
    ppermute x12, waiting for transfers between devices, pass_groups(): lax.ppermute(a, 'z', [(i, (i + k) % groups) for i in range(groups)])  38.4 us
    ppermute x21, starting transfers between devices, pass_plane(): lax.ppermute(a, 'p', [(i, i ^ k) for i in range(GROUP)])  28.6 us
    ppermute x12, starting transfers between devices, pass_groups(): lax.ppermute(a, 'z', [(i, (i + k) % groups) for i in range(groups)])  25.7 us
    ppermute x9, waiting for transfers between devices, later_grads(): lax.ppermute(lax.dynamic_index_in_dim(sent[i], there, 0, False), 'z', route)  22.9 us
  transfers between devices with their start and end apart: 43, of which 6 were waited for; matrix products, arithmetic and copies ran while one was open for 11% of the time, Pallas kernels for 9%

profile of v2, /device:TPU:0, one launch (start us, length us, event | category | flops | bytes accessed | tf_op | source)
XLA Modules:
  0.0 939.5 jit_solution(11967676967491873835)
XLA Ops:
  19.3 87.3 %shard_map.194 = (bf16[1040,1536]{1,0:T(8,128)(2,1)}, bf16[1024,1536]{1,0:T(8,128)(2,1)}, bf16[16,96,384]{2,1,0:T(8,128)(2,1)}, bf16[16,96,384]{2,1,0:T(8,128)(2...) custom-call(bf16[256,1536]{1,0:T(8,128)(2,1)} %bitcast.253, ...), custom_call_target="tpu_custom_call" | custom-call | tf_op jit(solution)/shard_map/pallas_call | solution.py:1176
  187.6 13.5 %collective-permute-done.4 = bf16[4,96,384]{2,0,1:T(4,128)(2,1)} collective-permute-done((bf16[4,96,384]{2,0,1:T(4,128)(2,1)}, bf16[4,96,384]{2,0,1:T(4,128)(2,1)}, u32[]{:S(2)}, u32[]{:S(2)}) %collective-permute-start.4) | collective-permute-done | bytes 294944 | tf_op jit(solution)/shard_map/ppermute | solution.py:1249
  214.6 12.5 %collective-permute-done.10 = bf16[4,96,384]{2,0,1:T(4,128)(2,1)S(1)} collective-permute-done((bf16[4,96,384]{2,0,1:T(4,128)(2,1)S(1)}, bf16[4,96,384]{2,0,1:T(4,128)(2,1)S(1)}, u32[]{:S(2)}, u32[]{:S(2)}) %collective-permute-start.10) | collective-permute-done | bytes 294944 | tf_op jit(solution)/shard_map/ppermute | solution.py:1249
  227.3 12.4 %collective-permute-done.23 = bf16[4,96,384]{2,0,1:T(4,128)(2,1)S(1)} collective-permute-done((bf16[4,96,384]{2,0,1:T(4,128)(2,1)S(1)}, bf16[4,96,384]{2,0,1:T(4,128)(2,1)S(1)}, u32[]{:S(2)}, u32[]{:S(2)}) %collective-permute-start.23) | collective-permute-done | bytes 294944 | tf_op jit(solution)/shard_map/ppermute | solution.py:1249
  247.0 18.6 %shard_map.195 = (bf16[1024,384]{1,0:T(8,128)(2,1)}, bf16[1040,384]{1,0:T(8,128)(2,1)}, bf16[1040,256]{1,0:T(8,128)(2,1)}, bf16[1024,384]{1,0:T(8,128)(2,1)}, bf...) custom-call(bf16[1040,1536]{1,0:T(8,128)(2,1)} %get-tuple-element.11, ...), custom_call_target="tpu_custom_call" | custom-call | tf_op jit(solution)/shard_map/pallas_call | solution.py:1176
  265.6 15.5 %shard_map.196 = (bf16[4,128,384]{2,1,0:T(8,128)(2,1)}, f32[4,8,384]{2,1,0:T(8,128)}) custom-call(bf16[128,384]{1,0:T(8,128)(2,1)} %get-tuple-element.116.state, f32[8,384]{1,0:T(8,128)} %get-tuple-element.117.decay), custom_call_target="tpu_custom_call" | custom-call | tf_op jit(solution)/shard_map/pallas_call | solution.py:1176
  291.6 50.0 %shard_map.198 = (bf16[1040,1536]{1,0:T(8,128)(2,1)}, f32[128,1536]{1,0:T(8,128)}, f32[128,1536]{1,0:T(8,128)}, f32[8,128]{1,0:T(8,128)}) custom-call(bf16[1024,1536]{1,0:T(8,128)(2,1)} %get-tuple-element.128.part, f32[8,1024]{1,0:T(8,128)} %get-tuple-element.129.squares, f32[128,1536]{1,0:T(8,128)} %get-tuple-element.130.resid, ...), custom_call_target="tpu_custom_call" | custom-call | tf_op jit(solution)/shard_map/pallas_call | solution.py:1176
  341.6 18.6 %shard_map.199 = (bf16[1024,384]{1,0:T(8,128)(2,1)}, bf16[1040,384]{1,0:T(8,128)(2,1)}, bf16[1040,256]{1,0:T(8,128)(2,1)}, bf16[1024,384]{1,0:T(8,128)(2,1)}, bf...) custom-call(bf16[1040,1536]{1,0:T(8,128)(2,1)} %get-tuple-element.13, ...), custom_call_target="tpu_custom_call" | custom-call | tf_op jit(solution)/shard_map/pallas_call | solution.py:1176
  360.1 15.7 %shard_map.200 = (bf16[4,128,384]{2,1,0:T(8,128)(2,1)}, f32[4,8,384]{2,1,0:T(8,128)}) custom-call(bf16[128,384]{1,0:T(8,128)(2,1)} %get-tuple-element.132.state, f32[8,384]{1,0:T(8,128)} %get-tuple-element.133.decay), custom_call_target="tpu_custom_call" | custom-call | tf_op jit(solution)/shard_map/pallas_call | solution.py:1176
  375.8 9.7 %shard_map.201 = (f32[1024,384]{1,0:T(8,128)}, f32[4,128,384]{2,1,0:T(8,128)}, bf16[1024,1536]{1,0:T(8,128)(2,1)}, f32[8,1024]{1,0:T(8,128)}) custom-call(bf16[4,128,384]{2,1,0:T(8,128)(2,1)} %get-tuple-element.134.sums, f32[4,8,384]{2,1,0:T(8,128)} %get-tuple-element.135.decays, f32[4,128,384]{2,1,0:T(8,128)} %get-tuple-element.136.local, ...), custom_call_target="tpu_custom_call" | custom-call | tf_op jit(solution)/shard_map/pallas_call | solution.py:1176
  385.5 30.2 %shard_map.202 = (bf16[256,1536]{1,0:T(8,128)(2,1)}, f32[8,1024]{1,0:T(8,128)}) custom-call(bf16[1024,1536]{1,0:T(8,128)(2,1)} %get-tuple-element.143.part, f32[8,1024]{1,0:T(8,128)} %get-tuple-element.144.squares, f32[128,1536]{1,0:T(8,128)} %get-tuple-element.145.resid, f32[128,1536]{1,0:T(8,128)} %get-tuple-element.146.cot.grad), custom_call_target="tpu_custom_call" | custom-call | tf_op jit(solution)/shard_map/pallas_call | solution.py:1176
  415.7 11.9 %shard_map.203 = (bf16[1024,384]{1,0:T(8,128)(2,1)}, bf16[1024,384]{1,0:T(8,128)(2,1)}, bf16[1536,384]{1,0:T(8,128)(2,1)}, f32[4,128,384]{2,1,0:T(8,128)}, bf16[...) custom-call(bf16[1024,1536]{1,0:T(8,128)(2,1)} %get-tuple-element.148.dmix, bf16[1536,384]{1,0:T(8,128)(2,1)} %bitcast.224, ...), custom_call_target="tpu_custom_call" | custom-call | tf_op jit(solution)/shard_map/pallas_call | solution.py:1176
  427.6 16.3 %shard_map.204 = (bf16[4,128,384]{2,1,0:T(8,128)(2,1)}, f32[4,8,384]{2,1,0:T(8,128)}) custom-call(bf16[128,384]{1,0:T(8,128)(2,1)} %get-tuple-element.151.state, f32[8,384]{1,0:T(8,128)} %get-tuple-element.152.decay), custom_call_target="tpu_custom_call" | custom-call | tf_op jit(solution)/shard_map/pallas_call | solution.py:1176
  443.9 19.8 %shard_map.205 = (bf16[1040,768]{1,0:T(8,128)(2,1)}, f32[8,384]{1,0:T(8,128)}, f32[8,256]{1,0:T(8,128)}, f32[8,128]{1,0:T(8,128)}) custom-call(bf16[4,128,384]{2,1,0:T(8,128)(2,1)} %get-tuple-element.153.sums, f32[4,8,384]{2,1,0:T(8,128)} %get-tuple-element.154.decays, f32[4,128,384]{2,1,0:T(8,128)} %get-tuple-element.155.prior, ...), custom_call_target="tpu_custom_call" | custom-call | tf_op jit(solution)/shard_map/pallas_call | solution.py:1176
  463.8 17.9 %shard_map.206 = (bf16[1040,1536]{1,0:T(8,128)(2,1)}, bf16[1536,384]{1,0:T(8,128)(2,1)}, bf16[1536,384]{1,0:T(8,128)(2,1)}, bf16[1536,256]{1,0:T(8,128)(2,1)}, bf16[16,1536]{1,0:T(8,128)(2,1)}) custom-call(bf16[1040,768]{1,0:T(8,128)(2,1)} %get-tuple-element.162.dcat, bf16[1024,384]{1,0:T(8,128)(2,1)} %get-tuple-element.163.dz, ...), custom_call_target="tpu_custom_call" | custom-call | tf_op jit(solution)/shard_map/pallas_call | solution.py:1176
  481.7 51.1 %shard_map.207 = (bf16[1024,1536]{1,0:T(8,128)(2,1)}, f32[8,1024]{1,0:T(8,128)}, f32[128,1536]{1,0:T(8,128)}, f32[8,1536]{1,0:T(8,128)}) custom-call(bf16[1040,1536]{1,0:T(8,128)(2,1)} %get-tuple-element.164.part, f32[128,1536]{1,0:T(8,128)} %get-tuple-element.146.cot.grad, f32[128,1536]{1,0:T(8,128)} %get-tuple-element.145.resid, ...), custom_call_target="tpu_custom_call" | custom-call | tf_op jit(solution)/shard_map/pallas_call | solution.py:1176
  532.8 11.9 %shard_map.208 = (bf16[1024,384]{1,0:T(8,128)(2,1)}, bf16[1024,384]{1,0:T(8,128)(2,1)}, bf16[1536,384]{1,0:T(8,128)(2,1)}, f32[4,128,384]{2,1,0:T(8,128)}, bf16[...) custom-call(bf16[1024,1536]{1,0:T(8,128)(2,1)} %get-tuple-element.167.dmix, bf16[1536,384]{1,0:T(8,128)(2,1)} %bitcast.230, ...), custom_call_target="tpu_custom_call" | custom-call | tf_op jit(solution)/shard_map/pallas_call | solution.py:1176
  544.7 15.2 %shard_map.209 = (bf16[4,128,384]{2,1,0:T(8,128)(2,1)}, f32[4,8,384]{2,1,0:T(8,128)}) custom-call(bf16[128,384]{1,0:T(8,128)(2,1)} %get-tuple-element.170.state, f32[8,384]{1,0:T(8,128)} %get-tuple-element.171.decay), custom_call_target="tpu_custom_call" | custom-call | tf_op jit(solution)/shard_map/pallas_call | solution.py:1176
  559.9 19.9 %shard_map.210 = (bf16[1040,768]{1,0:T(8,128)(2,1)}, f32[8,384]{1,0:T(8,128)}, f32[8,256]{1,0:T(8,128)}, f32[8,128]{1,0:T(8,128)}) custom-call(bf16[4,128,384]{2,1,0:T(8,128)(2,1)} %get-tuple-element.172.sums, f32[4,8,384]{2,1,0:T(8,128)} %get-tuple-element.173.decays, f32[4,128,384]{2,1,0:T(8,128)} %get-tuple-element.174.prior, ...), custom_call_target="tpu_custom_call" | custom-call | tf_op jit(solution)/shard_map/pallas_call | solution.py:1176
  582.5 18.1 %shard_map.211 = (bf16[1040,1536]{1,0:T(8,128)(2,1)}, bf16[1536,384]{1,0:T(8,128)(2,1)}, bf16[1536,384]{1,0:T(8,128)(2,1)}, bf16[1536,256]{1,0:T(8,128)(2,1)}, bf16[16,1536]{1,0:T(8,128)(2,1)}) custom-call(bf16[1040,768]{1,0:T(8,128)(2,1)} %get-tuple-element.181.dcat, bf16[1024,384]{1,0:T(8,128)(2,1)} %get-tuple-element.182.dz, ...), custom_call_target="tpu_custom_call" | custom-call | tf_op jit(solution)/shard_map/pallas_call | solution.py:1176
  602.1 29.1 %shard_map.212 = (bf16[256,1536]{1,0:T(8,128)(2,1)}, f32[8,1536]{1,0:T(8,128)}) custom-call(bf16[1040,1536]{1,0:T(8,128)(2,1)} %get-tuple-element.183.part, f32[128,1536]{1,0:T(8,128)} %get-tuple-element.184.grad, f32[128,1536]{1,0:T(8,128)} %get-tuple-element.130.resid, f32[1,1536]{1,0:T(1,128)} %get-tuple-element.288.gain), custom_call_target="tpu_custom_call" | custom-call | tf_op jit(solution)/shard_map/pallas_call | solution.py:1176
  635.5 151.6 %shard_map.213 = (bf16[96,1536]{1,0:T(8,128)(2,1)}, bf16[96,1536]{1,0:T(8,128)(2,1)}, bf16[96,1536]{1,0:T(8,128)(2,1)}, bf16[2,96,256]{2,1,0:T(8,128)(2,1)}, f32...) custom-call(bf16[16,96,384]{2,1,0:T(8,128)(2,1)} %bitcast.240, ...), custom_call_target="tpu_custom_call" | custom-call | tf_op jit(solution)/shard_map/pallas_call | solution.py:1176
  789.2 39.4 %collective-permute-start.37 = (bf16[4,96,384]{2,0,1:T(4,128)(2,1)S(1)}, bf16[4,96,384]{2,0,1:T(4,128)(2,1)}, u32[]{:S(2)}, u32[]{:S(2)}) collective-permute-start(bf16[4,96,384]{2,0,1:T(4,128)(2,1)S(1)} %bitcast.268), channel_id=1, source_target_pairs={{0,8},{8,16},{16,24},{24,0},{1,9},{9,17},{17,25},{25,1},{2,10},{10... | collective-permute-start | bytes 884744 | tf_op jit(solution)/shard_map/ppermute | solution.py:1423
  844.2 12.5 %collective-permute-done.38 = bf16[4,96,384]{2,0,1:T(4,128)(2,1)} collective-permute-done((bf16[4,96,384]{2,0,1:T(4,128)(2,1)S(1)}, bf16[4,96,384]{2,0,1:T(4,128)(2,1)}, u32[]{:S(2)}, u32[]{:S(2)}) %collective-permute-start.38) | collective-permute-done | bytes 294944 | tf_op jit(solution)/shard_map/ppermute | solution.py:1423
  (341 shorter events, 238.5 us)
Async XLA Ops:
  3.1 119.6 %collective-permute-start.12 = (bf16[1,128,128]{2,1,0:T(8,128)(2,1)}, bf16[1,128,128]{2,1,0:T(8,128)(2,1)}, u32[]{:S(2)}, u32[]{:S(2)}) collective-permute-start(bf16[1,128,128]{2,1,0:T(8,128)(2,1)} %maximum_bitcast_fusion.2), channel_id=1, source_target_pairs={{0,2},{2,0},{4,6},{6,4},{1,3},{3,1},{5,7},{7,5},{8,10},{10,8},{12,... | collective-permute-start | bytes 98312 | tf_op jit(solution)/shard_map/ppermute | solution.py:1240
  6.0 118.9 %collective-permute-start.13 = (bf16[1,128,128]{2,1,0:T(8,128)(2,1)}, bf16[1,128,128]{2,1,0:T(8,128)(2,1)}, u32[]{:S(2)}, u32[]{:S(2)}) collective-permute-start(bf16[1,128,128]{2,1,0:T(8,128)(2,1)} %maximum_bitcast_fusion.2), channel_id=1, source_target_pairs={{0,4},{2,6},{4,0},{6,2},{1,5},{3,7},{5,1},{7,3},{8,12},{10,14},{12... | collective-permute-start | bytes 98312 | tf_op jit(solution)/shard_map/ppermute | solution.py:1240
  7.5 122.8 %collective-permute-start.14 = (bf16[1,128,128]{2,1,0:T(8,128)(2,1)}, bf16[1,128,128]{2,1,0:T(8,128)(2,1)}, u32[]{:S(2)}, u32[]{:S(2)}) collective-permute-start(bf16[1,128,128]{2,1,0:T(8,128)(2,1)} %maximum_bitcast_fusion.2), channel_id=1, source_target_pairs={{0,6},{2,4},{4,2},{6,0},{1,7},{3,5},{5,3},{7,1},{8,14},{10,12},{12... | collective-permute-start | bytes 98312 | tf_op jit(solution)/shard_map/ppermute | solution.py:1240
  10.4 123.8 %collective-permute-start = (bf16[1,96,384]{2,0,1:T(2,128)(2,1)S(1)}, bf16[1,96,384]{2,0,1:T(2,128)(2,1)S(1)}, u32[]{:S(2)}, u32[]{:S(2)}) collective-permute-start(bf16[1,96,384]{2,0,1:T(2,128)(2,1)S(1)} %get-tuple-element.279), channel_id=1, source_target_pairs={{0,2},{2,0},{4,6},{6,4},{1,3},{3,1},{5,7},{7,5},{8,10},{10,8},{12,... | collective-permute-start | bytes 221192 | tf_op jit(solution)/shard_map/ppermute | solution.py:1240
  12.4 127.3 %collective-permute-start.1 = (bf16[1,96,384]{2,0,1:T(2,128)(2,1)S(1)}, bf16[1,96,384]{2,0,1:T(2,128)(2,1)S(1)}, u32[]{:S(2)}, u32[]{:S(2)}) collective-permute-start(bf16[1,96,384]{2,0,1:T(2,128)(2,1)S(1)} %get-tuple-element.278), channel_id=1, source_target_pairs={{0,4},{2,6},{4,0},{6,2},{1,5},{3,7},{5,1},{7,3},{8,12},{10,14},{12... | collective-permute-start | bytes 221192 | tf_op jit(solution)/shard_map/ppermute | solution.py:1240
  124.9 26.1 %collective-permute-start.6 = (bf16[1,96,384]{2,0,1:T(2,128)(2,1)S(1)}, bf16[1,96,384]{2,0,1:T(2,128)(2,1)S(1)}, u32[]{:S(2)}, u32[]{:S(2)}) collective-permute-start(bf16[1,96,384]{2,0,1:T(2,128)(2,1)S(1)} %get-tuple-element.275), channel_id=1, source_target_pairs={{0,2},{2,0},{4,6},{6,4},{1,3},{3,1},{5,7},{7,5},{8,10},{10,8},{12,... | collective-permute-start | bytes 221192 | tf_op jit(solution)/shard_map/ppermute | solution.py:1240
  168.5 32.7 %collective-permute-start.4 = (bf16[4,96,384]{2,0,1:T(4,128)(2,1)}, bf16[4,96,384]{2,0,1:T(4,128)(2,1)}, u32[]{:S(2)}, u32[]{:S(2)}) collective-permute-start(bf16[4,96,384]{2,0,1:T(4,128)(2,1)} %dynamic_update_slice.135), channel_id=1, source_target_pairs={{0,16},{8,24},{16,0},{24,8},{1,17},{9,25},{17,1},{25,9},{2,18},{10... | collective-permute-start | bytes 884744 | tf_op jit(solution)/shard_map/ppermute | solution.py:1249
  174.6 33.9 %collective-permute-start.5 = (bf16[4,96,384]{2,0,1:T(4,128)(2,1)}, bf16[4,96,384]{2,0,1:T(4,128)(2,1)S(1)}, u32[]{:S(2)}, u32[]{:S(2)}) collective-permute-start(bf16[4,96,384]{2,0,1:T(4,128)(2,1)} %dynamic_update_slice.135), channel_id=1, source_target_pairs={{0,24},{8,0},{16,8},{24,16},{1,25},{9,1},{17,9},{25,17},{2,26},{10... | collective-permute-start | bytes 884744 | tf_op jit(solution)/shard_map/ppermute | solution.py:1249
  179.1 33.1 %collective-permute-start.9 = (bf16[4,96,384]{2,0,1:T(4,128)(2,1)S(1)}, bf16[4,96,384]{2,0,1:T(4,128)(2,1)S(1)}, u32[]{:S(2)}, u32[]{:S(2)}) collective-permute-start(bf16[4,96,384]{2,0,1:T(4,128)(2,1)S(1)} %copy-done.9), channel_id=1, source_target_pairs={{0,8},{8,16},{16,24},{24,0},{1,9},{9,17},{17,25},{25,1},{2,10},{10... | collective-permute-start | bytes 884744 | tf_op jit(solution)/shard_map/ppermute | solution.py:1249
  180.7 46.4 %collective-permute-start.10 = (bf16[4,96,384]{2,0,1:T(4,128)(2,1)S(1)}, bf16[4,96,384]{2,0,1:T(4,128)(2,1)S(1)}, u32[]{:S(2)}, u32[]{:S(2)}) collective-permute-start(bf16[4,96,384]{2,0,1:T(4,128)(2,1)S(1)} %copy-done.9), channel_id=1, source_target_pairs={{0,16},{8,24},{16,0},{24,8},{1,17},{9,25},{17,1},{25,9},{2,18},{10... | collective-permute-start | bytes 884744 | tf_op jit(solution)/shard_map/ppermute | solution.py:1249
  183.5 43.6 %collective-permute-start.11 = (bf16[4,96,384]{2,0,1:T(4,128)(2,1)S(1)}, bf16[4,96,384]{2,0,1:T(4,128)(2,1)S(1)}, u32[]{:S(2)}, u32[]{:S(2)}) collective-permute-start(bf16[4,96,384]{2,0,1:T(4,128)(2,1)S(1)} %copy-done.9), channel_id=1, source_target_pairs={{0,24},{8,0},{16,8},{24,16},{1,25},{9,1},{17,9},{25,17},{2,26},{10... | collective-permute-start | bytes 884744 | tf_op jit(solution)/shard_map/ppermute | solution.py:1249
  208.4 31.2 %collective-permute-start.23 = (bf16[4,96,384]{2,0,1:T(4,128)(2,1)S(1)}, bf16[4,96,384]{2,0,1:T(4,128)(2,1)S(1)}, u32[]{:S(2)}, u32[]{:S(2)}) collective-permute-start(bf16[4,96,384]{2,0,1:T(4,128)(2,1)S(1)} %copy-done.11), channel_id=1, source_target_pairs={{0,16},{8,24},{16,0},{24,8},{1,17},{9,25},{17,1},{25,9},{2,18},{10... | collective-permute-start | bytes 884744 | tf_op jit(solution)/shard_map/ppermute | solution.py:1249
  212.2 27.5 %collective-permute-start.24 = (bf16[4,96,384]{2,0,1:T(4,128)(2,1)S(1)}, bf16[4,96,384]{2,0,1:T(4,128)(2,1)S(1)}, u32[]{:S(2)}, u32[]{:S(2)}) collective-permute-start(bf16[4,96,384]{2,0,1:T(4,128)(2,1)S(1)} %copy-done.11), channel_id=1, source_target_pairs={{0,24},{8,0},{16,8},{24,16},{1,25},{9,1},{17,9},{25,17},{2,26},{10... | collective-permute-start | bytes 884744 | tf_op jit(solution)/shard_map/ppermute | solution.py:1249
  789.2 53.6 %collective-permute-start.37 = (bf16[4,96,384]{2,0,1:T(4,128)(2,1)S(1)}, bf16[4,96,384]{2,0,1:T(4,128)(2,1)}, u32[]{:S(2)}, u32[]{:S(2)}) collective-permute-start(bf16[4,96,384]{2,0,1:T(4,128)(2,1)S(1)} %bitcast.268), channel_id=1, source_target_pairs={{0,8},{8,16},{16,24},{24,0},{1,9},{9,17},{17,25},{25,1},{2,10},{10... | collective-permute-start | bytes 884744 | tf_op jit(solution)/shard_map/ppermute | solution.py:1423
  828.7 27.9 %collective-permute-start.38 = (bf16[4,96,384]{2,0,1:T(4,128)(2,1)S(1)}, bf16[4,96,384]{2,0,1:T(4,128)(2,1)}, u32[]{:S(2)}, u32[]{:S(2)}) collective-permute-start(bf16[4,96,384]{2,0,1:T(4,128)(2,1)S(1)} %bitcast.267), channel_id=1, source_target_pairs={{0,16},{8,24},{16,0},{24,8},{1,17},{9,25},{17,1},{25,9},{2,18},{10... | collective-permute-start | bytes 884744 | tf_op jit(solution)/shard_map/ppermute | solution.py:1423
  829.0 31.6 %collective-permute-start.39 = (bf16[4,96,384]{2,0,1:T(4,128)(2,1)S(1)}, bf16[4,96,384]{2,0,1:T(4,128)(2,1)}, u32[]{:S(2)}, u32[]{:S(2)}) collective-permute-start(bf16[4,96,384]{2,0,1:T(4,128)(2,1)S(1)} %bitcast.265), channel_id=1, source_target_pairs={{0,24},{8,0},{16,8},{24,16},{1,25},{9,1},{17,9},{25,17},{2,26},{10... | collective-permute-start | bytes 884744 | tf_op jit(solution)/shard_map/ppermute | solution.py:1423
  836.6 34.2 %collective-permute-start.25 = (bf16[4,96,384]{2,0,1:T(4,128)(2,1)}, bf16[4,96,384]{2,0,1:T(4,128)(2,1)}, u32[]{:S(2)}, u32[]{:S(2)}) collective-permute-start(bf16[4,96,384]{2,0,1:T(4,128)(2,1)} %bitcast.209), channel_id=1, source_target_pairs={{0,8},{8,16},{16,24},{24,0},{1,9},{9,17},{17,25},{25,1},{2,10},{10... | collective-permute-start | bytes 884744 | tf_op jit(solution)/shard_map/ppermute | solution.py:1423
  837.5 42.9 %collective-permute-start.26 = (bf16[4,96,384]{2,0,1:T(4,128)(2,1)}, bf16[4,96,384]{2,0,1:T(4,128)(2,1)}, u32[]{:S(2)}, u32[]{:S(2)}) collective-permute-start(bf16[4,96,384]{2,0,1:T(4,128)(2,1)} %bitcast.208), channel_id=1, source_target_pairs={{0,16},{8,24},{16,0},{24,8},{1,17},{9,25},{17,1},{25,9},{2,18},{10... | collective-permute-start | bytes 884744 | tf_op jit(solution)/shard_map/ppermute | solution.py:1423
  842.8 38.1 %collective-permute-start.27 = (bf16[4,96,384]{2,0,1:T(4,128)(2,1)S(1)}, bf16[4,96,384]{2,0,1:T(4,128)(2,1)S(1)}, u32[]{:S(2)}, u32[]{:S(2)}) collective-permute-start(bf16[4,96,384]{2,0,1:T(4,128)(2,1)S(1)} %bitcast.270), channel_id=1, source_target_pairs={{0,24},{8,0},{16,8},{24,16},{1,25},{9,1},{17,9},{25,17},{2,26},{10... | collective-permute-start | bytes 884744 | tf_op jit(solution)/shard_map/ppermute | solution.py:1423
  856.7 27.1 %collective-permute-start.31 = (bf16[4,96,384]{2,0,1:T(4,128)(2,1)S(1)}, bf16[4,96,384]{2,0,1:T(4,128)(2,1)S(1)}, u32[]{:S(2)}, u32[]{:S(2)}) collective-permute-start(bf16[4,96,384]{2,0,1:T(4,128)(2,1)S(1)} %bitcast.269), channel_id=1, source_target_pairs={{0,8},{8,16},{16,24},{24,0},{1,9},{9,17},{17,25},{25,1},{2,10},{10... | collective-permute-start | bytes 884744 | tf_op jit(solution)/shard_map/ppermute | solution.py:1423
  860.6 31.3 %collective-permute-start.32 = (bf16[4,96,384]{2,0,1:T(4,128)(2,1)S(1)}, bf16[4,96,384]{2,0,1:T(4,128)(2,1)S(1)}, u32[]{:S(2)}, u32[]{:S(2)}) collective-permute-start(bf16[4,96,384]{2,0,1:T(4,128)(2,1)S(1)} %bitcast.266), channel_id=1, source_target_pairs={{0,16},{8,24},{16,0},{24,8},{1,17},{9,25},{17,1},{25,9},{2,18},{10... | collective-permute-start | bytes 884744 | tf_op jit(solution)/shard_map/ppermute | solution.py:1423
  896.5 27.0 %collective-permute-start.34 = (bf16[1,96,384]{2,0,1:T(2,128)(2,1)S(1)}, bf16[1,96,384]{2,0,1:T(2,128)(2,1)}, u32[]{:S(2)}, u32[]{:S(2)}) collective-permute-start(bf16[1,96,384]{2,0,1:T(2,128)(2,1)S(1)} %get-tuple-element.267), channel_id=1, source_target_pairs={{0,2},{2,0},{4,6},{6,4},{1,3},{3,1},{5,7},{7,5},{8,10},{10,8},{12,... | collective-permute-start | bytes 221192 | tf_op jit(solution)/shard_map/ppermute | solution.py:1240
  897.0 29.8 %collective-permute-start.35 = (bf16[1,96,384]{2,0,1:T(2,128)(2,1)S(1)}, bf16[1,96,384]{2,0,1:T(2,128)(2,1)}, u32[]{:S(2)}, u32[]{:S(2)}) collective-permute-start(bf16[1,96,384]{2,0,1:T(2,128)(2,1)S(1)} %get-tuple-element.266), channel_id=1, source_target_pairs={{0,4},{2,6},{4,0},{6,2},{1,5},{3,7},{5,1},{7,3},{8,12},{10,14},{12... | collective-permute-start | bytes 221192 | tf_op jit(solution)/shard_map/ppermute | solution.py:1240
  897.9 32.4 %collective-permute-start.36 = (bf16[1,96,384]{2,0,1:T(2,128)(2,1)S(1)}, bf16[1,96,384]{2,0,1:T(2,128)(2,1)}, u32[]{:S(2)}, u32[]{:S(2)}) collective-permute-start(bf16[1,96,384]{2,0,1:T(2,128)(2,1)S(1)} %get-tuple-element.265), channel_id=1, source_target_pairs={{0,6},{2,4},{4,2},{6,0},{1,7},{3,5},{5,3},{7,1},{8,14},{10,12},{12... | collective-permute-start | bytes 221192 | tf_op jit(solution)/shard_map/ppermute | solution.py:1240
  (58 other events, 955.8 us)

commit v3 on v2

v3 whole, which is shorter than its diff:
```python
import functools

import jax
import jax.numpy as jnp
from jax import lax
from jax.experimental import pallas as pl
from jax.experimental.pallas import tpu as pltpu
from jax.sharding import Mesh, PartitionSpec as P

HEADDIM = 64
STATE = 128
CONV = 4
SPAN = 256
GROUP = 4
EDGE = 16
EPS = 1e-05
HIGH = lax.Precision.HIGHEST
F32, BF16 = jnp.float32, jnp.bfloat16
NN = (((1,), (0,)), ((), ()))
NT = (((1,), (1,)), ((), ()))
TN = (((0,), (0,)), ((), ()))
VMEM_BYTES = 58 << 20


def dot(a, b, dims=NN):
    return lax.dot_general(a, b, dims, preferred_element_type=F32)


def dot_exact(a, b, dims=NN):
    return lax.dot_general(a, b, dims, precision=HIGH, preferred_element_type=F32)


def dot_split(a, b, dims=NN):
    high = a.astype(BF16)
    rest = (a - high.astype(F32)).astype(BF16)
    return dot(high, b, dims) + dot(rest, b, dims)


def sigmoid(v):
    return 1.0 / (1.0 + jnp.exp(-v))


def softplus(v):
    return jnp.maximum(v, 0.0) + jnp.log1p(jnp.exp(-jnp.abs(v)))


def silu_slope(v):
    sig = sigmoid(v)
    return sig * (1.0 + v * (1.0 - sig))


def iota(shape, dim):
    return lax.broadcasted_iota(jnp.int32, shape, dim)


def head_spread(inner):
    return (iota((128, inner), 0) == lax.shift_right_logical(iota((128, inner), 1), 6)).astype(BF16)


def triangle(lower):
    rows, cols = iota((SPAN, SPAN), 0), iota((SPAN, SPAN), 1)
    return ((cols <= rows) if lower else (cols >= rows)).astype(F32)


def half_masks():
    lane = iota((SPAN, 128), 1)
    return (lane < HEADDIM).astype(BF16), (lane >= HEADDIM).astype(BF16)


def conv_taps(window, taps):
    total = jnp.broadcast_to(taps[CONV : CONV + 1], (SPAN, window.shape[1]))
    for j in range(CONV):
        total = total + taps[j : j + 1] * window[EDGE - 3 + j : EDGE - 3 + j + SPAN]
    return total


def head_pick(place, heads):
    row, col = iota((128, 128), 0), iota((128, 128), 1)
    return jnp.logical_and(row == place * heads + col, col < heads).astype(BF16)


def project_and_convolve(
    place, normed, wx, wz, wbc, wdt, rowp, bcp, headp,
    z_out, xin_out, bcin_out, x_out, bc_out, dtraw_out, dt_out, s_out, decay_out,
    ext, local,
):
    inner = x_out.shape[1]
    spans = x_out.shape[0] // SPAN

    def bc_of(rows):
        return jnp.concatenate([dot(rows, wbc[0]), dot(rows, wbc[1])], axis=1).astype(BF16)

    edge = normed[0:EDGE]
    edge_x = dot(edge, wx[...]).astype(BF16)
    edge_bc = bc_of(edge)
    xin_out[0:EDGE] = edge_x
    bcin_out[0:EDGE] = edge_bc
    ext[0:EDGE, 0:inner] = edge_x.astype(F32)
    ext[0:EDGE, inner:] = edge_bc.astype(F32)
    spread = head_spread(inner)
    pick = head_pick(place, inner // HEADDIM)
    low_tri = triangle(True)
    rate = -jnp.exp(headp[0:1])
    bias = headp[1:2]

    def block(q, carry):
        state_sum, decay_all = carry
        at = pl.multiple_of(q * SPAN, SPAN)
        tok = pl.ds(at, SPAN)
        after = pl.ds(pl.multiple_of(at + EDGE, EDGE), SPAN)
        rows = normed[after, :]
        z_out[tok, :] = dot(rows, wz[...]).astype(BF16)
        xin = dot(rows, wx[...]).astype(BF16)
        bcin = bc_of(rows)
        dtraw = dot(dot(rows, wdt[...]).astype(BF16), pick).astype(BF16)
        xin_out[after, :] = xin
        bcin_out[after, :] = bcin
        dtraw_out[tok, :] = dtraw
        ext[after, 0:inner] = xin.astype(F32)
        ext[after, inner:] = bcin.astype(F32)
        window = pl.ds(at, SPAN + EDGE)
        pre_x = conv_taps(ext[window, 0:inner], rowp)
        x = (pre_x * sigmoid(pre_x)).astype(BF16)
        x_out[tok, :] = x
        pre_bc = conv_taps(ext[window, inner:], bcp)
        bc = (pre_bc * sigmoid(pre_bc)).astype(BF16)
        bc_out[tok, :] = bc
        dt = softplus(dtraw.astype(F32) + bias)
        s = dot_exact(low_tri, dt * rate)
        dt_out[tok, :] = dt
        s_out[tok, :] = s
        to_end = jnp.exp(s[SPAN - 1 : SPAN] - s) * dt
        weighted = (x.astype(F32) * dot_split(to_end, spread)).astype(BF16)
        fresh = dot(bc[:, :STATE], weighted, TN)
        decay = dot_split(jnp.exp(s[SPAN - 8 : SPAN]), spread)[7:8]
        local[q] = fresh
        decay_out[q] = jnp.broadcast_to(decay, (8, inner))
        return state_sum * decay + fresh, decay_all * decay

    return lax.fori_loop(0, spans, block, (jnp.zeros((STATE, inner), F32), jnp.ones((1, inner), F32)))


def mix_within_spans(x_in, bc_in, s_in, dt_in, y_out):
    inner = x_in.shape[1]

    def block(q, _):
        tok = pl.ds(pl.multiple_of(q * SPAN, SPAN), SPAN)
        x, bc, s = x_in[tok, :], bc_in[tok, :], s_in[tok, :]
        s_row, dt_row = s.T, dt_in[tok, :].T
        cb = dot(bc[:, STATE:], bc[:, :STATE], NT)
        causal = iota((SPAN, SPAN), 1) <= iota((SPAN, SPAN), 0)
        masks = half_masks()
        for pair in range(inner // 128):
            lanes = slice(pair * 128, pair * 128 + 128)
            x_pair = x[:, lanes]
            total = None
            for e in range(2):
                h = pair * 2 + e
                gap = jnp.where(causal, s[:, h : h + 1] - s_row[h : h + 1, :], -1e30)
                scores = (cb * (jnp.exp(gap) * dt_row[h : h + 1, :])).astype(BF16)
                term = dot(scores, x_pair * masks[e])
                total = term if total is None else total + term
            y_out[tok, lanes] = total
        return 0

    lax.fori_loop(0, x_in.shape[0] // SPAN, block, 0)


def entering_state(place, count, sums, decays, backward):
    inner = sums.shape[2]
    state = jnp.zeros((STATE, inner), F32)
    for turn in range(count):
        other = count - 1 - turn if backward else turn
        ahead = (place < other) if backward else (other < place)
        state = jnp.where(ahead, decays[other, 0:1] * state + sums[other].astype(F32), state)
    return state


def mix_out(state, local, decay, x, bc, z, s, wo, rowp, y_out, states_out, part_out, sq_out):
    inner = x.shape[1]
    spread = head_spread(inner)
    gain, skip = rowp[5:6], rowp[6:7]
    ones = jnp.ones((8, inner), F32)

    def block(q, state):
        tok = pl.ds(pl.multiple_of(q * SPAN, SPAN), SPAN)
        states_out[q] = state
        c = bc[tok, STATE:]
        carried = dot_split(jnp.exp(s[tok, :]), spread) * dot(c, state.astype(BF16))
        y = y_out[tok, :] + carried + skip * x[tok, :].astype(F32)
        y_out[tok, :] = y
        zf = z[tok, :].astype(F32)
        gated = y * (zf * sigmoid(zf))
        sq_out[:, tok] = dot_exact(ones, gated * gated, NT)
        part_out[tok, :] = dot((gated * gain).astype(BF16), wo[...], NT).astype(BF16)
        return decay[q, 0:1] * state + local[q]

    lax.fori_loop(0, x.shape[0] // SPAN, block, state)


def back_through_gate(
    inner_all, dmix, wo, y_in, z, x, bc, s, decay, token_scalars, rowp, dz_out, small_out, dy_out, prior, normed_out
):
    inner = x.shape[1]
    spans = x.shape[0] // SPAN
    spread = head_spread(inner)
    gain = rowp[5:6]

    def block(i, carry):
        grad_sum, gain_sum, skip_sum = carry
        q = spans - 1 - i
        tok = pl.ds(pl.multiple_of(q * SPAN, SPAN), SPAN)
        columns = token_scalars[:, tok].T
        inv, total_dot = columns[:, 0:1], columns[:, 1:2]
        zf = z[tok, :].astype(F32)
        sig = sigmoid(zf)
        act = zf * sig
        y = y_in[tok, :]
        gated = y * act
        d_no = dot(dmix[tok, :], wo[...])
        scaled = gated * inv
        normed_out[tok, :] = (scaled * gain).astype(BF16)
        gain_sum = gain_sum + jnp.sum(d_no * scaled, axis=0, keepdims=True)
        d_gated = inv * (d_no * gain) - gated * (inv * inv * inv * total_dot * (1.0 / inner_all))
        dz_out[tok, :] = (d_gated * y * (sig * (1.0 + zf * (1.0 - sig)))).astype(BF16)
        dy = d_gated * act
        xf = x[tok, :].astype(F32)
        skip_sum = skip_sum + jnp.sum(dy * xf, axis=0, keepdims=True)
        dy_low = dy.astype(BF16)
        dy_out[tok, :] = dy_low
        scaled_dy = (dy_low.astype(F32) * dot_split(jnp.exp(s[tok, :]), spread)).astype(BF16)
        fresh = dot(bc[tok, STATE:], scaled_dy, TN)
        prior[q] = fresh
        return fresh + decay[q, 0:1] * grad_sum, gain_sum, skip_sum

    zero = jnp.zeros((1, inner), F32)
    grad_sum, gain_sum, skip_sum = lax.fori_loop(
        0, spans, block, (jnp.zeros((STATE, inner), F32), zero, zero)
    )
    decay_all = decay[0, 0:1]
    for q in range(1, spans):
        decay_all = decay_all * decay[q, 0:1]
    small_out[0:1] = gain_sum
    small_out[1:2] = skip_sum
    small_out[2:8] = jnp.zeros((6, inner), F32)
    return grad_sum, decay_all


def out_gradient(dmix, normed_out, gwo_out):
    def rows_of(i, _):
        rows = pl.ds(pl.multiple_of(i * SPAN, SPAN), SPAN)
        gwo_out[rows, :] = dot(dmix[:, rows], normed_out[...], TN).astype(BF16)
        return 0

    lax.fori_loop(0, dmix.shape[1] // SPAN, rows_of, 0)


def back_within_spans(dy_in, x_in, bc_in, s_in, dt_in, dpre, flow_out, sum_out):
    inner = x_in.shape[1]

    def block(q, _):
        at = pl.multiple_of(q * SPAN, SPAN)
        tok = pl.ds(at, SPAN)
        after = pl.ds(pl.multiple_of(at + EDGE, EDGE), SPAN)
        x_low, dy = x_in[tok, :], dy_in[tok, :]
        b, c = bc_in[tok, :STATE], bc_in[tok, STATE:]
        s, dt = s_in[tok, :], dt_in[tok, :]
        s_row = s.T
        cb = dot(b, c, NT)
        seen = iota((SPAN, SPAN), 0) <= iota((SPAN, SPAN), 1)
        masks = half_masks()
        d_cb = jnp.zeros((SPAN, SPAN), F32)
        lane = iota((SPAN, 128), 1)
        row_id = iota((128, SPAN), 0)
        sum_k = jnp.zeros((128, SPAN), F32)
        sum_t = jnp.zeros((SPAN, 128), F32)
        for pair in range(inner // 128):
            lanes = slice(pair * 128, pair * 128 + 128)
            x_pair, dy_pair = x_low[:, lanes], dy[:, lanes]
            total = None
            for e in range(2):
                h = pair * 2 + e
                d_scores = dot(x_pair * masks[e], dy_pair, NT)
                fade = jnp.exp(jnp.where(seen, s_row[h : h + 1, :] - s[:, h : h + 1], -1e30))
                dt_h = dt[:, h : h + 1]
                fade_cb = cb * fade
                term = dot((fade_cb * dt_h).astype(BF16), dy_pair * masks[e])
                total = term if total is None else total + term
                d_cb = d_cb + d_scores * (fade * dt_h)
                flow = d_scores * fade_cb
                sum_t = jnp.where(lane == h, jnp.sum(flow, axis=1, keepdims=True), sum_t)
                sum_k = jnp.where(row_id == h, jnp.sum(flow * dt_h, axis=0, keepdims=True), sum_k)
            dpre[after, lanes] = total
        d_cb_low = d_cb.astype(BF16)
        dpre[after, inner : inner + STATE] = dot(d_cb_low, c)
        dpre[after, inner + STATE :] = dot(d_cb_low, b, TN)
        flow_out[tok, :] = sum_k.T - sum_t * dt
        sum_out[tok, :] = sum_t
        return 0

    lax.fori_loop(0, x_in.shape[0] // SPAN, block, 0)


def back_through_states(
    grad, prior, decay, states, dy_in, x, bc, s_in, dt_in, dtraw, xin, bcin, rowp, bcp, headp, flow_in, sum_in,
    dcat_out, row_out, bcrow_out, head_out,
    dpre, dend,
):
    inner = x.shape[1]
    spans = x.shape[0] // SPAN
    spread = head_spread(inner)
    up_tri = triangle(False)
    skip = rowp[6:7]
    rate = -jnp.exp(headp[0:1])
    bias = headp[1:2]
    width = inner + 2 * STATE

    def chain(i, grad):
        q = spans - 1 - i
        dend[q] = grad
        return prior[q] + decay[q, 0:1] * grad

    lax.fori_loop(0, spans, chain, grad)
    dpre[0:EDGE] = jnp.zeros((EDGE, width), F32)
    dpre[EDGE + spans * SPAN :] = jnp.zeros((EDGE, width), F32)
    row_out[...] = jnp.zeros_like(row_out)
    bcrow_out[...] = jnp.zeros_like(bcrow_out)
    head_out[...] = jnp.zeros_like(head_out)
    dcat_out[0:EDGE, width:] = jnp.zeros((EDGE, 128), BF16)

    def block(q, _):
        at = pl.multiple_of(q * SPAN, SPAN)
        tok = pl.ds(at, SPAN)
        after = pl.ds(pl.multiple_of(at + EDGE, EDGE), SPAN)
        window = pl.ds(at, SPAN + EDGE)
        x_low, dy = x[tok, :], dy_in[tok, :]
        xf, dyf = x_low.astype(F32), dy.astype(F32)
        b, c = bc[tok, :STATE], bc[tok, STATE:]
        s, dt = s_in[tok, :], dt_in[tok, :]
        exp_s = jnp.exp(s)
        to_end = jnp.exp(s[SPAN - 1 : SPAN] - s)
        w = to_end * dt
        w_all, s_all = dot_split(w, spread), dot_split(exp_s, spread)
        state, grad = states[q], dend[q]
        state_low, grad_low = state.astype(BF16), grad.astype(BF16)
        carried = s_all * dot(c, state_low)
        ds = dot_split(dyf * carried, spread, NT)
        d_c = dot((dyf * s_all).astype(BF16), state_low, NT)
        d_w = dot(b, grad_low)
        d_b = dot((xf * w_all).astype(BF16), grad_low, NT)
        dx = dpre[after, 0:inner] + dyf * skip + d_w * w_all
        dsw = dot_split(d_w * xf, spread, NT)
        end = dsw * w
        ds = ds + flow_in[tok, :] - end
        held = dot_split(jnp.broadcast_to(jnp.sum(grad * state, axis=0, keepdims=True), (8, inner)), spread, NT)[0:1]
        last = jnp.sum(end, axis=0, keepdims=True) + held * exp_s[SPAN - 1 : SPAN]
        ds = ds + jnp.where(iota((SPAN, 128), 0) == SPAN - 1, last, 0.0)
        da = dot_exact(up_tri, ds)
        d_dt = sum_in[tok, :] + dsw * to_end + da * rate
        d_raw = d_dt * sigmoid(dtraw[tok, :].astype(F32) + bias)
        d_raw = jnp.where(iota((SPAN, 128), 1) < inner // HEADDIM, d_raw, 0.0)
        head_out[0:1] += jnp.sum(da * (dt * rate), axis=0, keepdims=True)
        head_out[1:2] += jnp.sum(d_raw, axis=0, keepdims=True)
        dcat_out[after, width:] = d_raw.astype(BF16)

        win_x = xin[window, :].astype(F32)
        d_x = dx * silu_slope(conv_taps(win_x, rowp))
        dpre[after, 0:inner] = d_x
        for j in range(CONV):
            row_out[j : j + 1] += jnp.sum(d_x * win_x[EDGE - 3 + j : EDGE - 3 + j + SPAN], axis=0, keepdims=True)
        row_out[CONV : CONV + 1] += jnp.sum(d_x, axis=0, keepdims=True)
        win_bc = bcin[window, :].astype(F32)
        d_bc = dpre[after, inner:] + jnp.concatenate([d_b, d_c], axis=1)
        d_bc = d_bc * silu_slope(conv_taps(win_bc, bcp))
        dpre[after, inner:] = d_bc
        for j in range(CONV):
            bcrow_out[j : j + 1] += jnp.sum(d_bc * win_bc[EDGE - 3 + j : EDGE - 3 + j + SPAN], axis=0, keepdims=True)
        bcrow_out[CONV : CONV + 1] += jnp.sum(d_bc, axis=0, keepdims=True)
        return 0

    lax.fori_loop(0, spans, block, 0)

    def back(window, taps, rows):
        total = None
        for j in range(CONV):
            term = taps[j : j + 1] * window[CONV - 1 - j : CONV - 1 - j + rows]
            total = term if total is None else total + term
        return total.astype(BF16)

    dcat_out[0:EDGE, 0:inner] = back(dpre[0 : 2 * EDGE, 0:inner], rowp, EDGE)
    dcat_out[0:EDGE, inner:width] = back(dpre[0 : 2 * EDGE, inner:], bcp, EDGE)

    def conv_block(q, _):
        after = pl.ds(pl.multiple_of(q * SPAN + EDGE, EDGE), SPAN)
        window = pl.ds(pl.multiple_of(q * SPAN + EDGE, EDGE), SPAN + EDGE)
        dcat_out[after, 0:inner] = back(dpre[window, 0:inner], rowp, SPAN)
        dcat_out[after, inner:width] = back(dpre[window, inner:], bcp, SPAN)
        return 0

    lax.fori_loop(0, spans, conv_block, 0)


def backward_project(dcat, dz, normed, wx, wz, wbc, wdt, dn_out, gx_out, gz_out, gbc_out, gdt_out):
    inner = dz.shape[1]
    width = inner + 2 * STATE
    spans = dz.shape[0] // SPAN
    d_edge = dcat[0:EDGE]
    pick = head_pick(lax.axis_index("p"), inner // HEADDIM)
    dn_out[0:EDGE] = (
        dot(d_edge[:, 0:inner], wx[...], NT)
        + dot(d_edge[:, inner : inner + STATE], wbc[0], NT)
        + dot(d_edge[:, inner + STATE : width], wbc[1], NT)
    ).astype(BF16)

    def rows_of(q, _):
        at = pl.multiple_of(q * SPAN, SPAN)
        tok = pl.ds(at, SPAN)
        after = pl.ds(pl.multiple_of(at + EDGE, EDGE), SPAN)
        dn_out[after, :] = (
            dot(dz[tok, :], wz[...], NT)
            + dot(dcat[after, 0:inner], wx[...], NT)
            + dot(dcat[after, inner : inner + STATE], wbc[0], NT)
            + dot(dcat[after, inner + STATE : width], wbc[1], NT)
            + dot(dot(dcat[after, width:], pick, NT).astype(BF16), wdt[...], NT)
        ).astype(BF16)
        return 0

    lax.fori_loop(0, spans, rows_of, 0)

    def grads_of(i, _):
        cols = pl.ds(pl.multiple_of(i * SPAN, SPAN), SPAN)
        part = normed[:, cols]
        both = dot(part, dcat[:, 0:width], TN).astype(BF16)
        gx_out[cols, :] = both[:, 0:inner]
        gbc_out[cols, :] = both[:, inner:]
        gdt_out[:, cols] = dot(dcat[:, width:], part, TN)[0:EDGE].astype(BF16)
        gz_out[cols, :] = dot(part[EDGE:], dz[...], TN).astype(BF16)
        return 0

    lax.fori_loop(0, normed.shape[1] // SPAN, grads_of, 0)


HALF = 128
MESH = pl.DeviceIdType.MESH


class Links:
    def __init__(self, sends, recvs):
        self.z, self.p, self.c = lax.axis_index("z"), lax.axis_index("p"), lax.axis_index("head")
        self.groups = lax.axis_size("z")
        self.sends, self.recvs, self.used = sends, recvs, 0

    def copy(self, src, dst, device):
        i = self.used
        self.used += 1
        return pltpu.make_async_remote_copy(
            src_ref=src, dst_ref=dst, send_sem=self.sends.at[i], recv_sem=self.recvs.at[i],
            device_id=device, device_id_type=MESH,
        )

    def local(self, src, dst):
        i = self.used
        self.used += 1
        return pltpu.make_async_copy(src, dst, self.sends.at[i])

    def at(self, k, e):
        return (self.z, lax.bitwise_xor(self.p, jnp.int32(k)), lax.bitwise_xor(self.c, jnp.int32(e)))

    def last_of_plane(self):
        return jnp.logical_and(self.p == GROUP - 1, self.c == 1)

    def greet(self, plane=False, sibling=False, groups=False, edge=0):
        barrier = pltpu.get_barrier_semaphore()
        z, count = self.z, self.groups
        above = z < count - 1

        def signal(device):
            pl.semaphore_signal(barrier, 1, device_id=device, device_id_type=MESH)

        self.expected = jnp.int32(0)
        for k in range(GROUP):
            for e in range(2):
                if (k or e) if plane else (sibling and e and not k):
                    signal(self.at(k, e))
                    self.expected = self.expected + 1
        if groups:
            for k in range(1, count):
                signal((lax.rem(z + k, count), self.p, self.c))
            self.expected = self.expected + (count - 1)
        sending = jnp.logical_and(self.last_of_plane(), above)
        if edge == 1:
            pl.when(z > 0)(lambda: signal((z - 1, jnp.int32(GROUP - 1), jnp.int32(1))))
            self.expected = self.expected + 2 * GROUP * sending.astype(jnp.int32)
        if edge == -1:

            @pl.when(sending)
            def _():
                for p in range(GROUP):
                    for c in range(2):
                        signal((z + 1, jnp.int32(p), jnp.int32(c)))

            self.expected = self.expected + (z > 0).astype(jnp.int32)

    def meet(self):
        pl.semaphore_wait(pltpu.get_barrier_semaphore(), self.expected)

    def start_barrier(self, **who):
        self.greet(**who)
        self.meet()


class Spread:
    def __init__(self, links, own, out):
        rows = own.shape[0]
        there = out.at[pl.ds(pl.multiple_of(links.z * rows, EDGE), rows)]
        self.keep = links.local(own, there)
        self.copies = [
            links.copy(own, there, (lax.rem(links.z + k, links.groups), links.p, links.c)) for k in range(1, links.groups)
        ]

    def start(self):
        self.keep.start()
        for copy in self.copies:
            copy.start()

    def arrive(self):
        self.keep.wait()
        for copy in self.copies:
            copy.wait_recv()

    def finish(self):
        for copy in self.copies:
            copy.wait_send()


class Collect:
    def __init__(self, links, grad, out):
        rows = grad.shape[0] // links.groups
        z, groups = links.z, links.groups

        def block(index):
            return grad.at[pl.ds(pl.multiple_of(index * rows, EDGE), rows)]

        self.keep = links.local(block(z), out.at[0])
        self.copies = []
        for k in range(1, groups):
            to = lax.rem(z + k, groups)
            self.copies.append(links.copy(block(to), out.at[k], (to, links.p, links.c)))

    def start(self):
        self.keep.start()
        for copy in self.copies:
            copy.start()

    def arrive(self):
        self.keep.wait()
        for copy in self.copies:
            copy.wait_recv()

    def finish(self):
        for copy in self.copies:
            copy.wait_send()


class Deliver:
    def __init__(self, links, parts, final, out):
        self.links, self.parts, self.final, self.out = links, parts, final, out
        inner = parts.shape[2]
        self.mine = pl.ds(pl.multiple_of(links.p * inner, 128), inner)
        self.copies = [
            links.copy(final.at[lax.bitwise_xor(links.p, jnp.int32(k))], out.at[:, self.mine], links.at(k, 0))
            for k in (3, 1, 2)
        ]

    def start(self):
        total = self.parts[0].astype(F32)
        for k in range(1, self.parts.shape[0]):
            total = total + self.parts[k].astype(F32)
        shard = self.final.shape[1]
        for j in range(GROUP):
            self.final[j] = total[j * shard : (j + 1) * shard].astype(BF16)
        for copy in self.copies:
            copy.start()
        self.out[:, self.mine] = self.final[self.links.p]

    def finish(self):
        for copy in self.copies:
            copy.wait()


class States:
    def __init__(self, links, backward, state, decay, states, decays):
        z, groups = links.z, links.groups
        self.links, self.refs = links, (state, decay, states, decays)
        self.found = []
        for k in range(1, groups):
            to, source = (z - k, z + k) if backward else (z + k, z - k)
            sending, receiving = (to >= 0, source < groups) if backward else (to < groups, source >= 0)
            device = (jnp.clip(to, 0, groups - 1), links.p, links.c)
            pair = [links.copy(state, states.at[z], device), links.copy(decay, decays.at[z], device)]
            self.found.append((sending, receiving, pair))

    def start(self):
        for sending, _, pair in self.found:

            @pl.when(sending)
            def _(pair=pair):
                for copy in pair:
                    copy.start()

    def arrive(self):
        for _, receiving, pair in self.found:

            @pl.when(receiving)
            def _(pair=pair):
                for copy in pair:
                    copy.wait_recv()

    def finish(self):
        for sending, _, pair in self.found:

            @pl.when(sending)
            def _(pair=pair):
                for copy in pair:
                    copy.wait_send()


class Gather:
    def __init__(self, links, out, base):
        self.links, self.out, self.base = links, out, base

        def place(k, c):
            row = base + lax.bitwise_xor(links.p, jnp.int32(k)) * (2 * HALF) + c * HALF
            return out.at[pl.ds(pl.multiple_of(row, EDGE), HALF), :]

        own = place(0, links.c)
        self.out_copies = [links.copy(own, own, links.at(k, 0)) for k in (3, 1, 2)]
        self.shared = [links.copy(own, own, links.at(0, 1))]
        self.shared += [links.copy(place(k, links.c), place(k, links.c), links.at(0, 1)) for k in (1, 2, 3)]
        self.arrivals = [self.out_copies[1], self.out_copies[2], self.out_copies[0]]

    def own(self, start, size):
        row = self.base + self.links.p * (2 * HALF) + self.links.c * HALF + start
        return pl.ds(pl.multiple_of(row, EDGE), size)

    def start(self):
        for copy in self.out_copies:
            copy.start()
        self.shared[0].start()

    def pass_on(self):
        for k in range(3):
            self.arrivals[k].wait_recv()
            self.shared[k + 1].start()

    def finish(self):
        for copy in self.shared:
            copy.wait_recv()
        for copy in self.shared + self.out_copies:
            copy.wait_send()


class EdgeForward:
    def __init__(self, links, gather):
        self.links = links
        tail = gather.out.at[gather.own(HALF - EDGE, EDGE), :]
        first = links.used
        links.used += 2 * GROUP + 1
        recv = links.recvs.at[first + 2 * GROUP]
        self.out = gather.out
        self.copies = [
            pltpu.make_async_remote_copy(
                src_ref=tail, dst_ref=gather.out.at[0:EDGE, :], send_sem=links.sends.at[first + p * 2 + c], recv_sem=recv,
                device_id=(links.z + 1, jnp.int32(p), jnp.int32(c)), device_id_type=MESH,
            )
            for p in range(GROUP)
            for c in range(2)
        ]
        self.sending = jnp.logical_and(links.last_of_plane(), links.z < links.groups - 1)

    def start(self):
        @pl.when(self.sending)
        def _():
            for copy in self.copies:
                copy.start()

        @pl.when(self.links.z == 0)
        def _():
            self.out[0:EDGE, :] = jnp.zeros((EDGE, self.out.shape[1]), self.out.dtype)

    def finish(self):
        pl.when(self.links.z > 0)(self.copies[0].wait_recv)

        @pl.when(self.sending)
        def _():
            for copy in self.copies:
                copy.wait_send()


class Scatter:
    def __init__(self, links, part, base, sib, total, peer):
        self.links, self.part, self.base = links, part, base
        self.sib, self.total, self.peer = sib, total, peer
        other = 1 - links.c
        self.to_sibling = {
            k: links.copy(part.at[self.rows(k, other, 0, HALF), :], sib.at[k], links.at(0, 1)) for k in (3, 1, 2, 0)
        }
        self.to_peer = {k: links.copy(total.at[k - 1], peer.at[k - 1], links.at(k, 0)) for k in (3, 1, 2)}

    def rows(self, k, c, start, size):
        row = self.base + lax.bitwise_xor(self.links.p, jnp.int32(k)) * (2 * HALF) + c * HALF + start
        return pl.ds(pl.multiple_of(row, EDGE), size)

    def start(self):
        for copy in self.to_sibling.values():
            copy.start()

    def reduce(self):
        for k in (3, 1, 2):
            self.to_sibling[k].wait_recv()

            def add(i, _, k=k):
                at = pl.ds(pl.multiple_of(i * 32, 32), 32)
                mine = self.part[self.rows(k, self.links.c, i * 32, 32), :].astype(F32)
                self.total[k - 1, at, :] = (mine + self.sib[k, at, :].astype(F32)).astype(BF16)
                return 0

            lax.fori_loop(0, HALF // 32, add, 0)
            self.to_peer[k].start()
        self.to_sibling[0].wait_recv()
        for copy in self.to_peer.values():
            copy.wait_recv()

    def own(self, start, size):
        at = pl.ds(start, size)
        total = self.part[self.rows(0, self.links.c, start, size), :].astype(F32) + self.sib[0, at, :].astype(F32)
        for k in range(3):
            total = total + self.peer[k, at, :].astype(F32)
        return total

    def finish(self):
        for copy in list(self.to_sibling.values()) + list(self.to_peer.values()):
            copy.wait_send()


class SmallSum:
    def __init__(self, links, squares, slots):
        self.links, self.squares, self.slots = links, squares, slots
        self.copies = [
            links.copy(squares.at[:, self.lanes(k, e)], slots.at[2 * k + e - 1], links.at(k, e))
            for k in range(GROUP)
            for e in range(2)
            if k or e
        ]

    def lanes(self, k, e):
        links = self.links
        column = lax.bitwise_xor(links.p, jnp.int32(k)) * (2 * HALF) + lax.bitwise_xor(links.c, jnp.int32(e)) * HALF
        return pl.ds(pl.multiple_of(column, HALF), HALF)

    def start(self):
        for copy in self.copies:
            copy.start()

    def total(self):
        for copy in self.copies:
            copy.wait_recv()
        total = self.squares[:, self.lanes(0, 0)]
        for i in range(len(self.copies)):
            total = total + self.slots[i]
        return total

    def finish(self):
        for copy in self.copies:
            copy.wait_send()


class SmallGather:
    def __init__(self, links, out):
        self.out = out
        self.lanes = pl.ds(pl.multiple_of(links.p * (2 * HALF) + links.c * HALF, HALF), HALF)
        self.copies = [
            links.copy(out.at[:, self.lanes], out.at[:, self.lanes], links.at(k, e))
            for k in range(GROUP)
            for e in range(2)
            if k or e
        ]

    def start(self):
        for copy in self.copies:
            copy.start()

    def finish(self):
        for copy in self.copies:
            copy.wait()


def row_chunks(size=32):
    return [(start, size) for start in range(0, HALF, size)]


def rms_of(rows):
    return lax.rsqrt(jnp.mean(rows * rows, axis=-1, keepdims=True) + EPS)


def as_tile(columns):
    lane = iota((HALF, HALF), 1)
    wide = jnp.zeros((HALF, HALF), F32)
    for i, column in enumerate(columns):
        wide = jnp.where(lane == i, column, wide)
    return wide.T[0:8]


def begin_kernel(count, late, *refs):
    resid, cot, gain = refs[:3]
    shards, rest = refs[3 : 3 + count + late], refs[3 + count + late :]
    normed_out, dmix_out, resid_out, cot_out = rest[:4]
    outs = rest[4 : 4 + count + late]
    sends, recvs = rest[4 + count + late :]
    links = Links(sends, recvs)
    z, p, c, groups = links.z, links.p, links.c, links.groups
    inner = outs[0].shape[-1]
    mine = z * GROUP + p

    def source(i, k):
        if shards[i].shape[1] == STATE:
            return shards[i]
        to = lax.bitwise_xor(p, jnp.int32(k))
        return shards[i].at[:, pl.ds(pl.multiple_of(to * inner, 128), inner)]

    def block(i, at):
        return outs[i].at[c, at] if len(outs[i].shape) == 4 else outs[i].at[at]

    swaps, keeps = [], []
    for i in range(count + late):
        target = block(i, mine if i < count else p)
        swaps.append([links.copy(source(i, k), target, links.at(k, 0)) for k in (3, 1, 2)])
        keeps.append(links.local(source(i, 0), target))
    for copy in keeps:
        copy.start()

    gather = Gather(links, normed_out, EDGE)
    other = Gather(links, dmix_out, 0)
    edge = EdgeForward(links, gather)
    links.greet(plane=True, groups=True, edge=1)
    for start, size in row_chunks():
        rows = pl.ds(pl.multiple_of(c * HALF + start, EDGE), size)
        part = resid[rows, :].astype(F32)
        resid_out[start : start + size] = part
        normed_out[gather.own(start, size), :] = (part * rms_of(part) * gain[...]).astype(BF16)
        part = cot[rows, :]
        cot_out[start : start + size] = part.astype(F32)
        dmix_out[other.own(start, size), :] = part
    links.meet()
    for group in swaps[:count]:
        for copy in group:
            copy.start()

    def lines(step):
        found = []
        up, down = z - step + 1, z + step - 1
        for i in range(count):
            piece = block(i, pl.ds(jnp.maximum(up, 0) * GROUP, GROUP))
            sending = jnp.logical_and(up >= 0, z < groups - 1)
            found.append((sending, z - step >= 0, links.copy(piece, piece, (z + 1, p, c))))
            piece = block(i, pl.ds(jnp.minimum(down, groups - 1) * GROUP, GROUP))
            sending = jnp.logical_and(down < groups, z > 0)
            found.append((sending, z + step < groups, links.copy(piece, piece, (z - 1, p, c))))
        return found

    steps = [lines(step) for step in range(1, groups)]
    for i in range(count):
        keeps[i].wait()
        for copy in swaps[i]:
            copy.wait_recv()
        for can_send, _, copy in steps[0][2 * i : 2 * i + 2]:
            pl.when(can_send)(copy.start)
    gather.start()
    edge.start()
    gather.pass_on()
    other.start()
    for step in range(1, len(steps)):
        for i in range(2 * count):
            pl.when(steps[step - 1][i][1])(steps[step - 1][i][2].wait_recv)
            pl.when(steps[step][i][0])(steps[step][i][2].start)
        if step == 1:
            other.pass_on()
            for group in swaps[count:]:
                for copy in group:
                    copy.start()
    share = []
    for i in range(2 * count):
        pl.when(steps[-1][i][1])(steps[-1][i][2].wait_recv)
        if i % 2 and len(outs[i // 2].shape) == 4:
            whole = outs[i // 2].at[c]
            share.append(links.copy(whole, whole, links.at(0, 1)))
            share[-1].start()
    gather.finish()
    other.finish()
    edge.finish()
    for i in range(count, count + late):
        keeps[i].wait()
        for copy in swaps[i]:
            copy.wait_recv()
    for group in swaps:
        for copy in group:
            copy.wait_send()
    for found in steps:
        for can_send, _, copy in found:
            pl.when(can_send)(copy.wait_send)
    for copy in share:
        copy.wait()


def forward_kernel(last, *refs):
    normed, wx, wz, wbc, wdt, wo, rowp, bcp, headp = refs[:9]
    more = 0 if last else 2
    later, outs = refs[9 : 9 + more], refs[9 + more :]
    (z, xin, bcin, x, bc, dtraw, dt, s, y, states, decay, part, squares, wo_all) = outs[:14]
    later_out = outs[14 : 14 + more]
    ext, local, state_low, decay_row, states_in, decays_in, sends, recvs = outs[14 + more :]
    links = Links(sends, recvs)
    spread = Spread(links, wo, wo_all)
    passing = []
    if not last:
        passing = [Spread(links, later[0], later_out[0].at[links.c]), Spread(links, later[1], later_out[1])]
        whole = later_out[0].at[links.c]
        share = links.copy(whole, whole, links.at(0, 1))
    carried = States(links, False, state_low, decay_row, states_in, decays_in)
    links.start_barrier(sibling=not last, groups=True)
    spread.start()
    state_sum, decay_all = project_and_convolve(
        links.p, normed, wx, wz, wbc, wdt, rowp, bcp, headp,
        z, xin, bcin, x, bc, dtraw, dt, s, decay, ext, local,
    )
    state_low[...] = state_sum.astype(BF16)
    decay_row[...] = jnp.broadcast_to(decay_all, decay_row.shape)
    carried.start()
    for other in passing:
        other.start()
    mix_within_spans(x, bc, s, dt, y)
    carried.arrive()
    state = entering_state(links.z, links.groups, states_in, decays_in, False)
    spread.arrive()
    mix_out(state, local, decay, x, bc, z, s, wo_all, rowp, y, states, part, squares)
    for other in passing:
        other.arrive()
    if not last:
        share.start()
    carried.finish()
    for other in [spread] + passing:
        other.finish()
    if not last:
        share.wait()


def backward_kernel(inner_all, done, *refs):
    (dmix, wo, y, z, x, bc, s, dt, dtraw, xin, bcin, states, decay, token_scalars, rowp, bcp, headp) = refs[:17]
    parts, outs = refs[17 : 17 + done], refs[17 + done :]
    dz, dcat, go_parts, gate_small, row_small, bc_small, head_small = outs[:7]
    delivered = outs[7 : 7 + done]
    (
        dy, gwo, normed_out, prior, dend, dpre, flow, sums, final, state_low, decay_row, states_in, decays_in, sends, recvs
    ) = outs[7 + done :]
    links = Links(sends, recvs)
    carried = States(links, True, state_low, decay_row, states_in, decays_in)
    collect = Collect(links, gwo, go_parts)
    delivers = [Deliver(links, parts[i], final.at[i], delivered[i]) for i in range(done)]
    links.greet(plane=done > 0, groups=True)
    grad_sum, decay_all = back_through_gate(
        inner_all, dmix, wo, y, z, x, bc, s, decay, token_scalars, rowp, dz, gate_small, dy, prior, normed_out
    )
    state_low[...] = grad_sum.astype(BF16)
    decay_row[...] = jnp.broadcast_to(decay_all, decay_row.shape)
    links.meet()
    carried.start()
    out_gradient(dmix, normed_out, gwo)
    collect.start()
    for deliver in delivers:
        deliver.start()
    back_within_spans(dy, x, bc, s, dt, dpre, flow, sums)
    carried.arrive()
    grad = entering_state(links.z, links.groups, states_in, decays_in, True)
    back_through_states(
        grad, prior, decay, states, dy, x, bc, s, dt, dtraw, xin, bcin, rowp, bcp, headp, flow, sums,
        dcat, row_small, bc_small, head_small, dpre, dend,
    )
    carried.finish()
    collect.arrive()
    collect.finish()
    for deliver in delivers:
        deliver.finish()


def next_layer_kernel(
    inner_all, part, squares, resid, gain, wx, wz, normed_out, resid_out, mixed_out, inv_out, wx_out, wz_out,
    sib, total, peer, slots, sends, recvs,
):
    links = Links(sends, recvs)
    scatter = Scatter(links, part, 0, sib, total, peer)
    small = SmallSum(links, squares, slots)
    gather = Gather(links, normed_out, EDGE)
    edge = EdgeForward(links, gather)
    spreads = [Spread(links, wx, wx_out), Spread(links, wz, wz_out)]
    links.start_barrier(plane=True, groups=True, edge=1)
    scatter.start()
    small.start()
    for spread in spreads:
        spread.start()
    scatter.reduce()
    inv = lax.rsqrt(small.total() * (1.0 / inner_all) + EPS)
    inv_out[...] = inv
    column = inv.T[:, 0:1]
    for start, size in row_chunks():
        at = slice(start, start + size)
        mixed = scatter.own(start, size)
        mixed_out[at] = mixed
        fresh = resid[at] + column[at] * mixed
        resid_out[at] = fresh
        normed_out[gather.own(start, size), :] = (fresh * rms_of(fresh) * gain[...]).astype(BF16)
    gather.start()
    edge.start()
    gather.pass_on()
    scatter.finish()
    small.finish()
    gather.finish()
    edge.finish()
    for spread in spreads:
        spread.arrive()
        spread.finish()


def turn_kernel(
    inner_all, part, squares, resid, cot, block_out, scalars_out,
    sib, total, peer, slots, sends, recvs,
):
    links = Links(sends, recvs)
    scatter = Scatter(links, part, 0, sib, total, peer)
    small = SmallSum(links, squares, slots)
    spread = SmallGather(links, scalars_out)
    rows = pl.ds(pl.multiple_of(links.c * HALF, HALF), HALF)
    share = links.copy(block_out.at[rows, :], block_out.at[rows, :], links.at(0, 1))
    links.start_barrier(plane=True)
    scatter.start()
    small.start()
    scatter.reduce()
    inv = lax.rsqrt(small.total() * (1.0 / inner_all) + EPS)
    column = inv.T[:, 0:1]
    dots = []
    for start, size in row_chunks():
        at = slice(start, start + size)
        mixed = scatter.own(start, size)
        dots.append(jnp.sum(cot[at] * mixed, axis=-1, keepdims=True))
        block_out[pl.ds(pl.multiple_of(links.c * HALF + start, EDGE), size), :] = (
            resid[at] + column[at] * mixed
        ).astype(BF16)
    scalars_out[:, spread.lanes] = as_tile([column, jnp.concatenate(dots)])
    spread.start()
    share.start()
    scatter.finish()
    small.finish()
    spread.finish()
    share.wait()


def grad_rows(links, scatter, edge_slots, grad, resid, gain, gain_out, start, size):
    at = slice(start, start + size)
    d_normed = scatter.own(start, size)
    if start + size == HALF:
        extra = edge_slots[0].astype(F32)
        for i in range(1, 2 * GROUP):
            extra = extra + edge_slots[i].astype(F32)
        used = jnp.logical_and(links.last_of_plane(), links.z < links.groups - 1)
        extra = jnp.where(used, extra, 0.0)
        d_normed = d_normed + jnp.concatenate([jnp.zeros((size - EDGE, extra.shape[1]), F32), extra])
    rows = resid[at]
    inv_rms = rms_of(rows)
    gain_sum = jnp.sum(d_normed * rows * inv_rms, axis=0, keepdims=True)
    gain_out[0:1] = gain_sum if start == 0 else gain_out[0:1] + gain_sum
    d_hidden = d_normed * gain[...]
    return (
        grad[at]
        + inv_rms * d_hidden
        - rows * (inv_rms * inv_rms * inv_rms * jnp.mean(d_hidden * rows, axis=-1, keepdims=True))
    )


class EdgeBackward:
    def __init__(self, links, part, slots):
        self.links = links
        first = links.used
        links.used += 2 * GROUP + 1
        me = links.p * 2 + links.c
        self.send = pltpu.make_async_remote_copy(
            src_ref=part.at[0:EDGE, :], dst_ref=slots.at[me], send_sem=links.sends.at[first], recv_sem=links.recvs.at[first + me],
            device_id=(links.z - 1, jnp.int32(GROUP - 1), jnp.int32(1)), device_id_type=MESH,
        )
        self.recvs = [
            pltpu.make_async_remote_copy(
                src_ref=part.at[0:EDGE, :], dst_ref=slots.at[i], send_sem=links.sends.at[first], recv_sem=links.recvs.at[first + i],
                device_id=(links.z, links.p, 1 - links.c), device_id_type=MESH,
            )
            for i in range(2 * GROUP)
        ]
        self.receiving = jnp.logical_and(links.last_of_plane(), links.z < links.groups - 1)

    def start(self):
        pl.when(self.links.z > 0)(self.send.start)

    def receive(self):
        @pl.when(self.receiving)
        def _():
            for copy in self.recvs:
                copy.wait_recv()

    def finish(self):
        pl.when(self.links.z > 0)(self.send.wait_send)


def layer_below_kernel(
    part, grad, resid, gain, mixed, inv, gx, gz, dmix_out, scalars_out, grad_out, gain_out, gx_out, gz_out,
    sib, total, peer, edge_slots, sends, recvs,
):
    links = Links(sends, recvs)
    scatter = Scatter(links, part, EDGE, sib, total, peer)
    edge = EdgeBackward(links, part, edge_slots)
    gather = Gather(links, dmix_out, 0)
    spread = SmallGather(links, scalars_out)
    edge_slots[...] = jnp.zeros_like(edge_slots)
    collects = [Collect(links, gx, gx_out), Collect(links, gz, gz_out)]
    links.start_barrier(plane=True, groups=True, edge=-1)
    edge.start()
    scatter.start()
    for collect in collects:
        collect.start()
    scatter.reduce()
    edge.receive()
    gain_out[...] = jnp.zeros_like(gain_out)
    dots = []
    for start, size in row_chunks():
        at = slice(start, start + size)
        fresh = grad_rows(links, scatter, edge_slots, grad, resid, gain, gain_out, start, size)
        grad_out[at] = fresh
        low = fresh.astype(BF16)
        dmix_out[gather.own(start, size), :] = low
        dots.append(jnp.sum(low.astype(F32) * mixed[at], axis=-1, keepdims=True))
    scalars_out[:, spread.lanes] = as_tile([inv[...].T[:, 0:1], jnp.concatenate(dots)])
    gather.start()
    spread.start()
    gather.pass_on()
    scatter.finish()
    edge.finish()
    gather.finish()
    spread.finish()
    for collect in collects:
        collect.arrive()
        collect.finish()


class SmallSums:
    def __init__(self, links, bc, vec, dt, wide, bc_out, vec_out, dt_out, wide_out, bufs):
        self.links = links
        self.bc, self.vec, self.dt, self.wide = bc, vec, dt, wide
        self.bc_out, self.vec_out, self.dt_out, self.wide_out = bc_out, vec_out, dt_out, wide_out
        self.bc_in, self.bc_sum, self.bc_far, self.vec_in, self.vec_far, self.dt_far, self.wide_far = bufs
        z, p, c, groups = links.z, links.p, links.c, links.groups
        self.first, self.vec_first, self.second, self.third = [], [], [], []
        for k in range(GROUP):
            for e in range(2):
                if not (k or e):
                    continue
                slot = 2 * k + e
                to_p, to_c = lax.bitwise_xor(p, jnp.int32(k)), lax.bitwise_xor(c, jnp.int32(e))
                device = links.at(k, e)
                for layer in range(bc.shape[0]):
                    src = bc.at[layer, :, to_p, :, pl.ds(pl.multiple_of(to_c * STATE, STATE), STATE)]
                    self.first.append(links.copy(src, self.bc_in.at[layer, slot - 1], device))
                self.vec_first.append(links.copy(vec.at[to_p * 2 + to_c], self.vec_in.at[slot - 1], device))
                self.third.append(links.copy(vec_out.at[p * 2 + c], vec_out.at[p * 2 + c], device))
        for k in range(1, groups):
            to = lax.rem(z + k, groups)
            device = (to, p, c)
            for layer in range(bc.shape[0]):
                self.second.append(links.copy(self.bc_sum.at[layer, to], self.bc_far.at[layer, k - 1], device))
            self.second.append(links.copy(self.vec_in.at[7], self.vec_far.at[k - 1], device))
            self.second.append(links.copy(dt.at[to], self.dt_far.at[k - 1], device))
            self.second.append(links.copy(wide, self.wide_far.at[k - 1], device))
        for k in range(1, GROUP):
            device = links.at(k, 0)
            self.third.append(links.copy(dt_out.at[p], dt_out.at[p], device))
            self.third.append(links.copy(wide_out.at[p], wide_out.at[p], device))
        lanes = pl.ds(pl.multiple_of(c * STATE, STATE), STATE)
        self.third.append(links.copy(bc_out.at[:, :, lanes], bc_out.at[:, :, lanes], links.at(0, 1)))

    def round_one(self):
        for copy in self.vec_first + self.first:
            copy.start()

    def round_two(self):
        links = self.links
        for copy in self.vec_first + self.first:
            copy.wait_recv()
        own_lanes = pl.ds(pl.multiple_of(links.c * STATE, STATE), STATE)
        for layer in range(self.bc.shape[0]):

            def add(i, _, layer=layer):
                total = self.bc[layer, i, links.p, :, own_lanes].astype(F32)
                for slot in range(2 * GROUP - 1):
                    total = total + self.bc_in[layer, slot, i].astype(F32)
                self.bc_sum[layer, i] = total.astype(BF16)
                return 0

            lax.fori_loop(0, links.groups, add, 0)
        total = self.vec[links.p * 2 + links.c]
        for slot in range(2 * GROUP - 1):
            total = total + self.vec_in[slot]
        self.vec_in[7] = total
        for copy in self.second:
            copy.start()

    def round_three(self):
        links = self.links
        z, p, c = links.z, links.p, links.c
        for copy in self.second:
            copy.wait_recv()
        far = links.groups - 1
        lanes = pl.ds(pl.multiple_of(c * STATE, STATE), STATE)
        for layer in range(self.bc.shape[0]):
            total = self.bc_sum[layer, z].astype(F32)
            for k in range(far):
                total = total + self.bc_far[layer, k].astype(F32)
            self.bc_out[layer, :, lanes] = total.astype(BF16)
        total = self.vec_in[7]
        dt_total = self.dt[z].astype(F32)
        wide_total = self.wide[...]
        for k in range(far):
            total = total + self.vec_far[k]
            dt_total = dt_total + self.dt_far[k].astype(F32)
            wide_total = wide_total + self.wide_far[k]
        self.vec_out[p * 2 + c] = total
        self.dt_out[p] = dt_total.astype(BF16)
        self.wide_out[p] = wide_total
        for copy in self.third:
            copy.start()

    def finish(self):
        for copy in self.third:
            copy.wait_recv()
        for copy in self.vec_first + self.first + self.second + self.third:
            copy.wait_send()


def final_kernel(
    part, grad, resid, gain, gx, gz, go_parts, bc, vec, dt, wide,
    out, gx_out, gz_out, go_out, bc_out, vec_out, dt_out, wide_out,
    sib, total, peer, edge_slots, gain_row, vec_own, gx_parts, gz_parts, final,
    bc_in, bc_sum, bc_far, vec_in, vec_far, dt_far, wide_far, sends, recvs,
):
    links = Links(sends, recvs)
    scatter = Scatter(links, part, EDGE, sib, total, peer)
    edge = EdgeBackward(links, part, edge_slots)
    rows = pl.ds(pl.multiple_of(links.c * HALF, HALF), HALF)
    share = links.copy(out.at[rows, :], out.at[rows, :], links.at(0, 1))
    collects = [Collect(links, gx, gx_parts), Collect(links, gz, gz_parts)]
    small = SmallSums(
        links, bc, vec_own, dt, wide, bc_out, vec_out, dt_out, wide_out,
        (bc_in, bc_sum, bc_far, vec_in, vec_far, dt_far, wide_far),
    )
    delivers = [
        Deliver(links, parts, final.at[i], place)
        for i, (parts, place) in enumerate(((go_parts, go_out), (gx_parts, gx_out), (gz_parts, gz_out)))
    ]
    edge_slots[...] = jnp.zeros_like(edge_slots)
    links.start_barrier(plane=True, groups=True, edge=-1)
    edge.start()
    scatter.start()
    for collect in collects:
        collect.start()
    scatter.reduce()
    edge.receive()
    gain_row[...] = jnp.zeros_like(gain_row)
    for start, size in row_chunks():
        fresh = grad_rows(links, scatter, edge_slots, grad, resid, gain, gain_row, start, size)
        out[pl.ds(pl.multiple_of(links.c * HALF + start, EDGE), size), :] = fresh.astype(BF16)
    share.start()
    vec_own[...] = vec[...]
    for r in range(gain_row.shape[1] // 128):
        vec_own[r // 8, r % 8 : r % 8 + 1, :] = gain_row[0:1, r * 128 : r * 128 + 128]
    small.round_one()
    delivers[0].start()
    small.round_two()
    small.round_three()
    for i in range(2):
        collects[i].arrive()
        delivers[i + 1].start()
    small.finish()
    scatter.finish()
    edge.finish()
    share.wait()
    for collect in collects:
        collect.finish()
    for deliver in delivers:
        deliver.finish()


def call(body, outs, *args, scratch=(), collective=None, copies=0):
    vmem = pl.BlockSpec(memory_space=pltpu.VMEM)
    scratch = [pltpu.VMEM(shape, kind) for shape, kind in scratch]
    if collective is not None:
        scratch += [pltpu.SemaphoreType.DMA((copies,)), pltpu.SemaphoreType.DMA((copies,))]
    return pl.pallas_call(
        body,
        out_shape=tuple(jax.ShapeDtypeStruct(shape, kind) for shape, kind in outs),
        in_specs=[vmem] * len(args),
        out_specs=tuple([vmem] * len(outs)),
        scratch_shapes=scratch,
        compiler_params=pltpu.CompilerParams(
            vmem_limit_bytes=VMEM_BYTES, collective_id=collective, has_side_effects=collective is not None
        ),
    )(*args)


def on_device(resid_in, cotangent, norm_gain, w_zx, w_dt, w_bc, conv_x, conv_bc, head_params, gated_gain, w_out):
    layers, model = norm_gain.shape
    groups = lax.axis_size("z")
    place, core = lax.axis_index("p"), lax.axis_index("head")
    shard = w_dt.shape[1]
    inner_core = conv_x.shape[2]
    inner = inner_core // GROUP
    heads_core = head_params.shape[2]
    heads = heads_core // GROUP
    inner_all = inner_core * lax.axis_size("head")
    length = resid_in.shape[1]
    tokens = GROUP * length
    spans = tokens // SPAN
    sources = groups * GROUP
    rows = GROUP * shard

    def my_part(array, size):
        return lax.dynamic_slice_in_dim(array, place * size, size, array.ndim - 1)

    row_all, bc_all, head_all = [], [], []
    conv_mine = my_part(conv_x, inner).astype(F32)
    gain_mine = my_part(gated_gain, inner).astype(F32)
    head_mine = my_part(head_params, heads)
    gains = [norm_gain[layer].astype(F32)[None] for layer in range(layers)]
    for layer in range(layers):
        skip = jnp.repeat(head_mine[layer, 2], HEADDIM)
        row_all.append(
            jnp.concatenate([conv_mine[layer], gain_mine[layer][None], skip[None], jnp.zeros((1, inner), F32)])
        )
        bc_all.append(jnp.pad(conv_bc[layer].astype(F32), ((0, 3), (0, 0))))
        head_all.append(jnp.pad(head_mine[layer], ((0, 5), (0, 128 - heads))))

    def shards_of(layer):
        half = lax.dynamic_slice_in_dim(w_bc[layer], core * STATE, STATE, 1)
        steps = jnp.pad(w_dt[layer], ((0, 0), (0, STATE - heads_core)))
        return w_zx[layer, 1], w_zx[layer, 0], half, steps, w_out[layer].T

    half_scratch = [
        ((GROUP, HALF, model), BF16),
        ((GROUP - 1, HALF, model), BF16),
        ((GROUP - 1, HALF, model), BF16),
    ]
    slots = ((2 * GROUP - 1, 8, HALF), F32)
    edges = ((2 * GROUP, EDGE, model), BF16)
    own_rows = ((HALF, model), F32)

    shards = [shards_of(layer) for layer in range(layers)]
    early = list(shards[0][:4])
    late = [shards[0][4]] + [piece for layer in range(1, layers) for piece in shards[layer]]
    wide_piece, thin_piece = (sources, shard, inner), (sources, shard, STATE)
    late_shapes = [(GROUP, shard, a.shape[1] // (GROUP if a.shape[1] > STATE else 1)) for a in late]
    gathered = call(
        functools.partial(begin_kernel, len(early), len(late)),
        [
            ((tokens + EDGE, model), BF16),
            ((tokens, model), BF16),
            own_rows,
            own_rows,
            (wide_piece, BF16),
            (wide_piece, BF16),
            ((2, *thin_piece), BF16),
            (thin_piece, BF16),
        ]
        + [(shape, BF16) for shape in late_shapes],
        resid_in[0], cotangent[0], gains[0], *early, *late,
        collective=0, copies=30 + 4 * (len(early) + len(late)) + 2 * len(early) * (groups - 1),
    )
    normed, last_dmix, resid, grad, wx, wz, wbc, wdt = gathered[:8]
    wx, wz, wdt = [a.reshape(model, -1) for a in (wx, wz, wdt)]
    wbc = wbc.reshape(2, model, STATE)
    own = [a.reshape(rows, -1) for a in gathered[8:]]
    own = [(None, None, None, None, own[0])] + [own[1 + 5 * i : 6 + 5 * i] for i in range(layers - 1)]
    whole = ((model, inner), BF16)

    state_scratch = [
        ((STATE, inner), BF16),
        ((8, inner), F32),
        ((groups, STATE, inner), BF16),
        ((groups, 8, inner), F32),
    ]
    saved, weights = [], []
    for layer in range(layers):
        rowp, bcp, headp = row_all[layer], bc_all[layer], head_all[layer]
        last = layer == layers - 1
        passing = [] if last else [own[layer + 1][2], own[layer + 1][3]]
        results = call(
            functools.partial(forward_kernel, last),
            [
                ((tokens, inner), BF16),
                ((tokens + EDGE, inner), BF16),
                ((tokens + EDGE, 2 * STATE), BF16),
                ((tokens, inner), BF16),
                ((tokens, 2 * STATE), BF16),
                ((tokens, 128), BF16),
                ((tokens, 128), F32),
                ((tokens, 128), F32),
                ((tokens, inner), F32),
                ((spans, STATE, inner), F32),
                ((spans, 8, inner), F32),
                ((tokens, model), BF16),
                ((8, tokens), F32),
                whole,
            ]
            + ([] if last else [((2, model, STATE), BF16), ((model, STATE), BF16)]),
            normed, wx, wz, wbc, wdt, own[layer][4], rowp, bcp, headp, *passing,
            scratch=[((tokens + EDGE, inner + 2 * STATE), F32), ((spans, STATE, inner), F32)] + state_scratch,
            collective=2 if last else 1, copies=8 + 5 * groups,
        )
        z, xin, bcin, x, bc, dtraw, dt, s, y, states, decay, part, squares, wo = results[:14]
        weights.append((wx, wz, wbc, wdt, wo))
        kept = (resid, normed, (y, z, x, bc, s, dt, dtraw, xin, bcin, states, decay))
        if not last:
            wbc, wdt = results[14:]
            normed, resid, mixed, inv, wx, wz = call(
                functools.partial(next_layer_kernel, inner_all),
                [((tokens + EDGE, model), BF16), own_rows, own_rows, ((8, HALF), F32), whole, whole],
                part, squares, resid, gains[layer + 1], own[layer + 1][0], own[layer + 1][1],
                scratch=half_scratch + [slots], collective=3, copies=40 + 2 * groups,
            )
            saved.append((*kept, (mixed, inv)))
        else:
            block_out, token_scalars = call(
                functools.partial(turn_kernel, inner_all),
                [((length, model), BF16), ((8, tokens), F32)],
                part, squares, resid, grad,
                scratch=half_scratch + [slots], collective=4, copies=40,
            )
            saved.append((*kept, None))

    d_mix, ready, delivered = last_dmix, [], {}
    kinds, gain_rows = [None] * layers, [None] * layers
    grad_parts = ((groups, rows, inner), BF16)
    for layer in reversed(range(layers)):
        wx, wz, wbc, wdt, wo = weights[layer]
        rowp, bcp, headp = row_all[layer], bc_all[layer], head_all[layer]
        resid, normed, kept, _ = saved[layer]
        results = call(
            functools.partial(backward_kernel, inner_all, len(ready)),
            [
                ((tokens, inner), BF16),
                ((tokens + EDGE, inner + 2 * STATE + 128), BF16),
                grad_parts,
                ((8, inner), F32),
                ((8, inner), F32),
                ((8, 2 * STATE), F32),
                ((8, 128), F32),
            ]
            + [((shard, inner_core), BF16)] * len(ready),
            d_mix, wo, *kept, token_scalars, rowp, bcp, headp, *ready,
            scratch=[
                ((tokens, inner), BF16),
                whole,
                ((tokens, inner), BF16),
                ((spans, STATE, inner), F32),
                ((spans, STATE, inner), F32),
                ((tokens + 2 * EDGE, inner + 2 * STATE), F32),
                ((tokens, 128), F32),
                ((tokens, 128), F32),
                ((3, GROUP, shard, inner), BF16),
            ]
            + state_scratch,
            collective=5 if ready else 6, copies=20 + 3 * groups,
        )
        dz, dcat, go_parts, gate_small, row_small, bc_small, head_small = results[:7]
        if ready:
            delivered[layer + 1] = results[7:]
        part, gx, gz, gbc, gdt = call(
            backward_project,
            [((tokens + EDGE, model), BF16), whole, whole, ((model, 2 * STATE), BF16), ((EDGE, model), BF16)],
            dcat, dz, normed, wx, wz, wbc, wdt,
        )
        tall = jnp.pad(head_small[:2], ((0, 0), (0, inner - 128)))
        wide = jnp.concatenate([row_small[: CONV + 1], gate_small[:2], tall])
        kinds[layer] = (gbc, gdt, jnp.pad(wide, ((0, 7), (0, 0))), bc_small[: CONV + 1])
        if layer > 0:
            d_mix, token_scalars, grad, gain_rows[layer], gx_parts, gz_parts = call(
                layer_below_kernel,
                [((tokens, model), BF16), ((8, tokens), F32), own_rows, ((8, model), F32), grad_parts, grad_parts],
                part, grad, resid, gains[layer], *saved[layer - 1][3], gx, gz,
                scratch=half_scratch + [edges], collective=7, copies=60 + 2 * groups,
            )
            ready = [gx_parts, gz_parts, go_parts]

    vec = jnp.concatenate(
        [jnp.zeros((model,), F32)]
        + [gain_rows[layer][0] for layer in range(1, layers)]
        + [kinds[layer][3].reshape(-1) for layer in range(layers)]
    )
    vec = jnp.pad(vec, (0, 2 * GROUP * 1024 - vec.shape[0])).reshape(2 * GROUP, 8, 128)
    bc_grads = jnp.stack([kinds[layer][0].reshape(groups, GROUP, shard, 2 * STATE) for layer in range(layers)])
    dt_grads = jnp.concatenate([kinds[layer][1] for layer in range(layers)])
    dt_grads = jnp.swapaxes(dt_grads.reshape(layers * EDGE, groups, rows), 0, 1)
    wide = jnp.concatenate([kinds[layer][2] for layer in range(layers)])
    wide_shape, dt_shape, far = wide.shape, dt_grads.shape[1:], groups - 1
    grad_input, gx, gz, go, g_bc, vec, g_dt, wide = call(
        final_kernel,
        [
            ((length, model), BF16),
            ((shard, inner_core), BF16),
            ((shard, inner_core), BF16),
            ((shard, inner_core), BF16),
            ((layers, shard, 2 * STATE), BF16),
            (vec.shape, F32),
            ((GROUP, *dt_shape), BF16),
            ((GROUP, *wide_shape), F32),
        ],
        part, grad, resid, gains[0], gx, gz, go_parts, bc_grads, vec, dt_grads, wide,
        scratch=half_scratch + [
            edges,
            ((8, model), F32),
            (vec.shape, F32),
            grad_parts,
            grad_parts,
            ((3, GROUP, shard, inner), BF16),
            ((layers, 2 * GROUP - 1, groups, shard, STATE), BF16),
            ((layers, groups, shard, STATE), BF16),
            ((layers, far, shard, STATE), BF16),
            ((2 * GROUP, 8, 128), F32),
            ((far, 8, 128), F32),
            ((far, *dt_shape), BF16),
            ((far, *wide_shape), F32),
        ],
        collective=8, copies=100 + 8 * groups,
    )
    delivered[0] = (gx, gz, go)
    vec = vec.reshape(-1)
    grad_gain = vec[: layers * model].reshape(layers, model)
    grad_conv_bc = vec[layers * model :][: layers * (CONV + 1) * 2 * STATE].reshape(layers, CONV + 1, 2 * STATE)
    wide = wide.reshape(GROUP, layers, 16, inner)
    whole = jnp.moveaxis(wide, 0, 2).reshape(layers, 16, inner_core)
    skip_grad = jnp.sum(whole[:, CONV + 2].reshape(layers, heads_core, HEADDIM), axis=-1)
    tall = jnp.moveaxis(wide[:, :, CONV + 3 : CONV + 5, :heads], 0, 2).reshape(layers, 2, heads_core)
    grad_heads = jnp.concatenate([tall, skip_grad[:, None]], axis=1)
    g_dt = lax.dynamic_slice_in_dim(g_dt.reshape(GROUP, layers, EDGE, GROUP, shard), place, 1, 3)[:, :, :heads, 0]
    grad_dt = jnp.transpose(g_dt, (1, 3, 0, 2)).reshape(layers, shard, heads_core)
    low = lambda a: a.astype(BF16)
    return (
        block_out[None],
        grad_input[None],
        low(grad_gain),
        jnp.stack([jnp.stack([delivered[layer][1], delivered[layer][0]]) for layer in range(layers)]),
        grad_dt,
        g_bc,
        low(whole[:, : CONV + 1]),
        low(grad_conv_bc),
        low(grad_heads),
        low(whole[:, CONV + 1]),
        jnp.stack([delivered[layer][2].T for layer in range(layers)]),
    )


def solution(mesh):
    seq, head = mesh.shape["seq"], mesh.shape["head"]
    split = Mesh(mesh.devices.reshape(seq // GROUP, GROUP, head), ("z", "p", "head"))
    seq_axes = ("z", "p")
    specs = (
        P(None, seq_axes, None),
        P(None, seq_axes, None),
        P(),
        P(None, None, seq_axes, "head"),
        P(None, seq_axes, "head"),
        P(None, seq_axes, None),
        P(None, None, "head"),
        P(),
        P(None, None, "head"),
        P(None, "head"),
        P(None, "head", seq_axes),
    )
    return jax.shard_map(on_device, mesh=split, in_specs=specs, out_specs=specs, check_vma=False)
```

time: 956 us -> 602 us (0.63)
  starting transfers between devices: 117 us -> 0 us
  local copies, waits for them, and re-layouts: 122 us -> 18.2 us
  waiting for transfers between devices: 61.5 us -> 0 us
  Pallas kernels: 618 us -> 563 us
    ppermute x43 -> x0, starting transfers between devices: 117 us -> none  [the longest x9 62.9 us: later_grads(): lax.ppermute(lax.dynamic_index_in_dim(sent[i], there, 0, False), 'z', route)]
    dynamic_update_slice x43 -> x0, local copies, waits for them, and re-layouts: 78.4 us -> none  [the longest x21 54 us: pass_plane(): lax.dynamic_update_slice_in_dim(o, a, there, 0)]
    ppermute x43 -> x0, waiting for transfers between devices: 61.5 us -> none  [the longest x12 38.4 us: pass_groups(): lax.ppermute(a, 'z', [(i, (i + k) % groups) for i in range(groups)])]
    pallas_call x20 -> x11, Pallas kernels: 618 us -> 563 us  [call(): pl.pallas_call(body, out_shape=tuple((jax.ShapeDtypeStruct(shape, kind) f...]
  transfers between devices with their start and end apart: 43 -> 0, of which waited for: 6 -> 0; matrix products, arithmetic and copies ran while one was open for 11% -> 0% of each run, Pallas kernels for 9% -> 0%
where the time goes in v3:
time: 602 us; the launch traced here: 593 us
  Pallas kernels  563 us (94%)
  local copies, waits for them, and re-layouts  18.2 us (3%)
  other arithmetic  10.8 us (2%)
    pallas_call x11, Pallas kernels, call(): pl.pallas_call(body, out_shape=tuple((jax.ShapeDtypeStruct(shape, kind) f...  563 us

profile of v3, /device:TPU:0, one launch (start us, length us, event | category | flops | bytes accessed | tf_op | source)
XLA Modules:
  0.0 593.3 jit_solution(15942967337041622543)
XLA Ops:
  0.7 1.4 slice_convert_fusion
  2.0 2.3 slice_bitcast_fusion.1
  5.8 0.9 slice_bitcast_fusion
  7.3 79.8 %shard_map.194 = (bf16[1040,1536]{1,0:T(8,128)(2,1)}, bf16[1024,1536]{1,0:T(8,128)(2,1)}, f32[128,1536]{1,0:T(8,128)}, f32[128,1536]{1,0:T(8,128)}, bf16[16,96,3...) custom-call(bf16[256,1536]{1,0:T(8,128)(2,1)} %bitcast.112, ...), custom_call_target="tpu_custom_call" | custom-call | tf_op jit(solution)/shard_map/pallas_call | solution.py:1311
  87.4 0.7 fusion.2
  90.4 54.2 %shard_map.195 = (bf16[1024,384]{1,0:T(8,128)(2,1)}, bf16[1040,384]{1,0:T(8,128)(2,1)}, bf16[1040,256]{1,0:T(8,128)(2,1)}, bf16[1024,384]{1,0:T(8,128)(2,1)}, bf...) custom-call(bf16[1040,1536]{1,0:T(8,128)(2,1)} %get-tuple-element.10, ...), custom_call_target="tpu_custom_call" | custom-call | tf_op jit(solution)/shard_map/pallas_call | solution.py:1311
  144.6 66.1 %shard_map.196 = (bf16[1040,1536]{1,0:T(8,128)(2,1)}, f32[128,1536]{1,0:T(8,128)}, f32[128,1536]{1,0:T(8,128)}, f32[8,128]{1,0:T(8,128)}, bf16[1536,384]{1,0:T(8,128)(2,1)}, /*index=5*/bf16[1536,384]{1,0:T(8,128)(2,1)}) custom-call(bf16[1024,1536]{1,0:T(8,128)(2,1)} %get-tuple-element.112.part, f32[8,1024]{1,0:T(8,128)} %get-tuple-element.113.squares, ...), custom_call_target="tpu_custom_call" | custom-call | tf_op jit(solution)/shard_map/pallas_call | solution.py:1311
  211.9 42.0 %shard_map.197 = (bf16[1024,384]{1,0:T(8,128)(2,1)}, bf16[1040,384]{1,0:T(8,128)(2,1)}, bf16[1040,256]{1,0:T(8,128)(2,1)}, bf16[1024,384]{1,0:T(8,128)(2,1)}, bf...) custom-call(bf16[1040,1536]{1,0:T(8,128)(2,1)} %get-tuple-element.11, ...), custom_call_target="tpu_custom_call" | custom-call | tf_op jit(solution)/shard_map/pallas_call | solution.py:1311
  253.8 32.4 %shard_map.198 = (bf16[256,1536]{1,0:T(8,128)(2,1)}, f32[8,1024]{1,0:T(8,128)}) custom-call(bf16[1024,1536]{1,0:T(8,128)(2,1)} %get-tuple-element.123.part, f32[8,1024]{1,0:T(8,128)} %get-tuple-element.124.squares, f32[128,1536]{1,0:T(8,128)} %get-tuple-element.125.resid, f32[128,1536]{1,0:T(8,128)} %get-tuple-element.126.cot.grad), custom_call_target="tpu_custom_call" | custom-call | tf_op jit(solution)/shard_map/pallas_call | solution.py:1311
  286.2 61.6 %shard_map.199 = (bf16[1024,384]{1,0:T(8,128)(2,1)}, bf16[1040,768]{1,0:T(8,128)(2,1)}, bf16[4,384,384]{2,1,0:T(8,128)(2,1)}, f32[8,384]{1,0:T(8,128)}, f32[8,38...) custom-call(bf16[1024,1536]{1,0:T(8,128)(2,1)} %get-tuple-element.128.refs_0_, ...), custom_call_target="tpu_custom_call" | custom-call | tf_op jit(solution)/shard_map/pallas_call | solution.py:1311
  347.8 19.3 %shard_map.200 = (bf16[1040,1536]{1,0:T(8,128)(2,1)}, bf16[1536,384]{1,0:T(8,128)(2,1)}, bf16[1536,384]{1,0:T(8,128)(2,1)}, bf16[1536,256]{1,0:T(8,128)(2,1)}, bf16[16,1536]{1,0:T(8,128)(2,1)}) custom-call(bf16[1040,768]{1,0:T(8,128)(2,1)} %get-tuple-element.142.dcat, bf16[1024,384]{1,0:T(8,128)(2,1)} %get-tuple-element.143.dz, ...), custom_call_target="tpu_custom_call" | custom-call | tf_op jit(solution)/shard_map/pallas_call | solution.py:1311
  367.2 56.1 %shard_map.201 = (bf16[1024,1536]{1,0:T(8,128)(2,1)}, f32[8,1024]{1,0:T(8,128)}, f32[128,1536]{1,0:T(8,128)}, f32[8,1536]{1,0:T(8,128)}, bf16[4,384,384]{2,1,0:T(8,128)(2,1)}, /*index=5*/bf16[4,384,384]{2,1,0:T(8,128)(2,1)}) custom-call(bf16[1040,1536]{1,0:T(8,128)(2,1)} %get-tuple-element.144.part, f32[128,1536]{1,0:T(8,128)} %get-tuple-element.126.cot.grad, ...), custom_call_target="tpu_custom_call" | custom-call | tf_op jit(solution)/shard_map/pallas_call | solution.py:1311
  423.2 53.2 %shard_map.202 = (bf16[1024,384]{1,0:T(8,128)(2,1)}, bf16[1040,768]{1,0:T(8,128)(2,1)}, bf16[4,384,384]{2,1,0:T(8,128)(2,1)}, f32[8,384]{1,0:T(8,128)}, f32[8,38...) custom-call(bf16[1024,1536]{1,0:T(8,128)(2,1)} %get-tuple-element.14, ...), custom_call_target="tpu_custom_call" | custom-call | tf_op jit(solution)/shard_map/pallas_call | solution.py:1311
  476.5 19.4 %shard_map.203 = (bf16[1040,1536]{1,0:T(8,128)(2,1)}, bf16[1536,384]{1,0:T(8,128)(2,1)}, bf16[1536,384]{1,0:T(8,128)(2,1)}, bf16[1536,256]{1,0:T(8,128)(2,1)}, bf16[16,1536]{1,0:T(8,128)(2,1)}) custom-call(bf16[1040,768]{1,0:T(8,128)(2,1)} %get-tuple-element.166.dcat, bf16[1024,384]{1,0:T(8,128)(2,1)} %get-tuple-element.167.dz, ...), custom_call_target="tpu_custom_call" | custom-call | tf_op jit(solution)/shard_map/pallas_call | solution.py:1311
  495.9 2.5 pad_maximum_fusion.bc
  498.4 0.8 slice_reduce_fusion
  501.2 0.7 slice.157
  502.6 0.7 slice.154
  504.0 78.9 %shard_map.204 = (bf16[256,1536]{1,0:T(8,128)(2,1)}, bf16[96,1536]{1,0:T(8,128)(2,1)}, bf16[96,1536]{1,0:T(8,128)(2,1)}, bf16[96,1536]{1,0:T(8,128)(2,1)}, bf16[...) custom-call(bf16[1040,1536]{1,0:T(8,128)(2,1)} %get-tuple-element.168.part, ...), custom_call_target="tpu_custom_call" | custom-call | tf_op jit(solution)/shard_map/pallas_call | solution.py:1311
  582.9 0.8 convert.26
  584.5 1.1 pad_maximum_fusion.1
  589.5 0.9 pad_maximum_fusion.2
  590.4 0.9 copy.71
  591.3 0.9 copy.72
  (114 shorter events, 14.4 us)
Async XLA Ops:
  0.6 87.5 %copy-start = (bf16[2,5,1536]{2,0,1:T(2,128)(2,1)S(1)}, bf16[2,5,1536]{2,0,1:T(2,128)(2,1)}, u32[]{:S(2)}) copy-start(bf16[2,5,1536]{2,0,1:T(2,128)(2,1)} %param.17) | copy-start | bytes 92164
  2.0 2.3 copy-start.14
  2.0 3.0 copy-start.19
  2.0 3.7 copy-start.5
  7.3 79.8 %copy-start.24 = (f32[2,3,24]{2,0,1:T(2,128)S(1)}, f32[2,3,24]{2,0,1:T(2,128)}, u32[]{:S(2)}) copy-start(f32[2,3,24]{2,0,1:T(2,128)} %param.19) | copy-start | bytes 1732
  7.3 81.7 %copy-start.18 = (bf16[2,5,256]{2,0,1:T(2,128)(2,1)S(1)}, bf16[2,5,256]{2,0,1:T(2,128)(2,1)}, u32[]{:S(2)}) copy-start(bf16[2,5,256]{2,0,1:T(2,128)(2,1)} %param.18) | copy-start | bytes 15364
  476.5 19.4 %copy-start.4 = (bf16[1536,256]{1,0:T(8,128)(2,1)S(1)}, bf16[1536,256]{1,0:T(8,128)(2,1)}, u32[]{:S(2)}) copy-start(bf16[1536,256]{1,0:T(8,128)(2,1)} %get-tuple-element.174) | copy-start | bytes 2359300
  495.9 2.6 copy-start.22
  495.9 2.6 copy-start.23
  495.9 4.0 copy-start.16
  495.9 4.0 copy-start.17
  495.9 6.0 %copy-start.20 = (f32[8,384]{1,0:T(8,128)S(1)}, f32[8,384]{1,0:T(8,128)}, u32[]{:S(2)}) copy-start(f32[8,384]{1,0:T(8,128)} %get-tuple-element.183) | copy-start | bytes 36868
  495.9 7.4 %copy-start.21 = (f32[8,384]{1,0:T(8,128)S(1)}, f32[8,384]{1,0:T(8,128)}, u32[]{:S(2)}) copy-start(f32[8,384]{1,0:T(8,128)} %get-tuple-element.180) | copy-start | bytes 36868
  504.0 80.4 %copy-start.7 = (bf16[96,1536]{1,0:T(8,128)(2,1)S(1)}, bf16[96,1536]{1,0:T(8,128)(2,1)}, u32[]{:S(2)}) copy-start(bf16[96,1536]{1,0:T(8,128)(2,1)} %get-tuple-element.191) | copy-start | bytes 884740
  504.0 80.4 %copy-start.8 = (bf16[96,1536]{1,0:T(8,128)(2,1)S(1)}, bf16[96,1536]{1,0:T(8,128)(2,1)}, u32[]{:S(2)}) copy-start(bf16[96,1536]{1,0:T(8,128)(2,1)} %get-tuple-element.190) | copy-start | bytes 884740
  582.9 1.5 copy-start.10
  582.9 1.5 copy-start.11
  584.5 1.1 copy-start.13
  584.5 1.9 copy-start.12
  585.6 3.9 copy-start.6
  585.6 3.9 copy-start.9
  586.4 4.0 copy-start.2
  589.5 1.8 copy-start.3
  590.4 2.5 copy-start.1
  (1 other events, 1.0 us)

commit v4 on v3

--- a/solution.py
+++ b/solution.py
@@ -1,4 +1,5 @@
 import functools
+import typing
 
 import jax
 import jax.numpy as jnp
@@ -79,20 +80,33 @@
     return jnp.logical_and(row == place * heads + col, col < heads).astype(BF16)
 
 
+class Columns(typing.NamedTuple):
+    x: slice
+    z: slice
+    dt: slice
+    bc: slice
+    size: int
+
+
+def columns_of(inner):
+    first = 2 * inner + 128
+    return Columns(
+        slice(0, inner), slice(inner, 2 * inner), slice(2 * inner, first), slice(first, first + 2 * STATE), first + 2 * STATE
+    )
+
+
 def project_and_convolve(
-    place, normed, wx, wz, wbc, wdt, rowp, bcp, headp,
+    place, normed, w, rowp, bcp, headp,
     z_out, xin_out, bcin_out, x_out, bc_out, dtraw_out, dt_out, s_out, decay_out,
     ext, local,
 ):
     inner = x_out.shape[1]
     spans = x_out.shape[0] // SPAN
 
-    def bc_of(rows):
-        return jnp.concatenate([dot(rows, wbc[0]), dot(rows, wbc[1])], axis=1).astype(BF16)
-
+    cols = columns_of(inner)
     edge = normed[0:EDGE]
-    edge_x = dot(edge, wx[...]).astype(BF16)
-    edge_bc = bc_of(edge)
+    edge_x = dot(edge, w[:, cols.x]).astype(BF16)
+    edge_bc = dot(edge, w[:, cols.bc]).astype(BF16)
     xin_out[0:EDGE] = edge_x
     bcin_out[0:EDGE] = edge_bc
     ext[0:EDGE, 0:inner] = edge_x.astype(F32)
@@ -108,11 +122,10 @@
         at = pl.multiple_of(q * SPAN, SPAN)
         tok = pl.ds(at, SPAN)
         after = pl.ds(pl.multiple_of(at + EDGE, EDGE), SPAN)
-        rows = normed[after, :]
-        z_out[tok, :] = dot(rows, wz[...]).astype(BF16)
-        xin = dot(rows, wx[...]).astype(BF16)
-        bcin = bc_of(rows)
-        dtraw = dot(dot(rows, wdt[...]).astype(BF16), pick).astype(BF16)
+        product = dot(normed[after, :], w[...]).astype(BF16)
+        z_out[tok, :] = product[:, cols.z]
+        xin, bcin = product[:, cols.x], product[:, cols.bc]
+        dtraw = dot(product[:, cols.dt], pick).astype(BF16)
         xin_out[after, :] = xin
         bcin_out[after, :] = bcin
         dtraw_out[tok, :] = dtraw
@@ -199,12 +212,13 @@
 
 
 def back_through_gate(
-    inner_all, dmix, wo, y_in, z, x, bc, s, decay, token_scalars, rowp, dz_out, small_out, dy_out, prior, normed_out
+    inner_all, dmix, wo, y_in, z, x, bc, s, decay, token_scalars, rowp, cat_out, wide, dy_out, prior, normed_out
 ):
     inner = x.shape[1]
     spans = x.shape[0] // SPAN
     spread = head_spread(inner)
     gain = rowp[5:6]
+    cols = columns_of(inner)
 
     def block(i, carry):
         grad_sum, gain_sum, skip_sum = carry
@@ -222,7 +236,8 @@
         normed_out[tok, :] = (scaled * gain).astype(BF16)
         gain_sum = gain_sum + jnp.sum(d_no * scaled, axis=0, keepdims=True)
         d_gated = inv * (d_no * gain) - gated * (inv * inv * inv * total_dot * (1.0 / inner_all))
-        dz_out[tok, :] = (d_gated * y * (sig * (1.0 + zf * (1.0 - sig)))).astype(BF16)
+        after = pl.ds(pl.multiple_of(q * SPAN + EDGE, EDGE), SPAN)
+        cat_out[after, cols.z] = (d_gated * y * (sig * (1.0 + zf * (1.0 - sig)))).astype(BF16)
         dy = d_gated * act
         xf = x[tok, :].astype(F32)
         skip_sum = skip_sum + jnp.sum(dy * xf, axis=0, keepdims=True)
@@ -240,9 +255,9 @@
     decay_all = decay[0, 0:1]
     for q in range(1, spans):
         decay_all = decay_all * decay[q, 0:1]
-    small_out[0:1] = gain_sum
-    small_out[1:2] = skip_sum
-    small_out[2:8] = jnp.zeros((6, inner), F32)
+    wide[...] = jnp.zeros_like(wide)
+    wide[5:6] = gain_sum
+    wide[6:7] = skip_sum
     return grad_sum, decay_all
 
 
@@ -303,7 +318,7 @@
 
 def back_through_states(
     grad, prior, decay, states, dy_in, x, bc, s_in, dt_in, dtraw, xin, bcin, rowp, bcp, headp, flow_in, sum_in,
-    dcat_out, row_out, bcrow_out, head_out,
+    place, cat_out, step_out, row_out, bcrow_out,
     dpre, dend,
 ):
     inner = x.shape[1]
@@ -323,10 +338,11 @@
     lax.fori_loop(0, spans, chain, grad)
     dpre[0:EDGE] = jnp.zeros((EDGE, width), F32)
     dpre[EDGE + spans * SPAN :] = jnp.zeros((EDGE, width), F32)
-    row_out[...] = jnp.zeros_like(row_out)
     bcrow_out[...] = jnp.zeros_like(bcrow_out)
-    head_out[...] = jnp.zeros_like(head_out)
-    dcat_out[0:EDGE, width:] = jnp.zeros((EDGE, 128), BF16)
+    cols = columns_of(inner)
+    pick = head_pick(place, inner // HEADDIM)
+    cat_out[0:EDGE, cols.z] = jnp.zeros((EDGE, inner), BF16)
+    cat_out[0:EDGE, cols.dt] = jnp.zeros((EDGE, 128), BF16)
 
     def block(q, _):
         at = pl.multiple_of(q * SPAN, SPAN)
@@ -359,9 +375,11 @@
         d_dt = sum_in[tok, :] + dsw * to_end + da * rate
         d_raw = d_dt * sigmoid(dtraw[tok, :].astype(F32) + bias)
         d_raw = jnp.where(iota((SPAN, 128), 1) < inner // HEADDIM, d_raw, 0.0)
-        head_out[0:1] += jnp.sum(da * (dt * rate), axis=0, keepdims=True)
-        head_out[1:2] += jnp.sum(d_raw, axis=0, keepdims=True)
-        dcat_out[after, width:] = d_raw.astype(BF16)
+        row_out[7:8, 0:128] += jnp.sum(da * (dt * rate), axis=0, keepdims=True)
+        row_out[8:9, 0:128] += jnp.sum(d_raw, axis=0, keepdims=True)
+        d_low = d_raw.astype(BF16)
+        step_out[tok, :] = d_low
+        cat_out[after, cols.dt] = dot(d_low, pick, NT).astype(BF16)
 
         win_x = xin[window, :].astype(F32)
         d_x = dx * silu_slope(conv_taps(win_x, rowp))
@@ -387,57 +405,55 @@
             total = term if total is None else total + term
         return total.astype(BF16)
 
-    dcat_out[0:EDGE, 0:inner] = back(dpre[0 : 2 * EDGE, 0:inner], rowp, EDGE)
-    dcat_out[0:EDGE, inner:width] = back(dpre[0 : 2 * EDGE, inner:], bcp, EDGE)
+    cat_out[0:EDGE, cols.x] = back(dpre[0 : 2 * EDGE, 0:inner], rowp, EDGE)
+    cat_out[0:EDGE, cols.bc] = back(dpre[0 : 2 * EDGE, inner:], bcp, EDGE)
 
     def conv_block(q, _):
         after = pl.ds(pl.multiple_of(q * SPAN + EDGE, EDGE), SPAN)
         window = pl.ds(pl.multiple_of(q * SPAN + EDGE, EDGE), SPAN + EDGE)
-        dcat_out[after, 0:inner] = back(dpre[window, 0:inner], rowp, SPAN)
-        dcat_out[after, inner:width] = back(dpre[window, inner:], bcp, SPAN)
+        cat_out[after, cols.x] = back(dpre[window, 0:inner], rowp, SPAN)
+        cat_out[after, cols.bc] = back(dpre[window, inner:], bcp, SPAN)
         return 0
 
     lax.fori_loop(0, spans, conv_block, 0)
 
 
-def backward_project(dcat, dz, normed, wx, wz, wbc, wdt, dn_out, gx_out, gz_out, gbc_out, gdt_out):
-    inner = dz.shape[1]
-    width = inner + 2 * STATE
-    spans = dz.shape[0] // SPAN
-    d_edge = dcat[0:EDGE]
-    pick = head_pick(lax.axis_index("p"), inner // HEADDIM)
+def project_back(cat, w, dn_out):
+    cols = columns_of((w.shape[1] - 3 * STATE) // 2)
     dn_out[0:EDGE] = (
-        dot(d_edge[:, 0:inner], wx[...], NT)
-        + dot(d_edge[:, inner : inner + STATE], wbc[0], NT)
-        + dot(d_edge[:, inner + STATE : width], wbc[1], NT)
+        dot(cat[0:EDGE, cols.x], w[:, cols.x], NT) + dot(cat[0:EDGE, cols.bc], w[:, cols.bc], NT)
     ).astype(BF16)
 
     def rows_of(q, _):
-        at = pl.multiple_of(q * SPAN, SPAN)
-        tok = pl.ds(at, SPAN)
-        after = pl.ds(pl.multiple_of(at + EDGE, EDGE), SPAN)
-        dn_out[after, :] = (
-            dot(dz[tok, :], wz[...], NT)
-            + dot(dcat[after, 0:inner], wx[...], NT)
-            + dot(dcat[after, inner : inner + STATE], wbc[0], NT)
-            + dot(dcat[after, inner + STATE : width], wbc[1], NT)
-            + dot(dot(dcat[after, width:], pick, NT).astype(BF16), wdt[...], NT)
-        ).astype(BF16)
+        after = pl.ds(pl.multiple_of(q * SPAN + EDGE, EDGE), SPAN)
+        dn_out[after, :] = dot(cat[after, :], w[...], NT).astype(BF16)
         return 0
 
-    lax.fori_loop(0, spans, rows_of, 0)
-
-    def grads_of(i, _):
-        cols = pl.ds(pl.multiple_of(i * SPAN, SPAN), SPAN)
-        part = normed[:, cols]
-        both = dot(part, dcat[:, 0:width], TN).astype(BF16)
-        gx_out[cols, :] = both[:, 0:inner]
-        gbc_out[cols, :] = both[:, inner:]
-        gdt_out[:, cols] = dot(dcat[:, width:], part, TN)[0:EDGE].astype(BF16)
-        gz_out[cols, :] = dot(part[EDGE:], dz[...], TN).astype(BF16)
+    lax.fori_loop(0, (cat.shape[0] - EDGE) // SPAN, rows_of, 0)
+
+
+def weight_gradients(cat, steps, normed, gx_out, gz_out, gbc_out, gdt_out):
+    inner = gx_out.shape[1]
+    groups, parts, shard, _ = gbc_out.shape
+    rows = parts * shard
+    cols = columns_of(inner)
+
+    def rows_of(g, _):
+        at = pl.ds(pl.multiple_of(g * rows, 128), rows) if rows % 128 == 0 else pl.ds(g * rows, rows)
+        edge, tokens = normed[0:EDGE, at], normed[EDGE:, at]
+        both = dot(tokens, cat[EDGE:, 0 : 2 * inner], TN)
+        gx_out[at, :] = (both[:, 0:inner] + dot(edge, cat[0:EDGE, cols.x], TN)).astype(BF16)
+        gz_out[at, :] = both[:, inner:].astype(BF16)
+        bc = dot(tokens, cat[EDGE:, cols.bc], TN) + dot(edge, cat[0:EDGE, cols.bc], TN)
+        gbc_out[g] = bc.reshape(parts, shard, 2 * STATE).astype(BF16)
+        gdt_out[g] = dot(steps[...], tokens, TN)[0:EDGE].astype(BF16)
         return 0
 
-    lax.fori_loop(0, normed.shape[1] // SPAN, grads_of, 0)
+    if rows % 128 == 0:
+        lax.fori_loop(0, groups, rows_of, 0)
+    else:
+        for g in range(groups):
+            rows_of(g, 0)
 
 
 HALF = 128
@@ -509,24 +525,75 @@
         self.meet()
 
 
-class Spread:
-    def __init__(self, links, own, out):
-        rows = own.shape[0]
-        there = out.at[pl.ds(pl.multiple_of(links.z * rows, EDGE), rows)]
-        self.keep = links.local(own, there)
-        self.copies = [
-            links.copy(own, there, (lax.rem(links.z + k, links.groups), links.p, links.c)) for k in range(1, links.groups)
-        ]
+class Chain:
+    def __init__(self, links, pieces):
+        z, p, c, groups = links.z, links.p, links.c, links.groups
+        self.steps, self.now = [], 0
+        for step in range(1, groups):
+            found = []
+            up, down = z - step + 1, z + step - 1
+            for piece in pieces:
+                block = piece(jnp.maximum(up, 0))
+                sending = jnp.logical_and(up >= 0, z < groups - 1)
+                found.append((sending, z - step >= 0, links.copy(block, block, (z + 1, p, c))))
+                block = piece(jnp.minimum(down, groups - 1))
+                sending = jnp.logical_and(down < groups, z > 0)
+                found.append((sending, z + step < groups, links.copy(block, block, (z - 1, p, c))))
+            self.steps.append(found)
+
+    def begin(self):
+        for sending, _, copy in self.steps[0]:
+            pl.when(sending)(copy.start)
+
+    def advance(self):
+        if self.now + 1 < len(self.steps):
+            for (_, receiving, copy), (sending, _, later) in zip(self.steps[self.now], self.steps[self.now + 1]):
+                pl.when(receiving)(copy.wait_recv)
+                pl.when(sending)(later.start)
+            self.now += 1
+
+    def complete(self):
+        while self.now + 1 < len(self.steps):
+            self.advance()
+        for _, receiving, copy in self.steps[-1]:
+            pl.when(receiving)(copy.wait_recv)
+
+    def finish(self):
+        for found in self.steps:
+            for sending, _, copy in found:
+                pl.when(sending)(copy.wait_send)
+
+
+class Swap:
+    def __init__(self, links, shard, staging, out, lanes, width):
+        self.links, self.staging, self.out, self.lanes = links, staging, out, lanes
+
+        def source(k):
+            if shard.shape[1] == width:
+                return shard
+            to = lax.bitwise_xor(links.p, jnp.int32(k))
+            return shard.at[:, pl.ds(pl.multiple_of(to * width, 128), width)]
+
+        self.copies = [links.copy(source(k), staging.at[links.p], links.at(k, 0)) for k in (3, 1, 2)]
+        self.keep = links.local(source(0), staging.at[links.p])
 
     def start(self):
-        self.keep.start()
         for copy in self.copies:
             copy.start()
 
-    def arrive(self):
+    def settle(self):
         self.keep.wait()
         for copy in self.copies:
             copy.wait_recv()
+        parts, shard, width = self.staging.shape
+        rows = parts * shard
+        first = self.links.z * rows
+        if shard % EDGE == 0:
+            for j in range(parts):
+                self.out[pl.ds(pl.multiple_of(first + j * shard, EDGE), shard), self.lanes] = self.staging[j]
+        else:
+            block = self.staging[...].astype(F32).reshape(rows, width).astype(BF16)
+            self.out[pl.ds(pl.multiple_of(first, EDGE), rows), self.lanes] = block
 
     def finish(self):
         for copy in self.copies:
@@ -727,6 +794,8 @@
 
             lax.fori_loop(0, HALF // 32, add, 0)
             self.to_peer[k].start()
+
+    def arrive(self):
         self.to_sibling[0].wait_recv()
         for copy in self.to_peer.values():
             copy.wait_recv()
@@ -809,258 +878,6 @@
     for i, column in enumerate(columns):
         wide = jnp.where(lane == i, column, wide)
     return wide.T[0:8]
-
-
-def begin_kernel(count, late, *refs):
-    resid, cot, gain = refs[:3]
-    shards, rest = refs[3 : 3 + count + late], refs[3 + count + late :]
-    normed_out, dmix_out, resid_out, cot_out = rest[:4]
-    outs = rest[4 : 4 + count + late]
-    sends, recvs = rest[4 + count + late :]
-    links = Links(sends, recvs)
-    z, p, c, groups = links.z, links.p, links.c, links.groups
-    inner = outs[0].shape[-1]
-    mine = z * GROUP + p
-
-    def source(i, k):
-        if shards[i].shape[1] == STATE:
-            return shards[i]
-        to = lax.bitwise_xor(p, jnp.int32(k))
-        return shards[i].at[:, pl.ds(pl.multiple_of(to * inner, 128), inner)]
-
-    def block(i, at):
-        return outs[i].at[c, at] if len(outs[i].shape) == 4 else outs[i].at[at]
-
-    swaps, keeps = [], []
-    for i in range(count + late):
-        target = block(i, mine if i < count else p)
-        swaps.append([links.copy(source(i, k), target, links.at(k, 0)) for k in (3, 1, 2)])
-        keeps.append(links.local(source(i, 0), target))
-    for copy in keeps:
-        copy.start()
-
-    gather = Gather(links, normed_out, EDGE)
-    other = Gather(links, dmix_out, 0)
-    edge = EdgeForward(links, gather)
-    links.greet(plane=True, groups=True, edge=1)
-    for start, size in row_chunks():
-        rows = pl.ds(pl.multiple_of(c * HALF + start, EDGE), size)
-        part = resid[rows, :].astype(F32)
-        resid_out[start : start + size] = part
-        normed_out[gather.own(start, size), :] = (part * rms_of(part) * gain[...]).astype(BF16)
-        part = cot[rows, :]
-        cot_out[start : start + size] = part.astype(F32)
-        dmix_out[other.own(start, size), :] = part
-    links.meet()
-    for group in swaps[:count]:
-        for copy in group:
-            copy.start()
-
-    def lines(step):
-        found = []
-        up, down = z - step + 1, z + step - 1
-        for i in range(count):
-            piece = block(i, pl.ds(jnp.maximum(up, 0) * GROUP, GROUP))
-            sending = jnp.logical_and(up >= 0, z < groups - 1)
-            found.append((sending, z - step >= 0, links.copy(piece, piece, (z + 1, p, c))))
-            piece = block(i, pl.ds(jnp.minimum(down, groups - 1) * GROUP, GROUP))
-            sending = jnp.logical_and(down < groups, z > 0)
-            found.append((sending, z + step < groups, links.copy(piece, piece, (z - 1, p, c))))
-        return found
-
-    steps = [lines(step) for step in range(1, groups)]
-    for i in range(count):
-        keeps[i].wait()
-        for copy in swaps[i]:
-            copy.wait_recv()
-        for can_send, _, copy in steps[0][2 * i : 2 * i + 2]:
-            pl.when(can_send)(copy.start)
-    gather.start()
-    edge.start()
-    gather.pass_on()
-    other.start()
-    for step in range(1, len(steps)):
-        for i in range(2 * count):
-            pl.when(steps[step - 1][i][1])(steps[step - 1][i][2].wait_recv)
-            pl.when(steps[step][i][0])(steps[step][i][2].start)
-        if step == 1:
-            other.pass_on()
-            for group in swaps[count:]:
-                for copy in group:
-                    copy.start()
-    share = []
-    for i in range(2 * count):
-        pl.when(steps[-1][i][1])(steps[-1][i][2].wait_recv)
-        if i % 2 and len(outs[i // 2].shape) == 4:
-            whole = outs[i // 2].at[c]
-            share.append(links.copy(whole, whole, links.at(0, 1)))
-            share[-1].start()
-    gather.finish()
-    other.finish()
-    edge.finish()
-    for i in range(count, count + late):
-        keeps[i].wait()
-        for copy in swaps[i]:
-            copy.wait_recv()
-    for group in swaps:
-        for copy in group:
-            copy.wait_send()
-    for found in steps:
-        for can_send, _, copy in found:
-            pl.when(can_send)(copy.wait_send)
-    for copy in share:
-        copy.wait()
-
-
-def forward_kernel(last, *refs):
-    normed, wx, wz, wbc, wdt, wo, rowp, bcp, headp = refs[:9]
-    more = 0 if last else 2
-    later, outs = refs[9 : 9 + more], refs[9 + more :]
-    (z, xin, bcin, x, bc, dtraw, dt, s, y, states, decay, part, squares, wo_all) = outs[:14]
-    later_out = outs[14 : 14 + more]
-    ext, local, state_low, decay_row, states_in, decays_in, sends, recvs = outs[14 + more :]
-    links = Links(sends, recvs)
-    spread = Spread(links, wo, wo_all)
-    passing = []
-    if not last:
-        passing = [Spread(links, later[0], later_out[0].at[links.c]), Spread(links, later[1], later_out[1])]
-        whole = later_out[0].at[links.c]
-        share = links.copy(whole, whole, links.at(0, 1))
-    carried = States(links, False, state_low, decay_row, states_in, decays_in)
-    links.start_barrier(sibling=not last, groups=True)
-    spread.start()
-    state_sum, decay_all = project_and_convolve(
-        links.p, normed, wx, wz, wbc, wdt, rowp, bcp, headp,
-        z, xin, bcin, x, bc, dtraw, dt, s, decay, ext, local,
-    )
-    state_low[...] = state_sum.astype(BF16)
-    decay_row[...] = jnp.broadcast_to(decay_all, decay_row.shape)
-    carried.start()
-    for other in passing:
-        other.start()
-    mix_within_spans(x, bc, s, dt, y)
-    carried.arrive()
-    state = entering_state(links.z, links.groups, states_in, decays_in, False)
-    spread.arrive()
-    mix_out(state, local, decay, x, bc, z, s, wo_all, rowp, y, states, part, squares)
-    for other in passing:
-        other.arrive()
-    if not last:
-        share.start()
-    carried.finish()
-    for other in [spread] + passing:
-        other.finish()
-    if not last:
-        share.wait()
-
-
-def backward_kernel(inner_all, done, *refs):
-    (dmix, wo, y, z, x, bc, s, dt, dtraw, xin, bcin, states, decay, token_scalars, rowp, bcp, headp) = refs[:17]
-    parts, outs = refs[17 : 17 + done], refs[17 + done :]
-    dz, dcat, go_parts, gate_small, row_small, bc_small, head_small = outs[:7]
-    delivered = outs[7 : 7 + done]
-    (
-        dy, gwo, normed_out, prior, dend, dpre, flow, sums, final, state_low, decay_row, states_in, decays_in, sends, recvs
-    ) = outs[7 + done :]
-    links = Links(sends, recvs)
-    carried = States(links, True, state_low, decay_row, states_in, decays_in)
-    collect = Collect(links, gwo, go_parts)
-    delivers = [Deliver(links, parts[i], final.at[i], delivered[i]) for i in range(done)]
-    links.greet(plane=done > 0, groups=True)
-    grad_sum, decay_all = back_through_gate(
-        inner_all, dmix, wo, y, z, x, bc, s, decay, token_scalars, rowp, dz, gate_small, dy, prior, normed_out
-    )
-    state_low[...] = grad_sum.astype(BF16)
-    decay_row[...] = jnp.broadcast_to(decay_all, decay_row.shape)
-    links.meet()
-    carried.start()
-    out_gradient(dmix, normed_out, gwo)
-    collect.start()
-    for deliver in delivers:
-        deliver.start()
-    back_within_spans(dy, x, bc, s, dt, dpre, flow, sums)
-    carried.arrive()
-    grad = entering_state(links.z, links.groups, states_in, decays_in, True)
-    back_through_states(
-        grad, prior, decay, states, dy, x, bc, s, dt, dtraw, xin, bcin, rowp, bcp, headp, flow, sums,
-        dcat, row_small, bc_small, head_small, dpre, dend,
-    )
-    carried.finish()
-    collect.arrive()
-    collect.finish()
-    for deliver in delivers:
-        deliver.finish()
-
-
-def next_layer_kernel(
-    inner_all, part, squares, resid, gain, wx, wz, normed_out, resid_out, mixed_out, inv_out, wx_out, wz_out,
-    sib, total, peer, slots, sends, recvs,
-):
-    links = Links(sends, recvs)
-    scatter = Scatter(links, part, 0, sib, total, peer)
-    small = SmallSum(links, squares, slots)
-    gather = Gather(links, normed_out, EDGE)
-    edge = EdgeForward(links, gather)
-    spreads = [Spread(links, wx, wx_out), Spread(links, wz, wz_out)]
-    links.start_barrier(plane=True, groups=True, edge=1)
-    scatter.start()
-    small.start()
-    for spread in spreads:
-        spread.start()
-    scatter.reduce()
-    inv = lax.rsqrt(small.total() * (1.0 / inner_all) + EPS)
-    inv_out[...] = inv
-    column = inv.T[:, 0:1]
-    for start, size in row_chunks():
-        at = slice(start, start + size)
-        mixed = scatter.own(start, size)
-        mixed_out[at] = mixed
-        fresh = resid[at] + column[at] * mixed
-        resid_out[at] = fresh
-        normed_out[gather.own(start, size), :] = (fresh * rms_of(fresh) * gain[...]).astype(BF16)
-    gather.start()
-    edge.start()
-    gather.pass_on()
-    scatter.finish()
-    small.finish()
-    gather.finish()
-    edge.finish()
-    for spread in spreads:
-        spread.arrive()
-        spread.finish()
-
-
-def turn_kernel(
-    inner_all, part, squares, resid, cot, block_out, scalars_out,
-    sib, total, peer, slots, sends, recvs,
-):
-    links = Links(sends, recvs)
-    scatter = Scatter(links, part, 0, sib, total, peer)
-    small = SmallSum(links, squares, slots)
-    spread = SmallGather(links, scalars_out)
-    rows = pl.ds(pl.multiple_of(links.c * HALF, HALF), HALF)
-    share = links.copy(block_out.at[rows, :], block_out.at[rows, :], links.at(0, 1))
-    links.start_barrier(plane=True)
-    scatter.start()
-    small.start()
-    scatter.reduce()
-    inv = lax.rsqrt(small.total() * (1.0 / inner_all) + EPS)
-    column = inv.T[:, 0:1]
-    dots = []
-    for start, size in row_chunks():
-        at = slice(start, start + size)
-        mixed = scatter.own(start, size)
-        dots.append(jnp.sum(cot[at] * mixed, axis=-1, keepdims=True))
-        block_out[pl.ds(pl.multiple_of(links.c * HALF + start, EDGE), size), :] = (
-            resid[at] + column[at] * mixed
-        ).astype(BF16)
-    scalars_out[:, spread.lanes] = as_tile([column, jnp.concatenate(dots)])
-    spread.start()
-    share.start()
-    scatter.finish()
-    small.finish()
-    spread.finish()
-    share.wait()
 
 
 def grad_rows(links, scatter, edge_slots, grad, resid, gain, gain_out, start, size):
@@ -1117,46 +934,6 @@
         pl.when(self.links.z > 0)(self.send.wait_send)
 
 
-def layer_below_kernel(
-    part, grad, resid, gain, mixed, inv, gx, gz, dmix_out, scalars_out, grad_out, gain_out, gx_out, gz_out,
-    sib, total, peer, edge_slots, sends, recvs,
-):
-    links = Links(sends, recvs)
-    scatter = Scatter(links, part, EDGE, sib, total, peer)
-    edge = EdgeBackward(links, part, edge_slots)
-    gather = Gather(links, dmix_out, 0)
-    spread = SmallGather(links, scalars_out)
-    edge_slots[...] = jnp.zeros_like(edge_slots)
-    collects = [Collect(links, gx, gx_out), Collect(links, gz, gz_out)]
-    links.start_barrier(plane=True, groups=True, edge=-1)
-    edge.start()
-    scatter.start()
-    for collect in collects:
-        collect.start()
-    scatter.reduce()
-    edge.receive()
-    gain_out[...] = jnp.zeros_like(gain_out)
-    dots = []
-    for start, size in row_chunks():
-        at = slice(start, start + size)
-        fresh = grad_rows(links, scatter, edge_slots, grad, resid, gain, gain_out, start, size)
-        grad_out[at] = fresh
-        low = fresh.astype(BF16)
-        dmix_out[gather.own(start, size), :] = low
-        dots.append(jnp.sum(low.astype(F32) * mixed[at], axis=-1, keepdims=True))
-    scalars_out[:, spread.lanes] = as_tile([inv[...].T[:, 0:1], jnp.concatenate(dots)])
-    gather.start()
-    spread.start()
-    gather.pass_on()
-    scatter.finish()
-    edge.finish()
-    gather.finish()
-    spread.finish()
-    for collect in collects:
-        collect.arrive()
-        collect.finish()
-
-
 class SmallSums:
     def __init__(self, links, bc, vec, dt, wide, bc_out, vec_out, dt_out, wide_out, bufs):
         self.links = links
@@ -1172,15 +949,15 @@
                 slot = 2 * k + e
                 to_p, to_c = lax.bitwise_xor(p, jnp.int32(k)), lax.bitwise_xor(c, jnp.int32(e))
                 device = links.at(k, e)
-                for layer in range(bc.shape[0]):
-                    src = bc.at[layer, :, to_p, :, pl.ds(pl.multiple_of(to_c * STATE, STATE), STATE)]
+                for layer in range(len(bc)):
+                    src = bc[layer].at[:, to_p, :, pl.ds(pl.multiple_of(to_c * STATE, STATE), STATE)]
                     self.first.append(links.copy(src, self.bc_in.at[layer, slot - 1], device))
                 self.vec_first.append(links.copy(vec.at[to_p * 2 + to_c], self.vec_in.at[slot - 1], device))
                 self.third.append(links.copy(vec_out.at[p * 2 + c], vec_out.at[p * 2 + c], device))
         for k in range(1, groups):
             to = lax.rem(z + k, groups)
             device = (to, p, c)
-            for layer in range(bc.shape[0]):
+            for layer in range(len(bc)):
                 self.second.append(links.copy(self.bc_sum.at[layer, to], self.bc_far.at[layer, k - 1], device))
             self.second.append(links.copy(self.vec_in.at[7], self.vec_far.at[k - 1], device))
             self.second.append(links.copy(dt.at[to], self.dt_far.at[k - 1], device))
@@ -1201,10 +978,10 @@
         for copy in self.vec_first + self.first:
             copy.wait_recv()
         own_lanes = pl.ds(pl.multiple_of(links.c * STATE, STATE), STATE)
-        for layer in range(self.bc.shape[0]):
+        for layer in range(len(self.bc)):
 
             def add(i, _, layer=layer):
-                total = self.bc[layer, i, links.p, :, own_lanes].astype(F32)
+                total = self.bc[layer][i, links.p, :, own_lanes].astype(F32)
                 for slot in range(2 * GROUP - 1):
                     total = total + self.bc_in[layer, slot, i].astype(F32)
                 self.bc_sum[layer, i] = total.astype(BF16)
@@ -1225,7 +1002,7 @@
             copy.wait_recv()
         far = links.groups - 1
         lanes = pl.ds(pl.multiple_of(c * STATE, STATE), STATE)
-        for layer in range(self.bc.shape[0]):
+        for layer in range(len(self.bc)):
             total = self.bc_sum[layer, z].astype(F32)
             for k in range(far):
                 total = total + self.bc_far[layer, k].astype(F32)
@@ -1250,56 +1027,357 @@
             copy.wait_send()
 
 
-def final_kernel(
-    part, grad, resid, gain, gx, gz, go_parts, bc, vec, dt, wide,
-    out, gx_out, gz_out, go_out, bc_out, vec_out, dt_out, wide_out,
-    sib, total, peer, edge_slots, gain_row, vec_own, gx_parts, gz_parts, final,
-    bc_in, bc_sum, bc_far, vec_in, vec_far, dt_far, wide_far, sends, recvs,
-):
+def weight_chain(links, w, inner):
+    rows = w.shape[0] // links.groups
+    first = columns_of(inner).bc.start
+    half = pl.ds(pl.multiple_of(first + links.c * STATE, STATE), STATE)
+
+    def at(index):
+        return pl.ds(pl.multiple_of(index * rows, EDGE), rows)
+
+    chain = Chain(links, [lambda i: w.at[at(i), 0:first], lambda i: w.at[at(i), half]])
+    return chain, links.copy(w.at[:, half], w.at[:, half], links.at(0, 1))
+
+
+def out_chain(links, wo):
+    rows = wo.shape[0] // links.groups
+    return Chain(links, [lambda i: wo.at[pl.ds(pl.multiple_of(i * rows, EDGE), rows), :]])
+
+
+def weight_swaps(links, shards, stagings, w, inner):
+    cols = columns_of(inner)
+    half = pl.ds(pl.multiple_of(cols.bc.start + links.c * STATE, STATE), STATE)
+    places = ((cols.x, inner), (cols.z, inner), (cols.dt, STATE), (half, STATE))
+    return [Swap(links, shards[i], stagings[i], w, *places[i]) for i in range(4)]
+
+
+def forward_layer(links, normed, w, wo, wo_chain, params, saved, part, squares, work):
+    rowp, bcp, headp = params
+    y, z, x, bc, s, dt, dtraw, xin, bcin, states, decay = saved
+    ext, local, state_low, decay_row, states_in, decays_in = work
+    carried = States(links, False, state_low, decay_row, states_in, decays_in)
+    state_sum, decay_all = project_and_convolve(
+        links.p, normed, w, rowp, bcp, headp, z, xin, bcin, x, bc, dtraw, dt, s, decay, ext, local
+    )
+    state_low[...] = state_sum.astype(BF16)
+    decay_row[...] = jnp.broadcast_to(decay_all, decay_row.shape)
+    carried.start()
+    wo_chain.advance()
+    mix_within_spans(x, bc, s, dt, y)
+    wo_chain.complete()
+    carried.arrive()
+    state = entering_state(links.z, links.groups, states_in, decays_in, False)
+    return carried, lambda: mix_out(state, local, decay, x, bc, z, s, wo, rowp, y, states, part, squares)
+
+
+def first_kernel(inner_all, *refs):
+    resid, cot, gain, next_gain, rowp, bcp, headp = refs[:7]
+    shards, refs = (refs[7:12], refs[12:17]), refs[17:]
+    normed, dmix, w, wo, next_w, next_wo = refs[:6]
+    saved, refs = refs[6:17], refs[17:]
+    resid_out, cot_out, mixed_out, inv_out, normed_out, fresh_out, part, squares = refs[:8]
+    stagings, refs = (refs[8:13], refs[13:18]), refs[18:]
+    work, (sib, total, peer, slots, sends, recvs) = refs[:6], refs[6:]
+    links = Links(sends, recvs)
+    z, p, c = links.z, links.p, links.c
+    inner = wo.shape[1]
+    rows = wo.shape[0] // links.groups
+
+    swaps = weight_swaps(links, shards[0], stagings[0], w, inner)
+    swap_o = Swap(links, shards[0][4], stagings[0][4], wo, slice(0, inner), inner)
+    next_swaps = weight_swaps(links, shards[1], stagings[1], next_w, inner)
+    next_o = Swap(links, shards[1][4], stagings[1][4], next_wo, slice(0, inner), inner)
+    all_swaps = swaps + [swap_o] + next_swaps + [next_o]
+    gather, other = Gather(links, normed, EDGE), Gather(links, dmix, 0)
+    edge = EdgeForward(links, gather)
+    chain, share = weight_chain(links, w, inner)
+    chain_o = out_chain(links, wo)
+    next_chain, next_share = weight_chain(links, next_w, inner)
+    scatter = Scatter(links, part, 0, sib, total, peer)
+    small = SmallSum(links, squares, slots)
+    next_gather = Gather(links, normed_out, EDGE)
+    next_edge = EdgeForward(links, next_gather)
+
+    links.greet(plane=True, groups=True, edge=1)
+    for swap in all_swaps:
+        swap.keep.start()
+    for start, size in row_chunks():
+        at = pl.ds(pl.multiple_of(c * HALF + start, EDGE), size)
+        rows_in = resid[at, :].astype(F32)
+        resid_out[start : start + size] = rows_in
+        normed[gather.own(start, size), :] = (rows_in * rms_of(rows_in) * gain[...]).astype(BF16)
+        rows_in = cot[at, :]
+        cot_out[start : start + size] = rows_in.astype(F32)
+        dmix[other.own(start, size), :] = rows_in
+    links.meet()
+    for swap in swaps:
+        swap.start()
+    for swap in swaps:
+        swap.settle()
+    chain.begin()
+    gather.start()
+    edge.start()
+    swap_o.start()
+    gather.pass_on()
+    for swap in next_swaps + [next_o]:
+        swap.start()
+    other.start()
+    chain.advance()
+    other.pass_on()
+    chain.advance()
+    gather.finish()
+    edge.finish()
+    for swap in [swap_o] + next_swaps + [next_o]:
+        swap.settle()
+    chain.complete()
+    share.start()
+    chain_o.begin()
+    share.wait()
+    carried, mix = forward_layer(
+        links, normed, w, wo, chain_o, (rowp, bcp, headp), saved, part, squares, work
+    )
+    next_chain.begin()
+    mix()
+    scatter.start()
+    small.start()
+    scatter.reduce()
+    next_chain.advance()
+    scatter.arrive()
+    inv = lax.rsqrt(small.total() * (1.0 / inner_all) + EPS)
+    inv_out[...] = inv
+    column = inv.T[:, 0:1]
+    for start, size in row_chunks():
+        at = slice(start, start + size)
+        mixed = scatter.own(start, size)
+        mixed_out[at] = mixed
+        fresh = resid_out[at] + column[at] * mixed
+        fresh_out[at] = fresh
+        normed_out[next_gather.own(start, size), :] = (fresh * rms_of(fresh) * next_gain[...]).astype(BF16)
+    next_gather.start()
+    next_edge.start()
+    next_chain.advance()
+    next_gather.pass_on()
+    next_chain.complete()
+    next_share.start()
+    other.finish()
+    scatter.finish()
+    small.finish()
+    next_gather.finish()
+    next_edge.finish()
+    carried.finish()
+    for swap in all_swaps:
+        swap.finish()
+    for one in (chain, chain_o, next_chain):
+        one.finish()
+    next_share.wait()
+
+
+def second_kernel(inner_all, *refs):
+    normed, w, wo_own, rowp, bcp, headp, resid, cot = refs[:8]
+    wo, refs = refs[8], refs[9:]
+    saved, refs = refs[:11], refs[11:]
+    block_out, scalars_out, part, squares = refs[:4]
+    work, (sib, total, peer, slots, sends, recvs) = refs[4:10], refs[10:]
+    links = Links(sends, recvs)
+    rows = wo_own.shape[0]
+    keep = links.local(wo_own, wo.at[pl.ds(pl.multiple_of(links.z * rows, EDGE), rows), :])
+    chain_o = out_chain(links, wo)
+    scatter = Scatter(links, part, 0, sib, total, peer)
+    small = SmallSum(links, squares, slots)
+    spread = SmallGather(links, scalars_out)
+    at = pl.ds(pl.multiple_of(links.c * HALF, HALF), HALF)
+    share = links.copy(block_out.at[at, :], block_out.at[at, :], links.at(0, 1))
+    keep.start()
+    links.greet(plane=True, groups=True)
+    keep.wait()
+    links.meet()
+    chain_o.begin()
+    carried, mix = forward_layer(
+        links, normed, w, wo, chain_o, (rowp, bcp, headp), saved, part, squares, work
+    )
+    mix()
+    scatter.start()
+    small.start()
+    scatter.reduce()
+    scatter.arrive()
+    inv = lax.rsqrt(small.total() * (1.0 / inner_all) + EPS)
+    column = inv.T[:, 0:1]
+    dots = []
+    for start, size in row_chunks():
+        at = slice(start, start + size)
+        mixed = scatter.own(start, size)
+        dots.append(jnp.sum(cot[at] * mixed, axis=-1, keepdims=True))
+        block_out[pl.ds(pl.multiple_of(links.c * HALF + start, EDGE), size), :] = (
+            resid[at] + column[at] * mixed
+        ).astype(BF16)
+    scalars_out[:, spread.lanes] = as_tile([column, jnp.concatenate(dots)])
+    spread.start()
+    share.start()
+    scatter.finish()
+    small.finish()
+    carried.finish()
+    chain_o.finish()
+    spread.finish()
+    share.wait()
+
+
+def backward_layer(links, inner_all, dmix, scalars, wo, params, saved, outs, work, delivers):
+    rowp, bcp, headp = params
+    y, z, x, bc, s, dt, dtraw, xin, bcin, states, decay = saved
+    cat, steps, go_parts, wide, bc_rows = outs
+    dy, gwo, normed_out, prior, dend, dpre, flow, sums, state_low, decay_row, states_in, decays_in = work
+    carried = States(links, True, state_low, decay_row, states_in, decays_in)
+    collect = Collect(links, gwo, go_parts)
+    grad_sum, decay_all = back_through_gate(
+        inner_all, dmix, wo, y, z, x, bc, s, decay, scalars, rowp, cat, wide, dy, prior, normed_out
+    )
+    state_low[...] = grad_sum.astype(BF16)
+    decay_row[...] = jnp.broadcast_to(decay_all, decay_row.shape)
+    links.meet()
+    carried.start()
+    for deliver in delivers:
+        deliver.start()
+    out_gradient(dmix, normed_out, gwo)
+    back_within_spans(dy, x, bc, s, dt, dpre, flow, sums)
+    carried.arrive()
+    collect.start()
+    grad = entering_state(links.z, links.groups, states_in, decays_in, True)
+    back_through_states(
+        grad, prior, decay, states, dy, x, bc, s, dt, dtraw, xin, bcin, rowp, bcp, headp, flow, sums,
+        links.p, cat, steps, wide, bc_rows, dpre, dend,
+    )
+    return carried, collect
+
+
+def put_vector(vec, row, values):
+    for i in range(values.shape[0]):
+        for j in range(values.shape[1] // 128):
+            vec[row // 8, row % 8 : row % 8 + 1, :] = values[i : i + 1, j * 128 : j * 128 + 128]
+            row += 1
+
+
+def third_kernel(inner_all, *refs):
+    dmix, scalars, wo, w, normed, rowp, bcp, headp, grad, resid, gain, mixed, inv = refs[:13]
+    saved, refs = refs[13:24], refs[24:]
+    dmix_out, scalars_out, grad_out, go_parts, gx_parts, gz_parts, gbc, gdt, wide, vec = refs[:10]
+    work, refs = refs[10:22], refs[22:]
+    cat, steps, bc_rows, part, gx, gz, gain_row, sib, total, peer, edge_slots, sends, recvs = refs
     links = Links(sends, recvs)
     scatter = Scatter(links, part, EDGE, sib, total, peer)
     edge = EdgeBackward(links, part, edge_slots)
-    rows = pl.ds(pl.multiple_of(links.c * HALF, HALF), HALF)
-    share = links.copy(out.at[rows, :], out.at[rows, :], links.at(0, 1))
+    gather = Gather(links, dmix_out, 0)
+    spread = SmallGather(links, scalars_out)
     collects = [Collect(links, gx, gx_parts), Collect(links, gz, gz_parts)]
-    small = SmallSums(
-        links, bc, vec_own, dt, wide, bc_out, vec_out, dt_out, wide_out,
-        (bc_in, bc_sum, bc_far, vec_in, vec_far, dt_far, wide_far),
+    edge_slots[...] = jnp.zeros_like(edge_slots)
+    links.greet(plane=True, groups=True, edge=-1)
+    carried, collect = backward_layer(
+        links, inner_all, dmix, scalars, wo, (rowp, bcp, headp), saved, (cat, steps, go_parts, wide, bc_rows), work, []
     )
-    delivers = [
-        Deliver(links, parts, final.at[i], place)
+    project_back(cat, w, part)
+    edge.start()
+    scatter.start()
+    scatter.reduce()
+    weight_gradients(cat, steps, normed, gx, gz, gbc, gdt)
+    for one in collects:
+        one.start()
+    scatter.arrive()
+    edge.receive()
+    gain_row[...] = jnp.zeros_like(gain_row)
+    dots = []
+    for start, size in row_chunks():
+        at = slice(start, start + size)
+        fresh = grad_rows(links, scatter, edge_slots, grad, resid, gain, gain_row, start, size)
+        grad_out[at] = fresh
+        low = fresh.astype(BF16)
+        dmix_out[gather.own(start, size), :] = low
+        dots.append(jnp.sum(low.astype(F32) * mixed[at], axis=-1, keepdims=True))
+    scalars_out[:, spread.lanes] = as_tile([inv[...].T[:, 0:1], jnp.concatenate(dots)])
+    gather.start()
+    spread.start()
+    vec[...] = jnp.zeros_like(vec)
+    model = gain_row.shape[1]
+    put_vector(vec, model // 128, gain_row[0:1])
+    put_vector(vec, 2 * (model // 128) + 2 * (CONV + 1), bc_rows[0 : CONV + 1])
+    gather.pass_on()
+    scatter.finish()
+    edge.finish()
+    gather.finish()
+    spread.finish()
+    carried.finish()
+    for one in [collect] + collects:
+        one.arrive()
+        one.finish()
+
+
+def fourth_kernel(inner_all, *refs):
+    dmix, scalars, wo, w, normed, rowp, bcp, headp, grad, resid, gain = refs[:11]
+    saved, refs = refs[11:22], refs[22:]
+    above, refs = refs[:3], refs[3:]
+    above_bc, above_dt, above_wide, above_vec = refs[:4]
+    out, gx_out, gz_out, go_out = refs[4:8]
+    above_out, refs = refs[8:11], refs[11:]
+    bc_out, vec_out, dt_out, wide_out = refs[:4]
+    work, refs = refs[4:16], refs[16:]
+    cat, steps, bc_rows, part, gx, gz, gain_row, sib, total, peer, edge_slots = refs[:11]
+    go_parts, gx_parts, gz_parts, final, gbc, gdt, wide, vec, steps_all, wide_all = refs[11:21]
+    bufs, (sends, recvs) = refs[21:28], refs[28:]
+    links = Links(sends, recvs)
+    scatter = Scatter(links, part, EDGE, sib, total, peer)
+    edge = EdgeBackward(links, part, edge_slots)
+    at = pl.ds(pl.multiple_of(links.c * HALF, HALF), HALF)
+    share = links.copy(out.at[at, :], out.at[at, :], links.at(0, 1))
+    collects = [Collect(links, gx, gx_parts), Collect(links, gz, gz_parts)]
+    delivers = [Deliver(links, above[i], final.at[i], above_out[i]) for i in range(3)]
+    own_delivers = [
+        Deliver(links, parts, final.at[3 + i], place)
         for i, (parts, place) in enumerate(((go_parts, go_out), (gx_parts, gx_out), (gz_parts, gz_out)))
     ]
+    small = SmallSums(
+        links, (gbc, above_bc), vec, steps_all, wide_all, bc_out, vec_out, dt_out, wide_out, bufs
+    )
     edge_slots[...] = jnp.zeros_like(edge_slots)
-    links.start_barrier(plane=True, groups=True, edge=-1)
+    links.greet(plane=True, groups=True, edge=-1)
+    carried, collect = backward_layer(
+        links, inner_all, dmix, scalars, wo, (rowp, bcp, headp), saved, (cat, steps, go_parts, wide, bc_rows), work,
+        delivers,
+    )
+    weight_gradients(cat, steps, normed, gx, gz, gbc, gdt)
+    for one in collects:
+        one.start()
+    project_back(cat, w, part)
     edge.start()
     scatter.start()
-    for collect in collects:
-        collect.start()
     scatter.reduce()
+    steps_all[:, 0:EDGE, :] = gdt[...]
+    steps_all[:, EDGE:, :] = above_dt[...]
+    wide_all[0:16] = wide[...]
+    wide_all[16:32] = above_wide[...]
+    scatter.arrive()
     edge.receive()
     gain_row[...] = jnp.zeros_like(gain_row)
     for start, size in row_chunks():
         fresh = grad_rows(links, scatter, edge_slots, grad, resid, gain, gain_row, start, size)
         out[pl.ds(pl.multiple_of(links.c * HALF + start, EDGE), size), :] = fresh.astype(BF16)
     share.start()
-    vec_own[...] = vec[...]
-    for r in range(gain_row.shape[1] // 128):
-        vec_own[r // 8, r % 8 : r % 8 + 1, :] = gain_row[0:1, r * 128 : r * 128 + 128]
+    vec[...] = above_vec[...]
+    put_vector(vec, 0, gain_row[0:1])
+    put_vector(vec, 2 * (gain_row.shape[1] // 128), bc_rows[0 : CONV + 1])
     small.round_one()
-    delivers[0].start()
+    collect.arrive()
+    own_delivers[0].start()
     small.round_two()
     small.round_three()
     for i in range(2):
         collects[i].arrive()
-        delivers[i + 1].start()
+        own_delivers[i + 1].start()
     small.finish()
     scatter.finish()
     edge.finish()
     share.wait()
-    for collect in collects:
-        collect.finish()
-    for deliver in delivers:
+    carried.finish()
+    for one in [collect] + collects:
+        one.finish()
+    for deliver in delivers + own_delivers:
         deliver.finish()
 
 
@@ -1323,7 +1401,7 @@
 def on_device(resid_in, cotangent, norm_gain, w_zx, w_dt, w_bc, conv_x, conv_bc, head_params, gated_gain, w_out):
     layers, model = norm_gain.shape
     groups = lax.axis_size("z")
-    place, core = lax.axis_index("p"), lax.axis_index("head")
+    level, place, core = lax.axis_index("z"), lax.axis_index("p"), lax.axis_index("head")
     shard = w_dt.shape[1]
     inner_core = conv_x.shape[2]
     inner = inner_core // GROUP
@@ -1333,7 +1411,6 @@
     length = resid_in.shape[1]
     tokens = GROUP * length
     spans = tokens // SPAN
-    sources = groups * GROUP
     rows = GROUP * shard
 
     def my_part(array, size):
@@ -1355,7 +1432,7 @@
     def shards_of(layer):
         half = lax.dynamic_slice_in_dim(w_bc[layer], core * STATE, STATE, 1)
         steps = jnp.pad(w_dt[layer], ((0, 0), (0, STATE - heads_core)))
-        return w_zx[layer, 1], w_zx[layer, 0], half, steps, w_out[layer].T
+        return w_zx[layer, 1], w_zx[layer, 0], steps, half, w_out[layer].T
 
     half_scratch = [
         ((GROUP, HALF, model), BF16),
@@ -1365,175 +1442,117 @@
     slots = ((2 * GROUP - 1, 8, HALF), F32)
     edges = ((2 * GROUP, EDGE, model), BF16)
     own_rows = ((HALF, model), F32)
-
-    shards = [shards_of(layer) for layer in range(layers)]
-    early = list(shards[0][:4])
-    late = [shards[0][4]] + [piece for layer in range(1, layers) for piece in shards[layer]]
-    wide_piece, thin_piece = (sources, shard, inner), (sources, shard, STATE)
-    late_shapes = [(GROUP, shard, a.shape[1] // (GROUP if a.shape[1] > STATE else 1)) for a in late]
-    gathered = call(
-        functools.partial(begin_kernel, len(early), len(late)),
-        [
-            ((tokens + EDGE, model), BF16),
-            ((tokens, model), BF16),
-            own_rows,
-            own_rows,
-            (wide_piece, BF16),
-            (wide_piece, BF16),
-            ((2, *thin_piece), BF16),
-            (thin_piece, BF16),
-        ]
-        + [(shape, BF16) for shape in late_shapes],
-        resid_in[0], cotangent[0], gains[0], *early, *late,
-        collective=0, copies=30 + 4 * (len(early) + len(late)) + 2 * len(early) * (groups - 1),
-    )
-    normed, last_dmix, resid, grad, wx, wz, wbc, wdt = gathered[:8]
-    wx, wz, wdt = [a.reshape(model, -1) for a in (wx, wz, wdt)]
-    wbc = wbc.reshape(2, model, STATE)
-    own = [a.reshape(rows, -1) for a in gathered[8:]]
-    own = [(None, None, None, None, own[0])] + [own[1 + 5 * i : 6 + 5 * i] for i in range(layers - 1)]
-    whole = ((model, inner), BF16)
-
+    all_rows, edged_rows = ((tokens, model), BF16), ((tokens + EDGE, model), BF16)
+    columns = columns_of(inner).size
+    w_shape, wo_shape = ((model, columns), BF16), ((model, inner), BF16)
+    tile = ((8, HALF), F32)
+    scalars = ((8, tokens), F32)
+    state_shape = ((spans, STATE, inner), F32)
     state_scratch = [
         ((STATE, inner), BF16),
         ((8, inner), F32),
         ((groups, STATE, inner), BF16),
         ((groups, 8, inner), F32),
     ]
-    saved, weights = [], []
-    for layer in range(layers):
-        rowp, bcp, headp = row_all[layer], bc_all[layer], head_all[layer]
-        last = layer == layers - 1
-        passing = [] if last else [own[layer + 1][2], own[layer + 1][3]]
-        results = call(
-            functools.partial(forward_kernel, last),
-            [
-                ((tokens, inner), BF16),
-                ((tokens + EDGE, inner), BF16),
-                ((tokens + EDGE, 2 * STATE), BF16),
-                ((tokens, inner), BF16),
-                ((tokens, 2 * STATE), BF16),
-                ((tokens, 128), BF16),
-                ((tokens, 128), F32),
-                ((tokens, 128), F32),
-                ((tokens, inner), F32),
-                ((spans, STATE, inner), F32),
-                ((spans, 8, inner), F32),
-                ((tokens, model), BF16),
-                ((8, tokens), F32),
-                whole,
-            ]
-            + ([] if last else [((2, model, STATE), BF16), ((model, STATE), BF16)]),
-            normed, wx, wz, wbc, wdt, own[layer][4], rowp, bcp, headp, *passing,
-            scratch=[((tokens + EDGE, inner + 2 * STATE), F32), ((spans, STATE, inner), F32)] + state_scratch,
-            collective=2 if last else 1, copies=8 + 5 * groups,
-        )
-        z, xin, bcin, x, bc, dtraw, dt, s, y, states, decay, part, squares, wo = results[:14]
-        weights.append((wx, wz, wbc, wdt, wo))
-        kept = (resid, normed, (y, z, x, bc, s, dt, dtraw, xin, bcin, states, decay))
-        if not last:
-            wbc, wdt = results[14:]
-            normed, resid, mixed, inv, wx, wz = call(
-                functools.partial(next_layer_kernel, inner_all),
-                [((tokens + EDGE, model), BF16), own_rows, own_rows, ((8, HALF), F32), whole, whole],
-                part, squares, resid, gains[layer + 1], own[layer + 1][0], own[layer + 1][1],
-                scratch=half_scratch + [slots], collective=3, copies=40 + 2 * groups,
-            )
-            saved.append((*kept, (mixed, inv)))
-        else:
-            block_out, token_scalars = call(
-                functools.partial(turn_kernel, inner_all),
-                [((length, model), BF16), ((8, tokens), F32)],
-                part, squares, resid, grad,
-                scratch=half_scratch + [slots], collective=4, copies=40,
-            )
-            saved.append((*kept, None))
-
-    d_mix, ready, delivered = last_dmix, [], {}
-    kinds, gain_rows = [None] * layers, [None] * layers
+    saved_shapes = [
+        ((tokens, inner), F32),
+        ((tokens, inner), BF16),
+        ((tokens, inner), BF16),
+        ((tokens, 2 * STATE), BF16),
+        ((tokens, 128), F32),
+        ((tokens, 128), F32),
+        ((tokens, 128), BF16),
+        ((tokens + EDGE, inner), BF16),
+        ((tokens + EDGE, 2 * STATE), BF16),
+        state_shape,
+        ((spans, 8, inner), F32),
+    ]
+    forward_scratch = [((tokens + EDGE, inner + 2 * STATE), F32), state_shape] + state_scratch
+
+    def params(layer):
+        return row_all[layer], bc_all[layer], head_all[layer]
+
+    stagings = [((GROUP, shard, width), BF16) for width in (inner, inner, STATE, STATE, inner)]
+    results = call(
+        functools.partial(first_kernel, inner_all),
+        [edged_rows, all_rows, w_shape, wo_shape, w_shape, wo_shape]
+        + saved_shapes
+        + [own_rows, own_rows, own_rows, tile, edged_rows, own_rows],
+        resid_in[0], cotangent[0], gains[0], gains[1], *params(0), *shards_of(0), *shards_of(1),
+        scratch=[all_rows, scalars] + stagings + stagings + forward_scratch + half_scratch + [slots],
+        collective=0, copies=160 + 10 * (groups - 1) + 2 * groups,
+    )
+    normed0, d_mix, w0, wo0, w1, wo1 = results[:6]
+    saved0 = results[6:17]
+    resid0, grad, mixed, inv, normed1, resid1 = results[17:]
+    wo_own = lax.dynamic_slice_in_dim(wo1, level * rows, rows, 0)
+    results = call(
+        functools.partial(second_kernel, inner_all),
+        [wo_shape] + saved_shapes + [((length, model), BF16), scalars],
+        normed1, w1, wo_own, *params(1), resid1, grad,
+        scratch=[all_rows, scalars] + forward_scratch + half_scratch + [slots],
+        collective=1, copies=60 + 4 * groups,
+    )
+    wo1, saved1, (block_out, token_scalars) = results[0], results[1:12], results[12:]
+
     grad_parts = ((groups, rows, inner), BF16)
-    for layer in reversed(range(layers)):
-        wx, wz, wbc, wdt, wo = weights[layer]
-        rowp, bcp, headp = row_all[layer], bc_all[layer], head_all[layer]
-        resid, normed, kept, _ = saved[layer]
-        results = call(
-            functools.partial(backward_kernel, inner_all, len(ready)),
-            [
-                ((tokens, inner), BF16),
-                ((tokens + EDGE, inner + 2 * STATE + 128), BF16),
-                grad_parts,
-                ((8, inner), F32),
-                ((8, inner), F32),
-                ((8, 2 * STATE), F32),
-                ((8, 128), F32),
-            ]
-            + [((shard, inner_core), BF16)] * len(ready),
-            d_mix, wo, *kept, token_scalars, rowp, bcp, headp, *ready,
-            scratch=[
-                ((tokens, inner), BF16),
-                whole,
-                ((tokens, inner), BF16),
-                ((spans, STATE, inner), F32),
-                ((spans, STATE, inner), F32),
-                ((tokens + 2 * EDGE, inner + 2 * STATE), F32),
-                ((tokens, 128), F32),
-                ((tokens, 128), F32),
-                ((3, GROUP, shard, inner), BF16),
-            ]
-            + state_scratch,
-            collective=5 if ready else 6, copies=20 + 3 * groups,
-        )
-        dz, dcat, go_parts, gate_small, row_small, bc_small, head_small = results[:7]
-        if ready:
-            delivered[layer + 1] = results[7:]
-        part, gx, gz, gbc, gdt = call(
-            backward_project,
-            [((tokens + EDGE, model), BF16), whole, whole, ((model, 2 * STATE), BF16), ((EDGE, model), BF16)],
-            dcat, dz, normed, wx, wz, wbc, wdt,
-        )
-        tall = jnp.pad(head_small[:2], ((0, 0), (0, inner - 128)))
-        wide = jnp.concatenate([row_small[: CONV + 1], gate_small[:2], tall])
-        kinds[layer] = (gbc, gdt, jnp.pad(wide, ((0, 7), (0, 0))), bc_small[: CONV + 1])
-        if layer > 0:
-            d_mix, token_scalars, grad, gain_rows[layer], gx_parts, gz_parts = call(
-                layer_below_kernel,
-                [((tokens, model), BF16), ((8, tokens), F32), own_rows, ((8, model), F32), grad_parts, grad_parts],
-                part, grad, resid, gains[layer], *saved[layer - 1][3], gx, gz,
-                scratch=half_scratch + [edges], collective=7, copies=60 + 2 * groups,
-            )
-            ready = [gx_parts, gz_parts, go_parts]
-
-    vec = jnp.concatenate(
-        [jnp.zeros((model,), F32)]
-        + [gain_rows[layer][0] for layer in range(1, layers)]
-        + [kinds[layer][3].reshape(-1) for layer in range(layers)]
+    back_scratch = [
+        ((tokens, inner), BF16),
+        wo_shape,
+        ((tokens, inner), BF16),
+        state_shape,
+        state_shape,
+        ((tokens + 2 * EDGE, inner + 2 * STATE), F32),
+        ((tokens, 128), F32),
+        ((tokens, 128), F32),
+    ] + state_scratch
+    more_scratch = [
+        ((tokens + EDGE, columns), BF16),
+        ((tokens, 128), BF16),
+        ((8, 2 * STATE), F32),
+        edged_rows,
+        wo_shape,
+        wo_shape,
+        ((8, model), F32),
+    ]
+    bc_grad = ((groups, GROUP, shard, 2 * STATE), BF16)
+    dt_grad = ((groups, EDGE, rows), BF16)
+    wide_grad = ((16, inner), F32)
+    vec_shape = ((2 * GROUP, 8, 128), F32)
+    d_mix, token_scalars, grad, go_parts, gx_parts, gz_parts, gbc, gdt, wide, vec = call(
+        functools.partial(third_kernel, inner_all),
+        [all_rows, scalars, own_rows, grad_parts, grad_parts, grad_parts, bc_grad, dt_grad, wide_grad, vec_shape],
+        d_mix, token_scalars, wo1, w1, normed1, *params(1), grad, resid1, gains[1], mixed, inv, *saved1,
+        scratch=back_scratch + more_scratch + half_scratch + [edges],
+        collective=2, copies=60 + 6 * groups,
     )
-    vec = jnp.pad(vec, (0, 2 * GROUP * 1024 - vec.shape[0])).reshape(2 * GROUP, 8, 128)
-    bc_grads = jnp.stack([kinds[layer][0].reshape(groups, GROUP, shard, 2 * STATE) for layer in range(layers)])
-    dt_grads = jnp.concatenate([kinds[layer][1] for layer in range(layers)])
-    dt_grads = jnp.swapaxes(dt_grads.reshape(layers * EDGE, groups, rows), 0, 1)
-    wide = jnp.concatenate([kinds[layer][2] for layer in range(layers)])
-    wide_shape, dt_shape, far = wide.shape, dt_grads.shape[1:], groups - 1
-    grad_input, gx, gz, go, g_bc, vec, g_dt, wide = call(
-        final_kernel,
-        [
-            ((length, model), BF16),
-            ((shard, inner_core), BF16),
-            ((shard, inner_core), BF16),
-            ((shard, inner_core), BF16),
+    far = groups - 1
+    rows_shape = ((shard, inner_core), BF16)
+    dt_shape, wide_shape = (layers * EDGE, rows), (layers * 16, inner)
+    grad_input, gx0, gz0, go0, gx1, gz1, go1, g_bc, vec, g_dt, wide = call(
+        functools.partial(fourth_kernel, inner_all),
+        [((length, model), BF16)]
+        + [rows_shape] * 6
+        + [
             ((layers, shard, 2 * STATE), BF16),
-            (vec.shape, F32),
+            vec_shape,
             ((GROUP, *dt_shape), BF16),
             ((GROUP, *wide_shape), F32),
         ],
-        part, grad, resid, gains[0], gx, gz, go_parts, bc_grads, vec, dt_grads, wide,
-        scratch=half_scratch + [
+        d_mix, token_scalars, wo0, w0, normed0, *params(0), grad, resid0, gains[0], *saved0,
+        gx_parts, gz_parts, go_parts, gbc, gdt, wide, vec,
+        scratch=back_scratch + more_scratch + half_scratch + [
             edges,
-            ((8, model), F32),
-            (vec.shape, F32),
             grad_parts,
             grad_parts,
-            ((3, GROUP, shard, inner), BF16),
+            grad_parts,
+            ((6, GROUP, shard, inner), BF16),
+            bc_grad,
+            dt_grad,
+            wide_grad,
+            vec_shape,
+            ((groups, *dt_shape), BF16),
+            (wide_shape, F32),
             ((layers, 2 * GROUP - 1, groups, shard, STATE), BF16),
             ((layers, groups, shard, STATE), BF16),
             ((layers, far, shard, STATE), BF16),
@@ -1542,9 +1561,9 @@
             ((far, *dt_shape), BF16),
             ((far, *wide_shape), F32),
         ],
-        collective=8, copies=100 + 8 * groups,
+        collective=3, copies=120 + 12 * groups,
     )
-    delivered[0] = (gx, gz, go)
+    delivered = ((gx0, gz0, go0), (gx1, gz1, go1))
     vec = vec.reshape(-1)
     grad_gain = vec[: layers * model].reshape(layers, model)
     grad_conv_bc = vec[layers * model :][: layers * (CONV + 1) * 2 * STATE].reshape(layers, CONV + 1, 2 * STATE)

time: 602 us -> 525 us (0.87); the launches traced: 593 us -> 524 us
  Pallas kernels: 563 us -> 495 us
    pallas_call x11 -> x4, Pallas kernels: 563 us -> 495 us  [call(): pl.pallas_call(body, out_shape=tuple((jax.ShapeDtypeStruct(shape, kind) f...]
where the time goes in v4:
time: 525 us; the launch traced here: 524 us
  Pallas kernels  495 us (94%)
  local copies, waits for them, and re-layouts  21.3 us (4%)
  other arithmetic  6.95 us (1%)
    pallas_call x4, Pallas kernels, call(): pl.pallas_call(body, out_shape=tuple((jax.ShapeDtypeStruct(shape, kind) f...  495 us

profile of v4, /device:TPU:0, one launch (start us, length us, event | category | flops | bytes accessed | tf_op | source)
XLA Modules:
  0.0 524.1 jit_solution(15488706232327391747)
XLA Ops:
  0.8 0.9 dynamic-slice_bitcast_fusion.2
  1.6 0.8 constant_dynamic-slice_fusion.4
  3.1 0.7 fusion.1
  4.7 0.8 fusion.5
  6.7 1.4 slice_convert_fusion
  8.0 0.7 fusion.4
  8.8 0.7 maximum_maximum_fusion.1
  10.9 0.8 fusion.3
  12.3 0.9 slice_bitcast_fusion
  13.2 1.0 slice_bitcast_fusion.1
  14.2 172.9 %shard_map.194 = (bf16[1040,1536]{1,0:T(8,128)(2,1)}, bf16[1024,1536]{1,0:T(8,128)(2,1)}, bf16[1536,1152]{1,0:T(8,128)(2,1)}, bf16[1536,384]{1,0:T(8,128)(2,1)},...) custom-call(bf16[256,1536]{1,0:T(8,128)(2,1)} %bitcast.79, ...), custom_call_target="tpu_custom_call" | custom-call | tf_op jit(solution)/shard_map/pallas_call | solution.py:1389
  187.1 1.7 constant_dynamic-slice_fusion.3.refs_2_
  188.8 70.8 %shard_map.195 = (bf16[1536,384]{1,0:T(8,128)(2,1)}, f32[1024,384]{1,0:T(8,128)}, bf16[1024,384]{1,0:T(8,128)(2,1)}, bf16[1024,384]{1,0:T(8,128)(2,1)}, bf16[102...) custom-call(bf16[1040,1536]{1,0:T(8,128)(2,1)} %get-tuple-element.69, ...), custom_call_target="tpu_custom_call" | custom-call | tf_op jit(solution)/shard_map/pallas_call | solution.py:1389
  259.6 107.1 %shard_map.196 = (bf16[1024,1536]{1,0:T(8,128)(2,1)}, f32[8,1024]{1,0:T(8,128)}, f32[128,1536]{1,0:T(8,128)}, bf16[4,384,384]{2,1,0:T(8,128)(2,1)}, bf16[4,384,3...) custom-call(bf16[1024,1536]{1,0:T(8,128)(2,1)} %get-tuple-element.75, ...), custom_call_target="tpu_custom_call" | custom-call | tf_op jit(solution)/shard_map/pallas_call | solution.py:1389
  366.7 144.2 %shard_map.197 = (bf16[256,1536]{1,0:T(8,128)(2,1)}, bf16[96,1536]{1,0:T(8,128)(2,1)}, bf16[96,1536]{1,0:T(8,128)(2,1)}, bf16[96,1536]{1,0:T(8,128)(2,1)}, bf16[...) custom-call(bf16[1024,1536]{1,0:T(8,128)(2,1)} %get-tuple-element.91, ...), custom_call_target="tpu_custom_call" | custom-call | tf_op jit(solution)/shard_map/pallas_call | solution.py:1389
  510.9 0.9 slice.140
  511.9 0.8 convert.26
  513.9 1.0 reshape.55
  515.6 1.1 copy.39
  519.2 1.1 pad_maximum_fusion
  520.3 0.9 pad_maximum_fusion.1
  521.6 0.9 copy.67
  522.5 0.9 copy.68
  523.5 0.6 copy.69
  (67 shorter events, 9.8 us)
Async XLA Ops:
  0.6 4.0 copy-start
  0.7 11.7 %copy-start.4 = (bf16[2,1536,96]{1,2,0:T(8,128)(2,1)S(1)}, bf16[2,1536,96]{1,2,0:T(8,128)(2,1)}, u32[]{:S(2)}) copy-start(bf16[2,1536,96]{1,2,0:T(8,128)(2,1)} %param.21) | copy-start | bytes 1769476
  0.7 12.5 %copy-start.1 = (bf16[2,2,96,1536]{3,2,1,0:T(8,128)(2,1)S(1)}, bf16[2,2,96,1536]{3,2,1,0:T(8,128)(2,1)}, u32[]{:S(2)}) copy-start(bf16[2,2,96,1536]{3,2,1,0:T(8,128)(2,1)} %param.14) | copy-start | bytes 3538948
  510.9 8.1 %copy-start.9 = (bf16[96,1536]{1,0:T(8,128)(2,1)S(1)}, bf16[96,1536]{1,0:T(8,128)(2,1)}, u32[]{:S(2)}) copy-start(bf16[96,1536]{1,0:T(8,128)(2,1)} %get-tuple-element.119) | copy-start | bytes 884740
  510.9 8.1 %copy-start.10 = (bf16[96,1536]{1,0:T(8,128)(2,1)S(1)}, bf16[96,1536]{1,0:T(8,128)(2,1)}, u32[]{:S(2)}) copy-start(bf16[96,1536]{1,0:T(8,128)(2,1)} %get-tuple-element.118) | copy-start | bytes 884740
  515.6 3.4 copy-start.7
  515.6 3.4 copy-start.8
  519.2 1.1 copy-start.5
  519.2 1.1 copy-start.6
  520.3 1.3 copy-start.2
  520.3 2.2 copy-start.3
  522.5 1.0 copy-start.11

commit v5 on v4

--- a/solution.py
+++ b/solution.py
@@ -1,4 +1,5 @@
 import functools
+import types
 import typing
 
 import jax
@@ -98,7 +99,7 @@
 def project_and_convolve(
     place, normed, w, rowp, bcp, headp,
     z_out, xin_out, bcin_out, x_out, bc_out, dtraw_out, dt_out, s_out, decay_out,
-    ext, local,
+    ext, local, at_block,
 ):
     inner = x_out.shape[1]
     spans = x_out.shape[0] // SPAN
@@ -122,6 +123,7 @@
         at = pl.multiple_of(q * SPAN, SPAN)
         tok = pl.ds(at, SPAN)
         after = pl.ds(pl.multiple_of(at + EDGE, EDGE), SPAN)
+        at_block(q)
         product = dot(normed[after, :], w[...]).astype(BF16)
         z_out[tok, :] = product[:, cols.z]
         xin, bcin = product[:, cols.x], product[:, cols.bc]
@@ -189,26 +191,24 @@
     return state
 
 
-def mix_out(state, local, decay, x, bc, z, s, wo, rowp, y_out, states_out, part_out, sq_out):
+def chain_states(state, local, decay, states_out):
+    def block(q, state):
+        states_out[q] = state
+        return decay[q, 0:1] * state + local[q]
+
+    lax.fori_loop(0, local.shape[0], block, state)
+
+
+def mix_out(q, states, x, bc, z, s, wo, rowp, y_out, part_out, sq_out):
     inner = x.shape[1]
-    spread = head_spread(inner)
-    gain, skip = rowp[5:6], rowp[6:7]
-    ones = jnp.ones((8, inner), F32)
-
-    def block(q, state):
-        tok = pl.ds(pl.multiple_of(q * SPAN, SPAN), SPAN)
-        states_out[q] = state
-        c = bc[tok, STATE:]
-        carried = dot_split(jnp.exp(s[tok, :]), spread) * dot(c, state.astype(BF16))
-        y = y_out[tok, :] + carried + skip * x[tok, :].astype(F32)
-        y_out[tok, :] = y
-        zf = z[tok, :].astype(F32)
-        gated = y * (zf * sigmoid(zf))
-        sq_out[:, tok] = dot_exact(ones, gated * gated, NT)
-        part_out[tok, :] = dot((gated * gain).astype(BF16), wo[...], NT).astype(BF16)
-        return decay[q, 0:1] * state + local[q]
-
-    lax.fori_loop(0, x.shape[0] // SPAN, block, state)
+    tok = pl.ds(pl.multiple_of(q * SPAN, SPAN), SPAN)
+    carried = dot_split(jnp.exp(s[tok, :]), head_spread(inner)) * dot(bc[tok, STATE:], states[q].astype(BF16))
+    y = y_out[tok, :] + carried + rowp[6:7] * x[tok, :].astype(F32)
+    y_out[tok, :] = y
+    zf = z[tok, :].astype(F32)
+    gated = y * (zf * sigmoid(zf))
+    sq_out[:, tok] = dot_exact(jnp.ones((8, inner), F32), gated * gated, NT)
+    part_out[tok, :] = dot((gated * rowp[5:6]).astype(BF16), wo[...], NT).astype(BF16)
 
 
 def back_through_gate(
@@ -332,8 +332,9 @@
 
     def chain(i, grad):
         q = spans - 1 - i
+        before = prior[q] + decay[q, 0:1] * grad
         dend[q] = grad
-        return prior[q] + decay[q, 0:1] * grad
+        return before
 
     lax.fori_loop(0, spans, chain, grad)
     dpre[0:EDGE] = jnp.zeros((EDGE, width), F32)
@@ -418,42 +419,62 @@
     lax.fori_loop(0, spans, conv_block, 0)
 
 
-def project_back(cat, w, dn_out):
+def project_back_edge(cat, w, dn_out):
     cols = columns_of((w.shape[1] - 3 * STATE) // 2)
     dn_out[0:EDGE] = (
         dot(cat[0:EDGE, cols.x], w[:, cols.x], NT) + dot(cat[0:EDGE, cols.bc], w[:, cols.bc], NT)
     ).astype(BF16)
 
-    def rows_of(q, _):
-        after = pl.ds(pl.multiple_of(q * SPAN + EDGE, EDGE), SPAN)
-        dn_out[after, :] = dot(cat[after, :], w[...], NT).astype(BF16)
+
+def project_back(q, cat, w, dn_out):
+    after = pl.ds(pl.multiple_of(q * SPAN + EDGE, EDGE), SPAN)
+    dn_out[after, :] = dot(cat[after, :], w[...], NT).astype(BF16)
+
+
+def for_row_blocks(grad, body):
+    groups, rows = grad
+
+    def one(g, _):
+        body(pl.ds(pl.multiple_of(g * rows, 128), rows) if rows % 128 == 0 else pl.ds(g * rows, rows), g)
         return 0
 
-    lax.fori_loop(0, (cat.shape[0] - EDGE) // SPAN, rows_of, 0)
-
-
-def weight_gradients(cat, steps, normed, gx_out, gz_out, gbc_out, gdt_out):
-    inner = gx_out.shape[1]
+    if rows % 128 == 0:
+        lax.fori_loop(0, groups, one, 0)
+    else:
+        for g in range(groups):
+            one(g, 0)
+
+
+def x_gradient(cat, normed, gx_out):
+    cols = columns_of(gx_out.shape[1])
+
+    def body(at, _):
+        total = dot(normed[EDGE:, at], cat[EDGE:, cols.x], TN) + dot(normed[0:EDGE, at], cat[0:EDGE, cols.x], TN)
+        gx_out[at, :] = total.astype(BF16)
+
+    for_row_blocks((normed.shape[1] // SPAN, SPAN), body)
+
+
+def z_gradient(cat, normed, gz_out):
+    cols = columns_of(gz_out.shape[1])
+
+    def body(at, _):
+        gz_out[at, :] = dot(normed[EDGE:, at], cat[EDGE:, cols.z], TN).astype(BF16)
+
+    for_row_blocks((normed.shape[1] // SPAN, SPAN), body)
+
+
+def small_gradients(cat, steps, normed, gbc_out, gdt_out):
     groups, parts, shard, _ = gbc_out.shape
-    rows = parts * shard
-    cols = columns_of(inner)
-
-    def rows_of(g, _):
-        at = pl.ds(pl.multiple_of(g * rows, 128), rows) if rows % 128 == 0 else pl.ds(g * rows, rows)
+    cols = columns_of((cat.shape[1] - 3 * STATE) // 2)
+
+    def body(at, g):
         edge, tokens = normed[0:EDGE, at], normed[EDGE:, at]
-        both = dot(tokens, cat[EDGE:, 0 : 2 * inner], TN)
-        gx_out[at, :] = (both[:, 0:inner] + dot(edge, cat[0:EDGE, cols.x], TN)).astype(BF16)
-        gz_out[at, :] = both[:, inner:].astype(BF16)
         bc = dot(tokens, cat[EDGE:, cols.bc], TN) + dot(edge, cat[0:EDGE, cols.bc], TN)
         gbc_out[g] = bc.reshape(parts, shard, 2 * STATE).astype(BF16)
         gdt_out[g] = dot(steps[...], tokens, TN)[0:EDGE].astype(BF16)
-        return 0
-
-    if rows % 128 == 0:
-        lax.fori_loop(0, groups, rows_of, 0)
-    else:
-        for g in range(groups):
-            rows_of(g, 0)
+
+    for_row_blocks((groups, parts * shard), body)
 
 
 HALF = 128
@@ -778,25 +799,21 @@
         row = self.base + lax.bitwise_xor(self.links.p, jnp.int32(k)) * (2 * HALF) + c * HALF + start
         return pl.ds(pl.multiple_of(row, EDGE), size)
 
-    def start(self):
-        for copy in self.to_sibling.values():
-            copy.start()
-
-    def reduce(self):
-        for k in (3, 1, 2):
-            self.to_sibling[k].wait_recv()
-
-            def add(i, _, k=k):
-                at = pl.ds(pl.multiple_of(i * 32, 32), 32)
-                mine = self.part[self.rows(k, self.links.c, i * 32, 32), :].astype(F32)
-                self.total[k - 1, at, :] = (mine + self.sib[k, at, :].astype(F32)).astype(BF16)
-                return 0
-
-            lax.fori_loop(0, HALF // 32, add, 0)
-            self.to_peer[k].start()
+    def pass_on(self, k):
+        self.to_sibling[k].wait_recv()
+        if k == 0:
+            return
+
+        def add(i, _):
+            at = pl.ds(pl.multiple_of(i * 32, 32), 32)
+            mine = self.part[self.rows(k, self.links.c, i * 32, 32), :].astype(F32)
+            self.total[k - 1, at, :] = (mine + self.sib[k, at, :].astype(F32)).astype(BF16)
+            return 0
+
+        lax.fori_loop(0, HALF // 32, add, 0)
+        self.to_peer[k].start()
 
     def arrive(self):
-        self.to_sibling[0].wait_recv()
         for copy in self.to_peer.values():
             copy.wait_recv()
 
@@ -934,109 +951,190 @@
         pl.when(self.links.z > 0)(self.send.wait_send)
 
 
-class SmallSums:
-    def __init__(self, links, bc, vec, dt, wide, bc_out, vec_out, dt_out, wide_out, bufs):
-        self.links = links
-        self.bc, self.vec, self.dt, self.wide = bc, vec, dt, wide
-        self.bc_out, self.vec_out, self.dt_out, self.wide_out = bc_out, vec_out, dt_out, wide_out
-        self.bc_in, self.bc_sum, self.bc_far, self.vec_in, self.vec_far, self.dt_far, self.wide_far = bufs
+class BcSum:
+    def __init__(self, links, bc, out, bufs):
+        self.links, self.bc, self.out = links, bc, out
+        self.sib, self.chip, self.peer, self.total, self.far = bufs
+        p, c, groups = links.p, links.c, links.groups
+        self.own = pl.ds(pl.multiple_of(c * STATE, STATE), STATE)
+        other = pl.ds(pl.multiple_of((1 - c) * STATE, STATE), STATE)
+        self.first = [links.copy(bc.at[:, :, :, other], self.sib, links.at(0, 1))]
+        self.second = [
+            links.copy(self.chip.at[:, lax.bitwise_xor(p, jnp.int32(k))], self.peer.at[k - 1], links.at(k, 0))
+            for k in (3, 1, 2)
+        ]
+        self.third = []
+        for k in range(1, groups):
+            to = lax.rem(links.z + k, groups)
+            self.third.append(links.copy(self.total.at[to], self.far.at[k - 1], (to, p, c)))
+        self.fourth = [links.copy(out.at[:, self.own], out.at[:, self.own], links.at(0, 1))]
+
+    @staticmethod
+    def begin(copies):
+        for copy in copies:
+            copy.start()
+
+    @staticmethod
+    def arrive(copies):
+        for copy in copies:
+            copy.wait_recv()
+
+    def cores(self):
+        self.begin(self.first)
+
+    def plane(self):
+        self.arrive(self.first)
+
+        def add(i, _):
+            for q in range(GROUP):
+                mine = self.bc[i, q, :, self.own].astype(F32)
+                self.chip[i, q] = (mine + self.sib[i, q].astype(F32)).astype(BF16)
+            return 0
+
+        lax.fori_loop(0, self.links.groups, add, 0)
+        self.begin(self.second)
+
+    def groups(self):
+        self.arrive(self.second)
+
+        def add(i, _):
+            total = self.chip[i, self.links.p].astype(F32)
+            for k in range(GROUP - 1):
+                total = total + self.peer[k, i].astype(F32)
+            self.total[i] = total.astype(BF16)
+            return 0
+
+        lax.fori_loop(0, self.links.groups, add, 0)
+        self.begin(self.third)
+
+    def share(self):
+        self.arrive(self.third)
+        total = self.total[self.links.z].astype(F32)
+        for k in range(self.links.groups - 1):
+            total = total + self.far[k].astype(F32)
+        self.out[:, self.own] = total.astype(BF16)
+        self.begin(self.fourth)
+
+    def finish(self):
+        self.arrive(self.fourth)
+        for copy in self.first + self.second + self.third + self.fourth:
+            copy.wait_send()
+
+
+class LaidOut:
+    def __init__(self, links, dt, wide, dt_out, wide_out, dt_far, wide_far):
+        self.links, self.refs = links, (dt, wide, dt_out, wide_out, dt_far, wide_far)
         z, p, c, groups = links.z, links.p, links.c, links.groups
-        self.first, self.vec_first, self.second, self.third = [], [], [], []
+        self.first, self.second = [], []
+        for k in range(1, groups):
+            to = lax.rem(z + k, groups)
+            self.first.append(links.copy(dt.at[to], dt_far.at[k - 1], (to, p, c)))
+            self.first.append(links.copy(wide, wide_far.at[k - 1], (to, p, c)))
+        for k in range(1, GROUP):
+            self.second.append(links.copy(dt_out.at[p], dt_out.at[p], links.at(k, 0)))
+            self.second.append(links.copy(wide_out.at[p], wide_out.at[p], links.at(k, 0)))
+
+    def groups(self):
+        BcSum.begin(self.first)
+
+    def plane(self):
+        BcSum.arrive(self.first)
+        dt, wide, dt_out, wide_out, dt_far, wide_far = self.refs
+        dt_total, wide_total = dt[self.links.z].astype(F32), wide[...]
+        for k in range(self.links.groups - 1):
+            dt_total = dt_total + dt_far[k].astype(F32)
+            wide_total = wide_total + wide_far[k]
+        dt_out[self.links.p] = dt_total.astype(BF16)
+        wide_out[self.links.p] = wide_total
+        BcSum.begin(self.second)
+
+    def finish(self):
+        BcSum.arrive(self.second)
+        for copy in self.first + self.second:
+            copy.wait_send()
+
+
+class VecSum:
+    def __init__(self, links, vec, out, near, far):
+        self.links, self.refs = links, (vec, out, near, far)
+        z, p, c, groups = links.z, links.p, links.c, links.groups
+        self.first, self.second, self.third = [], [], []
         for k in range(GROUP):
             for e in range(2):
-                if not (k or e):
-                    continue
-                slot = 2 * k + e
-                to_p, to_c = lax.bitwise_xor(p, jnp.int32(k)), lax.bitwise_xor(c, jnp.int32(e))
-                device = links.at(k, e)
-                for layer in range(len(bc)):
-                    src = bc[layer].at[:, to_p, :, pl.ds(pl.multiple_of(to_c * STATE, STATE), STATE)]
-                    self.first.append(links.copy(src, self.bc_in.at[layer, slot - 1], device))
-                self.vec_first.append(links.copy(vec.at[to_p * 2 + to_c], self.vec_in.at[slot - 1], device))
-                self.third.append(links.copy(vec_out.at[p * 2 + c], vec_out.at[p * 2 + c], device))
+                if k or e:
+                    to = lax.bitwise_xor(p, jnp.int32(k)) * 2 + lax.bitwise_xor(c, jnp.int32(e))
+                    self.first.append(links.copy(vec.at[to], near.at[2 * k + e - 1], links.at(k, e)))
+                    self.third.append(links.copy(out.at[p * 2 + c], out.at[p * 2 + c], links.at(k, e)))
         for k in range(1, groups):
-            to = lax.rem(z + k, groups)
-            device = (to, p, c)
-            for layer in range(len(bc)):
-                self.second.append(links.copy(self.bc_sum.at[layer, to], self.bc_far.at[layer, k - 1], device))
-            self.second.append(links.copy(self.vec_in.at[7], self.vec_far.at[k - 1], device))
-            self.second.append(links.copy(dt.at[to], self.dt_far.at[k - 1], device))
-            self.second.append(links.copy(wide, self.wide_far.at[k - 1], device))
-        for k in range(1, GROUP):
-            device = links.at(k, 0)
-            self.third.append(links.copy(dt_out.at[p], dt_out.at[p], device))
-            self.third.append(links.copy(wide_out.at[p], wide_out.at[p], device))
-        lanes = pl.ds(pl.multiple_of(c * STATE, STATE), STATE)
-        self.third.append(links.copy(bc_out.at[:, :, lanes], bc_out.at[:, :, lanes], links.at(0, 1)))
-
-    def round_one(self):
-        for copy in self.vec_first + self.first:
-            copy.start()
-
-    def round_two(self):
-        links = self.links
-        for copy in self.vec_first + self.first:
-            copy.wait_recv()
-        own_lanes = pl.ds(pl.multiple_of(links.c * STATE, STATE), STATE)
-        for layer in range(len(self.bc)):
-
-            def add(i, _, layer=layer):
-                total = self.bc[layer][i, links.p, :, own_lanes].astype(F32)
-                for slot in range(2 * GROUP - 1):
-                    total = total + self.bc_in[layer, slot, i].astype(F32)
-                self.bc_sum[layer, i] = total.astype(BF16)
-                return 0
-
-            lax.fori_loop(0, links.groups, add, 0)
-        total = self.vec[links.p * 2 + links.c]
+            self.second.append(links.copy(near.at[7], far.at[k - 1], (lax.rem(z + k, groups), p, c)))
+
+    def plane(self):
+        BcSum.begin(self.first)
+
+    def groups(self):
+        BcSum.arrive(self.first)
+        vec, _, near, _ = self.refs
+        total = vec[self.links.p * 2 + self.links.c]
         for slot in range(2 * GROUP - 1):
-            total = total + self.vec_in[slot]
-        self.vec_in[7] = total
-        for copy in self.second:
-            copy.start()
-
-    def round_three(self):
-        links = self.links
-        z, p, c = links.z, links.p, links.c
-        for copy in self.second:
-            copy.wait_recv()
-        far = links.groups - 1
-        lanes = pl.ds(pl.multiple_of(c * STATE, STATE), STATE)
-        for layer in range(len(self.bc)):
-            total = self.bc_sum[layer, z].astype(F32)
-            for k in range(far):
-                total = total + self.bc_far[layer, k].astype(F32)
-            self.bc_out[layer, :, lanes] = total.astype(BF16)
-        total = self.vec_in[7]
-        dt_total = self.dt[z].astype(F32)
-        wide_total = self.wide[...]
-        for k in range(far):
-            total = total + self.vec_far[k]
-            dt_total = dt_total + self.dt_far[k].astype(F32)
-            wide_total = wide_total + self.wide_far[k]
-        self.vec_out[p * 2 + c] = total
-        self.dt_out[p] = dt_total.astype(BF16)
-        self.wide_out[p] = wide_total
-        for copy in self.third:
-            copy.start()
+            total = total + near[slot]
+        near[7] = total
+        BcSum.begin(self.second)
+
+    def back(self):
+        BcSum.arrive(self.second)
+        _, out, near, far = self.refs
+        total = near[7]
+        for k in range(self.links.groups - 1):
+            total = total + far[k]
+        out[self.links.p * 2 + self.links.c] = total
+        BcSum.begin(self.third)
 
     def finish(self):
-        for copy in self.third:
-            copy.wait_recv()
-        for copy in self.vec_first + self.first + self.second + self.third:
+        BcSum.arrive(self.third)
+        for copy in self.first + self.second + self.third:
             copy.wait_send()
+
+
+class Refs:
+    def __init__(self, refs, twins, sems):
+        self.__dict__.update(refs)
+        self.twins = {id(near): (far, near, sems.at[i]) for i, (far, near) in enumerate(twins)}
+        self.waits = []
+
+    def fetch(self, *refs):
+        for ref in refs:
+            far, near, sem = self.twins[id(ref)]
+            pltpu.make_async_copy(far, near, sem).start()
+
+    def need(self, *refs):
+        for ref in refs:
+            pltpu.make_async_copy(*self.twins[id(ref)]).wait()
+
+    def flush(self, *refs):
+        for ref in refs:
+            far, near, sem = self.twins[id(ref)]
+            self.waits.append(pltpu.make_async_copy(near, far, sem))
+            self.waits[-1].start()
+
+    def done(self):
+        for copy in self.waits:
+            copy.wait()
 
 
 def weight_chain(links, w, inner):
     rows = w.shape[0] // links.groups
-    first = columns_of(inner).bc.start
-    half = pl.ds(pl.multiple_of(first + links.c * STATE, STATE), STATE)
+    cols = columns_of(inner)
+    half = pl.ds(pl.multiple_of(cols.bc.start + links.c * STATE, STATE), STATE)
 
     def at(index):
         return pl.ds(pl.multiple_of(index * rows, EDGE), rows)
 
-    chain = Chain(links, [lambda i: w.at[at(i), 0:first], lambda i: w.at[at(i), half]])
-    return chain, links.copy(w.at[:, half], w.at[:, half], links.at(0, 1))
+    pieces = [
+        lambda i: w.at[at(i), cols.x],
+        lambda i: w.at[at(i), cols.z.start : cols.dt.stop],
+        lambda i: w.at[at(i), half],
+    ]
+    return Chain(links, pieces), links.copy(w.at[:, half], w.at[:, half], links.at(0, 1))
 
 
 def out_chain(links, wo):
@@ -1044,58 +1142,62 @@
     return Chain(links, [lambda i: wo.at[pl.ds(pl.multiple_of(i * rows, EDGE), rows), :]])
 
 
-def weight_swaps(links, shards, stagings, w, inner):
+def weight_swaps(links, shards, stagings, w, wo, inner):
     cols = columns_of(inner)
     half = pl.ds(pl.multiple_of(cols.bc.start + links.c * STATE, STATE), STATE)
     places = ((cols.x, inner), (cols.z, inner), (cols.dt, STATE), (half, STATE))
-    return [Swap(links, shards[i], stagings[i], w, *places[i]) for i in range(4)]
-
-
-def forward_layer(links, normed, w, wo, wo_chain, params, saved, part, squares, work):
-    rowp, bcp, headp = params
-    y, z, x, bc, s, dt, dtraw, xin, bcin, states, decay = saved
-    ext, local, state_low, decay_row, states_in, decays_in = work
-    carried = States(links, False, state_low, decay_row, states_in, decays_in)
+    swaps = [Swap(links, shards[i], stagings[i], w, *places[i]) for i in range(4)]
+    return swaps, Swap(links, shards[4], stagings[4], wo, slice(0, inner), inner)
+
+
+def scatter_blocks(scatter, compute):
+    before = None
+    for k in (3, 1, 2, 0):
+        compute(lax.bitwise_xor(scatter.links.p, jnp.int32(k)))
+        scatter.to_sibling[k].start()
+        if before is not None:
+            scatter.pass_on(before)
+        before = k
+
+
+def forward_layer(links, r, normed, w, wo, wo_chain, scatter, meanwhile):
+    carried = States(links, False, r.state_low, r.decay_row, r.states_in, r.decays_in)
     state_sum, decay_all = project_and_convolve(
-        links.p, normed, w, rowp, bcp, headp, z, xin, bcin, x, bc, dtraw, dt, s, decay, ext, local
+        links.p, normed, w, r.rowp, r.bcp, r.headp, r.z, r.xin, r.bcin, r.x, r.bc, r.dtraw, r.dt, r.s, r.decay, r.ext, r.local,
+        lambda q: pl.when(q == 3)(wo_chain.advance),
     )
-    state_low[...] = state_sum.astype(BF16)
-    decay_row[...] = jnp.broadcast_to(decay_all, decay_row.shape)
+    r.state_low[...] = state_sum.astype(BF16)
+    r.decay_row[...] = jnp.broadcast_to(decay_all, r.decay_row.shape)
     carried.start()
+    r.flush(r.z, r.xin, r.bcin, r.x, r.bc, r.dtraw, r.dt, r.s, r.decay)
     wo_chain.advance()
-    mix_within_spans(x, bc, s, dt, y)
+    mix_within_spans(r.x, r.bc, r.s, r.dt, r.y)
     wo_chain.complete()
+    meanwhile()
     carried.arrive()
-    state = entering_state(links.z, links.groups, states_in, decays_in, False)
-    return carried, lambda: mix_out(state, local, decay, x, bc, z, s, wo, rowp, y, states, part, squares)
-
-
-def first_kernel(inner_all, *refs):
-    resid, cot, gain, next_gain, rowp, bcp, headp = refs[:7]
-    shards, refs = (refs[7:12], refs[12:17]), refs[17:]
-    normed, dmix, w, wo, next_w, next_wo = refs[:6]
-    saved, refs = refs[6:17], refs[17:]
-    resid_out, cot_out, mixed_out, inv_out, normed_out, fresh_out, part, squares = refs[:8]
-    stagings, refs = (refs[8:13], refs[13:18]), refs[18:]
-    work, (sib, total, peer, slots, sends, recvs) = refs[:6], refs[6:]
-    links = Links(sends, recvs)
-    z, p, c = links.z, links.p, links.c
-    inner = wo.shape[1]
-    rows = wo.shape[0] // links.groups
-
-    swaps = weight_swaps(links, shards[0], stagings[0], w, inner)
-    swap_o = Swap(links, shards[0][4], stagings[0][4], wo, slice(0, inner), inner)
-    next_swaps = weight_swaps(links, shards[1], stagings[1], next_w, inner)
-    next_o = Swap(links, shards[1][4], stagings[1][4], next_wo, slice(0, inner), inner)
+    chain_states(entering_state(links.z, links.groups, r.states_in, r.decays_in, False), r.local, r.decay, r.states)
+    scatter_blocks(
+        scatter, lambda q: mix_out(q, r.states, r.x, r.bc, r.z, r.s, wo, r.rowp, r.y, r.part, r.squares)
+    )
+    r.flush(r.y, r.states)
+    return carried
+
+
+def first_kernel(inner_all, r):
+    links = Links(r.sends, r.recvs)
+    c = links.c
+    inner = r.wo.shape[1]
+    swaps, swap_o = weight_swaps(links, r.shards[0], r.stagings[0], r.w, r.wo, inner)
+    next_swaps, next_o = weight_swaps(links, r.shards[1], r.stagings[1], r.next_w, r.next_wo, inner)
     all_swaps = swaps + [swap_o] + next_swaps + [next_o]
-    gather, other = Gather(links, normed, EDGE), Gather(links, dmix, 0)
+    gather, other = Gather(links, r.normed, EDGE), Gather(links, r.dmix, 0)
     edge = EdgeForward(links, gather)
-    chain, share = weight_chain(links, w, inner)
-    chain_o = out_chain(links, wo)
-    next_chain, next_share = weight_chain(links, next_w, inner)
-    scatter = Scatter(links, part, 0, sib, total, peer)
-    small = SmallSum(links, squares, slots)
-    next_gather = Gather(links, normed_out, EDGE)
+    chain, share = weight_chain(links, r.w, inner)
+    chain_o = out_chain(links, r.wo)
+    next_chain, next_share = weight_chain(links, r.next_w, inner)
+    scatter = Scatter(links, r.part, 0, r.sib, r.total, r.peer)
+    small = SmallSum(links, r.squares, r.slots)
+    next_gather = Gather(links, r.next_normed, EDGE)
     next_edge = EdgeForward(links, next_gather)
 
     links.greet(plane=True, groups=True, edge=1)
@@ -1103,12 +1205,12 @@
         swap.keep.start()
     for start, size in row_chunks():
         at = pl.ds(pl.multiple_of(c * HALF + start, EDGE), size)
-        rows_in = resid[at, :].astype(F32)
-        resid_out[start : start + size] = rows_in
-        normed[gather.own(start, size), :] = (rows_in * rms_of(rows_in) * gain[...]).astype(BF16)
-        rows_in = cot[at, :]
-        cot_out[start : start + size] = rows_in.astype(F32)
-        dmix[other.own(start, size), :] = rows_in
+        rows_in = r.resid[at, :].astype(F32)
+        r.resid_out[start : start + size] = rows_in
+        r.normed[gather.own(start, size), :] = (rows_in * rms_of(rows_in) * r.gain[...]).astype(BF16)
+        rows_in = r.cot[at, :]
+        r.cot_out[start : start + size] = rows_in.astype(F32)
+        r.dmix[other.own(start, size), :] = rows_in
     links.meet()
     for swap in swaps:
         swap.start()
@@ -1118,48 +1220,52 @@
     gather.start()
     edge.start()
     swap_o.start()
+    chain.advance()
     gather.pass_on()
     for swap in next_swaps + [next_o]:
         swap.start()
-    other.start()
     chain.advance()
-    other.pass_on()
-    chain.advance()
+    swap_o.settle()
     gather.finish()
     edge.finish()
-    for swap in [swap_o] + next_swaps + [next_o]:
-        swap.settle()
     chain.complete()
     share.start()
     chain_o.begin()
+    other.start()
+    r.flush(r.normed)
     share.wait()
-    carried, mix = forward_layer(
-        links, normed, w, wo, chain_o, (rowp, bcp, headp), saved, part, squares, work
-    )
-    next_chain.begin()
-    mix()
-    scatter.start()
+    r.flush(r.w)
+
+    def meanwhile():
+        for swap in next_swaps + [next_o]:
+            swap.settle()
+        next_chain.begin()
+        other.pass_on()
+        r.flush(r.wo)
+
+    carried = forward_layer(links, r, r.normed, r.w, r.wo, chain_o, scatter, meanwhile)
     small.start()
-    scatter.reduce()
     next_chain.advance()
+    scatter.pass_on(0)
     scatter.arrive()
     inv = lax.rsqrt(small.total() * (1.0 / inner_all) + EPS)
-    inv_out[...] = inv
+    r.inv_out[...] = inv
     column = inv.T[:, 0:1]
     for start, size in row_chunks():
         at = slice(start, start + size)
         mixed = scatter.own(start, size)
-        mixed_out[at] = mixed
-        fresh = resid_out[at] + column[at] * mixed
-        fresh_out[at] = fresh
-        normed_out[next_gather.own(start, size), :] = (fresh * rms_of(fresh) * next_gain[...]).astype(BF16)
+        r.mixed_out[at] = mixed
+        fresh = r.resid_out[at] + column[at] * mixed
+        r.fresh_out[at] = fresh
+        r.next_normed[next_gather.own(start, size), :] = (fresh * rms_of(fresh) * r.next_gain[...]).astype(BF16)
     next_gather.start()
     next_edge.start()
+    other.finish()
+    r.flush(r.dmix)
     next_chain.advance()
     next_gather.pass_on()
     next_chain.complete()
     next_share.start()
-    other.finish()
     scatter.finish()
     small.finish()
     next_gather.finish()
@@ -1170,35 +1276,27 @@
     for one in (chain, chain_o, next_chain):
         one.finish()
     next_share.wait()
-
-
-def second_kernel(inner_all, *refs):
-    normed, w, wo_own, rowp, bcp, headp, resid, cot = refs[:8]
-    wo, refs = refs[8], refs[9:]
-    saved, refs = refs[:11], refs[11:]
-    block_out, scalars_out, part, squares = refs[:4]
-    work, (sib, total, peer, slots, sends, recvs) = refs[4:10], refs[10:]
-    links = Links(sends, recvs)
-    rows = wo_own.shape[0]
-    keep = links.local(wo_own, wo.at[pl.ds(pl.multiple_of(links.z * rows, EDGE), rows), :])
-    chain_o = out_chain(links, wo)
-    scatter = Scatter(links, part, 0, sib, total, peer)
-    small = SmallSum(links, squares, slots)
-    spread = SmallGather(links, scalars_out)
+    r.done()
+
+
+def second_kernel(inner_all, r):
+    links = Links(r.sends, r.recvs)
+    rows = r.wo_own.shape[0]
+    keep = links.local(r.wo_own, r.wo.at[pl.ds(pl.multiple_of(links.z * rows, EDGE), rows), :])
+    chain_o = out_chain(links, r.wo)
+    scatter = Scatter(links, r.part, 0, r.sib, r.total, r.peer)
+    small = SmallSum(links, r.squares, r.slots)
+    spread = SmallGather(links, r.scalars_out)
     at = pl.ds(pl.multiple_of(links.c * HALF, HALF), HALF)
-    share = links.copy(block_out.at[at, :], block_out.at[at, :], links.at(0, 1))
+    share = links.copy(r.block_out.at[at, :], r.block_out.at[at, :], links.at(0, 1))
     keep.start()
     links.greet(plane=True, groups=True)
     keep.wait()
     links.meet()
     chain_o.begin()
-    carried, mix = forward_layer(
-        links, normed, w, wo, chain_o, (rowp, bcp, headp), saved, part, squares, work
-    )
-    mix()
-    scatter.start()
+    carried = forward_layer(links, r, r.normed, r.w, r.wo, chain_o, scatter, lambda: r.flush(r.wo))
     small.start()
-    scatter.reduce()
+    scatter.pass_on(0)
     scatter.arrive()
     inv = lax.rsqrt(small.total() * (1.0 / inner_all) + EPS)
     column = inv.T[:, 0:1]
@@ -1206,11 +1304,11 @@
     for start, size in row_chunks():
         at = slice(start, start + size)
         mixed = scatter.own(start, size)
-        dots.append(jnp.sum(cot[at] * mixed, axis=-1, keepdims=True))
-        block_out[pl.ds(pl.multiple_of(links.c * HALF + start, EDGE), size), :] = (
-            resid[at] + column[at] * mixed
+        dots.append(jnp.sum(r.cot[at] * mixed, axis=-1, keepdims=True))
+        r.block_out[pl.ds(pl.multiple_of(links.c * HALF + start, EDGE), size), :] = (
+            r.resid[at] + column[at] * mixed
         ).astype(BF16)
-    scalars_out[:, spread.lanes] = as_tile([column, jnp.concatenate(dots)])
+    r.scalars_out[:, spread.lanes] = as_tile([column, jnp.concatenate(dots)])
     spread.start()
     share.start()
     scatter.finish()
@@ -1219,32 +1317,33 @@
     chain_o.finish()
     spread.finish()
     share.wait()
-
-
-def backward_layer(links, inner_all, dmix, scalars, wo, params, saved, outs, work, delivers):
-    rowp, bcp, headp = params
-    y, z, x, bc, s, dt, dtraw, xin, bcin, states, decay = saved
-    cat, steps, go_parts, wide, bc_rows = outs
-    dy, gwo, normed_out, prior, dend, dpre, flow, sums, state_low, decay_row, states_in, decays_in = work
-    carried = States(links, True, state_low, decay_row, states_in, decays_in)
-    collect = Collect(links, gwo, go_parts)
+    r.done()
+
+
+def backward_layer(links, inner_all, r, at_start, before_collect, at_middle):
+    carried = States(links, True, r.state_low, r.decay_row, r.states_in, r.decays_in)
+    collect = Collect(links, r.gwo, r.go_parts)
     grad_sum, decay_all = back_through_gate(
-        inner_all, dmix, wo, y, z, x, bc, s, decay, scalars, rowp, cat, wide, dy, prior, normed_out
+        inner_all, r.dmix, r.wo, r.y, r.z, r.x, r.bc, r.s, r.decay, r.scalars, r.rowp,
+        r.cat, r.wide, r.dy, r.prior, r.normed_out,
     )
-    state_low[...] = grad_sum.astype(BF16)
-    decay_row[...] = jnp.broadcast_to(decay_all, decay_row.shape)
+    r.state_low[...] = grad_sum.astype(BF16)
+    r.decay_row[...] = jnp.broadcast_to(decay_all, r.decay_row.shape)
     links.meet()
     carried.start()
-    for deliver in delivers:
-        deliver.start()
-    out_gradient(dmix, normed_out, gwo)
-    back_within_spans(dy, x, bc, s, dt, dpre, flow, sums)
+    at_start()
+    out_gradient(r.dmix, r.normed_out, r.gwo)
+    before_collect()
+    collect.start()
+    r.need(r.dt)
+    back_within_spans(r.dy, r.x, r.bc, r.s, r.dt, r.dpre, r.flow, r.sums)
+    at_middle()
     carried.arrive()
-    collect.start()
-    grad = entering_state(links.z, links.groups, states_in, decays_in, True)
+    grad = entering_state(links.z, links.groups, r.states_in, r.decays_in, True)
+    r.need(r.states, r.dtraw, r.xin, r.bcin)
     back_through_states(
-        grad, prior, decay, states, dy, x, bc, s, dt, dtraw, xin, bcin, rowp, bcp, headp, flow, sums,
-        links.p, cat, steps, wide, bc_rows, dpre, dend,
+        grad, r.prior, r.decay, r.states, r.dy, r.x, r.bc, r.s, r.dt, r.dtraw, r.xin, r.bcin, r.rowp, r.bcp, r.headp,
+        r.flow, r.sums, links.p, r.cat, r.steps, r.wide, r.bc_rows, r.dpre, r.prior,
     )
     return carried, collect
 
@@ -1256,48 +1355,46 @@
             row += 1
 
 
-def third_kernel(inner_all, *refs):
-    dmix, scalars, wo, w, normed, rowp, bcp, headp, grad, resid, gain, mixed, inv = refs[:13]
-    saved, refs = refs[13:24], refs[24:]
-    dmix_out, scalars_out, grad_out, go_parts, gx_parts, gz_parts, gbc, gdt, wide, vec = refs[:10]
-    work, refs = refs[10:22], refs[22:]
-    cat, steps, bc_rows, part, gx, gz, gain_row, sib, total, peer, edge_slots, sends, recvs = refs
-    links = Links(sends, recvs)
-    scatter = Scatter(links, part, EDGE, sib, total, peer)
-    edge = EdgeBackward(links, part, edge_slots)
-    gather = Gather(links, dmix_out, 0)
-    spread = SmallGather(links, scalars_out)
-    collects = [Collect(links, gx, gx_parts), Collect(links, gz, gz_parts)]
-    edge_slots[...] = jnp.zeros_like(edge_slots)
+def third_kernel(inner_all, r):
+    links = Links(r.sends, r.recvs)
+    r.fetch(r.dt, r.states, r.dtraw, r.xin, r.bcin, r.w, r.normed, r.grad, r.resid, r.mixed)
+    scatter = Scatter(links, r.part, EDGE, r.sib, r.total, r.peer)
+    edge = EdgeBackward(links, r.part, r.edge_slots)
+    gather = Gather(links, r.dmix_out, 0)
+    spread = SmallGather(links, r.scalars_out)
+    collects = [Collect(links, r.gx, r.gx_parts), Collect(links, r.gz, r.gz_parts)]
+    r.edge_slots[...] = jnp.zeros_like(r.edge_slots)
     links.greet(plane=True, groups=True, edge=-1)
-    carried, collect = backward_layer(
-        links, inner_all, dmix, scalars, wo, (rowp, bcp, headp), saved, (cat, steps, go_parts, wide, bc_rows), work, []
-    )
-    project_back(cat, w, part)
+    carried, collect = backward_layer(links, inner_all, r, lambda: None, lambda: None, lambda: None)
+    r.need(r.w, r.normed)
+    x_gradient(r.cat, r.normed, r.gx)
+    collects[0].start()
+    project_back_edge(r.cat, r.w, r.part)
     edge.start()
-    scatter.start()
-    scatter.reduce()
-    weight_gradients(cat, steps, normed, gx, gz, gbc, gdt)
-    for one in collects:
-        one.start()
+    scatter_blocks(scatter, lambda q: project_back(q, r.cat, r.w, r.part))
+    scatter.pass_on(0)
+    z_gradient(r.cat, r.normed, r.gz)
+    collects[1].start()
+    small_gradients(r.cat, r.steps, r.normed, r.gbc, r.gdt)
     scatter.arrive()
     edge.receive()
-    gain_row[...] = jnp.zeros_like(gain_row)
+    r.need(r.grad, r.resid, r.mixed)
+    r.gain_row[...] = jnp.zeros_like(r.gain_row)
     dots = []
     for start, size in row_chunks():
         at = slice(start, start + size)
-        fresh = grad_rows(links, scatter, edge_slots, grad, resid, gain, gain_row, start, size)
-        grad_out[at] = fresh
+        fresh = grad_rows(links, scatter, r.edge_slots, r.grad, r.resid, r.gain, r.gain_row, start, size)
+        r.grad_out[at] = fresh
         low = fresh.astype(BF16)
-        dmix_out[gather.own(start, size), :] = low
-        dots.append(jnp.sum(low.astype(F32) * mixed[at], axis=-1, keepdims=True))
-    scalars_out[:, spread.lanes] = as_tile([inv[...].T[:, 0:1], jnp.concatenate(dots)])
+        r.dmix_out[gather.own(start, size), :] = low
+        dots.append(jnp.sum(low.astype(F32) * r.mixed[at], axis=-1, keepdims=True))
+    r.scalars_out[:, spread.lanes] = as_tile([r.inv[...].T[:, 0:1], jnp.concatenate(dots)])
     gather.start()
     spread.start()
-    vec[...] = jnp.zeros_like(vec)
-    model = gain_row.shape[1]
-    put_vector(vec, model // 128, gain_row[0:1])
-    put_vector(vec, 2 * (model // 128) + 2 * (CONV + 1), bc_rows[0 : CONV + 1])
+    r.vec[...] = jnp.zeros_like(r.vec)
+    model = r.gain_row.shape[1]
+    put_vector(r.vec, model // 128, r.gain_row[0:1])
+    put_vector(r.vec, 2 * (model // 128) + 2 * (CONV + 1), r.bc_rows[0 : CONV + 1])
     gather.pass_on()
     scatter.finish()
     edge.finish()
@@ -1309,93 +1406,124 @@
         one.finish()
 
 
-def fourth_kernel(inner_all, *refs):
-    dmix, scalars, wo, w, normed, rowp, bcp, headp, grad, resid, gain = refs[:11]
-    saved, refs = refs[11:22], refs[22:]
-    above, refs = refs[:3], refs[3:]
-    above_bc, above_dt, above_wide, above_vec = refs[:4]
-    out, gx_out, gz_out, go_out = refs[4:8]
-    above_out, refs = refs[8:11], refs[11:]
-    bc_out, vec_out, dt_out, wide_out = refs[:4]
-    work, refs = refs[4:16], refs[16:]
-    cat, steps, bc_rows, part, gx, gz, gain_row, sib, total, peer, edge_slots = refs[:11]
-    go_parts, gx_parts, gz_parts, final, gbc, gdt, wide, vec, steps_all, wide_all = refs[11:21]
-    bufs, (sends, recvs) = refs[21:28], refs[28:]
-    links = Links(sends, recvs)
-    scatter = Scatter(links, part, EDGE, sib, total, peer)
-    edge = EdgeBackward(links, part, edge_slots)
+def fourth_kernel(inner_all, r):
+    links = Links(r.sends, r.recvs)
+    r.fetch(r.dt, r.states, r.dtraw, r.xin, r.bcin, r.above_bc, r.above_x, r.above_z, r.above_o, r.normed, r.w, r.grad, r.resid)
+    scatter = Scatter(links, r.part, EDGE, r.sib, r.total, r.peer)
+    edge = EdgeBackward(links, r.part, r.edge_slots)
     at = pl.ds(pl.multiple_of(links.c * HALF, HALF), HALF)
-    share = links.copy(out.at[at, :], out.at[at, :], links.at(0, 1))
-    collects = [Collect(links, gx, gx_parts), Collect(links, gz, gz_parts)]
-    delivers = [Deliver(links, above[i], final.at[i], above_out[i]) for i in range(3)]
-    own_delivers = [
-        Deliver(links, parts, final.at[3 + i], place)
-        for i, (parts, place) in enumerate(((go_parts, go_out), (gx_parts, gx_out), (gz_parts, gz_out)))
+    share = links.copy(r.out.at[at, :], r.out.at[at, :], links.at(0, 1))
+    collects = [Collect(links, r.gx, r.gx_parts), Collect(links, r.gz, r.gz_parts)]
+    above = zip((r.above_x, r.above_z, r.above_o), r.big_out[1])
+    own = ((r.go_parts, r.big_out[0][2]), (r.gx_parts, r.big_out[0][0]), (r.gz_parts, r.big_out[0][1]))
+    delivers = [Deliver(links, parts, r.final.at[i], out) for i, (parts, out) in enumerate(above)]
+    own_delivers = [Deliver(links, parts, r.final.at[3 + i], out) for i, (parts, out) in enumerate(own)]
+    bc_sums = [
+        BcSum(links, bc, r.bc_out.at[i], r.bc_bufs[i])
+        for i, bc in enumerate((r.gbc, r.above_bc))
     ]
-    small = SmallSums(
-        links, (gbc, above_bc), vec, steps_all, wide_all, bc_out, vec_out, dt_out, wide_out, bufs
-    )
-    edge_slots[...] = jnp.zeros_like(edge_slots)
+    laid = LaidOut(links, r.steps_all, r.wide_all, r.dt_out, r.wide_out, r.dt_far, r.wide_far)
+    vec_sum = VecSum(links, r.vec, r.vec_out, r.vec_near, r.vec_far)
+    r.edge_slots[...] = jnp.zeros_like(r.edge_slots)
     links.greet(plane=True, groups=True, edge=-1)
-    carried, collect = backward_layer(
-        links, inner_all, dmix, scalars, wo, (rowp, bcp, headp), saved, (cat, steps, go_parts, wide, bc_rows), work,
-        delivers,
-    )
-    weight_gradients(cat, steps, normed, gx, gz, gbc, gdt)
-    for one in collects:
-        one.start()
-    project_back(cat, w, part)
+
+    def at_start():
+        r.need(r.above_bc)
+        bc_sums[1].cores()
+
+    def at_middle():
+        bc_sums[1].groups()
+        r.need(r.above_x, r.above_z, r.above_o)
+        for deliver in delivers:
+            deliver.start()
+
+    carried, collect = backward_layer(links, inner_all, r, at_start, bc_sums[1].plane, at_middle)
+    r.need(r.normed)
+    small_gradients(r.cat, r.steps, r.normed, r.gbc, r.gdt)
+    bc_sums[0].cores()
+    r.steps_all[:, 0:EDGE, :] = r.gdt[...]
+    r.steps_all[:, EDGE:, :] = r.above_dt[...]
+    r.wide_all[0:16] = r.wide[...]
+    r.wide_all[16:32] = r.above_wide[...]
+    laid.groups()
+    x_gradient(r.cat, r.normed, r.gx)
+    collects[0].start()
+    bc_sums[0].plane()
+    r.need(r.w)
+    project_back_edge(r.cat, r.w, r.part)
     edge.start()
-    scatter.start()
-    scatter.reduce()
-    steps_all[:, 0:EDGE, :] = gdt[...]
-    steps_all[:, EDGE:, :] = above_dt[...]
-    wide_all[0:16] = wide[...]
-    wide_all[16:32] = above_wide[...]
+    scatter_blocks(scatter, lambda q: project_back(q, r.cat, r.w, r.part))
+    scatter.pass_on(0)
+    bc_sums[0].groups()
+    z_gradient(r.cat, r.normed, r.gz)
     scatter.arrive()
     edge.receive()
-    gain_row[...] = jnp.zeros_like(gain_row)
+    r.need(r.grad, r.resid)
+    r.gain_row[...] = jnp.zeros_like(r.gain_row)
     for start, size in row_chunks():
-        fresh = grad_rows(links, scatter, edge_slots, grad, resid, gain, gain_row, start, size)
-        out[pl.ds(pl.multiple_of(links.c * HALF + start, EDGE), size), :] = fresh.astype(BF16)
+        fresh = grad_rows(links, scatter, r.edge_slots, r.grad, r.resid, r.gain, r.gain_row, start, size)
+        r.out[pl.ds(pl.multiple_of(links.c * HALF + start, EDGE), size), :] = fresh.astype(BF16)
     share.start()
-    vec[...] = above_vec[...]
-    put_vector(vec, 0, gain_row[0:1])
-    put_vector(vec, 2 * (gain_row.shape[1] // 128), bc_rows[0 : CONV + 1])
-    small.round_one()
+    r.vec[...] = r.above_vec[...]
+    put_vector(r.vec, 0, r.gain_row[0:1])
+    put_vector(r.vec, 2 * (r.gain_row.shape[1] // 128), r.bc_rows[0 : CONV + 1])
+    vec_sum.plane()
+    vec_sum.groups()
+    collects[1].start()
     collect.arrive()
     own_delivers[0].start()
-    small.round_two()
-    small.round_three()
-    for i in range(2):
-        collects[i].arrive()
-        own_delivers[i + 1].start()
-    small.finish()
-    scatter.finish()
-    edge.finish()
+    bc_sums[1].share()
+    laid.plane()
+    collects[0].arrive()
+    own_delivers[1].start()
+    bc_sums[0].share()
+    vec_sum.back()
+    collects[1].arrive()
+    own_delivers[2].start()
+    for one in bc_sums + [laid, vec_sum, scatter, edge, carried, collect] + collects:
+        one.finish()
     share.wait()
-    carried.finish()
-    for one in [collect] + collects:
-        one.finish()
     for deliver in delivers + own_delivers:
         deliver.finish()
 
 
-def call(body, outs, *args, scratch=(), collective=None, copies=0):
-    vmem = pl.BlockSpec(memory_space=pltpu.VMEM)
-    scratch = [pltpu.VMEM(shape, kind) for shape, kind in scratch]
-    if collective is not None:
-        scratch += [pltpu.SemaphoreType.DMA((copies,)), pltpu.SemaphoreType.DMA((copies,))]
-    return pl.pallas_call(
-        body,
-        out_shape=tuple(jax.ShapeDtypeStruct(shape, kind) for shape, kind in outs),
-        in_specs=[vmem] * len(args),
-        out_specs=tuple([vmem] * len(outs)),
-        scratch_shapes=scratch,
+def flat(value):
+    return [a for member in value for a in flat(member)] if isinstance(value, list) else [value]
+
+
+def shaped(value, leaves):
+    return [shaped(member, leaves) for member in value] if isinstance(value, list) else leaves.pop(0)
+
+
+def call(body, collective, copies, outs, hbm_outs, ins, hbm_ins, scratch):
+    vmem, hbm = pl.BlockSpec(memory_space=pltpu.VMEM), pl.BlockSpec(memory_space=pl.ANY)
+    twins = {**{name: (a.shape, a.dtype) for name, a in hbm_ins.items()}, **hbm_outs}
+    sides = [list(ins.values()), list(hbm_ins.values()), list(outs.values()), list(hbm_outs.values())]
+    counts = [len(flat(side)) for side in sides]
+    buffers = flat([list(scratch.values()), list(twins.values())])
+
+    def kernel(*refs):
+        refs = list(refs)
+        groups = [shaped(side, refs) for side in sides]
+        inner = shaped([list(scratch.values()), list(twins.values())], refs)
+        sends, recvs, sems = refs
+        near = dict(zip(twins, inner[1]))
+        named = {**dict(zip(ins, groups[0])), **dict(zip(outs, groups[2])), **dict(zip(scratch, inner[0])), **near}
+        body(Refs(dict(named, sends=sends, recvs=recvs), list(zip(groups[1] + groups[3], inner[1])), sems))
+
+    results = pl.pallas_call(
+        kernel,
+        out_shape=tuple(jax.ShapeDtypeStruct(*a) for a in flat(sides[2:])),
+        in_specs=[vmem] * counts[0] + [hbm] * counts[1],
+        out_specs=tuple([vmem] * counts[2] + [hbm] * counts[3]),
+        scratch_shapes=[pltpu.VMEM(*a) for a in buffers]
+        + [pltpu.SemaphoreType.DMA((n,)) for n in (copies, copies, max(1, len(twins)))],
         compiler_params=pltpu.CompilerParams(
-            vmem_limit_bytes=VMEM_BYTES, collective_id=collective, has_side_effects=collective is not None
+            vmem_limit_bytes=VMEM_BYTES, collective_id=collective, has_side_effects=True
         ),
-    )(*args)
+    )(*flat(sides[:2]))
+    found = shaped(sides[2:], list(results))
+    return types.SimpleNamespace(**dict(zip(outs, found[0])), **dict(zip(hbm_outs, found[1])))
 
 
 def on_device(resid_in, cotangent, norm_gain, w_zx, w_dt, w_bc, conv_x, conv_bc, head_params, gated_gain, w_out):
@@ -1434,136 +1562,228 @@
         steps = jnp.pad(w_dt[layer], ((0, 0), (0, STATE - heads_core)))
         return w_zx[layer, 1], w_zx[layer, 0], steps, half, w_out[layer].T
 
-    half_scratch = [
-        ((GROUP, HALF, model), BF16),
-        ((GROUP - 1, HALF, model), BF16),
-        ((GROUP - 1, HALF, model), BF16),
-    ]
-    slots = ((2 * GROUP - 1, 8, HALF), F32)
-    edges = ((2 * GROUP, EDGE, model), BF16)
     own_rows = ((HALF, model), F32)
     all_rows, edged_rows = ((tokens, model), BF16), ((tokens + EDGE, model), BF16)
     columns = columns_of(inner).size
     w_shape, wo_shape = ((model, columns), BF16), ((model, inner), BF16)
-    tile = ((8, HALF), F32)
     scalars = ((8, tokens), F32)
     state_shape = ((spans, STATE, inner), F32)
-    state_scratch = [
-        ((STATE, inner), BF16),
-        ((8, inner), F32),
-        ((groups, STATE, inner), BF16),
-        ((groups, 8, inner), F32),
-    ]
-    saved_shapes = [
-        ((tokens, inner), F32),
-        ((tokens, inner), BF16),
-        ((tokens, inner), BF16),
-        ((tokens, 2 * STATE), BF16),
-        ((tokens, 128), F32),
-        ((tokens, 128), F32),
-        ((tokens, 128), BF16),
-        ((tokens + EDGE, inner), BF16),
-        ((tokens + EDGE, 2 * STATE), BF16),
-        state_shape,
-        ((spans, 8, inner), F32),
-    ]
-    forward_scratch = [((tokens + EDGE, inner + 2 * STATE), F32), state_shape] + state_scratch
+    low_rows, steps_shape = ((tokens, inner), BF16), ((tokens, 128), F32)
+    scatter_scratch = dict(
+        sib=((GROUP, HALF, model), BF16),
+        total=((GROUP - 1, HALF, model), BF16),
+        peer=((GROUP - 1, HALF, model), BF16),
+    )
+    state_scratch = dict(
+        state_low=((STATE, inner), BF16),
+        decay_row=((8, inner), F32),
+        states_in=((groups, STATE, inner), BF16),
+        decays_in=((groups, 8, inner), F32),
+    )
+    saved_shapes = dict(
+        y=((tokens, inner), F32),
+        z=low_rows,
+        x=low_rows,
+        bc=((tokens, 2 * STATE), BF16),
+        s=steps_shape,
+        dt=steps_shape,
+        dtraw=((tokens, 128), BF16),
+        xin=((tokens + EDGE, inner), BF16),
+        bcin=((tokens + EDGE, 2 * STATE), BF16),
+        states=state_shape,
+        decay=((spans, 8, inner), F32),
+    )
+    forward_scratch = dict(
+        ext=((tokens + EDGE, inner + 2 * STATE), F32),
+        local=state_shape,
+        part=all_rows,
+        squares=scalars,
+        slots=((2 * GROUP - 1, 8, HALF), F32),
+        **state_scratch,
+        **scatter_scratch,
+    )
 
     def params(layer):
-        return row_all[layer], bc_all[layer], head_all[layer]
+        return dict(rowp=row_all[layer], bcp=bc_all[layer], headp=head_all[layer])
 
     stagings = [((GROUP, shard, width), BF16) for width in (inner, inner, STATE, STATE, inner)]
-    results = call(
+    first = call(
         functools.partial(first_kernel, inner_all),
-        [edged_rows, all_rows, w_shape, wo_shape, w_shape, wo_shape]
-        + saved_shapes
-        + [own_rows, own_rows, own_rows, tile, edged_rows, own_rows],
-        resid_in[0], cotangent[0], gains[0], gains[1], *params(0), *shards_of(0), *shards_of(1),
-        scratch=[all_rows, scalars] + stagings + stagings + forward_scratch + half_scratch + [slots],
-        collective=0, copies=160 + 10 * (groups - 1) + 2 * groups,
+        0,
+        160 + 14 * (groups - 1) + 2 * groups,
+        dict(
+            next_w=w_shape,
+            next_wo=wo_shape,
+            next_normed=edged_rows,
+            resid_out=own_rows,
+            cot_out=own_rows,
+            mixed_out=own_rows,
+            fresh_out=own_rows,
+            inv_out=((8, HALF), F32),
+        ),
+        dict(normed=edged_rows, dmix=all_rows, w=w_shape, wo=wo_shape, **saved_shapes),
+        dict(
+            resid=resid_in[0],
+            cot=cotangent[0],
+            gain=gains[0],
+            next_gain=gains[1],
+            **params(0),
+            shards=[list(shards_of(0)), list(shards_of(1))],
+        ),
+        dict(),
+        dict(**forward_scratch, stagings=[stagings, stagings]),
     )
-    normed0, d_mix, w0, wo0, w1, wo1 = results[:6]
-    saved0 = results[6:17]
-    resid0, grad, mixed, inv, normed1, resid1 = results[17:]
-    wo_own = lax.dynamic_slice_in_dim(wo1, level * rows, rows, 0)
-    results = call(
+    second = call(
         functools.partial(second_kernel, inner_all),
-        [wo_shape] + saved_shapes + [((length, model), BF16), scalars],
-        normed1, w1, wo_own, *params(1), resid1, grad,
-        scratch=[all_rows, scalars] + forward_scratch + half_scratch + [slots],
-        collective=1, copies=60 + 4 * groups,
+        1,
+        60 + 4 * groups,
+        dict(block_out=((length, model), BF16), scalars_out=scalars),
+        dict(wo=wo_shape, **saved_shapes),
+        dict(
+            normed=first.next_normed,
+            w=first.next_w,
+            wo_own=lax.dynamic_slice_in_dim(first.next_wo, level * rows, rows, 0),
+            **params(1),
+            resid=first.fresh_out,
+            cot=first.cot_out,
+        ),
+        dict(),
+        forward_scratch,
     )
-    wo1, saved1, (block_out, token_scalars) = results[0], results[1:12], results[12:]
-
     grad_parts = ((groups, rows, inner), BF16)
-    back_scratch = [
-        ((tokens, inner), BF16),
-        wo_shape,
-        ((tokens, inner), BF16),
-        state_shape,
-        state_shape,
-        ((tokens + 2 * EDGE, inner + 2 * STATE), F32),
-        ((tokens, 128), F32),
-        ((tokens, 128), F32),
-    ] + state_scratch
-    more_scratch = [
-        ((tokens + EDGE, columns), BF16),
-        ((tokens, 128), BF16),
-        ((8, 2 * STATE), F32),
-        edged_rows,
-        wo_shape,
-        wo_shape,
-        ((8, model), F32),
-    ]
     bc_grad = ((groups, GROUP, shard, 2 * STATE), BF16)
     dt_grad = ((groups, EDGE, rows), BF16)
     wide_grad = ((16, inner), F32)
     vec_shape = ((2 * GROUP, 8, 128), F32)
-    d_mix, token_scalars, grad, go_parts, gx_parts, gz_parts, gbc, gdt, wide, vec = call(
+    back_scratch = dict(
+        dy=low_rows,
+        gwo=wo_shape,
+        normed_out=low_rows,
+        prior=state_shape,
+        dpre=((tokens + 2 * EDGE, inner + 2 * STATE), F32),
+        flow=steps_shape,
+        sums=steps_shape,
+        cat=((tokens + EDGE, columns), BF16),
+        steps=((tokens, 128), BF16),
+        bc_rows=((8, 2 * STATE), F32),
+        part=edged_rows,
+        gx=wo_shape,
+        gz=wo_shape,
+        gain_row=((8, model), F32),
+        edge_slots=((2 * GROUP, EDGE, model), BF16),
+        **state_scratch,
+        **scatter_scratch,
+    )
+    def at_once(run):
+        return dict(y=run.y, z=run.z, x=run.x, bc=run.bc, s=run.s, decay=run.decay)
+
+    def later(run):
+        return dict(dt=run.dt, states=run.states, dtraw=run.dtraw, xin=run.xin, bcin=run.bcin)
+
+    third = call(
         functools.partial(third_kernel, inner_all),
-        [all_rows, scalars, own_rows, grad_parts, grad_parts, grad_parts, bc_grad, dt_grad, wide_grad, vec_shape],
-        d_mix, token_scalars, wo1, w1, normed1, *params(1), grad, resid1, gains[1], mixed, inv, *saved1,
-        scratch=back_scratch + more_scratch + half_scratch + [edges],
-        collective=2, copies=60 + 6 * groups,
+        2,
+        60 + 6 * groups,
+        dict(
+            dmix_out=all_rows,
+            scalars_out=scalars,
+            grad_out=own_rows,
+            go_parts=grad_parts,
+            gx_parts=grad_parts,
+            gz_parts=grad_parts,
+            gbc=bc_grad,
+            gdt=dt_grad,
+            wide=wide_grad,
+            vec=vec_shape,
+        ),
+        dict(),
+        dict(
+            dmix=first.dmix,
+            scalars=second.scalars_out,
+            wo=second.wo,
+            **params(1),
+            gain=gains[1],
+            inv=first.inv_out,
+            **at_once(second),
+        ),
+        dict(
+            w=first.next_w,
+            normed=first.next_normed,
+            grad=first.cot_out,
+            resid=first.fresh_out,
+            mixed=first.mixed_out,
+            **later(second),
+        ),
+        back_scratch,
     )
     far = groups - 1
     rows_shape = ((shard, inner_core), BF16)
     dt_shape, wide_shape = (layers * EDGE, rows), (layers * 16, inner)
-    grad_input, gx0, gz0, go0, gx1, gz1, go1, g_bc, vec, g_dt, wide = call(
+    half_bc = (groups, GROUP, shard, STATE)
+    bc_bufs = [
+        (half_bc, BF16),
+        (half_bc, BF16),
+        ((GROUP - 1, groups, shard, STATE), BF16),
+        ((groups, shard, STATE), BF16),
+        ((far, shard, STATE), BF16),
+    ]
+    fourth = call(
         functools.partial(fourth_kernel, inner_all),
-        [((length, model), BF16)]
-        + [rows_shape] * 6
-        + [
-            ((layers, shard, 2 * STATE), BF16),
-            vec_shape,
-            ((GROUP, *dt_shape), BF16),
-            ((GROUP, *wide_shape), F32),
-        ],
-        d_mix, token_scalars, wo0, w0, normed0, *params(0), grad, resid0, gains[0], *saved0,
-        gx_parts, gz_parts, go_parts, gbc, gdt, wide, vec,
-        scratch=back_scratch + more_scratch + half_scratch + [
-            edges,
-            grad_parts,
-            grad_parts,
-            grad_parts,
-            ((6, GROUP, shard, inner), BF16),
-            bc_grad,
-            dt_grad,
-            wide_grad,
-            vec_shape,
-            ((groups, *dt_shape), BF16),
-            (wide_shape, F32),
-            ((layers, 2 * GROUP - 1, groups, shard, STATE), BF16),
-            ((layers, groups, shard, STATE), BF16),
-            ((layers, far, shard, STATE), BF16),
-            ((2 * GROUP, 8, 128), F32),
-            ((far, 8, 128), F32),
-            ((far, *dt_shape), BF16),
-            ((far, *wide_shape), F32),
-        ],
-        collective=3, copies=120 + 12 * groups,
+        3,
+        130 + 14 * groups,
+        dict(
+            out=((length, model), BF16),
+            big_out=[[rows_shape] * 3] * layers,
+            bc_out=((layers, shard, 2 * STATE), BF16),
+            vec_out=vec_shape,
+            dt_out=((GROUP, *dt_shape), BF16),
+            wide_out=((GROUP, *wide_shape), F32),
+        ),
+        dict(),
+        dict(
+            dmix=third.dmix_out,
+            scalars=third.scalars_out,
+            wo=first.wo,
+            **params(0),
+            gain=gains[0],
+            above_dt=third.gdt,
+            above_wide=third.wide,
+            above_vec=third.vec,
+            **at_once(first),
+        ),
+        dict(
+            w=first.w,
+            normed=first.normed,
+            grad=third.grad_out,
+            resid=first.resid_out,
+            above_x=third.gx_parts,
+            above_z=third.gz_parts,
+            above_o=third.go_parts,
+            above_bc=third.gbc,
+            **later(first),
+        ),
+        dict(
+            **back_scratch,
+            go_parts=grad_parts,
+            gx_parts=grad_parts,
+            gz_parts=grad_parts,
+            final=((6, GROUP, shard, inner), BF16),
+            gbc=bc_grad,
+            gdt=dt_grad,
+            wide=wide_grad,
+            vec=vec_shape,
+            steps_all=((groups, *dt_shape), BF16),
+            wide_all=(wide_shape, F32),
+            bc_bufs=[bc_bufs, bc_bufs],
+            vec_near=vec_shape,
+            vec_far=((far, 8, 128), F32),
+            dt_far=((far, *dt_shape), BF16),
+            wide_far=((far, *wide_shape), F32),
+        ),
     )
-    delivered = ((gx0, gz0, go0), (gx1, gz1, go1))
+    block_out, grad_input, g_bc = second.block_out, fourth.out, fourth.bc_out
+    vec, g_dt, wide = fourth.vec_out, fourth.dt_out, fourth.wide_out
+    delivered = fourth.big_out
     vec = vec.reshape(-1)
     grad_gain = vec[: layers * model].reshape(layers, model)
     grad_conv_bc = vec[layers * model :][: layers * (CONV + 1) * 2 * STATE].reshape(layers, CONV + 1, 2 * STATE)

time: 525 us -> 481 us (0.916)
  the two profiles are of different devices: /device:TPU:0 before, /device:TPU:25 now
where the time goes in v5:
time: 481 us; the launch traced here: 474 us
  Pallas kernels  444 us (92%)
  local copies, waits for them, and re-layouts  21.3 us (4%)
  other arithmetic  6.95 us (1%)
    pallas_call x4, Pallas kernels, call(): pl.pallas_call(kernel, out_shape=tuple((jax.ShapeDtypeStruct(*a) for a in...  444 us

profile of v5, /device:TPU:25, one launch (start us, length us, event | category | flops | bytes accessed | tf_op | source)
XLA Modules:
  0.0 473.7 jit_solution(9359956839680017430)
XLA Ops:
  0.8 0.9 dynamic-slice_bitcast_fusion.2
  1.6 0.8 constant_dynamic-slice_fusion.4
  3.1 0.7 fusion.1
  4.7 0.8 fusion.5
  6.7 1.4 slice_convert_fusion
  8.0 0.7 fusion.4
  8.8 0.7 maximum_maximum_fusion.1
  10.9 0.8 fusion.3
  12.3 0.9 slice_bitcast_fusion
  13.2 1.0 slice_bitcast_fusion.1
  14.2 152.9 %shard_map.194 = (bf16[1536,1152]{1,0:T(8,128)(2,1)}, bf16[1536,384]{1,0:T(8,128)(2,1)}, bf16[1040,1536]{1,0:T(8,128)(2,1)}, f32[128,1536]{1,0:T(8,128)}, f32[12...) custom-call(bf16[256,1536]{1,0:T(8,128)(2,1)} %bitcast.79, ...), custom_call_target="tpu_custom_call" | custom-call | tf_op jit(solution)/shard_map/pallas_call | solution.py:1514
  167.1 1.7 constant_dynamic-slice_fusion.3.refs_2_
  168.8 70.0 %shard_map.195 = (bf16[256,1536]{1,0:T(8,128)(2,1)}, f32[8,1024]{1,0:T(8,128)}, bf16[1536,384]{1,0:T(8,128)(2,1)}, f32[1024,384]{1,0:T(8,128)}, bf16[1024,384]{1...) custom-call(bf16[1040,1536]{1,0:T(8,128)(2,1)} %get-tuple-element.69, ...), custom_call_target="tpu_custom_call" | custom-call | tf_op jit(solution)/shard_map/pallas_call | solution.py:1514
  238.8 90.2 %shard_map.196 = (bf16[1024,1536]{1,0:T(8,128)(2,1)}, f32[8,1024]{1,0:T(8,128)}, f32[128,1536]{1,0:T(8,128)}, bf16[4,384,384]{2,1,0:T(8,128)(2,1)}, bf16[4,384,3...) custom-call(bf16[1024,1536]{1,0:T(8,128)(2,1)} %get-tuple-element.75, ...), custom_call_target="tpu_custom_call" | custom-call | tf_op jit(solution)/shard_map/pallas_call | solution.py:1514
  329.1 131.1 %shard_map.197 = (bf16[256,1536]{1,0:T(8,128)(2,1)}, bf16[96,1536]{1,0:T(8,128)(2,1)}, bf16[96,1536]{1,0:T(8,128)(2,1)}, bf16[96,1536]{1,0:T(8,128)(2,1)}, bf16[...) custom-call(bf16[1024,1536]{1,0:T(8,128)(2,1)} %get-tuple-element.91, ...), custom_call_target="tpu_custom_call" | custom-call | tf_op jit(solution)/shard_map/pallas_call | solution.py:1514
  460.2 0.9 slice.140
  461.2 0.8 convert.26
  463.2 1.0 reshape.55
  464.9 1.1 copy.39
  468.5 1.1 pad_maximum_fusion
  469.6 0.9 pad_maximum_fusion.1
  470.9 0.9 copy.67
  471.8 0.9 copy.68
  472.8 0.6 copy.69
  (67 shorter events, 9.8 us)
Async XLA Ops:
  0.6 4.0 copy-start
  0.7 11.7 %copy-start.4 = (bf16[2,1536,96]{1,2,0:T(8,128)(2,1)S(1)}, bf16[2,1536,96]{1,2,0:T(8,128)(2,1)}, u32[]{:S(2)}) copy-start(bf16[2,1536,96]{1,2,0:T(8,128)(2,1)} %param.21) | copy-start | bytes 1769476
  0.7 12.5 %copy-start.1 = (bf16[2,2,96,1536]{3,2,1,0:T(8,128)(2,1)S(1)}, bf16[2,2,96,1536]{3,2,1,0:T(8,128)(2,1)}, u32[]{:S(2)}) copy-start(bf16[2,2,96,1536]{3,2,1,0:T(8,128)(2,1)} %param.14) | copy-start | bytes 3538948
  460.2 8.1 %copy-start.9 = (bf16[96,1536]{1,0:T(8,128)(2,1)S(1)}, bf16[96,1536]{1,0:T(8,128)(2,1)}, u32[]{:S(2)}) copy-start(bf16[96,1536]{1,0:T(8,128)(2,1)} %get-tuple-element.119) | copy-start | bytes 884740
  460.2 8.1 %copy-start.10 = (bf16[96,1536]{1,0:T(8,128)(2,1)S(1)}, bf16[96,1536]{1,0:T(8,128)(2,1)}, u32[]{:S(2)}) copy-start(bf16[96,1536]{1,0:T(8,128)(2,1)} %get-tuple-element.118) | copy-start | bytes 884740
  464.9 3.4 copy-start.7
  464.9 3.4 copy-start.8
  468.5 1.1 copy-start.5
  468.5 1.1 copy-start.6
  469.6 1.3 copy-start.2
  469.6 2.2 copy-start.3
  471.8 1.0 copy-start.11

commit v6 on v5

--- a/solution.py
+++ b/solution.py
@@ -97,7 +97,7 @@
 
 
 def project_and_convolve(
-    place, normed, w, rowp, bcp, headp,
+    normed, w, rowp, bcp, headp,
     z_out, xin_out, bcin_out, x_out, bc_out, dtraw_out, dt_out, s_out, decay_out,
     ext, local, at_block,
 ):
@@ -113,7 +113,6 @@
     ext[0:EDGE, 0:inner] = edge_x.astype(F32)
     ext[0:EDGE, inner:] = edge_bc.astype(F32)
     spread = head_spread(inner)
-    pick = head_pick(place, inner // HEADDIM)
     low_tri = triangle(True)
     rate = -jnp.exp(headp[0:1])
     bias = headp[1:2]
@@ -127,7 +126,7 @@
         product = dot(normed[after, :], w[...]).astype(BF16)
         z_out[tok, :] = product[:, cols.z]
         xin, bcin = product[:, cols.x], product[:, cols.bc]
-        dtraw = dot(product[:, cols.dt], pick).astype(BF16)
+        dtraw = product[:, cols.dt]
         xin_out[after, :] = xin
         bcin_out[after, :] = bcin
         dtraw_out[tok, :] = dtraw
@@ -318,7 +317,7 @@
 
 def back_through_states(
     grad, prior, decay, states, dy_in, x, bc, s_in, dt_in, dtraw, xin, bcin, rowp, bcp, headp, flow_in, sum_in,
-    place, cat_out, step_out, row_out, bcrow_out,
+    cat_out, row_out, bcrow_out,
     dpre, dend,
 ):
     inner = x.shape[1]
@@ -341,7 +340,6 @@
     dpre[EDGE + spans * SPAN :] = jnp.zeros((EDGE, width), F32)
     bcrow_out[...] = jnp.zeros_like(bcrow_out)
     cols = columns_of(inner)
-    pick = head_pick(place, inner // HEADDIM)
     cat_out[0:EDGE, cols.z] = jnp.zeros((EDGE, inner), BF16)
     cat_out[0:EDGE, cols.dt] = jnp.zeros((EDGE, 128), BF16)
 
@@ -379,8 +377,7 @@
         row_out[7:8, 0:128] += jnp.sum(da * (dt * rate), axis=0, keepdims=True)
         row_out[8:9, 0:128] += jnp.sum(d_raw, axis=0, keepdims=True)
         d_low = d_raw.astype(BF16)
-        step_out[tok, :] = d_low
-        cat_out[after, cols.dt] = dot(d_low, pick, NT).astype(BF16)
+        cat_out[after, cols.dt] = d_low
 
         win_x = xin[window, :].astype(F32)
         d_x = dx * silu_slope(conv_taps(win_x, rowp))
@@ -464,7 +461,7 @@
     for_row_blocks((normed.shape[1] // SPAN, SPAN), body)
 
 
-def small_gradients(cat, steps, normed, gbc_out, gdt_out):
+def small_gradients(cat, normed, gbc_out, gdt_out):
     groups, parts, shard, _ = gbc_out.shape
     cols = columns_of((cat.shape[1] - 3 * STATE) // 2)
 
@@ -472,7 +469,7 @@
         edge, tokens = normed[0:EDGE, at], normed[EDGE:, at]
         bc = dot(tokens, cat[EDGE:, cols.bc], TN) + dot(edge, cat[0:EDGE, cols.bc], TN)
         gbc_out[g] = bc.reshape(parts, shard, 2 * STATE).astype(BF16)
-        gdt_out[g] = dot(steps[...], tokens, TN)[0:EDGE].astype(BF16)
+        gdt_out[g] = dot(cat[EDGE:, cols.dt], tokens, TN)[0:EDGE].astype(BF16)
 
     for_row_blocks((groups, parts * shard), body)
 
@@ -590,9 +587,11 @@
         self.links, self.staging, self.out, self.lanes = links, staging, out, lanes
 
         def source(k):
+            to = lax.bitwise_xor(links.p, jnp.int32(k))
+            if len(shard.shape) == 3:
+                return shard.at[to]
             if shard.shape[1] == width:
                 return shard
-            to = lax.bitwise_xor(links.p, jnp.int32(k))
             return shard.at[:, pl.ds(pl.multiple_of(to * width, 128), width)]
 
         self.copies = [links.copy(source(k), staging.at[links.p], links.at(k, 0)) for k in (3, 1, 2)]
@@ -608,7 +607,7 @@
             copy.wait_recv()
         parts, shard, width = self.staging.shape
         rows = parts * shard
-        first = self.links.z * rows
+        first = self.links.z * rows if self.out.shape[0] > rows else 0
         if shard % EDGE == 0:
             for j in range(parts):
                 self.out[pl.ds(pl.multiple_of(first + j * shard, EDGE), shard), self.lanes] = self.staging[j]
@@ -630,6 +629,7 @@
             return grad.at[pl.ds(pl.multiple_of(index * rows, EDGE), rows)]
 
         self.keep = links.local(block(z), out.at[0])
+        self.kept = False
         self.copies = []
         for k in range(1, groups):
             to = lax.rem(z + k, groups)
@@ -640,12 +640,18 @@
         for copy in self.copies:
             copy.start()
 
+    def keep_own(self):
+        if not self.kept:
+            self.keep.wait()
+        self.kept = True
+
     def arrive(self):
-        self.keep.wait()
+        self.keep_own()
         for copy in self.copies:
             copy.wait_recv()
 
     def finish(self):
+        self.keep_own()
         for copy in self.copies:
             copy.wait_send()
 
@@ -671,9 +677,13 @@
             copy.start()
         self.out[:, self.mine] = self.final[self.links.p]
 
+    def arrive(self):
+        for copy in self.copies:
+            copy.wait_recv()
+
     def finish(self):
         for copy in self.copies:
-            copy.wait()
+            copy.wait_send()
 
 
 class States:
@@ -1121,8 +1131,8 @@
             copy.wait()
 
 
-def weight_chain(links, w, inner):
-    rows = w.shape[0] // links.groups
+def weight_chain(links, w, steps, inner):
+    rows, step_rows = w.shape[0] // links.groups, steps.shape[0] // links.groups
     cols = columns_of(inner)
     half = pl.ds(pl.multiple_of(cols.bc.start + links.c * STATE, STATE), STATE)
 
@@ -1131,10 +1141,56 @@
 
     pieces = [
         lambda i: w.at[at(i), cols.x],
-        lambda i: w.at[at(i), cols.z.start : cols.dt.stop],
+        lambda i: w.at[at(i), cols.z],
         lambda i: w.at[at(i), half],
+        lambda i: steps.at[pl.ds(pl.multiple_of(i * step_rows, EDGE), step_rows), :],
     ]
     return Chain(links, pieces), links.copy(w.at[:, half], w.at[:, half], links.at(0, 1))
+
+
+def pack_steps(w_dt, steps_out, wide):
+    heads_core, shard = w_dt.shape
+    heads = heads_core // GROUP
+    wide[...] = jnp.zeros_like(wide)
+    wide[0:heads_core, 0:shard] = w_dt
+    row, col = iota((EDGE, 128), 0), iota((EDGE, 128), 1)
+    for q in range(GROUP):
+        pick = jnp.logical_and(col == q * heads + row, row < heads).astype(BF16)
+        steps_out[q] = dot(pick, wide[...]).astype(BF16)
+
+
+def unpack_steps(steps, w, shard, inner):
+    lanes = columns_of(inner).dt
+    rows = GROUP * shard
+    blank = jnp.zeros((128 - EDGE, 128), F32)
+
+    def block(g, _):
+        parts = []
+        for j in range(GROUP):
+            at = pl.ds(pl.multiple_of(g * (GROUP * EDGE) + j * EDGE, EDGE), EDGE)
+            parts.append(jnp.concatenate([steps[at, :].astype(F32), blank]).T[0:shard])
+        w[pl.ds(pl.multiple_of(g * rows, EDGE), rows), lanes] = jnp.concatenate(parts).astype(BF16)
+        return 0
+
+    lax.fori_loop(0, w.shape[0] // rows, block, 0)
+
+
+def prepare(links, r, layer):
+    inner = r.rowp.shape[1]
+    heads_core = r.head_params.shape[2]
+    lanes = pl.ds(pl.multiple_of(links.p * inner, 128), inner)
+    r.gains[...] = r.norm_gain[...].astype(F32)
+    r.headp[...] = jnp.zeros_like(r.headp)
+    for i in range(3):
+        r.headp[i : i + 1, 0:heads_core] = r.head_params[i, layer : layer + 1, :]
+    mine = dot_exact(r.headp[...], head_pick(links.p, inner // HEADDIM).astype(F32))
+    r.headp[...] = mine
+    r.rowp[...] = jnp.zeros_like(r.rowp)
+    r.rowp[0 : CONV + 1] = r.conv_x[:, :, lanes].astype(F32)[:, layer]
+    r.rowp[5:6] = r.gated_gain[:, lanes].astype(F32)[layer : layer + 1]
+    r.rowp[6:7] = dot_exact(mine, head_spread(inner).astype(F32))[2:3]
+    r.bcp[...] = jnp.zeros_like(r.bcp)
+    r.bcp[0 : CONV + 1] = r.conv_bc[...].astype(F32)[:, layer]
 
 
 def out_chain(links, wo):
@@ -1142,12 +1198,19 @@
     return Chain(links, [lambda i: wo.at[pl.ds(pl.multiple_of(i * rows, EDGE), rows), :]])
 
 
-def weight_swaps(links, shards, stagings, w, wo, inner):
+def weight_swaps(links, r, layer, w, steps, wo):
+    inner = wo.shape[1]
     cols = columns_of(inner)
+    stagings = r.stagings[layer]
+    here = pl.ds(pl.multiple_of(links.c * STATE, STATE), STATE)
     half = pl.ds(pl.multiple_of(cols.bc.start + links.c * STATE, STATE), STATE)
-    places = ((cols.x, inner), (cols.z, inner), (cols.dt, STATE), (half, STATE))
-    swaps = [Swap(links, shards[i], stagings[i], w, *places[i]) for i in range(4)]
-    return swaps, Swap(links, shards[4], stagings[4], wo, slice(0, inner), inner)
+    swaps = [
+        Swap(links, r.w_zx.at[layer, 1], stagings[0], w, cols.x, inner),
+        Swap(links, r.w_zx.at[layer, 0], stagings[1], w, cols.z, inner),
+        Swap(links, r.w_bc.at[layer, :, here], stagings[2], w, half, STATE),
+        Swap(links, r.packed_steps.at[layer], stagings[3], steps, slice(0, 128), 128),
+    ]
+    return swaps, Swap(links, r.w_out.at[layer], stagings[4], wo, slice(0, inner), inner)
 
 
 def scatter_blocks(scatter, compute):
@@ -1163,7 +1226,7 @@
 def forward_layer(links, r, normed, w, wo, wo_chain, scatter, meanwhile):
     carried = States(links, False, r.state_low, r.decay_row, r.states_in, r.decays_in)
     state_sum, decay_all = project_and_convolve(
-        links.p, normed, w, r.rowp, r.bcp, r.headp, r.z, r.xin, r.bcin, r.x, r.bc, r.dtraw, r.dt, r.s, r.decay, r.ext, r.local,
+        normed, w, r.rowp, r.bcp, r.headp, r.z, r.xin, r.bcin, r.x, r.bc, r.dtraw, r.dt, r.s, r.decay, r.ext, r.local,
         lambda q: pl.when(q == 3)(wo_chain.advance),
     )
     r.state_low[...] = state_sum.astype(BF16)
@@ -1187,27 +1250,31 @@
     links = Links(r.sends, r.recvs)
     c = links.c
     inner = r.wo.shape[1]
-    swaps, swap_o = weight_swaps(links, r.shards[0], r.stagings[0], r.w, r.wo, inner)
-    next_swaps, next_o = weight_swaps(links, r.shards[1], r.stagings[1], r.next_w, r.next_wo, inner)
+    shard = r.w_dt.shape[2]
+    links.greet(plane=True, groups=True, edge=1)
+    for layer in range(2):
+        pack_steps(r.w_dt[layer], r.packed_steps.at[layer], r.wide_steps)
+    swaps, swap_o = weight_swaps(links, r, 0, r.w, r.dt_rows, r.wo)
+    next_swaps, next_o = weight_swaps(links, r, 1, r.next_w, r.next_dt_rows, r.next_wo)
     all_swaps = swaps + [swap_o] + next_swaps + [next_o]
     gather, other = Gather(links, r.normed, EDGE), Gather(links, r.dmix, 0)
     edge = EdgeForward(links, gather)
-    chain, share = weight_chain(links, r.w, inner)
+    chain, share = weight_chain(links, r.w, r.dt_rows, inner)
     chain_o = out_chain(links, r.wo)
-    next_chain, next_share = weight_chain(links, r.next_w, inner)
+    next_chain, next_share = weight_chain(links, r.next_w, r.next_dt_rows, inner)
     scatter = Scatter(links, r.part, 0, r.sib, r.total, r.peer)
     small = SmallSum(links, r.squares, r.slots)
     next_gather = Gather(links, r.next_normed, EDGE)
     next_edge = EdgeForward(links, next_gather)
 
-    links.greet(plane=True, groups=True, edge=1)
+    prepare(links, r, 0)
     for swap in all_swaps:
         swap.keep.start()
     for start, size in row_chunks():
         at = pl.ds(pl.multiple_of(c * HALF + start, EDGE), size)
         rows_in = r.resid[at, :].astype(F32)
         r.resid_out[start : start + size] = rows_in
-        r.normed[gather.own(start, size), :] = (rows_in * rms_of(rows_in) * r.gain[...]).astype(BF16)
+        r.normed[gather.own(start, size), :] = (rows_in * rms_of(rows_in) * r.gains[0:1]).astype(BF16)
         rows_in = r.cot[at, :]
         r.cot_out[start : start + size] = rows_in.astype(F32)
         r.dmix[other.own(start, size), :] = rows_in
@@ -1232,6 +1299,7 @@
     share.start()
     chain_o.begin()
     other.start()
+    unpack_steps(r.dt_rows, r.w, shard, inner)
     r.flush(r.normed)
     share.wait()
     r.flush(r.w)
@@ -1257,7 +1325,7 @@
         r.mixed_out[at] = mixed
         fresh = r.resid_out[at] + column[at] * mixed
         r.fresh_out[at] = fresh
-        r.next_normed[next_gather.own(start, size), :] = (fresh * rms_of(fresh) * r.next_gain[...]).astype(BF16)
+        r.next_normed[next_gather.own(start, size), :] = (fresh * rms_of(fresh) * r.gains[1:2]).astype(BF16)
     next_gather.start()
     next_edge.start()
     other.finish()
@@ -1266,6 +1334,7 @@
     next_gather.pass_on()
     next_chain.complete()
     next_share.start()
+    unpack_steps(r.next_dt_rows, r.next_w, shard, inner)
     scatter.finish()
     small.finish()
     next_gather.finish()
@@ -1291,6 +1360,7 @@
     share = links.copy(r.block_out.at[at, :], r.block_out.at[at, :], links.at(0, 1))
     keep.start()
     links.greet(plane=True, groups=True)
+    prepare(links, r, 1)
     keep.wait()
     links.meet()
     chain_o.begin()
@@ -1343,7 +1413,7 @@
     r.need(r.states, r.dtraw, r.xin, r.bcin)
     back_through_states(
         grad, r.prior, r.decay, r.states, r.dy, r.x, r.bc, r.s, r.dt, r.dtraw, r.xin, r.bcin, r.rowp, r.bcp, r.headp,
-        r.flow, r.sums, links.p, r.cat, r.steps, r.wide, r.bc_rows, r.dpre, r.prior,
+        r.flow, r.sums, r.cat, r.wide, r.bc_rows, r.dpre, r.prior,
     )
     return carried, collect
 
@@ -1362,9 +1432,10 @@
     edge = EdgeBackward(links, r.part, r.edge_slots)
     gather = Gather(links, r.dmix_out, 0)
     spread = SmallGather(links, r.scalars_out)
-    collects = [Collect(links, r.gx, r.gx_parts), Collect(links, r.gz, r.gz_parts)]
+    collects = [Collect(links, r.gx, r.gx_parts), Collect(links, r.gwo, r.gz_parts)]
     r.edge_slots[...] = jnp.zeros_like(r.edge_slots)
     links.greet(plane=True, groups=True, edge=-1)
+    prepare(links, r, 1)
     carried, collect = backward_layer(links, inner_all, r, lambda: None, lambda: None, lambda: None)
     r.need(r.w, r.normed)
     x_gradient(r.cat, r.normed, r.gx)
@@ -1373,9 +1444,10 @@
     edge.start()
     scatter_blocks(scatter, lambda q: project_back(q, r.cat, r.w, r.part))
     scatter.pass_on(0)
-    z_gradient(r.cat, r.normed, r.gz)
+    collect.finish()
+    z_gradient(r.cat, r.normed, r.gwo)
     collects[1].start()
-    small_gradients(r.cat, r.steps, r.normed, r.gbc, r.gdt)
+    small_gradients(r.cat, r.normed, r.gbc, r.gdt)
     scatter.arrive()
     edge.receive()
     r.need(r.grad, r.resid, r.mixed)
@@ -1383,7 +1455,7 @@
     dots = []
     for start, size in row_chunks():
         at = slice(start, start + size)
-        fresh = grad_rows(links, scatter, r.edge_slots, r.grad, r.resid, r.gain, r.gain_row, start, size)
+        fresh = grad_rows(links, scatter, r.edge_slots, r.grad, r.resid, r.gains[1:2], r.gain_row, start, size)
         r.grad_out[at] = fresh
         low = fresh.astype(BF16)
         r.dmix_out[gather.own(start, size), :] = low
@@ -1403,6 +1475,7 @@
     carried.finish()
     for one in [collect] + collects:
         one.arrive()
+    for one in collects:
         one.finish()
 
 
@@ -1413,9 +1486,9 @@
     edge = EdgeBackward(links, r.part, r.edge_slots)
     at = pl.ds(pl.multiple_of(links.c * HALF, HALF), HALF)
     share = links.copy(r.out.at[at, :], r.out.at[at, :], links.at(0, 1))
-    collects = [Collect(links, r.gx, r.gx_parts), Collect(links, r.gz, r.gz_parts)]
-    above = zip((r.above_x, r.above_z, r.above_o), r.big_out[1])
-    own = ((r.go_parts, r.big_out[0][2]), (r.gx_parts, r.big_out[0][0]), (r.gz_parts, r.big_out[0][1]))
+    collects = [Collect(links, r.gx, r.gx_parts), Collect(links, r.gwo, r.gz_parts)]
+    above = ((r.above_x, r.g_zx.at[1, 1]), (r.above_z, r.g_zx.at[1, 0]), (r.above_o, r.g_out.at[1]))
+    own = ((r.go_parts, r.g_out.at[0]), (r.gx_parts, r.g_zx.at[0, 1]), (r.gz_parts, r.g_zx.at[0, 0]))
     delivers = [Deliver(links, parts, r.final.at[i], out) for i, (parts, out) in enumerate(above)]
     own_delivers = [Deliver(links, parts, r.final.at[3 + i], out) for i, (parts, out) in enumerate(own)]
     bc_sums = [
@@ -1426,6 +1499,7 @@
     vec_sum = VecSum(links, r.vec, r.vec_out, r.vec_near, r.vec_far)
     r.edge_slots[...] = jnp.zeros_like(r.edge_slots)
     links.greet(plane=True, groups=True, edge=-1)
+    prepare(links, r, 0)
 
     def at_start():
         r.need(r.above_bc)
@@ -1439,7 +1513,7 @@
 
     carried, collect = backward_layer(links, inner_all, r, at_start, bc_sums[1].plane, at_middle)
     r.need(r.normed)
-    small_gradients(r.cat, r.steps, r.normed, r.gbc, r.gdt)
+    small_gradients(r.cat, r.normed, r.gbc, r.gdt)
     bc_sums[0].cores()
     r.steps_all[:, 0:EDGE, :] = r.gdt[...]
     r.steps_all[:, EDGE:, :] = r.above_dt[...]
@@ -1455,13 +1529,15 @@
     scatter_blocks(scatter, lambda q: project_back(q, r.cat, r.w, r.part))
     scatter.pass_on(0)
     bc_sums[0].groups()
-    z_gradient(r.cat, r.normed, r.gz)
+    collect.finish()
+    z_gradient(r.cat, r.normed, r.gwo)
+    collects[1].start()
     scatter.arrive()
     edge.receive()
     r.need(r.grad, r.resid)
     r.gain_row[...] = jnp.zeros_like(r.gain_row)
     for start, size in row_chunks():
-        fresh = grad_rows(links, scatter, r.edge_slots, r.grad, r.resid, r.gain, r.gain_row, start, size)
+        fresh = grad_rows(links, scatter, r.edge_slots, r.grad, r.resid, r.gains[0:1], r.gain_row, start, size)
         r.out[pl.ds(pl.multiple_of(links.c * HALF + start, EDGE), size), :] = fresh.astype(BF16)
     share.start()
     r.vec[...] = r.above_vec[...]
@@ -1469,22 +1545,73 @@
     put_vector(r.vec, 2 * (r.gain_row.shape[1] // 128), r.bc_rows[0 : CONV + 1])
     vec_sum.plane()
     vec_sum.groups()
-    collects[1].start()
     collect.arrive()
     own_delivers[0].start()
     bc_sums[1].share()
     laid.plane()
     collects[0].arrive()
     own_delivers[1].start()
+    laid.finish()
+    lay_out_heads(links, r)
     bc_sums[0].share()
-    vec_sum.back()
     collects[1].arrive()
     own_delivers[2].start()
-    for one in bc_sums + [laid, vec_sum, scatter, edge, carried, collect] + collects:
+    vec_sum.back()
+    for one in bc_sums + [scatter, edge, carried] + collects:
         one.finish()
+    vec_sum.finish()
+    lay_out_vector(r)
     share.wait()
     for deliver in delivers + own_delivers:
+        deliver.arrive()
         deliver.finish()
+
+
+def lay_out_heads(links, r):
+    inner = r.wide.shape[1]
+    heads = inner // HEADDIM
+    heads_core, shard = r.g_dt.shape[1:]
+    spread = head_spread(inner).astype(F32)
+    row, col = iota((128, 128), 0), iota((128, 128), 1)
+    blank = jnp.zeros((128 - 2 * EDGE, r.dt_out.shape[2]), F32)
+    steps = [jnp.zeros((shard, 128), F32) for _ in range(2)]
+    tall = [jnp.zeros((8, 128), F32) for _ in range(2)]
+    for q in range(GROUP):
+        lanes = slice(q * inner, q * inner + inner)
+        r.step_rows[...] = jnp.concatenate([r.dt_out[q].astype(F32), blank]).T
+        mine = r.step_rows[pl.ds(pl.multiple_of(links.p * shard, 8), shard), :]
+        gains, taps = [], []
+        for layer in range(2):
+            first, second = r.wide_out[q, 16 * layer : 16 * layer + 8], r.wide_out[q, 16 * layer + 8 : 16 * layer + 16]
+            taps.append(first[0 : CONV + 1])
+            gains.append(first[5:6])
+            place = jnp.logical_and(row - EDGE * layer == col - q * heads, jnp.logical_and(row >= EDGE * layer, row < EDGE * layer + heads))
+            steps[layer] = steps[layer] + dot_exact(mine, place.astype(F32))
+            place = jnp.logical_and(row == col - q * heads, row < heads).astype(F32)
+            skip = dot_exact(first, spread, NT)[6:7]
+            rows = jnp.concatenate([first[7:8, 0:128], second[0:1, 0:128], skip, jnp.zeros((5, 128), F32)])
+            tall[layer] = tall[layer] + dot_exact(rows, place)
+        for j in range(CONV + 1):
+            r.g_conv_x[j, :, lanes] = jnp.concatenate([tap[j : j + 1] for tap in taps]).astype(BF16)
+        r.g_gain[:, lanes] = jnp.concatenate(gains).astype(BF16)
+    for layer in range(2):
+        r.g_dt[layer] = steps[layer].T[0:heads_core].astype(BF16)
+    for i in range(3):
+        r.g_head[i] = jnp.concatenate([one[i : i + 1, 0:heads_core] for one in tall]).astype(BF16)
+
+
+def lay_out_vector(r):
+    def row(i):
+        return r.vec_out[i // 8, i % 8 : i % 8 + 1, :]
+
+    count = r.g_norm.shape[1] // 128
+    for i in range(count):
+        r.g_norm[:, i * 128 : i * 128 + 128] = jnp.concatenate([row(i), row(count + i)]).astype(BF16)
+    for half in range(2):
+        for j in range(CONV + 1):
+            firsts = [2 * count + layer * 2 * (CONV + 1) + 2 * j + half for layer in range(2)]
+            rows = jnp.concatenate([row(first) for first in firsts])
+            r.g_conv_bc[j, :, half * 128 : half * 128 + 128] = rows.astype(BF16)
 
 
 def flat(value):
@@ -1529,38 +1656,15 @@
 def on_device(resid_in, cotangent, norm_gain, w_zx, w_dt, w_bc, conv_x, conv_bc, head_params, gated_gain, w_out):
     layers, model = norm_gain.shape
     groups = lax.axis_size("z")
-    level, place, core = lax.axis_index("z"), lax.axis_index("p"), lax.axis_index("head")
     shard = w_dt.shape[1]
     inner_core = conv_x.shape[2]
     inner = inner_core // GROUP
     heads_core = head_params.shape[2]
-    heads = heads_core // GROUP
     inner_all = inner_core * lax.axis_size("head")
     length = resid_in.shape[1]
     tokens = GROUP * length
     spans = tokens // SPAN
     rows = GROUP * shard
-
-    def my_part(array, size):
-        return lax.dynamic_slice_in_dim(array, place * size, size, array.ndim - 1)
-
-    row_all, bc_all, head_all = [], [], []
-    conv_mine = my_part(conv_x, inner).astype(F32)
-    gain_mine = my_part(gated_gain, inner).astype(F32)
-    head_mine = my_part(head_params, heads)
-    gains = [norm_gain[layer].astype(F32)[None] for layer in range(layers)]
-    for layer in range(layers):
-        skip = jnp.repeat(head_mine[layer, 2], HEADDIM)
-        row_all.append(
-            jnp.concatenate([conv_mine[layer], gain_mine[layer][None], skip[None], jnp.zeros((1, inner), F32)])
-        )
-        bc_all.append(jnp.pad(conv_bc[layer].astype(F32), ((0, 3), (0, 0))))
-        head_all.append(jnp.pad(head_mine[layer], ((0, 5), (0, 128 - heads))))
-
-    def shards_of(layer):
-        half = lax.dynamic_slice_in_dim(w_bc[layer], core * STATE, STATE, 1)
-        steps = jnp.pad(w_dt[layer], ((0, 0), (0, STATE - heads_core)))
-        return w_zx[layer, 1], w_zx[layer, 0], steps, half, w_out[layer].T
 
     own_rows = ((HALF, model), F32)
     all_rows, edged_rows = ((tokens, model), BF16), ((tokens + EDGE, model), BF16)
@@ -1603,17 +1707,25 @@
         **scatter_scratch,
     )
 
-    def params(layer):
-        return dict(rowp=row_all[layer], bcp=bc_all[layer], headp=head_all[layer])
-
-    stagings = [((GROUP, shard, width), BF16) for width in (inner, inner, STATE, STATE, inner)]
+    conv_x, conv_bc, head_params = [jnp.swapaxes(a, 0, 1) for a in (conv_x, conv_bc, head_params)]
+    w_dt, w_out = jnp.swapaxes(w_dt, 1, 2), jnp.swapaxes(w_out, 1, 2)
+    params = dict(
+        norm_gain=norm_gain, conv_x=conv_x, conv_bc=conv_bc, head_params=head_params, gated_gain=gated_gain
+    )
+    param_scratch = dict(
+        rowp=((8, inner), F32), bcp=((8, 2 * STATE), F32), headp=((8, 128), F32), gains=((layers, model), F32)
+    )
+    stagings = [((GROUP, rows_in, width), BF16) for rows_in, width in (
+        (shard, inner), (shard, inner), (shard, STATE), (EDGE, 128), (shard, inner)
+    )]
+    step_rows = ((groups * GROUP * EDGE, 128), BF16)
     first = call(
         functools.partial(first_kernel, inner_all),
         0,
         160 + 14 * (groups - 1) + 2 * groups,
         dict(
             next_w=w_shape,
-            next_wo=wo_shape,
+            next_wo=((rows, inner), BF16),
             next_normed=edged_rows,
             resid_out=own_rows,
             cot_out=own_rows,
@@ -1625,13 +1737,22 @@
         dict(
             resid=resid_in[0],
             cot=cotangent[0],
-            gain=gains[0],
-            next_gain=gains[1],
-            **params(0),
-            shards=[list(shards_of(0)), list(shards_of(1))],
+            w_zx=w_zx,
+            w_dt=w_dt,
+            w_bc=w_bc,
+            w_out=w_out,
+            **params,
         ),
         dict(),
-        dict(**forward_scratch, stagings=[stagings, stagings]),
+        dict(
+            **forward_scratch,
+            **param_scratch,
+            stagings=[stagings, stagings],
+            dt_rows=step_rows,
+            next_dt_rows=step_rows,
+            packed_steps=((layers, GROUP, EDGE, 128), BF16),
+            wide_steps=((128, 128), BF16),
+        ),
     )
     second = call(
         functools.partial(second_kernel, inner_all),
@@ -1642,13 +1763,13 @@
         dict(
             normed=first.next_normed,
             w=first.next_w,
-            wo_own=lax.dynamic_slice_in_dim(first.next_wo, level * rows, rows, 0),
-            **params(1),
+            wo_own=first.next_wo,
+            **params,
             resid=first.fresh_out,
             cot=first.cot_out,
         ),
         dict(),
-        forward_scratch,
+        dict(**forward_scratch, **param_scratch),
     )
     grad_parts = ((groups, rows, inner), BF16)
     bc_grad = ((groups, GROUP, shard, 2 * STATE), BF16)
@@ -1664,16 +1785,16 @@
         flow=steps_shape,
         sums=steps_shape,
         cat=((tokens + EDGE, columns), BF16),
-        steps=((tokens, 128), BF16),
         bc_rows=((8, 2 * STATE), F32),
         part=edged_rows,
         gx=wo_shape,
-        gz=wo_shape,
         gain_row=((8, model), F32),
         edge_slots=((2 * GROUP, EDGE, model), BF16),
         **state_scratch,
+        **param_scratch,
         **scatter_scratch,
     )
+
     def at_once(run):
         return dict(y=run.y, z=run.z, x=run.x, bc=run.bc, s=run.s, decay=run.decay)
 
@@ -1701,8 +1822,7 @@
             dmix=first.dmix,
             scalars=second.scalars_out,
             wo=second.wo,
-            **params(1),
-            gain=gains[1],
+            **params,
             inv=first.inv_out,
             **at_once(second),
         ),
@@ -1717,7 +1837,6 @@
         back_scratch,
     )
     far = groups - 1
-    rows_shape = ((shard, inner_core), BF16)
     dt_shape, wide_shape = (layers * EDGE, rows), (layers * 16, inner)
     half_bc = (groups, GROUP, shard, STATE)
     bc_bufs = [
@@ -1733,19 +1852,22 @@
         130 + 14 * groups,
         dict(
             out=((length, model), BF16),
-            big_out=[[rows_shape] * 3] * layers,
             bc_out=((layers, shard, 2 * STATE), BF16),
-            vec_out=vec_shape,
-            dt_out=((GROUP, *dt_shape), BF16),
-            wide_out=((GROUP, *wide_shape), F32),
+            g_norm=(norm_gain.shape, BF16),
+            g_zx=(w_zx.shape, BF16),
+            g_dt=(w_dt.shape, BF16),
+            g_conv_x=(conv_x.shape, BF16),
+            g_conv_bc=(conv_bc.shape, BF16),
+            g_head=(head_params.shape, BF16),
+            g_gain=(gated_gain.shape, BF16),
+            g_out=(w_out.shape, BF16),
         ),
         dict(),
         dict(
             dmix=third.dmix_out,
             scalars=third.scalars_out,
             wo=first.wo,
-            **params(0),
-            gain=gains[0],
+            **params,
             above_dt=third.gdt,
             above_wide=third.wide,
             above_vec=third.vec,
@@ -1764,6 +1886,10 @@
         ),
         dict(
             **back_scratch,
+            vec_out=vec_shape,
+            dt_out=((GROUP, *dt_shape), BF16),
+            wide_out=((GROUP, *wide_shape), F32),
+            step_rows=((rows, 128), F32),
             go_parts=grad_parts,
             gx_parts=grad_parts,
             gz_parts=grad_parts,
@@ -1781,32 +1907,16 @@
             wide_far=((far, *wide_shape), F32),
         ),
     )
-    block_out, grad_input, g_bc = second.block_out, fourth.out, fourth.bc_out
-    vec, g_dt, wide = fourth.vec_out, fourth.dt_out, fourth.wide_out
-    delivered = fourth.big_out
-    vec = vec.reshape(-1)
-    grad_gain = vec[: layers * model].reshape(layers, model)
-    grad_conv_bc = vec[layers * model :][: layers * (CONV + 1) * 2 * STATE].reshape(layers, CONV + 1, 2 * STATE)
-    wide = wide.reshape(GROUP, layers, 16, inner)
-    whole = jnp.moveaxis(wide, 0, 2).reshape(layers, 16, inner_core)
-    skip_grad = jnp.sum(whole[:, CONV + 2].reshape(layers, heads_core, HEADDIM), axis=-1)
-    tall = jnp.moveaxis(wide[:, :, CONV + 3 : CONV + 5, :heads], 0, 2).reshape(layers, 2, heads_core)
-    grad_heads = jnp.concatenate([tall, skip_grad[:, None]], axis=1)
-    g_dt = lax.dynamic_slice_in_dim(g_dt.reshape(GROUP, layers, EDGE, GROUP, shard), place, 1, 3)[:, :, :heads, 0]
-    grad_dt = jnp.transpose(g_dt, (1, 3, 0, 2)).reshape(layers, shard, heads_core)
-    low = lambda a: a.astype(BF16)
     return (
-        block_out[None],
-        grad_input[None],
-        low(grad_gain),
-        jnp.stack([jnp.stack([delivered[layer][1], delivered[layer][0]]) for layer in range(layers)]),
-        grad_dt,
-        g_bc,
-        low(whole[:, : CONV + 1]),
-        low(grad_conv_bc),
-        low(grad_heads),
-        low(whole[:, CONV + 1]),
-        jnp.stack([delivered[layer][2].T for layer in range(layers)]),
+        second.block_out[None],
+        fourth.out[None],
+        fourth.g_norm,
+        fourth.g_zx,
+        jnp.swapaxes(fourth.g_dt, 1, 2),
+        fourth.bc_out,
+        *[jnp.swapaxes(a, 0, 1) for a in (fourth.g_conv_x, fourth.g_conv_bc, fourth.g_head)],
+        fourth.g_gain,
+        jnp.swapaxes(fourth.g_out, 1, 2),
     )
 
 

time: 481 us -> 447 us (0.929)
  the two profiles are of different devices: /device:TPU:25 before, /device:TPU:9 now
where the time goes in v6:
time: 447 us; the launch traced here: 441 us
  Pallas kernels  431 us (96%)
  local copies, waits for them, and re-layouts  8.32 us (2%)
    pallas_call x4, Pallas kernels, call(): pl.pallas_call(kernel, out_shape=tuple((jax.ShapeDtypeStruct(*a) for a in...  431 us

profile of v6, /device:TPU:9, one launch (start us, length us, event | category | flops | bytes accessed | tf_op | source)
XLA Modules:
  0.0 440.6 jit_solution(18115623536771893982)
XLA Ops:
  0.6 133.5 %shard_map.194 = (bf16[1536,1152]{1,0:T(8,128)(2,1)}, bf16[384,384]{1,0:T(8,128)(2,1)}, bf16[1040,1536]{1,0:T(8,128)(2,1)}, f32[128,1536]{1,0:T(8,128)}, f32[128...) custom-call(bf16[256,1536]{1,0:T(8,128)(2,1)} %bitcast.16, ...), custom_call_target="tpu_custom_call" | custom-call | tf_op jit(solution)/shard_map/pallas_call | solution.py:1641
  134.2 69.9 %shard_map.195 = (bf16[256,1536]{1,0:T(8,128)(2,1)}, f32[8,1024]{1,0:T(8,128)}, bf16[1536,384]{1,0:T(8,128)(2,1)}, f32[1024,384]{1,0:T(8,128)}, bf16[1024,384]{1...) custom-call(bf16[1040,1536]{1,0:T(8,128)(2,1)} %get-tuple-element.68, ...), custom_call_target="tpu_custom_call" | custom-call | tf_op jit(solution)/shard_map/pallas_call | solution.py:1641
  204.1 108.7 %shard_map.196 = (bf16[1024,1536]{1,0:T(8,128)(2,1)}, f32[8,1024]{1,0:T(8,128)}, f32[128,1536]{1,0:T(8,128)}, bf16[4,384,384]{2,1,0:T(8,128)(2,1)}, bf16[4,384,3...) custom-call(bf16[1024,1536]{1,0:T(8,128)(2,1)} %get-tuple-element.74, ...), custom_call_target="tpu_custom_call" | custom-call | tf_op jit(solution)/shard_map/pallas_call | solution.py:1641
  312.8 119.2 %shard_map.197 = (bf16[256,1536]{1,0:T(8,128)(2,1)}, bf16[2,96,256]{2,1,0:T(8,128)(2,1)}, bf16[2,1536]{1,0:T(2,128)(2,1)}, bf16[2,2,96,1536]{3,2,1,0:T(8,128)(2,...) custom-call(bf16[1024,1536]{1,0:T(8,128)(2,1)} %get-tuple-element.90, ...), custom_call_target="tpu_custom_call" | custom-call | tf_op jit(solution)/shard_map/pallas_call | solution.py:1641
  432.0 0.9 copy.33
  432.9 0.5 copy-done.2
  433.4 0.9 copy.34
  434.3 0.0 copy-done.8
  434.3 0.0 copy-start.9
  434.3 0.0 copy-start.10
  434.3 0.0 copy-start.7
  434.3 0.0 copy-start.3
  434.4 0.6 copy.35
  435.0 1.0 copy.36
  436.0 0.6 copy.37
  436.6 0.0 copy-done.4
  436.6 0.6 copy.38
  437.2 0.6 copy.39
  437.8 0.6 copy.40
  438.4 0.0 copy-done.10
  438.4 0.6 copy.41
  439.0 0.0 copy-done.7
  439.0 0.6 copy.42
  439.6 0.8 copy.43
  (13 shorter events, 0.0 us)
Async XLA Ops:
  312.8 119.2 %copy-start.1 = (bf16[256,1536]{1,0:T(8,128)(2,1)S(1)}, bf16[256,1536]{1,0:T(8,128)(2,1)}, u32[]{:S(2)}) copy-start(bf16[256,1536]{1,0:T(8,128)(2,1)} %get-tuple-element.73) | copy-start | bytes 2359300
  432.0 1.4 copy-start.2
  432.0 2.3 copy-start.8
  432.0 2.9 copy-start
  434.3 1.7 copy-start.6
  434.3 2.3 copy-start.4
  434.3 2.9 copy-start.5
  434.3 3.5 copy-start.9
  434.3 4.1 copy-start.10
  434.3 4.7 %copy-start.7 = (bf16[2,1536]{1,0:T(2,128)(2,1)S(1)}, bf16[2,1536]{1,0:T(2,128)(2,1)}, u32[]{:S(2)}) copy-start(bf16[2,1536]{1,0:T(2,128)(2,1)} %get-tuple-element.145) | copy-start | bytes 18436
  434.3 5.2 %copy-start.3 = (bf16[2,96,1536]{2,1,0:T(8,128)(2,1)S(1)}, bf16[2,96,1536]{2,1,0:T(8,128)(2,1)}, u32[]{:S(2)}) copy-start(bf16[2,96,1536]{2,1,0:T(8,128)(2,1)} %get-tuple-element.124) | copy-start | bytes 1769476

commit v7 on v6

--- a/solution.py
+++ b/solution.py
@@ -318,7 +318,7 @@
 def back_through_states(
     grad, prior, decay, states, dy_in, x, bc, s_in, dt_in, dtraw, xin, bcin, rowp, bcp, headp, flow_in, sum_in,
     cat_out, row_out, bcrow_out,
-    dpre, dend,
+    dpre, dend, at_block,
 ):
     inner = x.shape[1]
     spans = x.shape[0] // SPAN
@@ -348,6 +348,7 @@
         tok = pl.ds(at, SPAN)
         after = pl.ds(pl.multiple_of(at + EDGE, EDGE), SPAN)
         window = pl.ds(at, SPAN + EDGE)
+        at_block(q)
         x_low, dy = x[tok, :], dy_in[tok, :]
         xf, dyf = x_low.astype(F32), dy.astype(F32)
         b, c = bc[tok, :STATE], bc[tok, STATE:]
@@ -620,62 +621,81 @@
             copy.wait_send()
 
 
-class Collect:
-    def __init__(self, links, grad, out):
-        rows = grad.shape[0] // links.groups
+class Halve:
+    def __init__(self, links, grad, arrived, sums):
+        self.links, self.grad, self.arrived, self.sums = links, grad, arrived, sums
         z, groups = links.z, links.groups
-
-        def block(index):
-            return grad.at[pl.ds(pl.multiple_of(index * rows, EDGE), rows)]
-
-        self.keep = links.local(block(z), out.at[0])
-        self.kept = False
-        self.copies = []
-        for k in range(1, groups):
-            to = lax.rem(z + k, groups)
-            self.copies.append(links.copy(block(to), out.at[k], (to, links.p, links.c)))
+        self.rows, self.steps, self.now = grad.shape[0] // groups, [], 0
+        first, bit = 0, 1
+        while bit < groups:
+            low = lax.rem(z, bit)
+            mine = lax.rem(lax.div(z, bit), 2)
+            device = (z + bit - 2 * bit * mine, links.p, links.c)
+            found = []
+            for j in range(groups // (2 * bit)):
+                away = j * 2 * bit + (1 - mine) * bit + low
+                kept = j * 2 * bit + mine * bit + low
+                copy = links.copy(self.held(away), arrived.at[first + j], device)
+                found.append((first + j, self.held(kept), copy))
+            self.steps.append(found)
+            self.before = (first, 2 * bit)
+            first, bit = first + groups // (2 * bit), 2 * bit
+
+    def held(self, target):
+        if not self.steps:
+            return self.grad.at[pl.ds(pl.multiple_of(target * self.rows, EDGE), self.rows), :]
+        first, size = self.before
+        return self.arrived.at[first + lax.div(target, size)]
+
+    def begin(self):
+        for _, _, copy in self.steps[0]:
+            copy.start()
+
+    def advance(self):
+        for slot, held, copy in self.steps[self.now]:
+            copy.wait_recv()
+
+            def add(i, _, slot=slot, held=held):
+                at = pl.ds(pl.multiple_of(i * 32, 32), 32)
+                total = self.arrived[slot, at, :].astype(F32) + held[at, :].astype(F32)
+                self.arrived[slot, at, :] = total.astype(BF16)
+                return 0
+
+            lax.fori_loop(0, self.rows // 32, add, 0)
+        self.now += 1
+        for _, _, copy in self.steps[self.now]:
+            copy.start()
+
+    def complete(self):
+        while self.now + 1 < len(self.steps):
+            self.advance()
+        ((slot, held, copy),) = self.steps[-1]
+        copy.wait_recv()
+        total = self.arrived[slot].astype(F32) + held[...].astype(F32)
+        shard = self.sums.shape[1]
+        for j in range(GROUP):
+            self.sums[j] = total[j * shard : (j + 1) * shard].astype(BF16)
+
+    def finish(self):
+        for found in self.steps:
+            for _, _, copy in found:
+                copy.wait_send()
+
+
+class Deliver:
+    def __init__(self, links, sums, out):
+        self.links, self.sums, self.out = links, sums, out
+        inner = sums.shape[2]
+        self.mine = pl.ds(pl.multiple_of(links.p * inner, 128), inner)
+        self.copies = [
+            links.copy(sums.at[lax.bitwise_xor(links.p, jnp.int32(k))], out.at[:, self.mine], links.at(k, 0))
+            for k in (3, 1, 2)
+        ]
 
     def start(self):
-        self.keep.start()
         for copy in self.copies:
             copy.start()
-
-    def keep_own(self):
-        if not self.kept:
-            self.keep.wait()
-        self.kept = True
-
-    def arrive(self):
-        self.keep_own()
-        for copy in self.copies:
-            copy.wait_recv()
-
-    def finish(self):
-        self.keep_own()
-        for copy in self.copies:
-            copy.wait_send()
-
-
-class Deliver:
-    def __init__(self, links, parts, final, out):
-        self.links, self.parts, self.final, self.out = links, parts, final, out
-        inner = parts.shape[2]
-        self.mine = pl.ds(pl.multiple_of(links.p * inner, 128), inner)
-        self.copies = [
-            links.copy(final.at[lax.bitwise_xor(links.p, jnp.int32(k))], out.at[:, self.mine], links.at(k, 0))
-            for k in (3, 1, 2)
-        ]
-
-    def start(self):
-        total = self.parts[0].astype(F32)
-        for k in range(1, self.parts.shape[0]):
-            total = total + self.parts[k].astype(F32)
-        shard = self.final.shape[1]
-        for j in range(GROUP):
-            self.final[j] = total[j * shard : (j + 1) * shard].astype(BF16)
-        for copy in self.copies:
-            copy.start()
-        self.out[:, self.mine] = self.final[self.links.p]
+        self.out[:, self.mine] = self.sums[self.links.p]
 
     def arrive(self):
         for copy in self.copies:
@@ -1392,7 +1412,7 @@
 
 def backward_layer(links, inner_all, r, at_start, before_collect, at_middle):
     carried = States(links, True, r.state_low, r.decay_row, r.states_in, r.decays_in)
-    collect = Collect(links, r.gwo, r.go_parts)
+    collect = Halve(links, r.gwo, r.go_in, r.go_sum)
     grad_sum, decay_all = back_through_gate(
         inner_all, r.dmix, r.wo, r.y, r.z, r.x, r.bc, r.s, r.decay, r.scalars, r.rowp,
         r.cat, r.wide, r.dy, r.prior, r.normed_out,
@@ -1404,7 +1424,7 @@
     at_start()
     out_gradient(r.dmix, r.normed_out, r.gwo)
     before_collect()
-    collect.start()
+    collect.begin()
     r.need(r.dt)
     back_within_spans(r.dy, r.x, r.bc, r.s, r.dt, r.dpre, r.flow, r.sums)
     at_middle()
@@ -1414,6 +1434,7 @@
     back_through_states(
         grad, r.prior, r.decay, r.states, r.dy, r.x, r.bc, r.s, r.dt, r.dtraw, r.xin, r.bcin, r.rowp, r.bcp, r.headp,
         r.flow, r.sums, r.cat, r.wide, r.bc_rows, r.dpre, r.prior,
+        lambda q: pl.when(q == 2)(collect.advance),
     )
     return carried, collect
 
@@ -1432,22 +1453,24 @@
     edge = EdgeBackward(links, r.part, r.edge_slots)
     gather = Gather(links, r.dmix_out, 0)
     spread = SmallGather(links, r.scalars_out)
-    collects = [Collect(links, r.gx, r.gx_parts), Collect(links, r.gwo, r.gz_parts)]
+    collects = [Halve(links, r.gx, r.gx_in, r.gx_sum), Halve(links, r.gwo, r.gz_in, r.gz_sum)]
     r.edge_slots[...] = jnp.zeros_like(r.edge_slots)
     links.greet(plane=True, groups=True, edge=-1)
     prepare(links, r, 1)
     carried, collect = backward_layer(links, inner_all, r, lambda: None, lambda: None, lambda: None)
     r.need(r.w, r.normed)
     x_gradient(r.cat, r.normed, r.gx)
-    collects[0].start()
+    collects[0].begin()
     project_back_edge(r.cat, r.w, r.part)
     edge.start()
     scatter_blocks(scatter, lambda q: project_back(q, r.cat, r.w, r.part))
     scatter.pass_on(0)
+    small_gradients(r.cat, r.normed, r.gbc, r.gdt)
+    collect.complete()
     collect.finish()
     z_gradient(r.cat, r.normed, r.gwo)
-    collects[1].start()
-    small_gradients(r.cat, r.normed, r.gbc, r.gdt)
+    collects[1].begin()
+    collects[0].advance()
     scatter.arrive()
     edge.receive()
     r.need(r.grad, r.resid, r.mixed)
@@ -1467,14 +1490,15 @@
     model = r.gain_row.shape[1]
     put_vector(r.vec, model // 128, r.gain_row[0:1])
     put_vector(r.vec, 2 * (model // 128) + 2 * (CONV + 1), r.bc_rows[0 : CONV + 1])
+    collects[1].advance()
     gather.pass_on()
+    collects[0].complete()
     scatter.finish()
     edge.finish()
     gather.finish()
     spread.finish()
     carried.finish()
-    for one in [collect] + collects:
-        one.arrive()
+    collects[1].complete()
     for one in collects:
         one.finish()
 
@@ -1486,11 +1510,11 @@
     edge = EdgeBackward(links, r.part, r.edge_slots)
     at = pl.ds(pl.multiple_of(links.c * HALF, HALF), HALF)
     share = links.copy(r.out.at[at, :], r.out.at[at, :], links.at(0, 1))
-    collects = [Collect(links, r.gx, r.gx_parts), Collect(links, r.gwo, r.gz_parts)]
+    collects = [Halve(links, r.gx, r.gx_in, r.gx_sum), Halve(links, r.gwo, r.gz_in, r.gz_sum)]
     above = ((r.above_x, r.g_zx.at[1, 1]), (r.above_z, r.g_zx.at[1, 0]), (r.above_o, r.g_out.at[1]))
-    own = ((r.go_parts, r.g_out.at[0]), (r.gx_parts, r.g_zx.at[0, 1]), (r.gz_parts, r.g_zx.at[0, 0]))
-    delivers = [Deliver(links, parts, r.final.at[i], out) for i, (parts, out) in enumerate(above)]
-    own_delivers = [Deliver(links, parts, r.final.at[3 + i], out) for i, (parts, out) in enumerate(own)]
+    own = ((r.go_sum, r.g_out.at[0]), (r.gx_sum, r.g_zx.at[0, 1]), (r.gz_sum, r.g_zx.at[0, 0]))
+    delivers = [Deliver(links, parts, out) for parts, out in above]
+    own_delivers = [Deliver(links, parts, out) for parts, out in own]
     bc_sums = [
         BcSum(links, bc, r.bc_out.at[i], r.bc_bufs[i])
         for i, bc in enumerate((r.gbc, r.above_bc))
@@ -1521,7 +1545,7 @@
     r.wide_all[16:32] = r.above_wide[...]
     laid.groups()
     x_gradient(r.cat, r.normed, r.gx)
-    collects[0].start()
+    collects[0].begin()
     bc_sums[0].plane()
     r.need(r.w)
     project_back_edge(r.cat, r.w, r.part)
@@ -1529,9 +1553,12 @@
     scatter_blocks(scatter, lambda q: project_back(q, r.cat, r.w, r.part))
     scatter.pass_on(0)
     bc_sums[0].groups()
+    collect.complete()
     collect.finish()
     z_gradient(r.cat, r.normed, r.gwo)
-    collects[1].start()
+    collects[1].begin()
+    collects[0].advance()
+    own_delivers[0].start()
     scatter.arrive()
     edge.receive()
     r.need(r.grad, r.resid)
@@ -1545,18 +1572,17 @@
     put_vector(r.vec, 2 * (r.gain_row.shape[1] // 128), r.bc_rows[0 : CONV + 1])
     vec_sum.plane()
     vec_sum.groups()
-    collect.arrive()
-    own_delivers[0].start()
+    collects[1].advance()
     bc_sums[1].share()
     laid.plane()
-    collects[0].arrive()
+    collects[0].complete()
     own_delivers[1].start()
     laid.finish()
     lay_out_heads(links, r)
     bc_sums[0].share()
-    collects[1].arrive()
+    vec_sum.back()
+    collects[1].complete()
     own_delivers[2].start()
-    vec_sum.back()
     for one in bc_sums + [scatter, edge, carried] + collects:
         one.finish()
     vec_sum.finish()
@@ -1771,7 +1797,8 @@
         dict(),
         dict(**forward_scratch, **param_scratch),
     )
-    grad_parts = ((groups, rows, inner), BF16)
+    grad_in = ((groups - 1, rows, inner), BF16)
+    grad_sum = ((GROUP, shard, inner), BF16)
     bc_grad = ((groups, GROUP, shard, 2 * STATE), BF16)
     dt_grad = ((groups, EDGE, rows), BF16)
     wide_grad = ((16, inner), F32)
@@ -1788,6 +1815,9 @@
         bc_rows=((8, 2 * STATE), F32),
         part=edged_rows,
         gx=wo_shape,
+        go_in=grad_in,
+        gx_in=grad_in,
+        gz_in=grad_in,
         gain_row=((8, model), F32),
         edge_slots=((2 * GROUP, EDGE, model), BF16),
         **state_scratch,
@@ -1809,9 +1839,9 @@
             dmix_out=all_rows,
             scalars_out=scalars,
             grad_out=own_rows,
-            go_parts=grad_parts,
-            gx_parts=grad_parts,
-            gz_parts=grad_parts,
+            go_sum=grad_sum,
+            gx_sum=grad_sum,
+            gz_sum=grad_sum,
             gbc=bc_grad,
             gdt=dt_grad,
             wide=wide_grad,
@@ -1878,9 +1908,9 @@
             normed=first.normed,
             grad=third.grad_out,
             resid=first.resid_out,
-            above_x=third.gx_parts,
-            above_z=third.gz_parts,
-            above_o=third.go_parts,
+            above_x=third.gx_sum,
+            above_z=third.gz_sum,
+            above_o=third.go_sum,
             above_bc=third.gbc,
             **later(first),
         ),
@@ -1890,10 +1920,9 @@
             dt_out=((GROUP, *dt_shape), BF16),
             wide_out=((GROUP, *wide_shape), F32),
             step_rows=((rows, 128), F32),
-            go_parts=grad_parts,
-            gx_parts=grad_parts,
-            gz_parts=grad_parts,
-            final=((6, GROUP, shard, inner), BF16),
+            go_sum=grad_sum,
+            gx_sum=grad_sum,
+            gz_sum=grad_sum,
             gbc=bc_grad,
             gdt=dt_grad,
             wide=wide_grad,

time: 447 us -> 431 us (0.964)
  the two profiles are of different devices: /device:TPU:9 before, /device:TPU:0 now
where the time goes in v7:
time: 431 us; the launch traced here: 425 us
  Pallas kernels  416 us (97%)
  local copies, waits for them, and re-layouts  8.32 us (2%)
    pallas_call x4, Pallas kernels, call(): pl.pallas_call(kernel, out_shape=tuple((jax.ShapeDtypeStruct(*a) for a in...  416 us

profile of v7, /device:TPU:0, one launch (start us, length us, event | category | flops | bytes accessed | tf_op | source)
XLA Modules:
  0.0 424.8 jit_solution(9144176953440108463)
XLA Ops:
  0.6 141.1 %shard_map.194 = (bf16[1536,1152]{1,0:T(8,128)(2,1)}, bf16[384,384]{1,0:T(8,128)(2,1)}, bf16[1040,1536]{1,0:T(8,128)(2,1)}, f32[128,1536]{1,0:T(8,128)}, f32[128...) custom-call(bf16[256,1536]{1,0:T(8,128)(2,1)} %bitcast.16, ...), custom_call_target="tpu_custom_call" | custom-call | tf_op jit(solution)/shard_map/pallas_call | solution.py:1667
  141.7 68.7 %shard_map.195 = (bf16[256,1536]{1,0:T(8,128)(2,1)}, f32[8,1024]{1,0:T(8,128)}, bf16[1536,384]{1,0:T(8,128)(2,1)}, f32[1024,384]{1,0:T(8,128)}, bf16[1024,384]{1...) custom-call(bf16[1040,1536]{1,0:T(8,128)(2,1)} %get-tuple-element.68, ...), custom_call_target="tpu_custom_call" | custom-call | tf_op jit(solution)/shard_map/pallas_call | solution.py:1667
  210.4 94.7 %shard_map.196 = (bf16[1024,1536]{1,0:T(8,128)(2,1)}, f32[8,1024]{1,0:T(8,128)}, f32[128,1536]{1,0:T(8,128)}, bf16[4,96,384]{2,1,0:T(8,128)(2,1)}, bf16[4,96,384...) custom-call(bf16[1024,1536]{1,0:T(8,128)(2,1)} %get-tuple-element.74, ...), custom_call_target="tpu_custom_call" | custom-call | tf_op jit(solution)/shard_map/pallas_call | solution.py:1667
  305.1 0.0 copy-start.1
  305.1 111.1 %shard_map.197 = (bf16[256,1536]{1,0:T(8,128)(2,1)}, bf16[2,96,256]{2,1,0:T(8,128)(2,1)}, bf16[2,1536]{1,0:T(2,128)(2,1)}, bf16[2,2,96,1536]{3,2,1,0:T(8,128)(2,...) custom-call(bf16[1024,1536]{1,0:T(8,128)(2,1)} %get-tuple-element.90, ...), custom_call_target="tpu_custom_call" | custom-call | tf_op jit(solution)/shard_map/pallas_call | solution.py:1667
  416.2 0.0 copy-start.2
  416.2 0.0 copy-done.1
  416.2 0.0 copy-start.8
  416.2 0.0 copy-start
  416.2 0.9 copy.33
  417.1 0.5 copy-done.2
  417.6 0.9 copy.34
  418.6 0.6 copy.35
  419.2 1.0 copy.36
  420.2 0.6 copy.37
  420.8 0.0 copy-done.4
  420.8 0.6 copy.38
  421.4 0.6 copy.39
  422.0 0.0 copy-done.9
  422.0 0.6 copy.40
  422.6 0.6 copy.41
  423.2 0.0 copy-done.7
  423.2 0.6 copy.42
  423.8 0.8 copy.43
  (13 shorter events, 0.0 us)
Async XLA Ops:
  305.1 111.1 %copy-start.1 = (bf16[256,1536]{1,0:T(8,128)(2,1)S(1)}, bf16[256,1536]{1,0:T(8,128)(2,1)}, u32[]{:S(2)}) copy-start(bf16[256,1536]{1,0:T(8,128)(2,1)} %get-tuple-element.73) | copy-start | bytes 2359300
  416.2 1.4 copy-start.2
  416.2 2.3 copy-start.8
  416.2 2.9 copy-start
  418.5 1.7 copy-start.6
  418.5 2.3 copy-start.4
  418.5 2.9 copy-start.5
  418.5 3.5 copy-start.9
  418.5 4.1 copy-start.10
  418.5 4.7 %copy-start.7 = (bf16[2,1536]{1,0:T(2,128)(2,1)S(1)}, bf16[2,1536]{1,0:T(2,128)(2,1)}, u32[]{:S(2)}) copy-start(bf16[2,1536]{1,0:T(2,128)(2,1)} %get-tuple-element.145) | copy-start | bytes 18436
  418.5 5.2 %copy-start.3 = (bf16[2,96,1536]{2,1,0:T(8,128)(2,1)S(1)}, bf16[2,96,1536]{2,1,0:T(8,128)(2,1)}, u32[]{:S(2)}) copy-start(bf16[2,96,1536]{2,1,0:T(8,128)(2,1)} %get-tuple-element.124) | copy-start | bytes 1769476

commit v8 on v7

--- a/solution.py
+++ b/solution.py
@@ -747,34 +747,46 @@
     def __init__(self, links, out, base):
         self.links, self.out, self.base = links, out, base
 
-        def place(k, c):
-            row = base + lax.bitwise_xor(links.p, jnp.int32(k)) * (2 * HALF) + c * HALF
-            return out.at[pl.ds(pl.multiple_of(row, EDGE), HALF), :]
-
-        own = place(0, links.c)
-        self.out_copies = [links.copy(own, own, links.at(k, 0)) for k in (3, 1, 2)]
-        self.shared = [links.copy(own, own, links.at(0, 1))]
-        self.shared += [links.copy(place(k, links.c), place(k, links.c), links.at(0, 1)) for k in (1, 2, 3)]
-        self.arrivals = [self.out_copies[1], self.out_copies[2], self.out_copies[0]]
+        def place(k, half=None):
+            row = base + lax.bitwise_xor(links.p, jnp.int32(k)) * (2 * HALF) + links.c * HALF
+            if half is None:
+                return out.at[pl.ds(pl.multiple_of(row, EDGE), HALF), :]
+            return out.at[pl.ds(pl.multiple_of(row + half * (HALF // 2), EDGE), HALF // 2), :]
+
+        def send(k, half, to, e=0):
+            return links.copy(place(k, half), place(k, half), links.at(to, e))
+
+        self.near = {(to, half): send(0, half, to) for half in range(2) for to in (1, 2)}
+        self.relays = {0: send(1, 0, 2), 1: send(2, 1, 1)}
+        self.own_share = send(0, None, 0, 1)
+        self.shares = {(k, half): send(k, half, 0, 1) for k in (1, 2, 3) for half in range(2)}
 
     def own(self, start, size):
         row = self.base + self.links.p * (2 * HALF) + self.links.c * HALF + start
         return pl.ds(pl.multiple_of(row, EDGE), size)
 
     def start(self):
-        for copy in self.out_copies:
-            copy.start()
-        self.shared[0].start()
+        for which in ((1, 0), (2, 1), (1, 1), (2, 0)):
+            self.near[which].start()
+        self.own_share.start()
 
     def pass_on(self):
-        for k in range(3):
-            self.arrivals[k].wait_recv()
-            self.shared[k + 1].start()
+        for k, half in ((1, 0), (2, 1)):
+            self.near[k, half].wait_recv()
+            self.relays[half].start()
+            self.shares[k, half].start()
+        for k, half in ((1, 1), (2, 0)):
+            self.near[k, half].wait_recv()
+            self.shares[k, half].start()
+        for half in range(2):
+            self.relays[half].wait_recv()
+            self.shares[3, half].start()
 
     def finish(self):
-        for copy in self.shared:
+        shares = [self.own_share, *self.shares.values()]
+        for copy in shares:
             copy.wait_recv()
-        for copy in self.shared + self.out_copies:
+        for copy in [*shares, *self.near.values(), *self.relays.values()]:
             copy.wait_send()
 
 
@@ -816,14 +828,20 @@
 
 
 class Scatter:
-    def __init__(self, links, part, base, sib, total, peer):
+    def __init__(self, links, part, base, sib, total, peer, via):
         self.links, self.part, self.base = links, part, base
-        self.sib, self.total, self.peer = sib, total, peer
+        self.sib, self.total, self.peer, self.via = sib, total, peer, via
         other = 1 - links.c
         self.to_sibling = {
             k: links.copy(part.at[self.rows(k, other, 0, HALF), :], sib.at[k], links.at(0, 1)) for k in (3, 1, 2, 0)
         }
-        self.to_peer = {k: links.copy(total.at[k - 1], peer.at[k - 1], links.at(k, 0)) for k in (3, 1, 2)}
+        halves = [slice(0, HALF // 2), slice(HALF // 2, HALF)]
+        self.across = [links.copy(total.at[2, halves[i]], via.at[i], links.at(i + 1, 0)) for i in range(2)]
+        self.to_peer = {
+            (k, i): links.copy(total.at[k - 1, halves[i]], peer.at[k - 1, halves[i]], links.at(k, 0))
+            for k in (1, 2)
+            for i in range(2)
+        }
 
     def rows(self, k, c, start, size):
         row = self.base + lax.bitwise_xor(self.links.p, jnp.int32(k)) * (2 * HALF) + c * HALF + start
@@ -832,6 +850,17 @@
     def pass_on(self, k):
         self.to_sibling[k].wait_recv()
         if k == 0:
+            for i in (1, 0):
+                self.across[i].wait_recv()
+
+                def join(j, _, i=i):
+                    at = pl.ds(pl.multiple_of(i * (HALF // 2) + j * 32, 32), 32)
+                    came = self.via[i, pl.ds(pl.multiple_of(j * 32, 32), 32), :].astype(F32)
+                    self.total[1 - i, at, :] = (self.total[1 - i, at, :].astype(F32) + came).astype(BF16)
+                    return 0
+
+                lax.fori_loop(0, HALF // 64, join, 0)
+                self.to_peer[2 - i, i].start()
             return
 
         def add(i, _):
@@ -841,7 +870,8 @@
             return 0
 
         lax.fori_loop(0, HALF // 32, add, 0)
-        self.to_peer[k].start()
+        for copy in self.across if k == 3 else [self.to_peer[k, k - 1]]:
+            copy.start()
 
     def arrive(self):
         for copy in self.to_peer.values():
@@ -850,12 +880,12 @@
     def own(self, start, size):
         at = pl.ds(start, size)
         total = self.part[self.rows(0, self.links.c, start, size), :].astype(F32) + self.sib[0, at, :].astype(F32)
-        for k in range(3):
+        for k in range(2):
             total = total + self.peer[k, at, :].astype(F32)
         return total
 
     def finish(self):
-        for copy in list(self.to_sibling.values()) + list(self.to_peer.values()):
+        for copy in [*self.to_sibling.values(), *self.across, *self.to_peer.values()]:
             copy.wait_send()
 
 
@@ -1255,8 +1285,9 @@
     r.flush(r.z, r.xin, r.bcin, r.x, r.bc, r.dtraw, r.dt, r.s, r.decay)
     wo_chain.advance()
     mix_within_spans(r.x, r.bc, r.s, r.dt, r.y)
+    meanwhile()
     wo_chain.complete()
-    meanwhile()
+    r.flush(r.wo)
     carried.arrive()
     chain_states(entering_state(links.z, links.groups, r.states_in, r.decays_in, False), r.local, r.decay, r.states)
     scatter_blocks(
@@ -1282,7 +1313,7 @@
     chain, share = weight_chain(links, r.w, r.dt_rows, inner)
     chain_o = out_chain(links, r.wo)
     next_chain, next_share = weight_chain(links, r.next_w, r.next_dt_rows, inner)
-    scatter = Scatter(links, r.part, 0, r.sib, r.total, r.peer)
+    scatter = Scatter(links, r.part, 0, r.sib, r.total, r.peer, r.via)
     small = SmallSum(links, r.squares, r.slots)
     next_gather = Gather(links, r.next_normed, EDGE)
     next_edge = EdgeForward(links, next_gather)
@@ -1329,12 +1360,11 @@
             swap.settle()
         next_chain.begin()
         other.pass_on()
-        r.flush(r.wo)
 
     carried = forward_layer(links, r, r.normed, r.w, r.wo, chain_o, scatter, meanwhile)
     small.start()
+    scatter.pass_on(0)
     next_chain.advance()
-    scatter.pass_on(0)
     scatter.arrive()
     inv = lax.rsqrt(small.total() * (1.0 / inner_all) + EPS)
     r.inv_out[...] = inv
@@ -1370,10 +1400,11 @@
 
 def second_kernel(inner_all, r):
     links = Links(r.sends, r.recvs)
+    r.fetch(r.normed, r.w)
     rows = r.wo_own.shape[0]
     keep = links.local(r.wo_own, r.wo.at[pl.ds(pl.multiple_of(links.z * rows, EDGE), rows), :])
     chain_o = out_chain(links, r.wo)
-    scatter = Scatter(links, r.part, 0, r.sib, r.total, r.peer)
+    scatter = Scatter(links, r.part, 0, r.sib, r.total, r.peer, r.via)
     small = SmallSum(links, r.squares, r.slots)
     spread = SmallGather(links, r.scalars_out)
     at = pl.ds(pl.multiple_of(links.c * HALF, HALF), HALF)
@@ -1384,7 +1415,8 @@
     keep.wait()
     links.meet()
     chain_o.begin()
-    carried = forward_layer(links, r, r.normed, r.w, r.wo, chain_o, scatter, lambda: r.flush(r.wo))
+    r.need(r.normed, r.w)
+    carried = forward_layer(links, r, r.normed, r.w, r.wo, chain_o, scatter, lambda: None)
     small.start()
     scatter.pass_on(0)
     scatter.arrive()
@@ -1449,7 +1481,7 @@
 def third_kernel(inner_all, r):
     links = Links(r.sends, r.recvs)
     r.fetch(r.dt, r.states, r.dtraw, r.xin, r.bcin, r.w, r.normed, r.grad, r.resid, r.mixed)
-    scatter = Scatter(links, r.part, EDGE, r.sib, r.total, r.peer)
+    scatter = Scatter(links, r.part, EDGE, r.sib, r.total, r.peer, r.via)
     edge = EdgeBackward(links, r.part, r.edge_slots)
     gather = Gather(links, r.dmix_out, 0)
     spread = SmallGather(links, r.scalars_out)
@@ -1506,7 +1538,7 @@
 def fourth_kernel(inner_all, r):
     links = Links(r.sends, r.recvs)
     r.fetch(r.dt, r.states, r.dtraw, r.xin, r.bcin, r.above_bc, r.above_x, r.above_z, r.above_o, r.normed, r.w, r.grad, r.resid)
-    scatter = Scatter(links, r.part, EDGE, r.sib, r.total, r.peer)
+    scatter = Scatter(links, r.part, EDGE, r.sib, r.total, r.peer, r.via)
     edge = EdgeBackward(links, r.part, r.edge_slots)
     at = pl.ds(pl.multiple_of(links.c * HALF, HALF), HALF)
     share = links.copy(r.out.at[at, :], r.out.at[at, :], links.at(0, 1))
@@ -1702,7 +1734,8 @@
     scatter_scratch = dict(
         sib=((GROUP, HALF, model), BF16),
         total=((GROUP - 1, HALF, model), BF16),
-        peer=((GROUP - 1, HALF, model), BF16),
+        peer=((2, HALF, model), BF16),
+        via=((2, HALF // 2, model), BF16),
     )
     state_scratch = dict(
         state_low=((STATE, inner), BF16),
@@ -1748,7 +1781,7 @@
     first = call(
         functools.partial(first_kernel, inner_all),
         0,
-        160 + 14 * (groups - 1) + 2 * groups,
+        200 + 14 * (groups - 1) + 2 * groups,
         dict(
             next_w=w_shape,
             next_wo=((rows, inner), BF16),
@@ -1787,14 +1820,12 @@
         dict(block_out=((length, model), BF16), scalars_out=scalars),
         dict(wo=wo_shape, **saved_shapes),
         dict(
-            normed=first.next_normed,
-            w=first.next_w,
             wo_own=first.next_wo,
             **params,
             resid=first.fresh_out,
             cot=first.cot_out,
         ),
-        dict(),
+        dict(normed=first.next_normed, w=first.next_w),
         dict(**forward_scratch, **param_scratch),
     )
     grad_in = ((groups - 1, rows, inner), BF16)

time: 431 us -> 423 us (0.981)
  Pallas kernels: 416 us -> 408 us
    pallas_call x4, Pallas kernels: 416 us -> 408 us  [call(): pl.pallas_call(kernel, out_shape=tuple((jax.ShapeDtypeStruct(*a) for a in...]
where the time goes in v8:
time: 423 us; the launch traced here: 417 us
  Pallas kernels  408 us (96%)
  local copies, waits for them, and re-layouts  8.32 us (2%)
    pallas_call x4, Pallas kernels, call(): pl.pallas_call(kernel, out_shape=tuple((jax.ShapeDtypeStruct(*a) for a in...  408 us

profile of v8, /device:TPU:0, one launch (start us, length us, event | category | flops | bytes accessed | tf_op | source)
XLA Modules:
  0.0 417.3 jit_solution(12207453660535575952)
XLA Ops:
  0.6 138.6 %shard_map.194 = (bf16[1536,1152]{1,0:T(8,128)(2,1)}, bf16[384,384]{1,0:T(8,128)(2,1)}, bf16[1040,1536]{1,0:T(8,128)(2,1)}, f32[128,1536]{1,0:T(8,128)}, f32[128...) custom-call(bf16[256,1536]{1,0:T(8,128)(2,1)} %bitcast.16, ...), custom_call_target="tpu_custom_call" | custom-call | tf_op jit(solution)/shard_map/pallas_call | solution.py:1699
  139.2 64.9 %shard_map.195 = (bf16[256,1536]{1,0:T(8,128)(2,1)}, f32[8,1024]{1,0:T(8,128)}, bf16[1536,384]{1,0:T(8,128)(2,1)}, f32[1024,384]{1,0:T(8,128)}, bf16[1024,384]{1...) custom-call(bf16[384,384]{1,0:T(8,128)(2,1)} %get-tuple-element.68.r, ...), custom_call_target="tpu_custom_call" | custom-call | tf_op jit(solution)/shard_map/pallas_call | solution.py:1699
  204.1 96.1 %shard_map.196 = (bf16[1024,1536]{1,0:T(8,128)(2,1)}, f32[8,1024]{1,0:T(8,128)}, f32[128,1536]{1,0:T(8,128)}, bf16[4,96,384]{2,1,0:T(8,128)(2,1)}, bf16[4,96,384...) custom-call(bf16[1024,1536]{1,0:T(8,128)(2,1)} %get-tuple-element.74, ...), custom_call_target="tpu_custom_call" | custom-call | tf_op jit(solution)/shard_map/pallas_call | solution.py:1699
  300.2 0.0 copy-start.1
  300.2 108.5 %shard_map.197 = (bf16[256,1536]{1,0:T(8,128)(2,1)}, bf16[2,96,256]{2,1,0:T(8,128)(2,1)}, bf16[2,1536]{1,0:T(2,128)(2,1)}, bf16[2,2,96,1536]{3,2,1,0:T(8,128)(2,...) custom-call(bf16[1024,1536]{1,0:T(8,128)(2,1)} %get-tuple-element.90, ...), custom_call_target="tpu_custom_call" | custom-call | tf_op jit(solution)/shard_map/pallas_call | solution.py:1699
  408.7 0.0 copy-start.2
  408.7 0.0 copy-done.1
  408.7 0.9 copy.33
  409.6 0.5 copy-done.2
  410.1 0.9 copy.34
  411.0 0.0 copy-done.8
  411.1 0.6 copy.35
  411.7 1.0 copy.36
  412.7 0.6 copy.37
  413.3 0.0 copy-done.4
  413.3 0.6 copy.38
  413.9 0.6 copy.39
  414.5 0.0 copy-done.9
  414.5 0.6 copy.40
  415.1 0.0 copy-done.10
  415.1 0.6 copy.41
  415.7 0.0 copy-done.7
  415.7 0.6 copy.42
  416.3 0.8 copy.43
  (13 shorter events, 0.0 us)
Async XLA Ops:
  300.2 108.5 %copy-start.1 = (bf16[256,1536]{1,0:T(8,128)(2,1)S(1)}, bf16[256,1536]{1,0:T(8,128)(2,1)}, u32[]{:S(2)}) copy-start(bf16[256,1536]{1,0:T(8,128)(2,1)} %get-tuple-element.73) | copy-start | bytes 2359300
  408.7 1.4 copy-start.2
  408.7 2.3 copy-start.8
  408.7 2.9 copy-start
  411.0 1.7 copy-start.6
  411.0 2.3 copy-start.4
  411.0 2.9 copy-start.5
  411.0 3.5 copy-start.9
  411.0 4.1 copy-start.10
  411.0 4.7 %copy-start.7 = (bf16[2,1536]{1,0:T(2,128)(2,1)S(1)}, bf16[2,1536]{1,0:T(2,128)(2,1)}, u32[]{:S(2)}) copy-start(bf16[2,1536]{1,0:T(2,128)(2,1)} %get-tuple-element.145) | copy-start | bytes 18436
  411.0 5.2 %copy-start.3 = (bf16[2,96,1536]{2,1,0:T(8,128)(2,1)S(1)}, bf16[2,96,1536]{2,1,0:T(8,128)(2,1)}, u32[]{:S(2)}) copy-start(bf16[2,96,1536]{2,1,0:T(8,128)(2,1)} %get-tuple-element.124) | copy-start | bytes 1769476

commit v9 on v8

--- a/solution.py
+++ b/solution.py
@@ -318,7 +318,7 @@
 def back_through_states(
     grad, prior, decay, states, dy_in, x, bc, s_in, dt_in, dtraw, xin, bcin, rowp, bcp, headp, flow_in, sum_in,
     cat_out, row_out, bcrow_out,
-    dpre, dend, at_block,
+    dpre, dend,
 ):
     inner = x.shape[1]
     spans = x.shape[0] // SPAN
@@ -348,7 +348,6 @@
         tok = pl.ds(at, SPAN)
         after = pl.ds(pl.multiple_of(at + EDGE, EDGE), SPAN)
         window = pl.ds(at, SPAN + EDGE)
-        at_block(q)
         x_low, dy = x[tok, :], dy_in[tok, :]
         xf, dyf = x_low.astype(F32), dy.astype(F32)
         b, c = bc[tok, :STATE], bc[tok, STATE:]
@@ -1277,7 +1276,7 @@
     carried = States(links, False, r.state_low, r.decay_row, r.states_in, r.decays_in)
     state_sum, decay_all = project_and_convolve(
         normed, w, r.rowp, r.bcp, r.headp, r.z, r.xin, r.bcin, r.x, r.bc, r.dtraw, r.dt, r.s, r.decay, r.ext, r.local,
-        lambda q: pl.when(q == 3)(wo_chain.advance),
+        lambda q: pl.when(q == 2)(wo_chain.advance),
     )
     r.state_low[...] = state_sum.astype(BF16)
     r.decay_row[...] = jnp.broadcast_to(decay_all, r.decay_row.shape)
@@ -1442,7 +1441,7 @@
     r.done()
 
 
-def backward_layer(links, inner_all, r, at_start, before_collect, at_middle):
+def backward_layer(links, inner_all, r, z_collect, at_start, before_collect, at_middle):
     carried = States(links, True, r.state_low, r.decay_row, r.states_in, r.decays_in)
     collect = Halve(links, r.gwo, r.go_in, r.go_sum)
     grad_sum, decay_all = back_through_gate(
@@ -1457,6 +1456,9 @@
     out_gradient(r.dmix, r.normed_out, r.gwo)
     before_collect()
     collect.begin()
+    r.need(r.normed)
+    z_gradient(r.cat, r.normed, r.gz)
+    z_collect.begin()
     r.need(r.dt)
     back_within_spans(r.dy, r.x, r.bc, r.s, r.dt, r.dpre, r.flow, r.sums)
     at_middle()
@@ -1466,8 +1468,8 @@
     back_through_states(
         grad, r.prior, r.decay, r.states, r.dy, r.x, r.bc, r.s, r.dt, r.dtraw, r.xin, r.bcin, r.rowp, r.bcp, r.headp,
         r.flow, r.sums, r.cat, r.wide, r.bc_rows, r.dpre, r.prior,
-        lambda q: pl.when(q == 2)(collect.advance),
     )
+    collect.advance()
     return carried, collect
 
 
@@ -1485,12 +1487,12 @@
     edge = EdgeBackward(links, r.part, r.edge_slots)
     gather = Gather(links, r.dmix_out, 0)
     spread = SmallGather(links, r.scalars_out)
-    collects = [Halve(links, r.gx, r.gx_in, r.gx_sum), Halve(links, r.gwo, r.gz_in, r.gz_sum)]
+    collects = [Halve(links, r.gx, r.gx_in, r.gx_sum), Halve(links, r.gz, r.gz_in, r.gz_sum)]
     r.edge_slots[...] = jnp.zeros_like(r.edge_slots)
     links.greet(plane=True, groups=True, edge=-1)
     prepare(links, r, 1)
-    carried, collect = backward_layer(links, inner_all, r, lambda: None, lambda: None, lambda: None)
-    r.need(r.w, r.normed)
+    carried, collect = backward_layer(links, inner_all, r, collects[1], lambda: None, lambda: None, lambda: None)
+    r.need(r.w)
     x_gradient(r.cat, r.normed, r.gx)
     collects[0].begin()
     project_back_edge(r.cat, r.w, r.part)
@@ -1499,10 +1501,7 @@
     scatter.pass_on(0)
     small_gradients(r.cat, r.normed, r.gbc, r.gdt)
     collect.complete()
-    collect.finish()
-    z_gradient(r.cat, r.normed, r.gwo)
-    collects[1].begin()
-    collects[0].advance()
+    collects[1].advance()
     scatter.arrive()
     edge.receive()
     r.need(r.grad, r.resid, r.mixed)
@@ -1522,16 +1521,16 @@
     model = r.gain_row.shape[1]
     put_vector(r.vec, model // 128, r.gain_row[0:1])
     put_vector(r.vec, 2 * (model // 128) + 2 * (CONV + 1), r.bc_rows[0 : CONV + 1])
-    collects[1].advance()
+    collects[0].advance()
     gather.pass_on()
-    collects[0].complete()
+    collects[1].complete()
     scatter.finish()
     edge.finish()
     gather.finish()
     spread.finish()
     carried.finish()
-    collects[1].complete()
-    for one in collects:
+    collects[0].complete()
+    for one in [collect] + collects:
         one.finish()
 
 
@@ -1542,7 +1541,7 @@
     edge = EdgeBackward(links, r.part, r.edge_slots)
     at = pl.ds(pl.multiple_of(links.c * HALF, HALF), HALF)
     share = links.copy(r.out.at[at, :], r.out.at[at, :], links.at(0, 1))
-    collects = [Halve(links, r.gx, r.gx_in, r.gx_sum), Halve(links, r.gwo, r.gz_in, r.gz_sum)]
+    collects = [Halve(links, r.gx, r.gx_in, r.gx_sum), Halve(links, r.gz, r.gz_in, r.gz_sum)]
     above = ((r.above_x, r.g_zx.at[1, 1]), (r.above_z, r.g_zx.at[1, 0]), (r.above_o, r.g_out.at[1]))
     own = ((r.go_sum, r.g_out.at[0]), (r.gx_sum, r.g_zx.at[0, 1]), (r.gz_sum, r.g_zx.at[0, 0]))
     delivers = [Deliver(links, parts, out) for parts, out in above]
@@ -1567,8 +1566,7 @@
         for deliver in delivers:
             deliver.start()
 
-    carried, collect = backward_layer(links, inner_all, r, at_start, bc_sums[1].plane, at_middle)
-    r.need(r.normed)
+    carried, collect = backward_layer(links, inner_all, r, collects[1], at_start, bc_sums[1].plane, at_middle)
     small_gradients(r.cat, r.normed, r.gbc, r.gdt)
     bc_sums[0].cores()
     r.steps_all[:, 0:EDGE, :] = r.gdt[...]
@@ -1586,11 +1584,8 @@
     scatter.pass_on(0)
     bc_sums[0].groups()
     collect.complete()
-    collect.finish()
-    z_gradient(r.cat, r.normed, r.gwo)
-    collects[1].begin()
-    collects[0].advance()
     own_delivers[0].start()
+    collects[1].advance()
     scatter.arrive()
     edge.receive()
     r.need(r.grad, r.resid)
@@ -1604,18 +1599,18 @@
     put_vector(r.vec, 2 * (r.gain_row.shape[1] // 128), r.bc_rows[0 : CONV + 1])
     vec_sum.plane()
     vec_sum.groups()
-    collects[1].advance()
+    collects[0].advance()
     bc_sums[1].share()
     laid.plane()
-    collects[0].complete()
-    own_delivers[1].start()
+    collects[1].complete()
+    own_delivers[2].start()
     laid.finish()
     lay_out_heads(links, r)
     bc_sums[0].share()
     vec_sum.back()
-    collects[1].complete()
-    own_delivers[2].start()
-    for one in bc_sums + [scatter, edge, carried] + collects:
+    collects[0].complete()
+    own_delivers[1].start()
+    for one in bc_sums + [scatter, edge, carried, collect] + collects:
         one.finish()
     vec_sum.finish()
     lay_out_vector(r)
@@ -1846,6 +1841,7 @@
         bc_rows=((8, 2 * STATE), F32),
         part=edged_rows,
         gx=wo_shape,
+        gz=wo_shape,
         go_in=grad_in,
         gx_in=grad_in,
         gz_in=grad_in,

time: 423 us -> 411 us (0.972)
  Pallas kernels: 408 us -> 395 us
    pallas_call x4, Pallas kernels: 408 us -> 395 us  [call(): pl.pallas_call(kernel, out_shape=tuple((jax.ShapeDtypeStruct(*a) for a in...]
where the time goes in v9:
time: 411 us; the launch traced here: 404 us
  Pallas kernels  395 us (96%)
  local copies, waits for them, and re-layouts  8.32 us (2%)
    pallas_call x4, Pallas kernels, call(): pl.pallas_call(kernel, out_shape=tuple((jax.ShapeDtypeStruct(*a) for a in...  395 us
    unnamed x33, local copies, waits for them, and re-layouts  8.32 us

profile of v9, /device:TPU:0, one launch (start us, length us, event | category | flops | bytes accessed | tf_op | source)
XLA Modules:
  0.0 404.3 jit_solution(18105126682359098361)
XLA Ops:
  0.6 138.6 %shard_map.194 = (bf16[1536,1152]{1,0:T(8,128)(2,1)}, bf16[384,384]{1,0:T(8,128)(2,1)}, bf16[1040,1536]{1,0:T(8,128)(2,1)}, f32[128,1536]{1,0:T(8,128)}, f32[128...) custom-call(bf16[256,1536]{1,0:T(8,128)(2,1)} %bitcast.16, ...), custom_call_target="tpu_custom_call" | custom-call | tf_op jit(solution)/shard_map/pallas_call | solution.py:1694
  139.2 64.9 %shard_map.195 = (bf16[256,1536]{1,0:T(8,128)(2,1)}, f32[8,1024]{1,0:T(8,128)}, bf16[1536,384]{1,0:T(8,128)(2,1)}, f32[1024,384]{1,0:T(8,128)}, bf16[1024,384]{1...) custom-call(bf16[384,384]{1,0:T(8,128)(2,1)} %get-tuple-element.68.r, ...), custom_call_target="tpu_custom_call" | custom-call | tf_op jit(solution)/shard_map/pallas_call | solution.py:1694
  204.1 92.8 %shard_map.196 = (bf16[1024,1536]{1,0:T(8,128)(2,1)}, f32[8,1024]{1,0:T(8,128)}, f32[128,1536]{1,0:T(8,128)}, bf16[4,96,384]{2,1,0:T(8,128)(2,1)}, bf16[4,96,384...) custom-call(bf16[1024,1536]{1,0:T(8,128)(2,1)} %get-tuple-element.74, ...), custom_call_target="tpu_custom_call" | custom-call | tf_op jit(solution)/shard_map/pallas_call | solution.py:1694
  296.8 0.0 copy-start.1
  296.9 98.8 %shard_map.197 = (bf16[256,1536]{1,0:T(8,128)(2,1)}, bf16[2,96,256]{2,1,0:T(8,128)(2,1)}, bf16[2,1536]{1,0:T(2,128)(2,1)}, bf16[2,2,96,1536]{3,2,1,0:T(8,128)(2,...) custom-call(bf16[1024,1536]{1,0:T(8,128)(2,1)} %get-tuple-element.90, ...), custom_call_target="tpu_custom_call" | custom-call | tf_op jit(solution)/shard_map/pallas_call | solution.py:1694
  395.6 0.0 copy-start.2
  395.6 0.0 copy-done.1
  395.6 0.0 copy-start.8
  395.7 0.0 copy-start
  395.7 0.9 copy.33
  396.6 0.5 copy-done.2
  397.0 0.9 copy.34
  397.9 0.0 copy-done.8
  397.9 0.0 copy-start.9
  398.0 0.6 copy.35
  398.6 0.0 copy-done
  398.6 1.0 copy.36
  399.6 0.6 copy.37
  400.2 0.6 copy.38
  400.8 0.6 copy.39
  401.5 0.6 copy.40
  402.0 0.6 copy.41
  402.6 0.6 copy.42
  403.2 0.8 copy.43
  (13 shorter events, 0.0 us)
Async XLA Ops:
  296.8 98.8 %copy-start.1 = (bf16[256,1536]{1,0:T(8,128)(2,1)S(1)}, bf16[256,1536]{1,0:T(8,128)(2,1)}, u32[]{:S(2)}) copy-start(bf16[256,1536]{1,0:T(8,128)(2,1)} %get-tuple-element.73) | copy-start | bytes 2359300
  395.6 1.4 copy-start.2
  395.6 2.3 copy-start.8
  395.7 2.9 copy-start
  397.9 1.7 copy-start.6
  397.9 2.3 copy-start.4
  397.9 2.9 copy-start.5
  397.9 3.5 copy-start.9
  397.9 4.1 %copy-start.10 = (bf16[3,2,24]{2,1,0:T(2,128)(2,1)S(1)}, bf16[3,2,24]{2,1,0:T(2,128)(2,1)}, u32[]{:S(2)}) copy-start(bf16[3,2,24]{2,1,0:T(2,128)(2,1)} %get-tuple-element.122) | copy-start | bytes 868
  398.0 4.7 %copy-start.7 = (bf16[2,1536]{1,0:T(2,128)(2,1)S(1)}, bf16[2,1536]{1,0:T(2,128)(2,1)}, u32[]{:S(2)}) copy-start(bf16[2,1536]{1,0:T(2,128)(2,1)} %get-tuple-element.145) | copy-start | bytes 18436
  398.0 5.2 %copy-start.3 = (bf16[2,96,1536]{2,1,0:T(8,128)(2,1)S(1)}, bf16[2,96,1536]{2,1,0:T(8,128)(2,1)}, u32[]{:S(2)}) copy-start(bf16[2,96,1536]{2,1,0:T(8,128)(2,1)} %get-tuple-element.124) | copy-start | bytes 1769476

commit v10 on v9

--- a/solution.py
+++ b/solution.py
@@ -559,8 +559,8 @@
                 found.append((sending, z + step < groups, links.copy(block, block, (z - 1, p, c))))
             self.steps.append(found)
 
-    def begin(self):
-        for sending, _, copy in self.steps[0]:
+    def begin(self, piece=None):
+        for sending, _, copy in self.steps[0] if piece is None else self.steps[0][2 * piece : 2 * piece + 2]:
             pl.when(sending)(copy.start)
 
     def advance(self):
@@ -1331,9 +1331,9 @@
     links.meet()
     for swap in swaps:
         swap.start()
-    for swap in swaps:
+    for i, swap in enumerate(swaps):
         swap.settle()
-    chain.begin()
+        chain.begin(i)
     gather.start()
     edge.start()
     swap_o.start()

time: 411 us -> 406 us (0.988)
  Pallas kernels: 395 us -> 390 us
    pallas_call x4, Pallas kernels: 395 us -> 390 us  [call(): pl.pallas_call(kernel, out_shape=tuple((jax.ShapeDtypeStruct(*a) for a in...]
where the time goes in v10:
time: 406 us; the launch traced here: 399 us
  Pallas kernels  390 us (96%)
  local copies, waits for them, and re-layouts  8.32 us (2%)
    pallas_call x4, Pallas kernels, call(): pl.pallas_call(kernel, out_shape=tuple((jax.ShapeDtypeStruct(*a) for a in...  390 us
    unnamed x33, local copies, waits for them, and re-layouts  8.32 us

profile of v10, /device:TPU:0, one launch (start us, length us, event | category | flops | bytes accessed | tf_op | source)
XLA Modules:
  0.0 399.0 jit_solution(6778322973876141246)
XLA Ops:
  0.6 133.4 %shard_map.194 = (bf16[1536,1152]{1,0:T(8,128)(2,1)}, bf16[384,384]{1,0:T(8,128)(2,1)}, bf16[1040,1536]{1,0:T(8,128)(2,1)}, f32[128,1536]{1,0:T(8,128)}, f32[128...) custom-call(bf16[256,1536]{1,0:T(8,128)(2,1)} %bitcast.16, ...), custom_call_target="tpu_custom_call" | custom-call | tf_op jit(solution)/shard_map/pallas_call | solution.py:1694
  134.1 64.7 %shard_map.195 = (bf16[256,1536]{1,0:T(8,128)(2,1)}, f32[8,1024]{1,0:T(8,128)}, bf16[1536,384]{1,0:T(8,128)(2,1)}, f32[1024,384]{1,0:T(8,128)}, bf16[1024,384]{1...) custom-call(bf16[384,384]{1,0:T(8,128)(2,1)} %get-tuple-element.68.r, ...), custom_call_target="tpu_custom_call" | custom-call | tf_op jit(solution)/shard_map/pallas_call | solution.py:1694
  198.8 92.7 %shard_map.196 = (bf16[1024,1536]{1,0:T(8,128)(2,1)}, f32[8,1024]{1,0:T(8,128)}, f32[128,1536]{1,0:T(8,128)}, bf16[4,96,384]{2,1,0:T(8,128)(2,1)}, bf16[4,96,384...) custom-call(bf16[1024,1536]{1,0:T(8,128)(2,1)} %get-tuple-element.74, ...), custom_call_target="tpu_custom_call" | custom-call | tf_op jit(solution)/shard_map/pallas_call | solution.py:1694
  291.5 0.0 copy-start.1
  291.5 98.9 %shard_map.197 = (bf16[256,1536]{1,0:T(8,128)(2,1)}, bf16[2,96,256]{2,1,0:T(8,128)(2,1)}, bf16[2,1536]{1,0:T(2,128)(2,1)}, bf16[2,2,96,1536]{3,2,1,0:T(8,128)(2,...) custom-call(bf16[1024,1536]{1,0:T(8,128)(2,1)} %get-tuple-element.90, ...), custom_call_target="tpu_custom_call" | custom-call | tf_op jit(solution)/shard_map/pallas_call | solution.py:1694
  390.4 0.0 copy-start.2
  390.4 0.0 copy-done.1
  390.4 0.0 copy-start.8
  390.4 0.0 copy-start
  390.4 0.9 copy.33
  391.3 0.5 copy-done.2
  391.8 0.9 copy.34
  392.7 0.0 copy-done.8
  392.7 0.0 copy-start.9
  392.7 0.6 copy.35
  393.3 1.0 copy.36
  394.4 0.0 copy-done.6
  394.4 0.6 copy.37
  395.0 0.6 copy.38
  395.6 0.6 copy.39
  396.2 0.6 copy.40
  396.8 0.6 copy.41
  397.4 0.6 copy.42
  398.0 0.8 copy.43
  (13 shorter events, 0.0 us)
Async XLA Ops:
  291.5 98.9 %copy-start.1 = (bf16[256,1536]{1,0:T(8,128)(2,1)S(1)}, bf16[256,1536]{1,0:T(8,128)(2,1)}, u32[]{:S(2)}) copy-start(bf16[256,1536]{1,0:T(8,128)(2,1)} %get-tuple-element.73) | copy-start | bytes 2359300
  390.4 1.4 copy-start.2
  390.4 2.3 copy-start.8
  390.4 2.9 copy-start
  392.7 1.7 copy-start.6
  392.7 2.3 copy-start.4
  392.7 2.9 copy-start.5
  392.7 3.5 copy-start.9
  392.7 4.1 %copy-start.10 = (bf16[3,2,24]{2,1,0:T(2,128)(2,1)S(1)}, bf16[3,2,24]{2,1,0:T(2,128)(2,1)}, u32[]{:S(2)}) copy-start(bf16[3,2,24]{2,1,0:T(2,128)(2,1)} %get-tuple-element.122) | copy-start | bytes 868
  392.7 4.7 %copy-start.7 = (bf16[2,1536]{1,0:T(2,128)(2,1)S(1)}, bf16[2,1536]{1,0:T(2,128)(2,1)}, u32[]{:S(2)}) copy-start(bf16[2,1536]{1,0:T(2,128)(2,1)} %get-tuple-element.145) | copy-start | bytes 18436
  392.7 5.2 %copy-start.3 = (bf16[2,96,1536]{2,1,0:T(8,128)(2,1)S(1)}, bf16[2,96,1536]{2,1,0:T(8,128)(2,1)}, u32[]{:S(2)}) copy-start(bf16[2,96,1536]{2,1,0:T(8,128)(2,1)} %get-tuple-element.124) | copy-start | bytes 1769476
